TPU v7x, 128 devices: a whole 4x4x4 slice. The times are simulated.
128 devices in a mesh: inter: 16 (over z_lo, y, core), intra: 8 (over x, z_hi).
Axes of the slice: x: 4, y: 4, z: 4 (z_hi: 2, z_lo: 2; z = z_hi * 2 + z_lo), core: 2. Of those that a mesh axis runs over, the one named last changes fastest.
Arguments:
- layer_input: bfloat16 [24576, 3584], P(('inter', 'intra')), may hold values from -6 to 6
- up_cotangent: bfloat16 [24576, 10240], P(('inter', 'intra')), may hold values from -24 to 24
- master: float32 [10240, 3584], P(('intra', 'inter')), may hold values from -0.6 to 0.6
- first_moment: float32 [10240, 3584], P(('intra', 'inter')), may hold values from -6 to 6
- second_moment: float32 [10240, 3584], P(('intra', 'inter')), may hold values from 0.2 to 0.5
Outputs:
- new_master: float32 [10240, 3584], P(('intra', 'inter'))
- new_first: float32 [10240, 3584], P(('intra', 'inter'))
- new_second: float32 [10240, 3584], P(('intra', 'inter'))
- new_copy: bfloat16 [10240, 3584], P('intra')
All inputs are finite; a program needn't handle non-finite values.
Results may differ from a plain program's by a relative error of at most 0.015.
Values may be sent and summed in bfloat16 or wider, within the bound.
No kernel may reach another device: no remote copies, remote signals or barrier semaphores. Data moves between devices by JAX's collectives and lax.ppermute only.
A program may use at most 128 MiB of HBM per device.

v0:
```python
import math

import jax
import jax.numpy as jnp
from jax import lax
from jax.sharding import PartitionSpec as P


def adamw(grad, master, first_moment, second_moment):
    new_first = 0.9 * first_moment + 0.1 * grad
    new_second = 0.95 * second_moment + 0.05 * (grad * grad)
    first_hat = new_first / (1.0 - 0.9**10)
    second_hat = new_second / (1.0 - 0.95**10)
    step_dir = first_hat / (jnp.sqrt(second_hat) + 1e-08) + 0.1 * master
    new_master = master - 0.02 * step_dir
    return (new_master, new_first, new_second)


def body(layer_input, up_cotangent, master, first_moment, second_moment):
    local_tokens = layer_input.shape[0]
    inter_count = lax.axis_size("inter")
    intra_count = lax.axis_size("intra")
    total_tokens = local_tokens * inter_count * intra_count
    contract = (((0,), (0,)), ((), ()))
    hidden_part = lax.all_to_all(up_cotangent, "intra", split_axis=1, concat_axis=0, tiled=True)
    gathered = lax.all_gather(layer_input, "intra", axis=0, tiled=True)
    summed = lax.psum_scatter(
        lax.dot_general(hidden_part, gathered, contract, preferred_element_type=jnp.float32).astype(
            jnp.bfloat16
        ),
        "inter",
        scatter_dimension=0,
        tiled=True,
    ).astype(jnp.float32)
    grad = summed * (1.0 / math.sqrt(total_tokens))
    new_master, new_first, new_second = adamw(grad, master, first_moment, second_moment)
    new_copy = lax.all_gather(new_master.astype(jnp.bfloat16), "inter", axis=0, tiled=True)
    return (new_master, new_first, new_second, new_copy)


def solution(mesh):
    in_specs = (
        P(("inter", "intra"), None),
        P(("inter", "intra"), None),
        P(("intra", "inter"), None),
        P(("intra", "inter"), None),
        P(("intra", "inter"), None),
    )
    out_specs = (
        P(("intra", "inter"), None),
        P(("intra", "inter"), None),
        P(("intra", "inter"), None),
        P("intra", None),
    )
    return jax.shard_map(body, mesh=mesh, in_specs=in_specs, out_specs=out_specs, check_vma=False)
```

profile of v0, /device:TPU:1, one launch (start us, length us, event | category | flops | bytes accessed | tf_op | source)
XLA Modules:
  0.0 349.5 jit_solution(15934528967366945626)
XLA Ops:
  7.2 0.0 all-gather.3.cloned.1.call-start
  7.2 0.7 all-gather.3.cloned.1.call-update
  7.9 0.0 reduce-scatter.2.cloned.1.call-start
  7.9 2.4 copy.13
  10.3 68.4 %all_to_all.19 = bf16[192,8,1280]{2,0,1:T(8,128)(2,1)} all-to-all(bf16[192,8,1280]{2,0,1:T(8,128)(2,1)S(1)} %bitcast.9), channel_id=1, replica_groups=mesh['inter'=16,'intra'=8] {'intra'}, dimensions={1} | all-to-all | bytes 7864320 | tf_op jit(solution)/shard_map/all_to_all | solution.py:25
  78.8 102.4 %all-gather.3.cloned.1.call-done = bf16[1536,3584]{1,0:T(8,128)(2,1)} async-done(((bf16[192,3584]{1,0:T(8,128)(2,1)}), bf16[1536,3584]{1,0:T(8,128)(2,1)}) %all-gather.3.cloned.1.call-update) | async-done | bytes 11010064 | tf_op jit(solution)/shard_map/all_gather | solution.py:26
  181.2 20.6 %convolution_convert_fusion = bf16[1280,3584]{1,0:T(8,128)(2,1)} fusion(bf16[1536,1280]{1,0:T(8,128)(2,1)} %bitcast.11, bf16[1536,3584]{1,0:T(8,128)(2,1)} %all-gather.3.cloned.1.call-done), kind=kOutput, calls=%fused_computation | convolution fusion | flops 14097448960 | bytes 24117248 | tf_op jit(solution)/shard_map/dot_general | solution.py:28
  201.8 0.0 copy-start
  201.8 0.0 copy-start.1
  201.8 0.0 copy-start.2
  201.8 0.0 reduce-scatter.2.cloned.1.call-update
  201.9 0.0 all-gather.5.cloned.1.call-start
  201.9 71.4 %reduce-scatter.2.cloned.1.call-done = bf16[80,3584]{1,0:T(8,128)(2,1)} async-done(((bf16[1280,3584]{1,0:T(8,128)(2,1)}), bf16[80,3584]{1,0:T(8,128)(2,1)}) %reduce-scatter.2.cloned.1.call-update) | async-done | bytes 573456 | tf_op jit(solution)/shard_map/reduce_scatter | solution.py:27
  273.3 0.0 copy-done
  273.3 0.0 copy-done.1
  273.3 0.0 copy-done.2
  273.3 3.7 %fusion.4 = (bf16[80,3584]{1,0:T(8,128)(2,1)}, f32[80,3584]{1,0:T(8,128)}, f32[80,3584]{1,0:T(8,128)}, f32[80,3584]{1,0:T(8,128)}) fusion(f32[80,3584]{1,0:T(8,128)S(1)} %copy-done, bf16[80,3584]{1,0:T(8,128)(2,1)} %reduce-scatter.2.cloned.1.call-done, f32[80,3584]{1,0:T(8,128)S(1)} %copy-done.1, f32[80,3584]{1,0:T(8,128)S(1)} %copy-done.2), kind=kLoop, calls=%fused_computation.9 | loop fusion | flops 5160960 | bytes 8028160 | tf_op jit(solution)/shard_map/convert_element_type | solution.py:37
  277.0 0.0 all-gather.5.cloned.1.call-update
  277.0 58.1 %all-gather.5.cloned.1.call-done = bf16[1280,3584]{1,0:T(8,128)(2,1)} async-done(((bf16[80,3584]{1,0:T(8,128)(2,1)}), bf16[1280,3584]{1,0:T(8,128)(2,1)}) %all-gather.5.cloned.1.call-update) | async-done | bytes 9175056 | tf_op jit(solution)/shard_map/all_gather | solution.py:37
  335.2 7.8 %copy.15 = bf16[1280,3584]{1,0:T(8,128)(2,1)} copy(bf16[1280,3584]{1,0:T(8,128)(2,1)} %all-gather.5.cloned.1.call-done) | data formatting | bytes 18350080
Async XLA Ops:
  7.2 174.0 %all-gather.3.cloned.1.call-start = ((), (), s32[]{:S(2)}) async-start(), calls=%async_computation.2 | async-start | bytes 12386304 | tf_op jit(solution)/shard_map/all_gather | solution.py:26
  7.9 265.4 %reduce-scatter.2.cloned.1.call-start = ((), (), s32[]{:S(2)}) async-start(), calls=%async_computation.3 | async-start | bytes 9748480 | tf_op jit(solution)/shard_map/reduce_scatter | solution.py:27
  201.8 71.5 %copy-start = (f32[80,3584]{1,0:T(8,128)S(1)}, f32[80,3584]{1,0:T(8,128)}, u32[]{:S(2)}) copy-start(f32[80,3584]{1,0:T(8,128)} %param.7) | copy-start | bytes 3440644
  201.8 71.5 %copy-start.1 = (f32[80,3584]{1,0:T(8,128)S(1)}, f32[80,3584]{1,0:T(8,128)}, u32[]{:S(2)}) copy-start(f32[80,3584]{1,0:T(8,128)} %param.8) | copy-start | bytes 3440644
  201.8 71.5 %copy-start.2 = (f32[80,3584]{1,0:T(8,128)S(1)}, f32[80,3584]{1,0:T(8,128)}, u32[]{:S(2)}) copy-start(f32[80,3584]{1,0:T(8,128)} %param.9) | copy-start | bytes 3440644
  201.9 133.3 %all-gather.5.cloned.1.call-start = ((), (), s32[]{:S(2)}) async-start(), calls=%async_computation.4 | async-start | bytes 9748480 | tf_op jit(solution)/shard_map/all_gather | solution.py:37
Sparse Core Ops, SparseCore 0:
  10.3 170.8 all-gather.2
  202.0 71.2 reduce-scatter.1
  277.1 57.9 all-gather.4
where the time goes:
time: 350 us
  waiting for transfers between devices  233 us (67%)
  blocking collectives  68.4 us (20%)
  matrix products  20.6 us (6%)
  between operations  13.8 us (4%)
  local copies, waits for them, and re-layouts  10.2 us (3%)
  other arithmetic  3.68 us (1%)
    all_gather x1, waiting for transfers between devices, body(): gathered = lax.all_gather(layer_input, 'intra', axis=0, tiled=True)  102 us
    reduce_scatter x1, waiting for transfers between devices, body(): lax.psum_scatter(lax.dot_general(hidden_part, gathered, contract, preferr...  71.4 us
    all_to_all x1, blocking collectives, body(): lax.all_to_all(up_cotangent, 'intra', split_axis=1, concat_axis=0, tiled=...  68.4 us
    all_gather x1, waiting for transfers between devices, body(): lax.all_gather(new_master.astype(jnp.bfloat16), 'inter', axis=0, tiled=True)  58.1 us
    dot_general x1, matrix products, body(): lax.dot_general(hidden_part, gathered, contract, preferred_element_type=j...  20.6 us
    unnamed x7, local copies, waits for them, and re-layouts  7.86 us
  transfers between devices with their start and end apart: 3, of which 3 were waited for; matrix products, arithmetic and copies ran while one was open for 1% of the time, Pallas kernels for 0%

commit v1 on v0

v1 whole, which is shorter than its diff:
```python
import functools
import math

import jax
import jax.numpy as jnp
from jax import lax
from jax.experimental import pallas as pl
from jax.experimental.pallas import tpu as pltpu
from jax.sharding import PartitionSpec as P

AXES = ("inter", "intra")
WIDTHS = (1024, 768)


def device(x, y, z, c):
    inter = (z % 2) * 8 + y * 2 + c
    intra = x * 2 + z // 2
    return inter * 8 + intra


def permutation(move):
    pairs = []
    for x in range(4):
        for y in range(4):
            for z in range(4):
                for c in range(2):
                    a, b, d, e = move(x, y, z, c)
                    pairs.append((device(x, y, z, c), device(a % 4, b % 4, d % 4, e)))
    return sorted(pairs)


def send(value, move):
    return lax.ppermute(value, AXES, permutation(move))


def sibling(x, y, z, c):
    return x, y, z, 1 - c


def along_z(sign):
    def move(x, y, z, c):
        return x, y, z + (sign if c == 0 else -sign), c

    return move


def two_z(x, y, z, c):
    return x, y, z + 2, c


def along_first(sign):
    def move(x, y, z, c):
        return (x + sign, y, z, c) if c == 0 else (x, y + sign, z, c)

    return move


def along_second(sign):
    def move(x, y, z, c):
        return (x, y + sign, z, c) if c == 0 else (x + sign, y, z, c)

    return move


def pack(where, cotangent):
    tokens, hidden = cotangent.shape
    piece = hidden // 16

    def kernel(where_ref, *refs):
        for source, target in zip(refs[:4], refs[4:]):
            target[...] = source[...]

    def source_map(step):
        def index(g, w):
            sign = 1 - 2 * w[3]
            offset = {0: 0, 1: sign, 2: -sign, 3: 2}[step]
            return 0, g * 4 + lax.rem(w[2] + offset + 4, 4)

        return index

    block = (tokens, piece)
    return pl.pallas_call(
        kernel,
        grid_spec=pltpu.PrefetchScalarGridSpec(
            num_scalar_prefetch=1,
            grid=(4,),
            in_specs=[pl.BlockSpec(block, source_map(step)) for step in range(4)],
            out_specs=[pl.BlockSpec(block, lambda g, w: (0, g))] * 4,
        ),
        out_shape=[jax.ShapeDtypeStruct((tokens, hidden // 4), cotangent.dtype)] * 4,
        name="pack_cotangent",
    )(where, *([cotangent] * 4))


def partial_sums(where, mine, other, inputs):
    tokens, rows = mine[0].shape
    width = inputs[0].shape[1]
    piece = rows // 4
    unit = piece // 8
    tile = 256

    def kernel(where_ref, *refs):
        own_refs, other_refs, input_refs = refs[:4], refs[4:8], refs[8:12]
        plus_ref, minus_ref, first_ref, third_ref, keep_ref = refs[12:17]
        held, turned, total = refs[17:]
        g = pl.program_id(0)

        @pl.when(g == 0)
        def _():
            for step in range(4):
                held[pl.ds(step * 2 * tokens, 2 * tokens), :] = input_refs[step][...]

        for step in range(4):
            both = jnp.concatenate([own_refs[step][...], other_refs[step][...]], axis=0)
            turned[:, pl.ds(step * 2 * tokens, 2 * tokens)] = both.T

        @pl.loop(0, width // tile)
        def _(column):
            at = pl.ds(pl.multiple_of(column * tile, tile), tile)
            total[:, at] = jnp.dot(
                turned[...], held[:, at], preferred_element_type=jnp.float32
            ).astype(jnp.bfloat16)

        x, y, c = where_ref[0], where_ref[1], where_ref[3]
        step_x = lax.rem(g - x + 4, 4)
        for to_y in range(4):
            step_y = lax.rem(to_y - y + 4, 4)
            first = jnp.where(c == 0, step_x, step_y)
            second = jnp.where(c == 0, step_y, step_x)
            for half in range(2):
                start = (to_y * 2 + half) * unit
                places = {
                    0: (keep_ref, half),
                    1: (first_ref, None) if half == 0 else (plus_ref, 1),
                    2: (plus_ref, 0) if half == 0 else (minus_ref, 0),
                    3: (minus_ref, 1) if half == 0 else (third_ref, None),
                }
                for distance, (ref, slot) in places.items():

                    @pl.when(first == distance)
                    def _(ref=ref, slot=slot, start=start, second=second):
                        value = total[pl.ds(start, unit), :]
                        if slot is None:
                            ref[second] = value
                        else:
                            ref[slot, second] = value

    def whole(shape):
        return pl.BlockSpec(shape, lambda g, w: (0,) * len(shape))

    two, one = (2, 4, unit, width), (4, unit, width)
    shapes = (two, two, one, one, two)
    flops = 2 * 8 * tokens * rows * width
    return pl.pallas_call(
        kernel,
        grid_spec=pltpu.PrefetchScalarGridSpec(
            num_scalar_prefetch=1,
            grid=(4,),
            in_specs=[pl.BlockSpec((tokens, piece), lambda g, w: (0, g))] * 8
            + [whole(value.shape) for value in inputs],
            out_specs=[whole(shape) for shape in shapes],
            scratch_shapes=[
                pltpu.VMEM((8 * tokens, width), jnp.bfloat16),
                pltpu.VMEM((piece, 8 * tokens), jnp.bfloat16),
                pltpu.VMEM((piece, width), jnp.bfloat16),
            ],
        ),
        out_shape=[jax.ShapeDtypeStruct(shape, jnp.bfloat16) for shape in shapes],
        compiler_params=pltpu.CompilerParams(vmem_limit_bytes=48 * 1024 * 1024),
        cost_estimate=pl.CostEstimate(
            flops=flops, bytes_accessed=8 * tokens * (rows + width) * 2 + rows * width * 2, transcendentals=0
        ),
        name="partial_sums",
    )(where, *mine, *other, *inputs)


def wide(value):
    return value.astype(jnp.float32)


def narrow(value):
    return value.astype(jnp.bfloat16)


def ring_sum(plus, minus, first, third, keep, along):
    from_left = send(plus, along(1))
    from_right = send(minus, along(-1))
    left = send(narrow(wide(first) + wide(from_left[0])), along(1))
    right = send(narrow(wide(third) + wide(from_right[0])), along(-1))
    low = wide(keep[0]) + wide(from_right[1]) + wide(left)
    high = wide(keep[1]) + wide(from_left[1]) + wide(right)
    return low, high


def reduce_scatter(plus, minus, first, third, keep):
    low, high = ring_sum(plus, minus, first, third, keep, along_first)
    low, high = narrow(low), narrow(high)
    low, high = ring_sum(
        jnp.stack([low[2], high[1]]),
        jnp.stack([high[2], low[3]]),
        low[1],
        high[3],
        jnp.stack([low[0], high[0]]),
        along_second,
    )
    return narrow(low), narrow(high)


def adamw(grad, master, first_moment, second_moment):
    new_first = 0.9 * first_moment + 0.1 * grad
    new_second = 0.95 * second_moment + 0.05 * (grad * grad)
    first_hat = new_first / (1.0 - 0.9**10)
    second_hat = new_second / (1.0 - 0.95**10)
    step_dir = first_hat / (jnp.sqrt(second_hat) + 1e-08) + 0.1 * master
    new_master = master - 0.02 * step_dir
    return (new_master, new_first, new_second)


def body(layer_input, up_cotangent, master, first_moment, second_moment):
    tokens, columns = layer_input.shape
    total_tokens = tokens * 128
    inter, intra = lax.axis_index("inter"), lax.axis_index("intra")
    c = inter % 2
    x, y, z = intra // 2, (inter // 2) % 4, (intra % 2) * 2 + inter // 8
    where = jnp.stack([x, y, z, c]).astype(jnp.int32)
    half = columns // 2

    low, high = layer_input[:, :half], layer_input[:, half:]
    kept = jnp.where(c == 0, low, high)
    given = jnp.where(c == 0, high, low)
    chip_input = jnp.concatenate([kept, send(given, sibling)], axis=0)

    blocks = pack(where, up_cotangent)
    mine = [
        blocks[0],
        send(blocks[1], along_z(1)),
        send(blocks[2], along_z(-1)),
        send(blocks[3], two_z),
    ]
    other = [send(mine[step], sibling) for step in (0, 2, 1, 3)]

    grads, copies = [], []
    start = 0
    scale = 1.0 / math.sqrt(total_tokens)
    for width in WIDTHS:
        own = chip_input[:, start : start + width]
        near = send(own, along_z(1))
        far = send(own, along_z(-1))
        last = send(near, along_z(1))
        pieces = partial_sums(where, mine, other, [own, near, far, last])
        low, high = reduce_scatter(*pieces)
        ours = jnp.where(c == 0, low, high)
        theirs = send(jnp.where(c == 0, high, low), sibling)
        grad = wide(jnp.concatenate([jnp.where(c == 0, ours, theirs), jnp.where(c == 0, theirs, ours)], axis=1)) * scale
        grads.append(grad)

        def part(value):
            return jnp.concatenate(
                [value[:, start : start + width], value[:, half + start : half + start + width]], axis=1
            )

        fresh = narrow(adamw(grad, part(master), part(first_moment), part(second_moment))[0])
        copies.append(lax.all_gather(fresh, "inter", axis=0, tiled=True))
        start += width

    def joined(parts):
        return jnp.concatenate(
            [part[:, :width] for part, width in zip(parts, WIDTHS)]
            + [part[:, width:] for part, width in zip(parts, WIDTHS)],
            axis=1,
        )

    new_master, new_first, new_second = adamw(joined(grads), master, first_moment, second_moment)
    return (new_master, new_first, new_second, joined(copies))


def solution(mesh):
    in_specs = (
        P(("inter", "intra"), None),
        P(("inter", "intra"), None),
        P(("intra", "inter"), None),
        P(("intra", "inter"), None),
        P(("intra", "inter"), None),
    )
    out_specs = (
        P(("intra", "inter"), None),
        P(("intra", "inter"), None),
        P(("intra", "inter"), None),
        P("intra", None),
    )
    return jax.shard_map(body, mesh=mesh, in_specs=in_specs, out_specs=out_specs, check_vma=False)
```

time: 350 us -> 312 us (0.89)
  waiting for transfers between devices: 233 us -> 164 us
  blocking collectives: 68.4 us -> 0 us
  starting transfers between devices: 0.12 us -> 67.1 us
  Pallas kernels: 0 us -> 38.7 us
  matrix products: 20.6 us -> 0 us
  other arithmetic: 3.68 us -> 13.9 us
    ppermute x0 -> x32, waiting for transfers between devices: none -> 134 us  [send(): return lax.ppermute(value, AXES, permutation(move))]
    all_gather x2, waiting for transfers between devices: 161 us -> 29.8 us  [body(): copies.append(lax.all_gather(fresh, 'inter', axis=0, tiled=True))]
    reduce_scatter x1 -> x0, waiting for transfers between devices: 71.4 us -> none  [body(): lax.psum_scatter(lax.dot_general(hidden_part, gathered, contract, preferr...]
    all_to_all x1 -> x0, blocking collectives: 68.4 us -> none  [body(): lax.all_to_all(up_cotangent, 'intra', split_axis=1, concat_axis=0, tiled=...]
    ppermute x0 -> x32, starting transfers between devices: none -> 67 us  [send(): return lax.ppermute(value, AXES, permutation(move))]
    pallas_call x0 -> x3, Pallas kernels: none -> 38.7 us  [the longest x2 33.3 us: partial_sums(): pl.pallas_call(kernel, grid_spec=pltpu.PrefetchScalarGridSpec(num_scalar_...]
    dot_general x1 -> x0, matrix products: 20.6 us -> none  [body(): lax.dot_general(hidden_part, gathered, contract, preferred_element_type=j...]
    slice x0 -> x10, local copies, waits for them, and re-layouts: none -> 10.9 us  [the longest x4 8.11 us: joined(): part[:, :width]]
  transfers between devices with their start and end apart: 3 -> 34, of which waited for: 3 -> 21; matrix products, arithmetic and copies ran while one was open for 1% -> 5% of each run, Pallas kernels for 0% -> 8%
where the time goes in v1:
time: 312 us; the launch traced here: 311 us
  waiting for transfers between devices  164 us (53%)
  starting transfers between devices  67.1 us (22%)
  Pallas kernels  38.7 us (12%)
  between operations  14.4 us (5%)
  other arithmetic  13.9 us (4%)
  local copies, waits for them, and re-layouts  13.4 us (4%)
    ppermute x32, waiting for transfers between devices, send(): return lax.ppermute(value, AXES, permutation(move))  134 us
    ppermute x32, starting transfers between devices, send(): return lax.ppermute(value, AXES, permutation(move))  67 us
    pallas_call x2, Pallas kernels, partial_sums(): pl.pallas_call(kernel, grid_spec=pltpu.PrefetchScalarGridSpec(num_scalar_...  33.3 us
    all_gather x2, waiting for transfers between devices, body(): copies.append(lax.all_gather(fresh, 'inter', axis=0, tiled=True))  29.8 us
    slice x4, local copies, waits for them, and re-layouts, joined(): part[:, :width]  8.11 us
  transfers between devices with their start and end apart: 34, of which 21 were waited for; matrix products, arithmetic and copies ran while one was open for 5% of the time, Pallas kernels for 8%

profile of v1, /device:TPU:1, one launch (start us, length us, event | category | flops | bytes accessed | tf_op | source)
XLA Modules:
  0.0 311.3 jit_solution(1889166194036344342)
XLA Ops:
  10.8 5.4 %pack_cotangent.1 = (bf16[192,2560]{1,0:T(8,128)(2,1)}, bf16[192,2560]{1,0:T(8,128)(2,1)}, bf16[192,2560]{1,0:T(8,128)(2,1)}, bf16[192,2560]{1,0:T(8,128)(2,1)}) custom-call(s32[4]{0:T(128)} %pad_add_fusion.where_ref, bf16[192,10240]{1,0:T(8,128)(2,1)} %refs_3_.1, bf16[192,10240]{1,0:T(8,128)(2,1)} %refs_3_.1, bf16[192,10240]{1,0:T(8,128)(2,1)} %refs_3_.1, ...), custom_call_target="tpu_custom_call" | custom-call | tf_op jit(solution)/shard_map/pack_cotangent/pallas_call | solution.py:82
  23.5 15.5 %collective-permute-done.1.refs_2_ = bf16[192,2560]{1,0:T(8,128)(2,1)S(1)} collective-permute-done((bf16[192,2560]{1,0:T(8,128)(2,1)}, bf16[192,2560]{1,0:T(8,128)(2,1)S(1)}, u32[]{:S(2)}, u32[]{:S(2)}) %collective-permute-start.1) | collective-permute-done | bytes 983072 | tf_op jit(solution)/shard_map/ppermute | solution.py:33
  39.0 24.8 %collective-permute-start.4 = (bf16[192,2560]{1,0:T(8,128)(2,1)S(1)}, bf16[192,2560]{1,0:T(8,128)(2,1)S(1)}, u32[]{:S(2)}, u32[]{:S(2)}) collective-permute-start(bf16[192,2560]{1,0:T(8,128)(2,1)S(1)} %collective-permute-done.1.refs_2_), channel_id=1, source_target_pairs={{0,8},{1,9},{2,10},{3,11},{4,12},{5,13},{6,14},{7,15},{8,0},{9,1},... | collective-permute-start | bytes 2949128 | tf_op jit(solution)/shard_map/ppermute | solution.py:33
  65.4 4.4 %collective-permute-done.20.refs_9_ = bf16[384,768]{1,0:T(8,128)(2,1)S(1)} collective-permute-done((bf16[384,768]{1,0:T(8,128)(2,1)S(1)}, bf16[384,768]{1,0:T(8,128)(2,1)S(1)}, u32[]{:S(2)}, u32[]{:S(2)}) %collective-permute-start.20) | collective-permute-done | bytes 589856 | tf_op jit(solution)/shard_map/ppermute | solution.py:33
  69.8 3.4 %collective-permute-start.22 = (bf16[384,768]{1,0:T(8,128)(2,1)S(1)}, bf16[384,768]{1,0:T(8,128)(2,1)S(1)}, u32[]{:S(2)}, u32[]{:S(2)}) collective-permute-start(bf16[384,768]{1,0:T(8,128)(2,1)S(1)} %collective-permute-done.20.refs_9_), channel_id=1, source_target_pairs={{0,64},{1,65},{2,66},{3,67},{4,68},{5,69},{6,70},{7,71},{8,73},{9,... | collective-permute-start | bytes 1769480 | tf_op jit(solution)/shard_map/ppermute | solution.py:33
  73.2 3.9 %collective-permute-done.21.refs_10_ = bf16[384,768]{1,0:T(8,128)(2,1)S(1)} collective-permute-done((bf16[384,768]{1,0:T(8,128)(2,1)S(1)}, bf16[384,768]{1,0:T(8,128)(2,1)S(1)}, u32[]{:S(2)}, u32[]{:S(2)}) %collective-permute-start.21) | collective-permute-done | bytes 589856 | tf_op jit(solution)/shard_map/ppermute | solution.py:33
  77.1 4.8 %collective-permute-done.22.refs_11_ = bf16[384,768]{1,0:T(8,128)(2,1)S(1)} collective-permute-done((bf16[384,768]{1,0:T(8,128)(2,1)S(1)}, bf16[384,768]{1,0:T(8,128)(2,1)S(1)}, u32[]{:S(2)}, u32[]{:S(2)}) %collective-permute-start.22) | collective-permute-done | bytes 589856 | tf_op jit(solution)/shard_map/ppermute | solution.py:33
  84.3 14.6 %partial_sums.3 = (bf16[2,4,80,768]{3,2,1,0:T(8,128)(2,1)S(1)}, bf16[2,4,80,768]{3,2,1,0:T(8,128)(2,1)S(1)}, bf16[4,80,768]{2,1,0:T(8,128)(2,1)S(1)}, bf16[4,80,...) custom-call(s32[4]{0:T(128)S(1)} %copy-done, bf16[192,2560]{1,0:T(8,128)(2,1)} %get-tuple-element.18.refs_0_, ...), custom_call_target="tpu_custom_call" | custom-call | flops 6039797760 | bytes 14155776 | tf_op jit(solution)/shard_map/partial_sums/pallas_call | solution.py:154
  98.9 2.7 collective-permute-start.23
  101.7 11.0 %collective-permute-done.23 = bf16[2,4,80,768]{3,2,1,0:T(8,128)(2,1)S(1)} collective-permute-done((bf16[2,4,80,768]{3,2,1,0:T(8,128)(2,1)S(1)}, bf16[2,4,80,768]{3,2,1,0:T(8,128)(2,1)S(1)}, u32[]{:S(2)}, u32[]{:S(2)}) %collective-permute-start.23) | collective-permute-done | bytes 983072 | tf_op jit(solution)/shard_map/ppermute | solution.py:33
  112.8 3.5 %collective-permute-start.26 = (bf16[4,80,768]{2,1,0:T(8,128)(2,1)S(1)}, bf16[4,80,768]{2,1,0:T(8,128)(2,1)S(1)}, u32[]{:S(2)}, u32[]{:S(2)}) collective-permute-start(bf16[4,80,768]{2,1,0:T(8,128)(2,1)S(1)} %fusion.4), channel_id=1, source_target_pairs={{0,6},{1,7},{2,0},{3,1},{4,2},{5,3},{6,4},{7,5},{8,56},{9,57},{10,... | collective-permute-start | bytes 1474568 | tf_op jit(solution)/shard_map/ppermute | solution.py:33
  116.5 5.6 %collective-permute-done.26 = bf16[4,80,768]{2,1,0:T(8,128)(2,1)S(1)} collective-permute-done((bf16[4,80,768]{2,1,0:T(8,128)(2,1)S(1)}, bf16[4,80,768]{2,1,0:T(8,128)(2,1)S(1)}, u32[]{:S(2)}, u32[]{:S(2)}) %collective-permute-start.26) | collective-permute-done | bytes 491552 | tf_op jit(solution)/shard_map/ppermute | solution.py:33
  122.1 3.6 %collective-permute-done.25 = bf16[4,80,768]{2,1,0:T(8,128)(2,1)S(1)} collective-permute-done((bf16[4,80,768]{2,1,0:T(8,128)(2,1)S(1)}, bf16[4,80,768]{2,1,0:T(8,128)(2,1)S(1)}, u32[]{:S(2)}, u32[]{:S(2)}) %collective-permute-start.25) | collective-permute-done | bytes 491552 | tf_op jit(solution)/shard_map/ppermute | solution.py:33
  131.5 3.2 %collective-permute-start.30 = (bf16[80,768]{1,0:T(8,128)(2,1)S(1)}, bf16[80,768]{1,0:T(8,128)(2,1)S(1)}, u32[]{:S(2)}, u32[]{:S(2)}) collective-permute-start(bf16[80,768]{1,0:T(8,128)(2,1)S(1)} %fusion.38), channel_id=1, source_target_pairs={{0,48},{1,49},{2,50},{3,51},{4,52},{5,53},{6,54},{7,55},{8,14},{9,... | collective-permute-start | bytes 368648 | tf_op jit(solution)/shard_map/ppermute | solution.py:33
  136.6 3.2 %collective-permute-done.29 = bf16[80,768]{1,0:T(8,128)(2,1)S(1)} collective-permute-done((bf16[80,768]{1,0:T(8,128)(2,1)S(1)}, bf16[80,768]{1,0:T(8,128)(2,1)S(1)}, u32[]{:S(2)}, u32[]{:S(2)}) %collective-permute-start.29) | collective-permute-done | bytes 122912 | tf_op jit(solution)/shard_map/ppermute | solution.py:33
  139.9 6.0 %collective-permute-start.31 = (bf16[80,768]{1,0:T(8,128)(2,1)S(1)}, bf16[80,768]{1,0:T(8,128)(2,1)S(1)}, u32[]{:S(2)}, u32[]{:S(2)}) collective-permute-start(bf16[80,768]{1,0:T(8,128)(2,1)S(1)} %get-tuple-element.38), channel_id=1, source_target_pairs={{0,8},{1,9},{2,10},{3,11},{4,12},{5,13},{6,14},{7,15},{8,0},{9,1},... | collective-permute-start | bytes 368648 | tf_op jit(solution)/shard_map/ppermute | solution.py:33
  149.1 21.0 %collective-permute-done.8.refs_9_ = bf16[384,1024]{1,0:T(8,128)(2,1)S(1)} collective-permute-done((bf16[384,1024]{1,0:T(8,128)(2,1)S(1)}, bf16[384,1024]{1,0:T(8,128)(2,1)S(1)}, u32[]{:S(2)}, u32[]{:S(2)}) %collective-permute-start.8) | collective-permute-done | bytes 786464 | tf_op jit(solution)/shard_map/ppermute | solution.py:33
  170.1 9.4 %collective-permute-done.9.refs_10_ = bf16[384,1024]{1,0:T(8,128)(2,1)S(1)} collective-permute-done((bf16[384,1024]{1,0:T(8,128)(2,1)S(1)}, bf16[384,1024]{1,0:T(8,128)(2,1)S(1)}, u32[]{:S(2)}, u32[]{:S(2)}) %collective-permute-start.9) | collective-permute-done | bytes 786464 | tf_op jit(solution)/shard_map/ppermute | solution.py:33
  179.5 12.7 %collective-permute-done.10.refs_11_ = bf16[384,1024]{1,0:T(8,128)(2,1)S(1)} collective-permute-done((bf16[384,1024]{1,0:T(8,128)(2,1)S(1)}, bf16[384,1024]{1,0:T(8,128)(2,1)S(1)}, u32[]{:S(2)}, u32[]{:S(2)}) %collective-permute-start.10) | collective-permute-done | bytes 786464 | tf_op jit(solution)/shard_map/ppermute | solution.py:33
  192.2 18.7 %partial_sums.2 = (bf16[2,4,80,1024]{3,2,1,0:T(8,128)(2,1)}, bf16[2,4,80,1024]{3,2,1,0:T(8,128)(2,1)}, bf16[4,80,1024]{2,1,0:T(8,128)(2,1)S(1)}, bf16[4,80,1024]...) custom-call(s32[4]{0:T(128)S(1)} %copy-done, bf16[192,2560]{1,0:T(8,128)(2,1)S(1)} %copy-done.1, bf16[192,2560]{1,0:T(8,128)(2,1)} %copy-done.10, ...), custom_call_target="tpu_custom_call" | custom-call | flops 8053063680 | bytes 16252928 | tf_op jit(solution)/shard_map/partial_sums/pallas_call | solution.py:154
  212.4 15.5 %collective-permute-done.11 = bf16[2,4,80,1024]{3,2,1,0:T(8,128)(2,1)S(1)} collective-permute-done((bf16[2,4,80,1024]{3,2,1,0:T(8,128)(2,1)}, bf16[2,4,80,1024]{3,2,1,0:T(8,128)(2,1)S(1)}, u32[]{:S(2)}, u32[]{:S(2)}) %collective-permute-start.11) | collective-permute-done | bytes 1310752 | tf_op jit(solution)/shard_map/ppermute | solution.py:33
  230.0 7.9 %collective-permute-done.14 = bf16[4,80,1024]{2,1,0:T(8,128)(2,1)S(1)} collective-permute-done((bf16[4,80,1024]{2,1,0:T(8,128)(2,1)S(1)}, bf16[4,80,1024]{2,1,0:T(8,128)(2,1)S(1)}, u32[]{:S(2)}, u32[]{:S(2)}) %collective-permute-start.14) | collective-permute-done | bytes 655392 | tf_op jit(solution)/shard_map/ppermute | solution.py:33
  237.9 2.4 collective-permute-done.13
  243.0 4.6 %collective-permute-done.15 = bf16[2,80,1024]{2,1,0:T(8,128)(2,1)S(1)} collective-permute-done((bf16[2,80,1024]{2,1,0:T(8,128)(2,1)S(1)}, bf16[2,80,1024]{2,1,0:T(8,128)(2,1)S(1)}, u32[]{:S(2)}, u32[]{:S(2)}) %collective-permute-start.15) | collective-permute-done | bytes 327712 | tf_op jit(solution)/shard_map/ppermute | solution.py:33
  249.5 2.4 collective-permute-done.18
  252.0 2.5 collective-permute-done.17
  254.7 2.8 collective-permute-start.19
  261.4 2.3 multiply_subtract_fusion
  263.8 3.7 %fusion.44 = (bf16[1280,768]{1,0:T(8,128)(2,1)S(1)}, bf16[1280,768]{1,0:T(8,128)(2,1)}) fusion(bf16[1280,1536]{1,0:T(8,128)(2,1)} %all-gather.5.cloned.1.call-done), kind=kLoop, calls=%fused_computation.95 | loop fusion | bytes 7864320 | tf_op jit(solution)/shard_map/slice | solution.py:268
  267.4 29.8 %all-gather.3.cloned.1.call-done = bf16[1280,2048]{1,0:T(8,128)(2,1)} async-done(((bf16[80,2048]{1,0:T(8,128)(2,1)}), bf16[1280,2048]{1,0:T(8,128)(2,1)}) %all-gather.3.cloned.1.call-update) | async-done | bytes 5242896 | tf_op jit(solution)/shard_map/all_gather | solution.py:263
  297.2 3.2 %fusion.43 = (bf16[1280,1024]{1,0:T(8,128)(2,1)S(1)}, bf16[1280,1024]{1,0:T(8,128)(2,1)S(1)}) fusion(bf16[1280,2048]{1,0:T(8,128)(2,1)} %all-gather.3.cloned.1.call-done), kind=kLoop, calls=%fused_computation.94 | loop fusion | bytes 10485760 | tf_op jit(solution)/shard_map/slice | solution.py:268
  300.4 4.1 %pad_maximum_fusion = bf16[1280,3584]{1,0:T(8,128)(2,1)} fusion(bf16[1280,768]{1,0:T(8,128)(2,1)S(1)} %copy-done.2, bf16[1280,1024]{1,0:T(8,128)(2,1)S(1)} %get-tuple-element.42, bf16[1280,768]{1,0:T(8,128)(2,1)S(1)} %get-tuple-element.43, bf16[1280,1024]{1,0:T(8,128)(2,1)S(1)} %get-tuple-element.41), kind=kLoop, calls=%fused_computation | loop fusion | flops 36700160 | bytes 18350080 | tf_op jit(solution)/shard_map/concatenate | solution.py:267
  (109 shorter events, 38.0 us)
Async XLA Ops:
  7.2 256.6 %all-gather.5.cloned.1.call-start = ((), (), s32[]{:S(2)}) async-start(), calls=%async_computation.1 | async-start | bytes 4177920 | tf_op jit(solution)/shard_map/all_gather | solution.py:263
  8.6 13.7 %collective-permute-start.7 = (bf16[192,1792]{1,0:T(8,128)(2,1)S(1)}, bf16[192,1792]{1,0:T(8,128)(2,1)S(1)}, u32[]{:S(2)}, u32[]{:S(2)}) collective-permute-start(bf16[192,1792]{1,0:T(8,128)(2,1)S(1)} %get-tuple-element.46), channel_id=1, source_target_pairs={{0,8},{1,9},{2,10},{3,11},{4,12},{5,13},{6,14},{7,15},{8,0},{9,1},... | collective-permute-start | bytes 2064392 | tf_op jit(solution)/shard_map/ppermute | solution.py:33
  16.2 22.9 %collective-permute-start.1 = (bf16[192,2560]{1,0:T(8,128)(2,1)}, bf16[192,2560]{1,0:T(8,128)(2,1)S(1)}, u32[]{:S(2)}, u32[]{:S(2)}) collective-permute-start(bf16[192,2560]{1,0:T(8,128)(2,1)} %get-tuple-element.20), channel_id=1, source_target_pairs={{0,65},{1,64},{2,67},{3,66},{4,69},{5,68},{6,71},{7,70},{8,72},{9,... | collective-permute-start | bytes 2949128 | tf_op jit(solution)/shard_map/ppermute | solution.py:33
  18.0 45.9 %collective-permute-start = (bf16[192,2560]{1,0:T(8,128)(2,1)}, bf16[192,2560]{1,0:T(8,128)(2,1)S(1)}, u32[]{:S(2)}, u32[]{:S(2)}) collective-permute-start(bf16[192,2560]{1,0:T(8,128)(2,1)} %get-tuple-element.19), channel_id=1, source_target_pairs={{0,64},{1,65},{2,66},{3,67},{4,68},{5,69},{6,70},{7,71},{8,73},{9,... | collective-permute-start | bytes 2949128 | tf_op jit(solution)/shard_map/ppermute | solution.py:33
  20.2 43.8 %collective-permute-start.2 = (bf16[192,2560]{1,0:T(8,128)(2,1)}, bf16[192,2560]{1,0:T(8,128)(2,1)S(1)}, u32[]{:S(2)}, u32[]{:S(2)}) collective-permute-start(bf16[192,2560]{1,0:T(8,128)(2,1)} %get-tuple-element.21), channel_id=1, source_target_pairs={{0,1},{1,0},{2,3},{3,2},{4,5},{5,4},{6,7},{7,6},{8,9},{9,8},{10,11... | collective-permute-start | bytes 2949128 | tf_op jit(solution)/shard_map/ppermute | solution.py:33
  21.4 44.0 %collective-permute-start.3 = (bf16[192,2560]{1,0:T(8,128)(2,1)}, bf16[192,2560]{1,0:T(8,128)(2,1)S(1)}, u32[]{:S(2)}, u32[]{:S(2)}) collective-permute-start(bf16[192,2560]{1,0:T(8,128)(2,1)} %get-tuple-element.18.refs_0_), channel_id=1, source_target_pairs={{0,8},{1,9},{2,10},{3,11},{4,12},{5,13},{6,14},{7,15},{8,0},{9,1},... | collective-permute-start | bytes 2949128 | tf_op jit(solution)/shard_map/ppermute | solution.py:33
  22.3 47.5 %collective-permute-start.20 = (bf16[384,768]{1,0:T(8,128)(2,1)S(1)}, bf16[384,768]{1,0:T(8,128)(2,1)S(1)}, u32[]{:S(2)}, u32[]{:S(2)}) collective-permute-start(bf16[384,768]{1,0:T(8,128)(2,1)S(1)} %pad_maximum_fusion.3.refs_8_), channel_id=1, source_target_pairs={{0,64},{1,65},{2,66},{3,67},{4,68},{5,69},{6,70},{7,71},{8,73},{9,... | collective-permute-start | bytes 1769480 | tf_op jit(solution)/shard_map/ppermute | solution.py:33
  39.0 42.9 %collective-permute-start.4 = (bf16[192,2560]{1,0:T(8,128)(2,1)S(1)}, bf16[192,2560]{1,0:T(8,128)(2,1)S(1)}, u32[]{:S(2)}, u32[]{:S(2)}) collective-permute-start(bf16[192,2560]{1,0:T(8,128)(2,1)S(1)} %collective-permute-done.1.refs_2_), channel_id=1, source_target_pairs={{0,8},{1,9},{2,10},{3,11},{4,12},{5,13},{6,14},{7,15},{8,0},{9,1},... | collective-permute-start | bytes 2949128 | tf_op jit(solution)/shard_map/ppermute | solution.py:33
  63.9 18.1 %collective-permute-start.5 = (bf16[192,2560]{1,0:T(8,128)(2,1)S(1)}, bf16[192,2560]{1,0:T(8,128)(2,1)S(1)}, u32[]{:S(2)}, u32[]{:S(2)}) collective-permute-start(bf16[192,2560]{1,0:T(8,128)(2,1)S(1)} %collective-permute-done.refs_1_), channel_id=1, source_target_pairs={{0,8},{1,9},{2,10},{3,11},{4,12},{5,13},{6,14},{7,15},{8,0},{9,1},... | collective-permute-start | bytes 2949128 | tf_op jit(solution)/shard_map/ppermute | solution.py:33
  64.0 18.0 %collective-permute-start.6 = (bf16[192,2560]{1,0:T(8,128)(2,1)S(1)}, bf16[192,2560]{1,0:T(8,128)(2,1)S(1)}, u32[]{:S(2)}, u32[]{:S(2)}) collective-permute-start(bf16[192,2560]{1,0:T(8,128)(2,1)S(1)} %collective-permute-done.2.refs_3_), channel_id=1, source_target_pairs={{0,8},{1,9},{2,10},{3,11},{4,12},{5,13},{6,14},{7,15},{8,0},{9,1},... | collective-permute-start | bytes 2949128 | tf_op jit(solution)/shard_map/ppermute | solution.py:33
  65.3 11.8 %collective-permute-start.21 = (bf16[384,768]{1,0:T(8,128)(2,1)S(1)}, bf16[384,768]{1,0:T(8,128)(2,1)S(1)}, u32[]{:S(2)}, u32[]{:S(2)}) collective-permute-start(bf16[384,768]{1,0:T(8,128)(2,1)S(1)} %pad_maximum_fusion.3.refs_8_), channel_id=1, source_target_pairs={{0,65},{1,64},{2,67},{3,66},{4,69},{5,68},{6,71},{7,70},{8,72},{9,... | collective-permute-start | bytes 1769480 | tf_op jit(solution)/shard_map/ppermute | solution.py:33
  69.8 12.2 %collective-permute-start.22 = (bf16[384,768]{1,0:T(8,128)(2,1)S(1)}, bf16[384,768]{1,0:T(8,128)(2,1)S(1)}, u32[]{:S(2)}, u32[]{:S(2)}) collective-permute-start(bf16[384,768]{1,0:T(8,128)(2,1)S(1)} %collective-permute-done.20.refs_9_), channel_id=1, source_target_pairs={{0,64},{1,65},{2,66},{3,67},{4,68},{5,69},{6,70},{7,71},{8,73},{9,... | collective-permute-start | bytes 1769480 | tf_op jit(solution)/shard_map/ppermute | solution.py:33
  98.9 13.8 %collective-permute-start.23 = (bf16[2,4,80,768]{3,2,1,0:T(8,128)(2,1)S(1)}, bf16[2,4,80,768]{3,2,1,0:T(8,128)(2,1)S(1)}, u32[]{:S(2)}, u32[]{:S(2)}) collective-permute-start(bf16[2,4,80,768]{3,2,1,0:T(8,128)(2,1)S(1)} %get-tuple-element.28), channel_id=1, source_target_pairs={{0,6},{1,7},{2,0},{3,1},{4,2},{5,3},{6,4},{7,5},{8,56},{9,57},{10,... | collective-permute-start | bytes 2949128 | tf_op jit(solution)/shard_map/ppermute | solution.py:33
  101.7 14.6 %collective-permute-start.24 = (bf16[2,4,80,768]{3,2,1,0:T(8,128)(2,1)S(1)}, bf16[2,4,80,768]{3,2,1,0:T(8,128)(2,1)S(1)}, u32[]{:S(2)}, u32[]{:S(2)}) collective-permute-start(bf16[2,4,80,768]{3,2,1,0:T(8,128)(2,1)S(1)} %get-tuple-element.30), channel_id=1, source_target_pairs={{0,2},{1,3},{2,4},{3,5},{4,6},{5,7},{6,0},{7,1},{8,24},{9,25},{10,... | collective-permute-start | bytes 2949128 | tf_op jit(solution)/shard_map/ppermute | solution.py:33
  112.8 9.3 %collective-permute-start.26 = (bf16[4,80,768]{2,1,0:T(8,128)(2,1)S(1)}, bf16[4,80,768]{2,1,0:T(8,128)(2,1)S(1)}, u32[]{:S(2)}, u32[]{:S(2)}) collective-permute-start(bf16[4,80,768]{2,1,0:T(8,128)(2,1)S(1)} %fusion.4), channel_id=1, source_target_pairs={{0,6},{1,7},{2,0},{3,1},{4,2},{5,3},{6,4},{7,5},{8,56},{9,57},{10,... | collective-permute-start | bytes 1474568 | tf_op jit(solution)/shard_map/ppermute | solution.py:33
  116.4 9.3 %collective-permute-start.25 = (bf16[4,80,768]{2,1,0:T(8,128)(2,1)S(1)}, bf16[4,80,768]{2,1,0:T(8,128)(2,1)S(1)}, u32[]{:S(2)}, u32[]{:S(2)}) collective-permute-start(bf16[4,80,768]{2,1,0:T(8,128)(2,1)S(1)} %fusion.5), channel_id=1, source_target_pairs={{0,2},{1,3},{2,4},{3,5},{4,6},{5,7},{6,0},{7,1},{8,24},{9,25},{10,... | collective-permute-start | bytes 1474568 | tf_op jit(solution)/shard_map/ppermute | solution.py:33
  126.1 5.4 %collective-permute-start.27 = (bf16[2,80,768]{2,1,0:T(8,128)(2,1)S(1)}, bf16[2,80,768]{2,1,0:T(8,128)(2,1)S(1)}, u32[]{:S(2)}, u32[]{:S(2)}) collective-permute-start(bf16[2,80,768]{2,1,0:T(8,128)(2,1)S(1)} %pad_maximum_fusion.8), channel_id=1, source_target_pairs={{0,48},{1,49},{2,50},{3,51},{4,52},{5,53},{6,54},{7,55},{8,14},{9,... | collective-permute-start | bytes 737288 | tf_op jit(solution)/shard_map/ppermute | solution.py:33
  128.4 6.3 %collective-permute-start.28 = (bf16[2,80,768]{2,1,0:T(8,128)(2,1)S(1)}, bf16[2,80,768]{2,1,0:T(8,128)(2,1)S(1)}, u32[]{:S(2)}, u32[]{:S(2)}) collective-permute-start(bf16[2,80,768]{2,1,0:T(8,128)(2,1)S(1)} %pad_maximum_fusion.9), channel_id=1, source_target_pairs={{0,16},{1,17},{2,18},{3,19},{4,20},{5,21},{6,22},{7,23},{8,10},{9,... | collective-permute-start | bytes 737288 | tf_op jit(solution)/shard_map/ppermute | solution.py:33
  131.5 5.1 %collective-permute-start.30 = (bf16[80,768]{1,0:T(8,128)(2,1)S(1)}, bf16[80,768]{1,0:T(8,128)(2,1)S(1)}, u32[]{:S(2)}, u32[]{:S(2)}) collective-permute-start(bf16[80,768]{1,0:T(8,128)(2,1)S(1)} %fusion.38), channel_id=1, source_target_pairs={{0,48},{1,49},{2,50},{3,51},{4,52},{5,53},{6,54},{7,55},{8,14},{9,... | collective-permute-start | bytes 368648 | tf_op jit(solution)/shard_map/ppermute | solution.py:33
  134.8 5.0 %collective-permute-start.29 = (bf16[80,768]{1,0:T(8,128)(2,1)S(1)}, bf16[80,768]{1,0:T(8,128)(2,1)S(1)}, u32[]{:S(2)}, u32[]{:S(2)}) collective-permute-start(bf16[80,768]{1,0:T(8,128)(2,1)S(1)} %fusion.37), channel_id=1, source_target_pairs={{0,16},{1,17},{2,18},{3,19},{4,20},{5,21},{6,22},{7,23},{8,10},{9,... | collective-permute-start | bytes 368648 | tf_op jit(solution)/shard_map/ppermute | solution.py:33
  139.9 7.7 %collective-permute-start.31 = (bf16[80,768]{1,0:T(8,128)(2,1)S(1)}, bf16[80,768]{1,0:T(8,128)(2,1)S(1)}, u32[]{:S(2)}, u32[]{:S(2)}) collective-permute-start(bf16[80,768]{1,0:T(8,128)(2,1)S(1)} %get-tuple-element.38), channel_id=1, source_target_pairs={{0,8},{1,9},{2,10},{3,11},{4,12},{5,13},{6,14},{7,15},{8,0},{9,1},... | collective-permute-start | bytes 368648 | tf_op jit(solution)/shard_map/ppermute | solution.py:33
  146.0 24.1 %collective-permute-start.8 = (bf16[384,1024]{1,0:T(8,128)(2,1)S(1)}, bf16[384,1024]{1,0:T(8,128)(2,1)S(1)}, u32[]{:S(2)}, u32[]{:S(2)}) collective-permute-start(bf16[384,1024]{1,0:T(8,128)(2,1)S(1)} %fusion.8.refs_8_), channel_id=1, source_target_pairs={{0,64},{1,65},{2,66},{3,67},{4,68},{5,69},{6,70},{7,71},{8,73},{9,... | collective-permute-start | bytes 2359304 | tf_op jit(solution)/shard_map/ppermute | solution.py:33
  148.9 148.2 %all-gather.3.cloned.1.call-start = ((), (), s32[]{:S(2)}) async-start(), calls=%async_computation | async-start | bytes 5570560 | tf_op jit(solution)/shard_map/all_gather | solution.py:263
  149.0 30.5 %collective-permute-start.9 = (bf16[384,1024]{1,0:T(8,128)(2,1)S(1)}, bf16[384,1024]{1,0:T(8,128)(2,1)S(1)}, u32[]{:S(2)}, u32[]{:S(2)}) collective-permute-start(bf16[384,1024]{1,0:T(8,128)(2,1)S(1)} %fusion.8.refs_8_), channel_id=1, source_target_pairs={{0,65},{1,64},{2,67},{3,66},{4,69},{5,68},{6,71},{7,70},{8,72},{9,... | collective-permute-start | bytes 2359304 | tf_op jit(solution)/shard_map/ppermute | solution.py:33
  170.1 22.1 %collective-permute-start.10 = (bf16[384,1024]{1,0:T(8,128)(2,1)S(1)}, bf16[384,1024]{1,0:T(8,128)(2,1)S(1)}, u32[]{:S(2)}, u32[]{:S(2)}) collective-permute-start(bf16[384,1024]{1,0:T(8,128)(2,1)S(1)} %collective-permute-done.8.refs_9_), channel_id=1, source_target_pairs={{0,64},{1,65},{2,66},{3,67},{4,68},{5,69},{6,70},{7,71},{8,73},{9,... | collective-permute-start | bytes 2359304 | tf_op jit(solution)/shard_map/ppermute | solution.py:33
  210.9 17.0 %collective-permute-start.11 = (bf16[2,4,80,1024]{3,2,1,0:T(8,128)(2,1)}, bf16[2,4,80,1024]{3,2,1,0:T(8,128)(2,1)S(1)}, u32[]{:S(2)}, u32[]{:S(2)}) collective-permute-start(bf16[2,4,80,1024]{3,2,1,0:T(8,128)(2,1)} %get-tuple-element.23), channel_id=1, source_target_pairs={{0,6},{1,7},{2,0},{3,1},{4,2},{5,3},{6,4},{7,5},{8,56},{9,57},{10,... | collective-permute-start | bytes 3932168 | tf_op jit(solution)/shard_map/ppermute | solution.py:33
  210.9 18.2 %collective-permute-start.12 = (bf16[2,4,80,1024]{3,2,1,0:T(8,128)(2,1)}, bf16[2,4,80,1024]{3,2,1,0:T(8,128)(2,1)S(1)}, u32[]{:S(2)}, u32[]{:S(2)}) collective-permute-start(bf16[2,4,80,1024]{3,2,1,0:T(8,128)(2,1)} %get-tuple-element.25), channel_id=1, source_target_pairs={{0,2},{1,3},{2,4},{3,5},{4,6},{5,7},{6,0},{7,1},{8,24},{9,25},{10,... | collective-permute-start | bytes 3932168 | tf_op jit(solution)/shard_map/ppermute | solution.py:33
  228.1 9.8 %collective-permute-start.14 = (bf16[4,80,1024]{2,1,0:T(8,128)(2,1)S(1)}, bf16[4,80,1024]{2,1,0:T(8,128)(2,1)S(1)}, u32[]{:S(2)}, u32[]{:S(2)}) collective-permute-start(bf16[4,80,1024]{2,1,0:T(8,128)(2,1)S(1)} %fusion), channel_id=1, source_target_pairs={{0,6},{1,7},{2,0},{3,1},{4,2},{5,3},{6,4},{7,5},{8,56},{9,57},{10,... | collective-permute-start | bytes 1966088 | tf_op jit(solution)/shard_map/ppermute | solution.py:33
  229.4 11.0 %collective-permute-start.13 = (bf16[4,80,1024]{2,1,0:T(8,128)(2,1)S(1)}, bf16[4,80,1024]{2,1,0:T(8,128)(2,1)S(1)}, u32[]{:S(2)}, u32[]{:S(2)}) collective-permute-start(bf16[4,80,1024]{2,1,0:T(8,128)(2,1)S(1)} %fusion.1), channel_id=1, source_target_pairs={{0,2},{1,3},{2,4},{3,5},{4,6},{5,7},{6,0},{7,1},{8,24},{9,25},{10,... | collective-permute-start | bytes 1966088 | tf_op jit(solution)/shard_map/ppermute | solution.py:33
  241.4 6.3 %collective-permute-start.15 = (bf16[2,80,1024]{2,1,0:T(8,128)(2,1)S(1)}, bf16[2,80,1024]{2,1,0:T(8,128)(2,1)S(1)}, u32[]{:S(2)}, u32[]{:S(2)}) collective-permute-start(bf16[2,80,1024]{2,1,0:T(8,128)(2,1)S(1)} %pad_maximum_fusion.5), channel_id=1, source_target_pairs={{0,48},{1,49},{2,50},{3,51},{4,52},{5,53},{6,54},{7,55},{8,14},{9,... | collective-permute-start | bytes 983048 | tf_op jit(solution)/shard_map/ppermute | solution.py:33
  241.5 7.5 %collective-permute-start.16 = (bf16[2,80,1024]{2,1,0:T(8,128)(2,1)S(1)}, bf16[2,80,1024]{2,1,0:T(8,128)(2,1)S(1)}, u32[]{:S(2)}, u32[]{:S(2)}) collective-permute-start(bf16[2,80,1024]{2,1,0:T(8,128)(2,1)S(1)} %pad_maximum_fusion.6), channel_id=1, source_target_pairs={{0,16},{1,17},{2,18},{3,19},{4,20},{5,21},{6,22},{7,23},{8,10},{9,... | collective-permute-start | bytes 983048 | tf_op jit(solution)/shard_map/ppermute | solution.py:33
  249.1 5.4 %collective-permute-start.17 = (bf16[80,1024]{1,0:T(8,128)(2,1)S(1)}, bf16[80,1024]{1,0:T(8,128)(2,1)S(1)}, u32[]{:S(2)}, u32[]{:S(2)}) collective-permute-start(bf16[80,1024]{1,0:T(8,128)(2,1)S(1)} %fusion.35), channel_id=1, source_target_pairs={{0,16},{1,17},{2,18},{3,19},{4,20},{5,21},{6,22},{7,23},{8,10},{9,... | collective-permute-start | bytes 491528 | tf_op jit(solution)/shard_map/ppermute | solution.py:33
  (18 other events, 273.9 us)
Sparse Core Ops, SparseCore 0:
  149.0 41.2 all-gather.4
  260.2 36.9 all-gather.2

commit v2 on v1

v2 whole, which is shorter than its diff:
```python
import functools
import math

import jax
import jax.numpy as jnp
from jax import lax
from jax.experimental import pallas as pl
from jax.experimental.pallas import tpu as pltpu
from jax.sharding import PartitionSpec as P

AXES = ("inter", "intra")
WIDTHS = (512, 1280)


def device(x, y, z, c):
    inter = (z % 2) * 8 + y * 2 + c
    intra = x * 2 + z // 2
    return inter * 8 + intra


def permutation(move):
    pairs = []
    for x in range(4):
        for y in range(4):
            for z in range(4):
                for c in range(2):
                    a, b, d, e = move(x, y, z, c)
                    pairs.append((device(x, y, z, c), device(a % 4, b % 4, d % 4, e)))
    return sorted(pairs)


def send(value, move):
    return lax.ppermute(value, AXES, permutation(move))


def sibling(x, y, z, c):
    return x, y, z, 1 - c


def along_rows(step):
    def move(x, y, z, c):
        return (x, y, z + step, c) if c == 0 else (x + step, y, z, c)

    return move


def along_sums(step):
    def move(x, y, z, c):
        return (x + step, y, z, c) if c == 0 else (x, y, z + step, c)

    return move


def along_y(step):
    def move(x, y, z, c):
        return x, y + step, z, c

    return move


def pack(where, mine, other, steps):
    tokens, hidden = mine.shape
    piece = hidden // 16
    count = len(steps)

    def kernel(where_ref, *refs):
        for place in range(count):
            target = refs[2 * count + place]
            target[:tokens, :] = refs[place][...]
            target[tokens:, :] = refs[count + place][...]

    def source_map(step):
        def index(g, w):
            at = lax.rem(w[0] + step, 4)
            return 0, jnp.where(w[3] == 0, g * 4 + at, at * 4 + g)

        return index

    maps = [pl.BlockSpec((tokens, piece), source_map(step)) for step in steps]
    return pl.pallas_call(
        kernel,
        grid_spec=pltpu.PrefetchScalarGridSpec(
            num_scalar_prefetch=1,
            grid=(4,),
            in_specs=maps + maps,
            out_specs=[pl.BlockSpec((2 * tokens, piece), lambda g, w: (0, g))] * count,
        ),
        out_shape=[jax.ShapeDtypeStruct((2 * tokens, hidden // 4), mine.dtype)] * count,
        cost_estimate=pl.CostEstimate(
            flops=0, bytes_accessed=count * 2 * tokens * hidden, transcendentals=0
        ),
        name="pack_cotangent",
    )(where, *([mine] * count), *([other] * count))


def partial_sums(where, blocks, inputs, y_first):
    tokens, rows = blocks[0].shape
    width = inputs[0].shape[1]
    piece = rows // 4
    unit = piece // 8
    tile = 256

    def kernel(where_ref, *refs):
        block_refs, input_refs = refs[:4], refs[4:8]
        plus_ref, minus_ref, first_ref, third_ref, keep_ref = refs[8:13]
        held, turned, total = refs[13:]
        g = pl.program_id(0)

        @pl.when(g == 0)
        def _():
            for step in range(4):
                held[pl.ds(step * tokens, tokens), :] = input_refs[step][...]

        for step in range(4):
            turned[:, pl.ds(step * tokens, tokens)] = block_refs[step][...].T

        @pl.loop(0, width // tile)
        def _(column):
            at = pl.ds(pl.multiple_of(column * tile, tile), tile)
            total[:, at] = jnp.dot(
                turned[...], held[:, at], preferred_element_type=jnp.float32
            ).astype(jnp.bfloat16)

        step_g = lax.rem(g - where_ref[1] + 4, 4)
        for to_y in range(4):
            step_y = lax.rem(to_y - where_ref[2] + 4, 4)
            first, second = (step_y, step_g) if y_first else (step_g, step_y)
            for half in range(2):
                start = (to_y * 2 + half) * unit
                places = {
                    0: (keep_ref, half),
                    1: (first_ref, None) if half == 0 else (plus_ref, 1),
                    2: (plus_ref, 0) if half == 0 else (minus_ref, 0),
                    3: (minus_ref, 1) if half == 0 else (third_ref, None),
                }
                for distance, (ref, slot) in places.items():

                    @pl.when(first == distance)
                    def _(ref=ref, slot=slot, start=start, second=second):
                        value = total[pl.ds(start, unit), :]
                        if slot is None:
                            ref[second] = value
                        else:
                            ref[slot, second] = value

    def whole(shape):
        return pl.BlockSpec(shape, lambda g, w: (0,) * len(shape))

    two, one = (2, 4, unit, width), (4, unit, width)
    shapes = (two, two, one, one, two)
    return pl.pallas_call(
        kernel,
        grid_spec=pltpu.PrefetchScalarGridSpec(
            num_scalar_prefetch=1,
            grid=(4,),
            in_specs=[pl.BlockSpec((tokens, piece), lambda g, w: (0, g))] * 4
            + [whole(value.shape) for value in inputs],
            out_specs=[whole(shape) for shape in shapes],
            scratch_shapes=[
                pltpu.VMEM((4 * tokens, width), jnp.bfloat16),
                pltpu.VMEM((piece, 4 * tokens), jnp.bfloat16),
                pltpu.VMEM((piece, width), jnp.bfloat16),
            ],
        ),
        out_shape=[jax.ShapeDtypeStruct(shape, jnp.bfloat16) for shape in shapes],
        compiler_params=pltpu.CompilerParams(vmem_limit_bytes=48 * 1024 * 1024),
        cost_estimate=pl.CostEstimate(
            flops=2 * 4 * tokens * rows * width,
            bytes_accessed=4 * tokens * (rows + width) * 2 + rows * width * 2,
            transcendentals=0,
        ),
        name="partial_sums",
    )(where, *blocks, *inputs)


def wide(value):
    return value.astype(jnp.float32)


def narrow(value):
    return value.astype(jnp.bfloat16)


def after(value, *others):
    return lax.optimization_barrier((value, others))[0]


def ring_send(plus, minus, along):
    return send(plus, along(1)), send(minus, along(-1))


def ring_turn(first, third, from_left, from_right, along):
    left = send(narrow(wide(first) + wide(from_left[0])), along(1))
    right = send(narrow(wide(third) + wide(from_right[0])), along(-1))
    return left, right


def ring_end(keep, from_left, from_right, left, right):
    low = wide(keep[0]) + wide(from_right[1]) + wide(left)
    high = wide(keep[1]) + wide(from_left[1]) + wide(right)
    return narrow(low), narrow(high)


def second_round(low, high):
    plus, minus = jnp.stack([low[2], high[1]]), jnp.stack([high[2], low[3]])
    return plus, minus, low[1], high[3], jnp.stack([low[0], high[0]])


def adamw(grad, master, first_moment, second_moment):
    new_first = 0.9 * first_moment + 0.1 * grad
    new_second = 0.95 * second_moment + 0.05 * (grad * grad)
    first_hat = new_first / (1.0 - 0.9**10)
    second_hat = new_second / (1.0 - 0.95**10)
    step_dir = first_hat / (jnp.sqrt(second_hat) + 1e-08) + 0.1 * master
    new_master = master - 0.02 * step_dir
    return (new_master, new_first, new_second)


def body(layer_input, up_cotangent, master, first_moment, second_moment):
    tokens, columns = layer_input.shape
    total_tokens = tokens * 128
    inter, intra = lax.axis_index("inter"), lax.axis_index("intra")
    c = inter % 2
    x, y, z = intra // 2, (inter // 2) % 4, (intra % 2) * 2 + inter // 8
    where = jnp.stack([jnp.where(c == 0, z, x), jnp.where(c == 0, x, z), y, c]).astype(jnp.int32)
    half = columns // 2

    low, high = layer_input[:, :half], layer_input[:, half:]
    kept = jnp.where(c == 0, low, high)
    given = jnp.where(c == 0, high, low)
    chip_input = jnp.concatenate([kept, send(given, sibling)], axis=0)
    other = send(up_cotangent, sibling)

    def spread(value):
        return [send(value, along_rows(step)) for step in (1, 3, 2)]

    starts = [sum(WIDTHS[:place]) for place in range(len(WIDTHS))]
    inputs = [chip_input[:, start : start + width] for start, width in zip(starts, WIDTHS)]
    inputs_0 = [inputs[0], *spread(inputs[0])]
    near, far = pack(where, up_cotangent, other, (1, 3))
    own, last = pack(where, up_cotangent, other, (0, 2))
    blocks = [own, send(near, along_rows(1)), send(far, along_rows(3)), send(last, along_rows(2))]
    inputs_1 = [inputs[1], *spread(inputs[1])]

    plus_0, minus_0, first_0, third_0, keep_0 = partial_sums(where, blocks, inputs_0, True)
    sent_0 = ring_send(plus_0, minus_0, along_y)
    pieces_1 = partial_sums(where, blocks, inputs_1, False)
    sent_0, pieces_1 = lax.optimization_barrier((sent_0, pieces_1))
    plus_1, minus_1, first_1, third_1, keep_1 = pieces_1
    sent_1 = ring_send(plus_1, minus_1, along_sums)
    turned_0 = ring_turn(first_0, third_0, *sent_0, along_y)
    next_0 = second_round(*ring_end(keep_0, *sent_0, *turned_0))
    again_0 = ring_send(next_0[0], next_0[1], along_sums)
    turned_1 = ring_turn(first_1, third_1, *sent_1, along_sums)
    last_0 = ring_turn(next_0[2], next_0[3], *again_0, along_sums)
    summed_0 = ring_end(next_0[4], *again_0, *last_0)
    next_1 = second_round(*ring_end(keep_1, *sent_1, *turned_1))
    again_1 = ring_send(next_1[0], next_1[1], along_y)
    last_1 = ring_turn(next_1[2], next_1[3], *again_1, along_y)
    summed_1 = ring_end(next_1[4], *again_1, *last_1)

    scale = 1.0 / math.sqrt(total_tokens)
    grads, copies = [], []
    for (low, high), start, width in zip((summed_0, summed_1), starts, WIDTHS):
        ours = jnp.where(c == 0, low, high)
        theirs = send(jnp.where(c == 0, high, low), sibling)
        grad = wide(jnp.concatenate([jnp.where(c == 0, ours, theirs), jnp.where(c == 0, theirs, ours)], axis=1)) * scale
        grads.append(grad)

        def part(value):
            return jnp.concatenate(
                [value[:, start : start + width], value[:, half + start : half + start + width]], axis=1
            )

        fresh = narrow(adamw(grad, part(master), part(first_moment), part(second_moment))[0])
        copies.append(lax.all_gather(fresh, "inter", axis=0, tiled=True))

    def joined(parts):
        return jnp.concatenate(
            [part[:, :width] for part, width in zip(parts, WIDTHS)]
            + [part[:, width:] for part, width in zip(parts, WIDTHS)],
            axis=1,
        )

    new_master, new_first, new_second = adamw(joined(grads), master, first_moment, second_moment)
    return (new_master, new_first, new_second, joined(copies))


def solution(mesh):
    in_specs = (
        P(("inter", "intra"), None),
        P(("inter", "intra"), None),
        P(("intra", "inter"), None),
        P(("intra", "inter"), None),
        P(("intra", "inter"), None),
    )
    out_specs = (
        P(("intra", "inter"), None),
        P(("intra", "inter"), None),
        P(("intra", "inter"), None),
        P("intra", None),
    )
    return jax.shard_map(body, mesh=mesh, in_specs=in_specs, out_specs=out_specs, check_vma=False)
```

time: 312 us -> 267 us (0.86)
  waiting for transfers between devices: 164 us -> 125 us
  starting transfers between devices: 67.1 us -> 59 us
  Pallas kernels: 38.7 us -> 43 us
  local copies, waits for them, and re-layouts: 13.4 us -> 9.14 us
    ppermute x32 -> x29, waiting for transfers between devices: 134 us -> 89 us  [send(): return lax.ppermute(value, AXES, permutation(move))]
    ppermute x32 -> x29, starting transfers between devices: 67 us -> 58.9 us  [send(): return lax.ppermute(value, AXES, permutation(move))]
    all_gather x2, waiting for transfers between devices: 29.8 us -> 36.1 us  [body(): copies.append(lax.all_gather(fresh, 'inter', axis=0, tiled=True))]
    pallas_call x1 -> x2, Pallas kernels: 5.37 us -> 10.9 us  [pack(): pl.pallas_call(kernel, grid_spec=pltpu.PrefetchScalarGridSpec(num_scalar_...]
    convert_element_type x12, other arithmetic: 4.87 us -> 8.82 us  [narrow(): return value.astype(jnp.bfloat16)]
  transfers between devices with their start and end apart: 34 -> 31, of which waited for: 21 -> 14; matrix products, arithmetic and copies ran while one was open for 5% -> 6% of each run, Pallas kernels for 8% -> 14%
where the time goes in v2:
time: 267 us
  waiting for transfers between devices  125 us (47%)
  starting transfers between devices  59 us (22%)
  Pallas kernels  43 us (16%)
  other arithmetic  16.5 us (6%)
  between operations  14.3 us (5%)
  local copies, waits for them, and re-layouts  9.14 us (3%)
    ppermute x29, waiting for transfers between devices, send(): return lax.ppermute(value, AXES, permutation(move))  89 us
    ppermute x29, starting transfers between devices, send(): return lax.ppermute(value, AXES, permutation(move))  58.9 us
    all_gather x2, waiting for transfers between devices, body(): copies.append(lax.all_gather(fresh, 'inter', axis=0, tiled=True))  36.1 us
    pallas_call x2, Pallas kernels, partial_sums(): pl.pallas_call(kernel, grid_spec=pltpu.PrefetchScalarGridSpec(num_scalar_...  32.1 us
    pallas_call x2, Pallas kernels, pack(): pl.pallas_call(kernel, grid_spec=pltpu.PrefetchScalarGridSpec(num_scalar_...  10.9 us
    convert_element_type x12, other arithmetic, narrow(): return value.astype(jnp.bfloat16)  8.82 us
    slice x4, local copies, waits for them, and re-layouts, joined(): part[:, :width]  7.43 us
  transfers between devices with their start and end apart: 31, of which 14 were waited for; matrix products, arithmetic and copies ran while one was open for 6% of the time, Pallas kernels for 14%

profile of v2, /device:TPU:1, one launch (start us, length us, event | category | flops | bytes accessed | tf_op | source)
XLA Modules:
  0.0 267.1 jit_solution(17229803063686987942)
XLA Ops:
  9.4 6.1 %collective-permute-done.refs_2_.refs_3_ = bf16[192,10240]{1,0:T(8,128)(2,1)} collective-permute-done((bf16[192,10240]{1,0:T(8,128)(2,1)}, bf16[192,10240]{1,0:T(8,128)(2,1)}, u32[]{:S(2)}, u32[]{:S(2)}) %collective-permute-start) | collective-permute-done | bytes 3932192 | tf_op jit(solution)/shard_map/ppermute | solution.py:33
  15.5 5.5 %pack_cotangent.3 = (bf16[384,2560]{1,0:T(8,128)(2,1)}, bf16[384,2560]{1,0:T(8,128)(2,1)}) custom-call(s32[4]{0:T(128)} %pad_add_fusion.where_ref, bf16[192,10240]{1,0:T(8,128)(2,1)} %refs_1_.3, bf16[192,10240]{1,0:T(8,128)(2,1)} %refs_1_.3, bf16[192,10240]{1,0:T(8,128)(2,1)} %collective-permute-done.refs_2_.refs_3_, ...), custom_call_target="tpu_custom_call" | custom-call | bytes 7864320 | tf_op jit(solution)/shard_map/pack_cotangent/pallas_call | solution.py:80
  23.5 2.5 collective-permute-start.2
  26.0 5.4 %pack_cotangent.2 = (bf16[384,2560]{1,0:T(8,128)(2,1)}, bf16[384,2560]{1,0:T(8,128)(2,1)}) custom-call(s32[4]{0:T(128)} %pad_add_fusion.where_ref, bf16[192,10240]{1,0:T(8,128)(2,1)} %refs_1_.3, bf16[192,10240]{1,0:T(8,128)(2,1)} %refs_1_.3, bf16[192,10240]{1,0:T(8,128)(2,1)} %collective-permute-done.refs_2_.refs_3_, ...), custom_call_target="tpu_custom_call" | custom-call | bytes 7864320 | tf_op jit(solution)/shard_map/pack_cotangent/pallas_call | solution.py:80
  32.6 2.1 collective-permute-start.6
  34.7 36.7 %collective-permute-done.5.refs_5_ = bf16[384,512]{1,0:T(8,128)(2,1)S(1)} collective-permute-done((bf16[384,512]{1,0:T(8,128)(2,1)S(1)}, bf16[384,512]{1,0:T(8,128)(2,1)S(1)}, u32[]{:S(2)}, u32[]{:S(2)}) %collective-permute-start.5) | collective-permute-done | bytes 393248 | tf_op jit(solution)/shard_map/ppermute | solution.py:33
  74.0 5.9 %collective-permute-done.7.refs_7_ = bf16[384,512]{1,0:T(8,128)(2,1)S(1)} collective-permute-done((bf16[384,512]{1,0:T(8,128)(2,1)S(1)}, bf16[384,512]{1,0:T(8,128)(2,1)S(1)}, u32[]{:S(2)}, u32[]{:S(2)}) %collective-permute-start.7) | collective-permute-done | bytes 393248 | tf_op jit(solution)/shard_map/ppermute | solution.py:33
  83.1 10.7 %partial_sums.2 = (bf16[2,4,80,512]{3,2,1,0:T(8,128)(2,1)S(1)}, bf16[2,4,80,512]{3,2,1,0:T(8,128)(2,1)S(1)}, bf16[4,80,512]{2,1,0:T(8,128)(2,1)S(1)}, bf16[4,80,...) custom-call(s32[4]{0:T(128)S(1)} %copy-done, bf16[384,2560]{1,0:T(8,128)(2,1)S(1)} %copy-done.1, ...), custom_call_target="tpu_custom_call" | custom-call | flops 4026531840 | bytes 12058624 | tf_op jit(solution)/shard_map/partial_sums/pallas_call | solution.py:151
  96.7 4.3 %collective-permute-done.12.refs_7_ = bf16[384,1280]{1,0:T(8,128)(2,1)S(1)} collective-permute-done((bf16[384,1280]{1,0:T(8,128)(2,1)S(1)}, bf16[384,1280]{1,0:T(8,128)(2,1)S(1)}, u32[]{:S(2)}, u32[]{:S(2)}) %collective-permute-start.12) | collective-permute-done | bytes 983072 | tf_op jit(solution)/shard_map/ppermute | solution.py:33
  100.9 21.4 %partial_sums.3 = (bf16[2,4,80,1280]{3,2,1,0:T(8,128)(2,1)}, bf16[2,4,80,1280]{3,2,1,0:T(8,128)(2,1)}, bf16[4,80,1280]{2,1,0:T(8,128)(2,1)S(1)}, bf16[4,80,1280]...) custom-call(s32[4]{0:T(128)S(1)} %copy-done, bf16[384,2560]{1,0:T(8,128)(2,1)} %get-tuple-element.25.refs_0_, ...), custom_call_target="tpu_custom_call" | custom-call | flops 10066329600 | bytes 18350080 | tf_op jit(solution)/shard_map/partial_sums/pallas_call | solution.py:151
  122.4 2.9 %collective-permute-start.14 = (bf16[4,80,512]{2,1,0:T(8,128)(2,1)S(1)}, bf16[4,80,512]{2,1,0:T(8,128)(2,1)S(1)}, u32[]{:S(2)}, u32[]{:S(2)}) collective-permute-start(bf16[4,80,512]{2,1,0:T(8,128)(2,1)S(1)} %fusion.15), channel_id=1, source_target_pairs={{0,48},{1,49},{2,50},{3,51},{4,52},{5,53},{6,54},{7,55},{8,56},{9,... | collective-permute-start | bytes 983048 | tf_op jit(solution)/shard_map/ppermute | solution.py:33
  125.5 3.8 %collective-permute-start.20 = (bf16[2,4,80,1280]{3,2,1,0:T(8,128)(2,1)}, bf16[2,4,80,1280]{3,2,1,0:T(8,128)(2,1)S(1)}, u32[]{:S(2)}, u32[]{:S(2)}) collective-permute-start(bf16[2,4,80,1280]{3,2,1,0:T(8,128)(2,1)} %get-tuple-element.42), channel_id=1, source_target_pairs={{0,6},{1,7},{2,0},{3,1},{4,2},{5,3},{6,4},{7,5},{8,73},{9,72},{10,... | collective-permute-start | bytes 4915208 | tf_op jit(solution)/shard_map/ppermute | solution.py:33
  129.3 3.3 %collective-permute-done.13 = bf16[4,80,512]{2,1,0:T(8,128)(2,1)S(1)} collective-permute-done((bf16[4,80,512]{2,1,0:T(8,128)(2,1)S(1)}, bf16[4,80,512]{2,1,0:T(8,128)(2,1)S(1)}, u32[]{:S(2)}, u32[]{:S(2)}) %collective-permute-start.13) | collective-permute-done | bytes 327712 | tf_op jit(solution)/shard_map/ppermute | solution.py:33
  132.9 3.8 %collective-permute-start.15 = (bf16[2,80,512]{2,1,0:T(8,128)(2,1)S(1)}, bf16[2,80,512]{2,1,0:T(8,128)(2,1)S(1)}, u32[]{:S(2)}, u32[]{:S(2)}) collective-permute-start(bf16[2,80,512]{2,1,0:T(8,128)(2,1)S(1)} %pad_maximum_fusion.9), channel_id=1, source_target_pairs={{0,6},{1,7},{2,0},{3,1},{4,2},{5,3},{6,4},{7,5},{8,73},{9,72},{10,... | collective-permute-start | bytes 491528 | tf_op jit(solution)/shard_map/ppermute | solution.py:33
  137.5 11.9 %collective-permute-done.15 = bf16[2,80,512]{2,1,0:T(8,128)(2,1)S(1)} collective-permute-done((bf16[2,80,512]{2,1,0:T(8,128)(2,1)S(1)}, bf16[2,80,512]{2,1,0:T(8,128)(2,1)S(1)}, u32[]{:S(2)}, u32[]{:S(2)}) %collective-permute-start.15) | collective-permute-done | bytes 163872 | tf_op jit(solution)/shard_map/ppermute | solution.py:33
  149.5 3.4 %collective-permute-start.18 = (bf16[80,512]{1,0:T(8,128)(2,1)S(1)}, bf16[80,512]{1,0:T(8,128)(2,1)S(1)}, u32[]{:S(2)}, u32[]{:S(2)}) collective-permute-start(bf16[80,512]{1,0:T(8,128)(2,1)S(1)} %fusion.37), channel_id=1, source_target_pairs={{0,6},{1,7},{2,0},{3,1},{4,2},{5,3},{6,4},{7,5},{8,73},{9,72},{10,... | collective-permute-start | bytes 245768 | tf_op jit(solution)/shard_map/ppermute | solution.py:33
  154.4 2.7 collective-permute-start.23
  158.5 6.8 %collective-permute-start.19 = (bf16[80,512]{1,0:T(8,128)(2,1)S(1)}, bf16[80,512]{1,0:T(8,128)(2,1)S(1)}, u32[]{:S(2)}, u32[]{:S(2)}) collective-permute-start(bf16[80,512]{1,0:T(8,128)(2,1)S(1)} %get-tuple-element.49), channel_id=1, source_target_pairs={{0,8},{1,9},{2,10},{3,11},{4,12},{5,13},{6,14},{7,15},{8,0},{9,1},... | collective-permute-start | bytes 245768 | tf_op jit(solution)/shard_map/ppermute | solution.py:33
  167.4 4.0 %collective-permute-done.22 = bf16[4,80,1280]{2,1,0:T(8,128)(2,1)} collective-permute-done((bf16[4,80,1280]{2,1,0:T(8,128)(2,1)}, bf16[4,80,1280]{2,1,0:T(8,128)(2,1)}, u32[]{:S(2)}, u32[]{:S(2)}) %collective-permute-start.22) | collective-permute-done | bytes 819232 | tf_op jit(solution)/shard_map/ppermute | solution.py:33
  171.4 3.0 %fusion.3 = (bf16[4,80,1280]{2,1,0:T(8,128)(2,1)S(1)}, bf16[4,80,1280]{2,1,0:T(8,128)(2,1)S(1)}) fusion(bf16[4,80,1280]{2,1,0:T(8,128)(2,1)} %collective-permute-done.22, bf16[2,4,80,1280]{3,2,1,0:T(8,128)(2,1)} %copy-done.5, bf16[2,4,80,1280]{3,2,1,0:T(8,128)(2,1)} %get-tuple-element.41, bf16[4,80,1280]{2,1,0:T(8,128)(2,1)} %collective-permute-done.23, ...), kind=kLoop, calls=%fused_computation.8 | loop fusion | flops 4915200 | bytes 6553600 | tf_op jit(solution)/shard_map/convert_element_type | solution.py:181
  174.5 2.7 collective-permute-start.24
  177.3 6.2 %collective-permute-done.24 = bf16[2,80,1280]{2,1,0:T(8,128)(2,1)S(1)} collective-permute-done((bf16[2,80,1280]{2,1,0:T(8,128)(2,1)S(1)}, bf16[2,80,1280]{2,1,0:T(8,128)(2,1)S(1)}, u32[]{:S(2)}, u32[]{:S(2)}) %collective-permute-start.24) | collective-permute-done | bytes 409632 | tf_op jit(solution)/shard_map/ppermute | solution.py:33
  183.6 1.7 collective-permute-start.27
  186.2 2.4 collective-permute-start.26
  188.7 5.0 %collective-permute-done.27 = bf16[80,1280]{1,0:T(8,128)(2,1)S(1)} collective-permute-done((bf16[80,1280]{1,0:T(8,128)(2,1)S(1)}, bf16[80,1280]{1,0:T(8,128)(2,1)S(1)}, u32[]{:S(2)}, u32[]{:S(2)}) %collective-permute-start.27) | collective-permute-done | bytes 204832 | tf_op jit(solution)/shard_map/ppermute | solution.py:33
  193.7 2.8 %collective-permute-done.26 = bf16[80,1280]{1,0:T(8,128)(2,1)S(1)} collective-permute-done((bf16[80,1280]{1,0:T(8,128)(2,1)S(1)}, bf16[80,1280]{1,0:T(8,128)(2,1)S(1)}, u32[]{:S(2)}, u32[]{:S(2)}) %collective-permute-start.26) | collective-permute-done | bytes 204832 | tf_op jit(solution)/shard_map/ppermute | solution.py:33
  196.7 10.8 %collective-permute-start.28 = (bf16[80,1280]{1,0:T(8,128)(2,1)S(1)}, bf16[80,1280]{1,0:T(8,128)(2,1)S(1)}, u32[]{:S(2)}, u32[]{:S(2)}) collective-permute-start(bf16[80,1280]{1,0:T(8,128)(2,1)S(1)} %get-tuple-element.52), channel_id=1, source_target_pairs={{0,8},{1,9},{2,10},{3,11},{4,12},{5,13},{6,14},{7,15},{8,0},{9,1},... | collective-permute-start | bytes 614408 | tf_op jit(solution)/shard_map/ppermute | solution.py:33
  212.5 2.3 multiply_subtract_fusion
  214.8 1.9 fusion.43
  216.7 36.1 %all-gather.5.cloned.1.call-done = bf16[1280,2560]{1,0:T(8,128)(2,1)} async-done(((bf16[80,2560]{1,0:T(8,128)(2,1)}), bf16[1280,2560]{1,0:T(8,128)(2,1)}) %all-gather.5.cloned.1.call-update) | async-done | bytes 6553616 | tf_op jit(solution)/shard_map/all_gather | solution.py:276
  252.8 3.3 %fusion.42 = (bf16[1280,1280]{1,0:T(8,128)(2,1)S(1)}, bf16[1280,1280]{1,0:T(8,128)(2,1)S(1)}) fusion(bf16[1280,2560]{1,0:T(8,128)(2,1)} %all-gather.5.cloned.1.call-done), kind=kLoop, calls=%fused_computation.90 | loop fusion | bytes 13107200 | tf_op jit(solution)/shard_map/slice | solution.py:280
  256.2 4.1 %pad_maximum_fusion = bf16[1280,3584]{1,0:T(8,128)(2,1)} fusion(bf16[1280,1280]{1,0:T(8,128)(2,1)S(1)} %get-tuple-element.56, bf16[1280,512]{1,0:T(8,128)(2,1)S(1)} %get-tuple-element.58, bf16[1280,1280]{1,0:T(8,128)(2,1)S(1)} %get-tuple-element.55, bf16[1280,512]{1,0:T(8,128)(2,1)S(1)} %get-tuple-element.57), kind=kLoop, calls=%fused_computation | loop fusion | flops 36700160 | bytes 18350080 | tf_op jit(solution)/shard_map/concatenate | solution.py:279
  (92 shorter events, 27.4 us)
Async XLA Ops:
  7.2 207.6 %all-gather.3.cloned.1.call-start = ((), (), s32[]{:S(2)}) async-start(), calls=%async_computation | async-start | bytes 2785280 | tf_op jit(solution)/shard_map/all_gather | solution.py:276
  7.2 8.3 %collective-permute-start = (bf16[192,10240]{1,0:T(8,128)(2,1)}, bf16[192,10240]{1,0:T(8,128)(2,1)}, u32[]{:S(2)}, u32[]{:S(2)}) collective-permute-start(bf16[192,10240]{1,0:T(8,128)(2,1)} %refs_1_.3), channel_id=1, source_target_pairs={{0,8},{1,9},{2,10},{3,11},{4,12},{5,13},{6,14},{7,15},{8,0},{9,1},... | collective-permute-start | bytes 11796488 | tf_op jit(solution)/shard_map/ppermute | solution.py:33
  20.9 60.3 %collective-permute-start.1 = (bf16[384,2560]{1,0:T(8,128)(2,1)}, bf16[384,2560]{1,0:T(8,128)(2,1)}, u32[]{:S(2)}, u32[]{:S(2)}) collective-permute-start(bf16[384,2560]{1,0:T(8,128)(2,1)} %get-tuple-element.26), channel_id=1, source_target_pairs={{0,64},{1,65},{2,66},{3,67},{4,68},{5,69},{6,70},{7,71},{8,10},{9,... | collective-permute-start | bytes 5898248 | tf_op jit(solution)/shard_map/ppermute | solution.py:33
  22.3 9.6 %collective-permute-start.4 = (bf16[192,1792]{1,0:T(8,128)(2,1)S(1)}, bf16[192,1792]{1,0:T(8,128)(2,1)S(1)}, u32[]{:S(2)}, u32[]{:S(2)}) collective-permute-start(bf16[192,1792]{1,0:T(8,128)(2,1)S(1)} %get-tuple-element.62), channel_id=1, source_target_pairs={{0,8},{1,9},{2,10},{3,11},{4,12},{5,13},{6,14},{7,15},{8,0},{9,1},... | collective-permute-start | bytes 2064392 | tf_op jit(solution)/shard_map/ppermute | solution.py:33
  23.5 58.3 %collective-permute-start.2 = (bf16[384,2560]{1,0:T(8,128)(2,1)}, bf16[384,2560]{1,0:T(8,128)(2,1)}, u32[]{:S(2)}, u32[]{:S(2)}) collective-permute-start(bf16[384,2560]{1,0:T(8,128)(2,1)} %get-tuple-element.27), channel_id=1, source_target_pairs={{0,65},{1,64},{2,67},{3,66},{4,69},{5,68},{6,71},{7,70},{8,14},{9,... | collective-permute-start | bytes 5898248 | tf_op jit(solution)/shard_map/ppermute | solution.py:33
  31.4 50.4 %collective-permute-start.3 = (bf16[384,2560]{1,0:T(8,128)(2,1)}, bf16[384,2560]{1,0:T(8,128)(2,1)S(1)}, u32[]{:S(2)}, u32[]{:S(2)}) collective-permute-start(bf16[384,2560]{1,0:T(8,128)(2,1)} %get-tuple-element.28), channel_id=1, source_target_pairs={{0,1},{1,0},{2,3},{3,2},{4,5},{5,4},{6,7},{7,6},{8,12},{9,13},{10,... | collective-permute-start | bytes 5898248 | tf_op jit(solution)/shard_map/ppermute | solution.py:33
  31.9 51.2 %copy-start.1 = (bf16[384,2560]{1,0:T(8,128)(2,1)S(1)}, bf16[384,2560]{1,0:T(8,128)(2,1)}, u32[]{:S(2)}) copy-start(bf16[384,2560]{1,0:T(8,128)(2,1)} %get-tuple-element.25.refs_0_) | copy-start | bytes 5898244
  32.0 39.5 %collective-permute-start.5 = (bf16[384,512]{1,0:T(8,128)(2,1)S(1)}, bf16[384,512]{1,0:T(8,128)(2,1)S(1)}, u32[]{:S(2)}, u32[]{:S(2)}) collective-permute-start(bf16[384,512]{1,0:T(8,128)(2,1)S(1)} %pad_maximum_fusion.7.refs_4_), channel_id=1, source_target_pairs={{0,64},{1,65},{2,66},{3,67},{4,68},{5,69},{6,70},{7,71},{8,10},{9,... | collective-permute-start | bytes 1179656 | tf_op jit(solution)/shard_map/ppermute | solution.py:33
  32.6 40.5 %collective-permute-start.6 = (bf16[384,512]{1,0:T(8,128)(2,1)S(1)}, bf16[384,512]{1,0:T(8,128)(2,1)S(1)}, u32[]{:S(2)}, u32[]{:S(2)}) collective-permute-start(bf16[384,512]{1,0:T(8,128)(2,1)S(1)} %pad_maximum_fusion.7.refs_4_), channel_id=1, source_target_pairs={{0,65},{1,64},{2,67},{3,66},{4,69},{5,68},{6,71},{7,70},{8,14},{9,... | collective-permute-start | bytes 1179656 | tf_op jit(solution)/shard_map/ppermute | solution.py:33
  71.4 8.5 %collective-permute-start.7 = (bf16[384,512]{1,0:T(8,128)(2,1)S(1)}, bf16[384,512]{1,0:T(8,128)(2,1)S(1)}, u32[]{:S(2)}, u32[]{:S(2)}) collective-permute-start(bf16[384,512]{1,0:T(8,128)(2,1)S(1)} %pad_maximum_fusion.7.refs_4_), channel_id=1, source_target_pairs={{0,1},{1,0},{2,3},{3,2},{4,5},{5,4},{6,7},{7,6},{8,12},{9,13},{10,... | collective-permute-start | bytes 1179656 | tf_op jit(solution)/shard_map/ppermute | solution.py:33
  73.1 23.6 %collective-permute-start.10 = (bf16[384,1280]{1,0:T(8,128)(2,1)S(1)}, bf16[384,1280]{1,0:T(8,128)(2,1)S(1)}, u32[]{:S(2)}, u32[]{:S(2)}) collective-permute-start(bf16[384,1280]{1,0:T(8,128)(2,1)S(1)} %pad_maximum_fusion.2.refs_4_), channel_id=1, source_target_pairs={{0,64},{1,65},{2,66},{3,67},{4,68},{5,69},{6,70},{7,71},{8,10},{9,... | collective-permute-start | bytes 2949128 | tf_op jit(solution)/shard_map/ppermute | solution.py:33
  79.9 16.8 %collective-permute-start.11 = (bf16[384,1280]{1,0:T(8,128)(2,1)S(1)}, bf16[384,1280]{1,0:T(8,128)(2,1)S(1)}, u32[]{:S(2)}, u32[]{:S(2)}) collective-permute-start(bf16[384,1280]{1,0:T(8,128)(2,1)S(1)} %pad_maximum_fusion.2.refs_4_), channel_id=1, source_target_pairs={{0,65},{1,64},{2,67},{3,66},{4,69},{5,68},{6,71},{7,70},{8,14},{9,... | collective-permute-start | bytes 2949128 | tf_op jit(solution)/shard_map/ppermute | solution.py:33
  81.2 19.7 %collective-permute-start.12 = (bf16[384,1280]{1,0:T(8,128)(2,1)S(1)}, bf16[384,1280]{1,0:T(8,128)(2,1)S(1)}, u32[]{:S(2)}, u32[]{:S(2)}) collective-permute-start(bf16[384,1280]{1,0:T(8,128)(2,1)S(1)} %pad_maximum_fusion.2.refs_4_), channel_id=1, source_target_pairs={{0,1},{1,0},{2,3},{3,2},{4,5},{5,4},{6,7},{7,6},{8,12},{9,13},{10,... | collective-permute-start | bytes 2949128 | tf_op jit(solution)/shard_map/ppermute | solution.py:33
  93.8 28.5 %collective-permute-start.8 = (bf16[2,4,80,512]{3,2,1,0:T(8,128)(2,1)S(1)}, bf16[2,4,80,512]{3,2,1,0:T(8,128)(2,1)S(1)}, u32[]{:S(2)}, u32[]{:S(2)}) collective-permute-start(bf16[2,4,80,512]{3,2,1,0:T(8,128)(2,1)S(1)} %get-tuple-element.30), channel_id=1, source_target_pairs={{0,16},{1,17},{2,18},{3,19},{4,20},{5,21},{6,22},{7,23},{8,24},{9,... | collective-permute-start | bytes 1966088 | tf_op jit(solution)/shard_map/ppermute | solution.py:33
  95.2 27.2 %collective-permute-start.9 = (bf16[2,4,80,512]{3,2,1,0:T(8,128)(2,1)S(1)}, bf16[2,4,80,512]{3,2,1,0:T(8,128)(2,1)S(1)}, u32[]{:S(2)}, u32[]{:S(2)}) collective-permute-start(bf16[2,4,80,512]{3,2,1,0:T(8,128)(2,1)S(1)} %get-tuple-element.31), channel_id=1, source_target_pairs={{0,48},{1,49},{2,50},{3,51},{4,52},{5,53},{6,54},{7,55},{8,56},{9,... | collective-permute-start | bytes 1966088 | tf_op jit(solution)/shard_map/ppermute | solution.py:33
  122.4 6.9 %collective-permute-start.14 = (bf16[4,80,512]{2,1,0:T(8,128)(2,1)S(1)}, bf16[4,80,512]{2,1,0:T(8,128)(2,1)S(1)}, u32[]{:S(2)}, u32[]{:S(2)}) collective-permute-start(bf16[4,80,512]{2,1,0:T(8,128)(2,1)S(1)} %fusion.15), channel_id=1, source_target_pairs={{0,48},{1,49},{2,50},{3,51},{4,52},{5,53},{6,54},{7,55},{8,56},{9,... | collective-permute-start | bytes 983048 | tf_op jit(solution)/shard_map/ppermute | solution.py:33
  125.4 7.2 %collective-permute-start.13 = (bf16[4,80,512]{2,1,0:T(8,128)(2,1)S(1)}, bf16[4,80,512]{2,1,0:T(8,128)(2,1)S(1)}, u32[]{:S(2)}, u32[]{:S(2)}) collective-permute-start(bf16[4,80,512]{2,1,0:T(8,128)(2,1)S(1)} %fusion.16), channel_id=1, source_target_pairs={{0,16},{1,17},{2,18},{3,19},{4,20},{5,21},{6,22},{7,23},{8,24},{9,... | collective-permute-start | bytes 983048 | tf_op jit(solution)/shard_map/ppermute | solution.py:33
  125.5 27.7 %collective-permute-start.20 = (bf16[2,4,80,1280]{3,2,1,0:T(8,128)(2,1)}, bf16[2,4,80,1280]{3,2,1,0:T(8,128)(2,1)S(1)}, u32[]{:S(2)}, u32[]{:S(2)}) collective-permute-start(bf16[2,4,80,1280]{3,2,1,0:T(8,128)(2,1)} %get-tuple-element.42), channel_id=1, source_target_pairs={{0,6},{1,7},{2,0},{3,1},{4,2},{5,3},{6,4},{7,5},{8,73},{9,72},{10,... | collective-permute-start | bytes 4915208 | tf_op jit(solution)/shard_map/ppermute | solution.py:33
  129.3 27.8 %collective-permute-start.21 = (bf16[2,4,80,1280]{3,2,1,0:T(8,128)(2,1)S(1)}, bf16[2,4,80,1280]{3,2,1,0:T(8,128)(2,1)S(1)}, u32[]{:S(2)}, u32[]{:S(2)}) collective-permute-start(bf16[2,4,80,1280]{3,2,1,0:T(8,128)(2,1)S(1)} %copy-done.9), channel_id=1, source_target_pairs={{0,2},{1,3},{2,4},{3,5},{4,6},{5,7},{6,0},{7,1},{8,72},{9,73},{10,... | collective-permute-start | bytes 4915208 | tf_op jit(solution)/shard_map/ppermute | solution.py:33
  132.9 16.5 %collective-permute-start.15 = (bf16[2,80,512]{2,1,0:T(8,128)(2,1)S(1)}, bf16[2,80,512]{2,1,0:T(8,128)(2,1)S(1)}, u32[]{:S(2)}, u32[]{:S(2)}) collective-permute-start(bf16[2,80,512]{2,1,0:T(8,128)(2,1)S(1)} %pad_maximum_fusion.9), channel_id=1, source_target_pairs={{0,6},{1,7},{2,0},{3,1},{4,2},{5,3},{6,4},{7,5},{8,73},{9,72},{10,... | collective-permute-start | bytes 491528 | tf_op jit(solution)/shard_map/ppermute | solution.py:33
  136.9 16.0 %collective-permute-start.16 = (bf16[2,80,512]{2,1,0:T(8,128)(2,1)S(1)}, bf16[2,80,512]{2,1,0:T(8,128)(2,1)S(1)}, u32[]{:S(2)}, u32[]{:S(2)}) collective-permute-start(bf16[2,80,512]{2,1,0:T(8,128)(2,1)S(1)} %pad_maximum_fusion.10), channel_id=1, source_target_pairs={{0,2},{1,3},{2,4},{3,5},{4,6},{5,7},{6,0},{7,1},{8,72},{9,73},{10,... | collective-permute-start | bytes 491528 | tf_op jit(solution)/shard_map/ppermute | solution.py:33
  149.5 8.9 %collective-permute-start.18 = (bf16[80,512]{1,0:T(8,128)(2,1)S(1)}, bf16[80,512]{1,0:T(8,128)(2,1)S(1)}, u32[]{:S(2)}, u32[]{:S(2)}) collective-permute-start(bf16[80,512]{1,0:T(8,128)(2,1)S(1)} %fusion.37), channel_id=1, source_target_pairs={{0,6},{1,7},{2,0},{3,1},{4,2},{5,3},{6,4},{7,5},{8,73},{9,72},{10,... | collective-permute-start | bytes 245768 | tf_op jit(solution)/shard_map/ppermute | solution.py:33
  152.9 5.5 %collective-permute-start.17 = (bf16[80,512]{1,0:T(8,128)(2,1)S(1)}, bf16[80,512]{1,0:T(8,128)(2,1)S(1)}, u32[]{:S(2)}, u32[]{:S(2)}) collective-permute-start(bf16[80,512]{1,0:T(8,128)(2,1)S(1)} %fusion.36), channel_id=1, source_target_pairs={{0,2},{1,3},{2,4},{3,5},{4,6},{5,7},{6,0},{7,1},{8,72},{9,73},{10,... | collective-permute-start | bytes 245768 | tf_op jit(solution)/shard_map/ppermute | solution.py:33
  154.4 12.9 %collective-permute-start.23 = (bf16[4,80,1280]{2,1,0:T(8,128)(2,1)}, bf16[4,80,1280]{2,1,0:T(8,128)(2,1)}, u32[]{:S(2)}, u32[]{:S(2)}) collective-permute-start(bf16[4,80,1280]{2,1,0:T(8,128)(2,1)} %fusion), channel_id=1, source_target_pairs={{0,6},{1,7},{2,0},{3,1},{4,2},{5,3},{6,4},{7,5},{8,73},{9,72},{10,... | collective-permute-start | bytes 2457608 | tf_op jit(solution)/shard_map/ppermute | solution.py:33
  158.4 13.0 %collective-permute-start.22 = (bf16[4,80,1280]{2,1,0:T(8,128)(2,1)}, bf16[4,80,1280]{2,1,0:T(8,128)(2,1)}, u32[]{:S(2)}, u32[]{:S(2)}) collective-permute-start(bf16[4,80,1280]{2,1,0:T(8,128)(2,1)} %fusion.1), channel_id=1, source_target_pairs={{0,2},{1,3},{2,4},{3,5},{4,6},{5,7},{6,0},{7,1},{8,72},{9,73},{10,... | collective-permute-start | bytes 2457608 | tf_op jit(solution)/shard_map/ppermute | solution.py:33
  158.5 7.7 %collective-permute-start.19 = (bf16[80,512]{1,0:T(8,128)(2,1)S(1)}, bf16[80,512]{1,0:T(8,128)(2,1)S(1)}, u32[]{:S(2)}, u32[]{:S(2)}) collective-permute-start(bf16[80,512]{1,0:T(8,128)(2,1)S(1)} %get-tuple-element.49), channel_id=1, source_target_pairs={{0,8},{1,9},{2,10},{3,11},{4,12},{5,13},{6,14},{7,15},{8,0},{9,1},... | collective-permute-start | bytes 245768 | tf_op jit(solution)/shard_map/ppermute | solution.py:33
  167.3 85.5 %all-gather.5.cloned.1.call-start = ((), (), s32[]{:S(2)}) async-start(), calls=%async_computation.1 | async-start | bytes 6963200 | tf_op jit(solution)/shard_map/all_gather | solution.py:276
  174.5 9.0 %collective-permute-start.24 = (bf16[2,80,1280]{2,1,0:T(8,128)(2,1)S(1)}, bf16[2,80,1280]{2,1,0:T(8,128)(2,1)S(1)}, u32[]{:S(2)}, u32[]{:S(2)}) collective-permute-start(bf16[2,80,1280]{2,1,0:T(8,128)(2,1)S(1)} %pad_maximum_fusion.4), channel_id=1, source_target_pairs={{0,48},{1,49},{2,50},{3,51},{4,52},{5,53},{6,54},{7,55},{8,56},{9,... | collective-permute-start | bytes 1228808 | tf_op jit(solution)/shard_map/ppermute | solution.py:33
  177.2 8.9 %collective-permute-start.25 = (bf16[2,80,1280]{2,1,0:T(8,128)(2,1)S(1)}, bf16[2,80,1280]{2,1,0:T(8,128)(2,1)S(1)}, u32[]{:S(2)}, u32[]{:S(2)}) collective-permute-start(bf16[2,80,1280]{2,1,0:T(8,128)(2,1)S(1)} %pad_maximum_fusion.5), channel_id=1, source_target_pairs={{0,16},{1,17},{2,18},{3,19},{4,20},{5,21},{6,22},{7,23},{8,24},{9,... | collective-permute-start | bytes 1228808 | tf_op jit(solution)/shard_map/ppermute | solution.py:33
  183.6 10.2 %collective-permute-start.27 = (bf16[80,1280]{1,0:T(8,128)(2,1)S(1)}, bf16[80,1280]{1,0:T(8,128)(2,1)S(1)}, u32[]{:S(2)}, u32[]{:S(2)}) collective-permute-start(bf16[80,1280]{1,0:T(8,128)(2,1)S(1)} %fusion.33), channel_id=1, source_target_pairs={{0,48},{1,49},{2,50},{3,51},{4,52},{5,53},{6,54},{7,55},{8,56},{9,... | collective-permute-start | bytes 614408 | tf_op jit(solution)/shard_map/ppermute | solution.py:33
  186.2 10.3 %collective-permute-start.26 = (bf16[80,1280]{1,0:T(8,128)(2,1)S(1)}, bf16[80,1280]{1,0:T(8,128)(2,1)S(1)}, u32[]{:S(2)}, u32[]{:S(2)}) collective-permute-start(bf16[80,1280]{1,0:T(8,128)(2,1)S(1)} %fusion.32), channel_id=1, source_target_pairs={{0,16},{1,17},{2,18},{3,19},{4,20},{5,21},{6,22},{7,23},{8,24},{9,... | collective-permute-start | bytes 614408 | tf_op jit(solution)/shard_map/ppermute | solution.py:33
  196.7 11.9 %collective-permute-start.28 = (bf16[80,1280]{1,0:T(8,128)(2,1)S(1)}, bf16[80,1280]{1,0:T(8,128)(2,1)S(1)}, u32[]{:S(2)}, u32[]{:S(2)}) collective-permute-start(bf16[80,1280]{1,0:T(8,128)(2,1)S(1)} %get-tuple-element.52), channel_id=1, source_target_pairs={{0,8},{1,9},{2,10},{3,11},{4,12},{5,13},{6,14},{7,15},{8,0},{9,1},... | collective-permute-start | bytes 614408 | tf_op jit(solution)/shard_map/ppermute | solution.py:33
  (9 other events, 105.0 us)
Sparse Core Ops, SparseCore 0:
  167.4 39.6 all-gather.2
  210.4 42.3 all-gather.4

commit v3 on v2

--- a/solution.py
+++ b/solution.py
@@ -9,7 +9,7 @@
 from jax.sharding import PartitionSpec as P
 
 AXES = ("inter", "intra")
-WIDTHS = (512, 1280)
+WIDTHS = (768, 1024)
 
 
 def device(x, y, z, c):
@@ -65,9 +65,8 @@
 
     def kernel(where_ref, *refs):
         for place in range(count):
-            target = refs[2 * count + place]
-            target[:tokens, :] = refs[place][...]
-            target[tokens:, :] = refs[count + place][...]
+            both = jnp.concatenate([refs[place][...], refs[count + place][...]], axis=0)
+            refs[2 * count + place][...] = both.T
 
     def source_map(step):
         def index(g, w):
@@ -83,9 +82,9 @@
             num_scalar_prefetch=1,
             grid=(4,),
             in_specs=maps + maps,
-            out_specs=[pl.BlockSpec((2 * tokens, piece), lambda g, w: (0, g))] * count,
-        ),
-        out_shape=[jax.ShapeDtypeStruct((2 * tokens, hidden // 4), mine.dtype)] * count,
+            out_specs=[pl.BlockSpec((piece, 2 * tokens), lambda g, w: (g, 0))] * count,
+        ),
+        out_shape=[jax.ShapeDtypeStruct((hidden // 4, 2 * tokens), mine.dtype)] * count,
         cost_estimate=pl.CostEstimate(
             flops=0, bytes_accessed=count * 2 * tokens * hidden, transcendentals=0
         ),
@@ -94,16 +93,15 @@
 
 
 def partial_sums(where, blocks, inputs, y_first):
-    tokens, rows = blocks[0].shape
+    rows, tokens = blocks[0].shape
     width = inputs[0].shape[1]
     piece = rows // 4
     unit = piece // 8
-    tile = 256
 
     def kernel(where_ref, *refs):
         block_refs, input_refs = refs[:4], refs[4:8]
-        plus_ref, minus_ref, first_ref, third_ref, keep_ref = refs[8:13]
-        held, turned, total = refs[13:]
+        out_refs = refs[8:-2]
+        held, total = refs[-2:]
         g = pl.program_id(0)
 
         @pl.when(g == 0)
@@ -111,20 +109,22 @@
             for step in range(4):
                 held[pl.ds(step * tokens, tokens), :] = input_refs[step][...]
 
-        for step in range(4):
-            turned[:, pl.ds(step * tokens, tokens)] = block_refs[step][...].T
-
-        @pl.loop(0, width // tile)
-        def _(column):
-            at = pl.ds(pl.multiple_of(column * tile, tile), tile)
-            total[:, at] = jnp.dot(
-                turned[...], held[:, at], preferred_element_type=jnp.float32
-            ).astype(jnp.bfloat16)
+        turned = jnp.concatenate([ref[...] for ref in block_refs], axis=1)
+        total[...] = jnp.dot(turned, held[...], preferred_element_type=jnp.float32).astype(jnp.bfloat16)
 
         step_g = lax.rem(g - where_ref[1] + 4, 4)
+        if not y_first:
+            for distance, ref in enumerate(out_refs):
+
+                @pl.when(step_g == distance)
+                def _(ref=ref):
+                    for to_y in range(4):
+                        ref[lax.rem(to_y - where_ref[2] + 4, 4)] = total[pl.ds(to_y * 2 * unit, 2 * unit), :]
+
+            return
+        plus_ref, minus_ref, first_ref, third_ref, keep_ref = out_refs
         for to_y in range(4):
             step_y = lax.rem(to_y - where_ref[2] + 4, 4)
-            first, second = (step_y, step_g) if y_first else (step_g, step_y)
             for half in range(2):
                 start = (to_y * 2 + half) * unit
                 places = {
@@ -135,35 +135,37 @@
                 }
                 for distance, (ref, slot) in places.items():
 
-                    @pl.when(first == distance)
-                    def _(ref=ref, slot=slot, start=start, second=second):
+                    @pl.when(step_y == distance)
+                    def _(ref=ref, slot=slot, start=start):
                         value = total[pl.ds(start, unit), :]
                         if slot is None:
-                            ref[second] = value
+                            ref[step_g] = value
                         else:
-                            ref[slot, second] = value
+                            ref[slot, step_g] = value
 
     def whole(shape):
         return pl.BlockSpec(shape, lambda g, w: (0,) * len(shape))
 
-    two, one = (2, 4, unit, width), (4, unit, width)
-    shapes = (two, two, one, one, two)
+    if y_first:
+        two, one = (2, 4, unit, width), (4, unit, width)
+        shapes = (two, two, one, one, two)
+    else:
+        shapes = ((4, 2 * unit, width),) * 4
     return pl.pallas_call(
         kernel,
         grid_spec=pltpu.PrefetchScalarGridSpec(
             num_scalar_prefetch=1,
             grid=(4,),
-            in_specs=[pl.BlockSpec((tokens, piece), lambda g, w: (0, g))] * 4
+            in_specs=[pl.BlockSpec((piece, tokens), lambda g, w: (g, 0))] * 4
             + [whole(value.shape) for value in inputs],
             out_specs=[whole(shape) for shape in shapes],
             scratch_shapes=[
                 pltpu.VMEM((4 * tokens, width), jnp.bfloat16),
-                pltpu.VMEM((piece, 4 * tokens), jnp.bfloat16),
                 pltpu.VMEM((piece, width), jnp.bfloat16),
             ],
         ),
         out_shape=[jax.ShapeDtypeStruct(shape, jnp.bfloat16) for shape in shapes],
-        compiler_params=pltpu.CompilerParams(vmem_limit_bytes=48 * 1024 * 1024),
+        compiler_params=pltpu.CompilerParams(vmem_limit_bytes=40 * 1024 * 1024),
         cost_estimate=pl.CostEstimate(
             flops=2 * 4 * tokens * rows * width,
             bytes_accessed=4 * tokens * (rows + width) * 2 + rows * width * 2,
@@ -195,15 +197,87 @@
     return left, right
 
 
-def ring_end(keep, from_left, from_right, left, right):
-    low = wide(keep[0]) + wide(from_right[1]) + wide(left)
-    high = wide(keep[1]) + wide(from_left[1]) + wide(right)
-    return narrow(low), narrow(high)
-
-
-def second_round(low, high):
-    plus, minus = jnp.stack([low[2], high[1]]), jnp.stack([high[2], low[3]])
-    return plus, minus, low[1], high[3], jnp.stack([low[0], high[0]])
+def ring_end(keep, from_left, from_right, left, right, place):
+    low = wide(keep[0, place]) + wide(from_right[1, place]) + wide(left[place])
+    high = wide(keep[1, place]) + wide(from_left[1, place]) + wide(right[place])
+    return narrow(jnp.concatenate([low, high], axis=0))
+
+
+def direct(pieces, along):
+    return [pieces[0]] + [send(pieces[step], along(step)) for step in (1, 3, 2)]
+
+
+def summed(received, place=None):
+    return narrow(sum(wide(value if place is None else value[place]) for value in received))
+
+
+def near_and_pair(first, second):
+    def move(x, y, z, c):
+        steps = first if c == 0 else second
+        return (x, y, z ^ 1, c) if steps is None else (x, y + steps, z, c)
+
+    return move
+
+
+def gather_rows(value, c):
+    def choose(low, high):
+        return jnp.where(c == 0, low, high)
+
+    one = send(value, near_and_pair(1, None))
+    two = send(value, near_and_pair(-1, 1))
+    three = send(value, near_and_pair(2, -1))
+    four = send(value, near_and_pair(None, 2))
+    five = send(one, near_and_pair(None, 1))
+    six = send(choose(two, one), near_and_pair(None, -1))
+    seven = send(choose(three, one), near_and_pair(None, 2))
+    own = [value, one, two, three, four, five, six, seven]
+    swapped = [send(part, sibling) for part in own]
+    y_steps = jnp.where(c == 0, jnp.array([0, 3, 1, 2, 0, 3, 1, 2]), jnp.array([0, 0, 3, 1, 2, 3, 1, 2]))
+    z_steps = jnp.where(c == 0, jnp.array([0, 0, 0, 0, 1, 1, 1, 1]), jnp.array([0, 1, 0, 0, 0, 1, 1, 1]))
+    other_y = jnp.where(c == 1, jnp.array([0, 3, 1, 2, 0, 3, 1, 2]), jnp.array([0, 0, 3, 1, 2, 3, 1, 2]))
+    other_z = jnp.where(c == 1, jnp.array([0, 0, 0, 0, 1, 1, 1, 1]), jnp.array([0, 1, 0, 0, 0, 1, 1, 1]))
+    return own + swapped, jnp.concatenate([y_steps, other_y]), jnp.concatenate([z_steps, other_z])
+
+
+def assemble(places, gathered, parts, columns):
+    rows, first = gathered.shape
+    unit, second = parts[0].shape
+    first, second, half = first // 2, second // 2, columns // 2
+
+    def kernel(places_ref, gathered_ref, *refs):
+        part_refs, out_ref, semaphores = refs[:-2], refs[-2], refs[-1]
+        copies = []
+        for side in range(2):
+            copies.append((gathered_ref.at[:, pl.ds(side * first, first)], out_ref.at[:, pl.ds(side * half, first)]))
+            for place, ref in enumerate(part_refs):
+                start = pl.multiple_of(places_ref[place] * unit, unit)
+                copies.append(
+                    (
+                        ref.at[:, pl.ds(side * second, second)],
+                        out_ref.at[pl.ds(start, unit), pl.ds(side * half + first, second)],
+                    )
+                )
+        copies = [
+            pltpu.make_async_copy(source, target, semaphores.at[place]) for place, (source, target) in enumerate(copies)
+        ]
+        for copy in copies:
+            copy.start()
+        for copy in copies:
+            copy.wait()
+
+    anywhere = pl.BlockSpec(memory_space=pl.ANY)
+    return pl.pallas_call(
+        kernel,
+        grid_spec=pltpu.PrefetchScalarGridSpec(
+            num_scalar_prefetch=1,
+            grid=(1,),
+            in_specs=[anywhere] * (1 + len(parts)),
+            out_specs=anywhere,
+            scratch_shapes=[pltpu.SemaphoreType.DMA((2 * (1 + len(parts)),))],
+        ),
+        out_shape=jax.ShapeDtypeStruct((rows, columns), jnp.bfloat16),
+        name="assemble_copy",
+    )(places, gathered, *parts)
 
 
 def adamw(grad, master, first_moment, second_moment):
@@ -229,7 +303,7 @@
     kept = jnp.where(c == 0, low, high)
     given = jnp.where(c == 0, high, low)
     chip_input = jnp.concatenate([kept, send(given, sibling)], axis=0)
-    other = send(up_cotangent, sibling)
+    other = send(after(up_cotangent, given), sibling)
 
     def spread(value):
         return [send(value, along_rows(step)) for step in (1, 3, 2)]
@@ -238,30 +312,24 @@
     inputs = [chip_input[:, start : start + width] for start, width in zip(starts, WIDTHS)]
     inputs_0 = [inputs[0], *spread(inputs[0])]
     near, far = pack(where, up_cotangent, other, (1, 3))
-    own, last = pack(where, up_cotangent, other, (0, 2))
+    near, far = after((near, far), inputs_0)
+    own, last = pack(after(where, near), up_cotangent, other, (0, 2))
     blocks = [own, send(near, along_rows(1)), send(far, along_rows(3)), send(last, along_rows(2))]
-    inputs_1 = [inputs[1], *spread(inputs[1])]
-
-    plus_0, minus_0, first_0, third_0, keep_0 = partial_sums(where, blocks, inputs_0, True)
-    sent_0 = ring_send(plus_0, minus_0, along_y)
+    inputs_1 = [inputs[1], *spread(after(inputs[1], blocks))]
+
+    plus, minus, first, third, keep = partial_sums(where, blocks, inputs_0, True)
+    sent_0 = ring_send(plus, minus, along_y)
     pieces_1 = partial_sums(where, blocks, inputs_1, False)
     sent_0, pieces_1 = lax.optimization_barrier((sent_0, pieces_1))
-    plus_1, minus_1, first_1, third_1, keep_1 = pieces_1
-    sent_1 = ring_send(plus_1, minus_1, along_sums)
-    turned_0 = ring_turn(first_0, third_0, *sent_0, along_y)
-    next_0 = second_round(*ring_end(keep_0, *sent_0, *turned_0))
-    again_0 = ring_send(next_0[0], next_0[1], along_sums)
-    turned_1 = ring_turn(first_1, third_1, *sent_1, along_sums)
-    last_0 = ring_turn(next_0[2], next_0[3], *again_0, along_sums)
-    summed_0 = ring_end(next_0[4], *again_0, *last_0)
-    next_1 = second_round(*ring_end(keep_1, *sent_1, *turned_1))
-    again_1 = ring_send(next_1[0], next_1[1], along_y)
-    last_1 = ring_turn(next_1[2], next_1[3], *again_1, along_y)
-    summed_1 = ring_end(next_1[4], *again_1, *last_1)
+    sent_1 = direct(pieces_1, along_sums)
+    turned_0 = ring_turn(first, third, *sent_0, along_y)
+    again_0 = direct([ring_end(keep, *sent_0, *turned_0, place) for place in range(4)], along_sums)
+    again_1 = direct([summed(sent_1, place) for place in range(4)], along_y)
 
     scale = 1.0 / math.sqrt(total_tokens)
     grads, copies = [], []
-    for (low, high), start, width in zip((summed_0, summed_1), starts, WIDTHS):
+    for rows, start, width in zip((summed(again_0), summed(again_1)), starts, WIDTHS):
+        low, high = rows[: rows.shape[0] // 2], rows[rows.shape[0] // 2 :]
         ours = jnp.where(c == 0, low, high)
         theirs = send(jnp.where(c == 0, high, low), sibling)
         grad = wide(jnp.concatenate([jnp.where(c == 0, ours, theirs), jnp.where(c == 0, theirs, ours)], axis=1)) * scale
@@ -272,8 +340,7 @@
                 [value[:, start : start + width], value[:, half + start : half + start + width]], axis=1
             )
 
-        fresh = narrow(adamw(grad, part(master), part(first_moment), part(second_moment))[0])
-        copies.append(lax.all_gather(fresh, "inter", axis=0, tiled=True))
+        copies.append(narrow(adamw(grad, part(master), part(first_moment), part(second_moment))[0]))
 
     def joined(parts):
         return jnp.concatenate(
@@ -282,8 +349,13 @@
             axis=1,
         )
 
+    gathered = lax.all_gather(copies[0], "inter", axis=0, tiled=True)
+    parts, y_steps, z_steps = gather_rows(copies[1], c)
+    cores = jnp.array([0] * 8 + [1] * 8)
+    places = (((z + z_steps) % 2) * 8 + ((y + y_steps) % 4) * 2 + (c + cores) % 2).astype(jnp.int32)
+    new_copy = assemble(places, gathered, parts, columns)
     new_master, new_first, new_second = adamw(joined(grads), master, first_moment, second_moment)
-    return (new_master, new_first, new_second, joined(copies))
+    return (new_master, new_first, new_second, new_copy)
 
 
 def solution(mesh):

time: 267 us -> 551 us (2.06)
  Pallas kernels: 43 us -> 311 us
  waiting for transfers between devices: 125 us -> 149 us
  starting transfers between devices: 59 us -> 52.5 us
    pallas_call x0 -> x1, Pallas kernels: none -> 280 us  [assemble(): pl.pallas_call(kernel, grid_spec=pltpu.PrefetchScalarGridSpec(num_scalar_...]
    ppermute x29 -> x41, waiting for transfers between devices: 89 us -> 149 us  [send(): return lax.ppermute(value, AXES, permutation(move))]
    all_gather x2 -> x1, waiting for transfers between devices: 36.1 us -> 0.02 us  [body(): gathered = lax.all_gather(copies[0], 'inter', axis=0, tiled=True)]
    pallas_call x2, Pallas kernels: 32.1 us -> 19.5 us  [partial_sums(): pl.pallas_call(kernel, grid_spec=pltpu.PrefetchScalarGridSpec(num_scalar_...]
    slice x4 -> x2, local copies, waits for them, and re-layouts: 7.43 us -> 0.09 us  [joined(): part[:, :width]]
    ppermute x29 -> x41, starting transfers between devices: 58.9 us -> 52.5 us  [send(): return lax.ppermute(value, AXES, permutation(move))]
    unnamed x20 -> x80, local copies, waits for them, and re-layouts: 1.35 us -> 7.64 us
  transfers between devices with their start and end apart: 31 -> 42, of which waited for: 14 -> 23; matrix products, arithmetic and copies ran while one was open for 6% -> 2% of each run, Pallas kernels for 14% -> 6%
where the time goes in v3:
time: 551 us
  Pallas kernels  311 us (56%)
  waiting for transfers between devices  149 us (27%)
  starting transfers between devices  52.5 us (10%)
  between operations  14.6 us (3%)
  other arithmetic  12.4 us (2%)
  local copies, waits for them, and re-layouts  11.5 us (2%)
    pallas_call x1, Pallas kernels, assemble(): pl.pallas_call(kernel, grid_spec=pltpu.PrefetchScalarGridSpec(num_scalar_...  280 us
    ppermute x41, waiting for transfers between devices, send(): return lax.ppermute(value, AXES, permutation(move))  149 us
    ppermute x41, starting transfers between devices, send(): return lax.ppermute(value, AXES, permutation(move))  52.5 us
    pallas_call x2, Pallas kernels, partial_sums(): pl.pallas_call(kernel, grid_spec=pltpu.PrefetchScalarGridSpec(num_scalar_...  19.5 us
    pallas_call x2, Pallas kernels, pack(): pl.pallas_call(kernel, grid_spec=pltpu.PrefetchScalarGridSpec(num_scalar_...  11.5 us
  transfers between devices with their start and end apart: 42, of which 23 were waited for; matrix products, arithmetic and copies ran while one was open for 2% of the time, Pallas kernels for 6%

profile of v3, /device:TPU:1, one launch (start us, length us, event | category | flops | bytes accessed | tf_op | source)
XLA Modules:
  0.0 550.8 jit_solution(15927388072322158939)
XLA Ops:
  10.2 7.2 %collective-permute-done.1 = bf16[192,1792]{1,0:T(8,128)(2,1)S(1)} collective-permute-done((bf16[192,1792]{1,0:T(8,128)(2,1)S(1)}, bf16[192,1792]{1,0:T(8,128)(2,1)S(1)}, u32[]{:S(2)}, u32[]{:S(2)}) %collective-permute-start.1) | collective-permute-done | bytes 688160 | tf_op jit(solution)/shard_map/ppermute | solution.py:33
  22.5 5.8 %pack_cotangent.2 = (bf16[2560,384]{1,0:T(8,128)(2,1)}, bf16[2560,384]{1,0:T(8,128)(2,1)}) custom-call(s32[4]{0:T(128)} %pad_add_fusion.where_ref, bf16[192,10240]{1,0:T(8,128)(2,1)} %refs_1_.3, bf16[192,10240]{1,0:T(8,128)(2,1)} %refs_1_.3, bf16[192,10240]{1,0:T(8,128)(2,1)} %collective-permute-done.refs_2_.refs_3_, ...), custom_call_target="tpu_custom_call" | custom-call | bytes 7864320 | tf_op jit(solution)/shard_map/pack_cotangent/pallas_call | solution.py:79
  29.1 6.1 %collective-permute-done.4.refs_7_ = bf16[384,768]{1,0:T(8,128)(2,1)S(1)} collective-permute-done((bf16[384,768]{1,0:T(8,128)(2,1)S(1)}, bf16[384,768]{1,0:T(8,128)(2,1)S(1)}, u32[]{:S(2)}, u32[]{:S(2)}) %collective-permute-start.4) | collective-permute-done | bytes 589856 | tf_op jit(solution)/shard_map/ppermute | solution.py:33
  36.8 5.7 %pack_cotangent.3 = (bf16[2560,384]{1,0:T(8,128)(2,1)}, bf16[2560,384]{1,0:T(8,128)(2,1)}) custom-call(s32[4]{0:T(128)} %pad_add_fusion.where_ref, bf16[192,10240]{1,0:T(8,128)(2,1)} %refs_1_.3, bf16[192,10240]{1,0:T(8,128)(2,1)} %refs_1_.3, bf16[192,10240]{1,0:T(8,128)(2,1)} %collective-permute-done.refs_2_.refs_3_, ...), custom_call_target="tpu_custom_call" | custom-call | bytes 7864320 | tf_op jit(solution)/shard_map/pack_cotangent/pallas_call | solution.py:79
  42.6 2.8 collective-permute-start.7
  46.6 36.6 %collective-permute-done.7.refs_3_ = bf16[2560,384]{1,0:T(8,128)(2,1)S(1)} collective-permute-done((bf16[2560,384]{1,0:T(8,128)(2,1)}, bf16[2560,384]{1,0:T(8,128)(2,1)S(1)}, u32[]{:S(2)}, u32[]{:S(2)}) %collective-permute-start.7) | collective-permute-done | bytes 1966112 | tf_op jit(solution)/shard_map/ppermute | solution.py:33
  83.2 5.5 collective-permute-done.6.refs_2_
  89.2 2.1 collective-permute-start.11
  94.0 8.4 %partial_sums.2 = (bf16[2,4,80,768]{3,2,1,0:T(8,128)(2,1)S(1)}, bf16[2,4,80,768]{3,2,1,0:T(8,128)(2,1)S(1)}, bf16[4,80,768]{2,1,0:T(8,128)(2,1)S(1)}, bf16[4,80,...) custom-call(s32[4]{0:T(128)S(1)} %copy-done, bf16[2560,384]{1,0:T(8,128)(2,1)S(1)} %copy-done.1, ...), custom_call_target="tpu_custom_call" | custom-call | flops 6039797760 | bytes 14155776 | tf_op jit(solution)/shard_map/partial_sums/pallas_call | solution.py:154
  105.3 3.4 collective-permute-done.11.refs_6_
  110.0 11.1 %partial_sums.3 = (bf16[4,160,1024]{2,1,0:T(8,128)(2,1)S(1)}, bf16[4,160,1024]{2,1,0:T(8,128)(2,1)S(1)}, bf16[4,160,1024]{2,1,0:T(8,128)(2,1)S(1)}, bf16[4,160,1024]{2,1,0:T(8,128)(2,1)S(1)}) custom-call(s32[4]{0:T(128)S(1)} %copy-done, bf16[2560,384]{1,0:T(8,128)(2,1)S(1)} %copy-done.1, bf16[2560,384]{1,0:T(8,128)(2,1)S(1)} %collective-permute-done.5.refs_1_, ...), custom_call_target="tpu_custom_call" | custom-call | flops 8053063680 | bytes 16252928 | tf_op jit(solution)/shard_map/partial_sums/pallas_call | solution.py:154
  124.1 2.3 collective-permute-start.14
  126.4 6.1 %collective-permute-done.13 = bf16[4,80,768]{2,1,0:T(8,128)(2,1)S(1)} collective-permute-done((bf16[4,80,768]{2,1,0:T(8,128)(2,1)S(1)}, bf16[4,80,768]{2,1,0:T(8,128)(2,1)S(1)}, u32[]{:S(2)}, u32[]{:S(2)}) %collective-permute-start.13) | collective-permute-done | bytes 491552 | tf_op jit(solution)/shard_map/ppermute | solution.py:33
  134.4 7.5 %collective-permute-start.16 = (bf16[160,768]{1,0:T(8,128)(2,1)S(1)}, bf16[160,768]{1,0:T(8,128)(2,1)S(1)}, u32[]{:S(2)}, u32[]{:S(2)}) collective-permute-start(bf16[160,768]{1,0:T(8,128)(2,1)S(1)} %pad_maximum_fusion.7), channel_id=1, source_target_pairs={{0,6},{1,7},{2,0},{3,1},{4,2},{5,3},{6,4},{7,5},{8,73},{9,72},{10,... | collective-permute-start | bytes 737288 | tf_op jit(solution)/shard_map/ppermute | solution.py:33
  145.7 2.0 collective-permute-done.16
  149.6 1.9 collective-permute-start.18
  155.0 4.0 collective-permute-start.20
  160.1 17.4 %collective-permute-done.19 = bf16[4,160,1024]{2,1,0:T(8,128)(2,1)S(1)} collective-permute-done((bf16[4,160,1024]{2,1,0:T(8,128)(2,1)}, bf16[4,160,1024]{2,1,0:T(8,128)(2,1)S(1)}, u32[]{:S(2)}, u32[]{:S(2)}) %collective-permute-start.19) | collective-permute-done | bytes 1310752 | tf_op jit(solution)/shard_map/ppermute | solution.py:33
  177.5 3.1 collective-permute-done.20
  180.6 27.2 %collective-permute-done.21 = bf16[4,160,1024]{2,1,0:T(8,128)(2,1)S(1)} collective-permute-done((bf16[4,160,1024]{2,1,0:T(8,128)(2,1)S(1)}, bf16[4,160,1024]{2,1,0:T(8,128)(2,1)S(1)}, u32[]{:S(2)}, u32[]{:S(2)}) %collective-permute-start.21) | collective-permute-done | bytes 1310752 | tf_op jit(solution)/shard_map/ppermute | solution.py:33
  209.6 2.8 collective-permute-start.23
  214.7 2.4 collective-permute-done.22
  217.0 3.1 collective-permute-done.23
  221.7 1.9 fusion.14
  227.6 1.8 collective-permute-start.28
  232.1 5.5 collective-permute-done.27.refs_2_
  237.5 6.2 %collective-permute-done.28.refs_3_ = bf16[80,2048]{1,0:T(8,128)(2,1)S(1)} collective-permute-done((bf16[80,2048]{1,0:T(8,128)(2,1)S(1)}, bf16[80,2048]{1,0:T(8,128)(2,1)S(1)}, u32[]{:S(2)}, u32[]{:S(2)}) %collective-permute-start.28) | collective-permute-done | bytes 327712 | tf_op jit(solution)/shard_map/ppermute | solution.py:33
  243.8 3.6 collective-permute-start.31
  249.0 6.0 %collective-permute-done.31.refs_6_ = bf16[80,2048]{1,0:T(8,128)(2,1)S(1)} collective-permute-done((bf16[80,2048]{1,0:T(8,128)(2,1)S(1)}, bf16[80,2048]{1,0:T(8,128)(2,1)S(1)}, u32[]{:S(2)}, u32[]{:S(2)}) %collective-permute-start.31) | collective-permute-done | bytes 327712 | tf_op jit(solution)/shard_map/ppermute | solution.py:33
  255.6 2.5 collective-permute-done.30.refs_5_
  260.4 2.3 multiply_subtract_fusion
  263.9 280.0 %assemble_copy.1 = bf16[1280,3584]{1,0:T(8,128)(2,1)} custom-call(s32[16]{0:T(128)} %fusion.39.places_ref, bf16[1280,1536]{1,0:T(8,128)(2,1)} %all-gather.2.cloned.1.call-done.gathered_ref, bf16[80,2048]{1,0:T(8,128)(2,1)} %copy-done.19, bf16[80,2048]{1,0:T(8,128)(2,1)} %copy-done.20, bf16[80,2048]{1,0:T(8,128)(2,1)} %copy-done.21, ...), custom_call_target="tpu_custom_call" | custom-call | tf_op jit(solution)/shard_map/assemble_copy/pallas_call | solution.py:269
  (168 shorter events, 52.0 us)
Async XLA Ops:
  7.2 255.7 %all-gather.2.cloned.1.call-start = ((), (), s32[]{:S(2)}) async-start(), calls=%async_computation | async-start | bytes 4177920 | tf_op jit(solution)/shard_map/all_gather | solution.py:352
  8.6 13.8 %collective-permute-start = (bf16[192,10240]{1,0:T(8,128)(2,1)}, bf16[192,10240]{1,0:T(8,128)(2,1)}, u32[]{:S(2)}, u32[]{:S(2)}) collective-permute-start(bf16[192,10240]{1,0:T(8,128)(2,1)} %refs_1_.3), channel_id=1, source_target_pairs={{0,8},{1,9},{2,10},{3,11},{4,12},{5,13},{6,14},{7,15},{8,0},{9,1},... | collective-permute-start | bytes 11796488 | tf_op jit(solution)/shard_map/ppermute | solution.py:33
  17.5 10.8 %collective-permute-start.2 = (bf16[384,768]{1,0:T(8,128)(2,1)S(1)}, bf16[384,768]{1,0:T(8,128)(2,1)S(1)}, u32[]{:S(2)}, u32[]{:S(2)}) collective-permute-start(bf16[384,768]{1,0:T(8,128)(2,1)S(1)} %pad_maximum_fusion.3.refs_4_), channel_id=1, source_target_pairs={{0,64},{1,65},{2,66},{3,67},{4,68},{5,69},{6,70},{7,71},{8,10},{9,... | collective-permute-start | bytes 1769480 | tf_op jit(solution)/shard_map/ppermute | solution.py:33
  18.8 9.4 %collective-permute-start.3 = (bf16[384,768]{1,0:T(8,128)(2,1)S(1)}, bf16[384,768]{1,0:T(8,128)(2,1)S(1)}, u32[]{:S(2)}, u32[]{:S(2)}) collective-permute-start(bf16[384,768]{1,0:T(8,128)(2,1)S(1)} %pad_maximum_fusion.3.refs_4_), channel_id=1, source_target_pairs={{0,65},{1,64},{2,67},{3,66},{4,69},{5,68},{6,71},{7,70},{8,14},{9,... | collective-permute-start | bytes 1769480 | tf_op jit(solution)/shard_map/ppermute | solution.py:33
  20.2 14.9 %collective-permute-start.4 = (bf16[384,768]{1,0:T(8,128)(2,1)S(1)}, bf16[384,768]{1,0:T(8,128)(2,1)S(1)}, u32[]{:S(2)}, u32[]{:S(2)}) collective-permute-start(bf16[384,768]{1,0:T(8,128)(2,1)S(1)} %pad_maximum_fusion.3.refs_4_), channel_id=1, source_target_pairs={{0,1},{1,0},{2,3},{3,2},{4,5},{5,4},{6,7},{7,6},{8,12},{9,13},{10,... | collective-permute-start | bytes 1769480 | tf_op jit(solution)/shard_map/ppermute | solution.py:33
  36.0 47.2 %collective-permute-start.5 = (bf16[2560,384]{1,0:T(8,128)(2,1)}, bf16[2560,384]{1,0:T(8,128)(2,1)S(1)}, u32[]{:S(2)}, u32[]{:S(2)}) collective-permute-start(bf16[2560,384]{1,0:T(8,128)(2,1)} %get-tuple-element.31), channel_id=1, source_target_pairs={{0,64},{1,65},{2,66},{3,67},{4,68},{5,69},{6,70},{7,71},{8,10},{9,... | collective-permute-start | bytes 5898248 | tf_op jit(solution)/shard_map/ppermute | solution.py:33
  42.6 40.6 %collective-permute-start.7 = (bf16[2560,384]{1,0:T(8,128)(2,1)}, bf16[2560,384]{1,0:T(8,128)(2,1)S(1)}, u32[]{:S(2)}, u32[]{:S(2)}) collective-permute-start(bf16[2560,384]{1,0:T(8,128)(2,1)} %get-tuple-element.35), channel_id=1, source_target_pairs={{0,1},{1,0},{2,3},{3,2},{4,5},{5,4},{6,7},{7,6},{8,12},{9,13},{10,... | collective-permute-start | bytes 5898248 | tf_op jit(solution)/shard_map/ppermute | solution.py:33
  45.4 43.3 %collective-permute-start.6 = (bf16[2560,384]{1,0:T(8,128)(2,1)}, bf16[2560,384]{1,0:T(8,128)(2,1)S(1)}, u32[]{:S(2)}, u32[]{:S(2)}) collective-permute-start(bf16[2560,384]{1,0:T(8,128)(2,1)} %get-tuple-element.34), channel_id=1, source_target_pairs={{0,65},{1,64},{2,67},{3,66},{4,69},{5,68},{6,71},{7,70},{8,14},{9,... | collective-permute-start | bytes 5898248 | tf_op jit(solution)/shard_map/ppermute | solution.py:33
  88.7 16.7 %collective-permute-start.10 = (bf16[384,1024]{1,0:T(8,128)(2,1)S(1)}, bf16[384,1024]{1,0:T(8,128)(2,1)S(1)}, u32[]{:S(2)}, u32[]{:S(2)}) collective-permute-start(bf16[384,1024]{1,0:T(8,128)(2,1)S(1)} %pad_maximum_fusion.1.refs_4_), channel_id=1, source_target_pairs={{0,64},{1,65},{2,66},{3,67},{4,68},{5,69},{6,70},{7,71},{8,10},{9,... | collective-permute-start | bytes 2359304 | tf_op jit(solution)/shard_map/ppermute | solution.py:33
  89.2 19.5 %collective-permute-start.11 = (bf16[384,1024]{1,0:T(8,128)(2,1)S(1)}, bf16[384,1024]{1,0:T(8,128)(2,1)S(1)}, u32[]{:S(2)}, u32[]{:S(2)}) collective-permute-start(bf16[384,1024]{1,0:T(8,128)(2,1)S(1)} %pad_maximum_fusion.1.refs_4_), channel_id=1, source_target_pairs={{0,65},{1,64},{2,67},{3,66},{4,69},{5,68},{6,71},{7,70},{8,14},{9,... | collective-permute-start | bytes 2359304 | tf_op jit(solution)/shard_map/ppermute | solution.py:33
  91.3 18.7 %collective-permute-start.12 = (bf16[384,1024]{1,0:T(8,128)(2,1)S(1)}, bf16[384,1024]{1,0:T(8,128)(2,1)S(1)}, u32[]{:S(2)}, u32[]{:S(2)}) collective-permute-start(bf16[384,1024]{1,0:T(8,128)(2,1)S(1)} %pad_maximum_fusion.1.refs_4_), channel_id=1, source_target_pairs={{0,1},{1,0},{2,3},{3,2},{4,5},{5,4},{6,7},{7,6},{8,12},{9,13},{10,... | collective-permute-start | bytes 2359304 | tf_op jit(solution)/shard_map/ppermute | solution.py:33
  102.4 20.4 %collective-permute-start.8 = (bf16[2,4,80,768]{3,2,1,0:T(8,128)(2,1)S(1)}, bf16[2,4,80,768]{3,2,1,0:T(8,128)(2,1)S(1)}, u32[]{:S(2)}, u32[]{:S(2)}) collective-permute-start(bf16[2,4,80,768]{3,2,1,0:T(8,128)(2,1)S(1)} %get-tuple-element.37), channel_id=1, source_target_pairs={{0,16},{1,17},{2,18},{3,19},{4,20},{5,21},{6,22},{7,23},{8,24},{9,... | collective-permute-start | bytes 2949128 | tf_op jit(solution)/shard_map/ppermute | solution.py:33
  103.8 19.0 %collective-permute-start.9 = (bf16[2,4,80,768]{3,2,1,0:T(8,128)(2,1)S(1)}, bf16[2,4,80,768]{3,2,1,0:T(8,128)(2,1)S(1)}, u32[]{:S(2)}, u32[]{:S(2)}) collective-permute-start(bf16[2,4,80,768]{3,2,1,0:T(8,128)(2,1)S(1)} %get-tuple-element.38), channel_id=1, source_target_pairs={{0,48},{1,49},{2,50},{3,51},{4,52},{5,53},{6,54},{7,55},{8,56},{9,... | collective-permute-start | bytes 2949128 | tf_op jit(solution)/shard_map/ppermute | solution.py:33
  123.0 9.5 %collective-permute-start.13 = (bf16[4,80,768]{2,1,0:T(8,128)(2,1)S(1)}, bf16[4,80,768]{2,1,0:T(8,128)(2,1)S(1)}, u32[]{:S(2)}, u32[]{:S(2)}) collective-permute-start(bf16[4,80,768]{2,1,0:T(8,128)(2,1)S(1)} %fusion.1), channel_id=1, source_target_pairs={{0,16},{1,17},{2,18},{3,19},{4,20},{5,21},{6,22},{7,23},{8,24},{9,... | collective-permute-start | bytes 1474568 | tf_op jit(solution)/shard_map/ppermute | solution.py:33
  124.1 8.6 %collective-permute-start.14 = (bf16[4,80,768]{2,1,0:T(8,128)(2,1)S(1)}, bf16[4,80,768]{2,1,0:T(8,128)(2,1)S(1)}, u32[]{:S(2)}, u32[]{:S(2)}) collective-permute-start(bf16[4,80,768]{2,1,0:T(8,128)(2,1)S(1)} %fusion), channel_id=1, source_target_pairs={{0,48},{1,49},{2,50},{3,51},{4,52},{5,53},{6,54},{7,55},{8,56},{9,... | collective-permute-start | bytes 1474568 | tf_op jit(solution)/shard_map/ppermute | solution.py:33
  132.9 12.7 %collective-permute-start.15 = (bf16[160,768]{1,0:T(8,128)(2,1)S(1)}, bf16[160,768]{1,0:T(8,128)(2,1)S(1)}, u32[]{:S(2)}, u32[]{:S(2)}) collective-permute-start(bf16[160,768]{1,0:T(8,128)(2,1)S(1)} %pad_maximum_fusion.6), channel_id=1, source_target_pairs={{0,2},{1,3},{2,4},{3,5},{4,6},{5,7},{6,0},{7,1},{8,72},{9,73},{10,... | collective-permute-start | bytes 737288 | tf_op jit(solution)/shard_map/ppermute | solution.py:33
  134.4 13.3 %collective-permute-start.16 = (bf16[160,768]{1,0:T(8,128)(2,1)S(1)}, bf16[160,768]{1,0:T(8,128)(2,1)S(1)}, u32[]{:S(2)}, u32[]{:S(2)}) collective-permute-start(bf16[160,768]{1,0:T(8,128)(2,1)S(1)} %pad_maximum_fusion.7), channel_id=1, source_target_pairs={{0,6},{1,7},{2,0},{3,1},{4,2},{5,3},{6,4},{7,5},{8,73},{9,72},{10,... | collective-permute-start | bytes 737288 | tf_op jit(solution)/shard_map/ppermute | solution.py:33
  153.8 23.7 %collective-permute-start.19 = (bf16[4,160,1024]{2,1,0:T(8,128)(2,1)}, bf16[4,160,1024]{2,1,0:T(8,128)(2,1)S(1)}, u32[]{:S(2)}, u32[]{:S(2)}) collective-permute-start(bf16[4,160,1024]{2,1,0:T(8,128)(2,1)} %copy-done.6), channel_id=1, source_target_pairs={{0,2},{1,3},{2,4},{3,5},{4,6},{5,7},{6,0},{7,1},{8,72},{9,73},{10,... | collective-permute-start | bytes 3932168 | tf_op jit(solution)/shard_map/ppermute | solution.py:33
  155.0 25.6 %collective-permute-start.20 = (bf16[4,160,1024]{2,1,0:T(8,128)(2,1)}, bf16[4,160,1024]{2,1,0:T(8,128)(2,1)S(1)}, u32[]{:S(2)}, u32[]{:S(2)}) collective-permute-start(bf16[4,160,1024]{2,1,0:T(8,128)(2,1)} %copy-done.5), channel_id=1, source_target_pairs={{0,6},{1,7},{2,0},{3,1},{4,2},{5,3},{6,4},{7,5},{8,73},{9,72},{10,... | collective-permute-start | bytes 3932168 | tf_op jit(solution)/shard_map/ppermute | solution.py:33
  159.0 48.8 %collective-permute-start.21 = (bf16[4,160,1024]{2,1,0:T(8,128)(2,1)S(1)}, bf16[4,160,1024]{2,1,0:T(8,128)(2,1)S(1)}, u32[]{:S(2)}, u32[]{:S(2)}) collective-permute-start(bf16[4,160,1024]{2,1,0:T(8,128)(2,1)S(1)} %copy-done.4), channel_id=1, source_target_pairs={{0,4},{1,5},{2,6},{3,7},{4,0},{5,1},{6,2},{7,3},{8,9},{9,8},{10,11... | collective-permute-start | bytes 3932168 | tf_op jit(solution)/shard_map/ppermute | solution.py:33
  209.6 10.6 %collective-permute-start.23 = (bf16[160,1024]{1,0:T(8,128)(2,1)}, bf16[160,1024]{1,0:T(8,128)(2,1)}, u32[]{:S(2)}, u32[]{:S(2)}) collective-permute-start(bf16[160,1024]{1,0:T(8,128)(2,1)} %get-tuple-element.57), channel_id=1, source_target_pairs={{0,48},{1,49},{2,50},{3,51},{4,52},{5,53},{6,54},{7,55},{8,56},{9,... | collective-permute-start | bytes 983048 | tf_op jit(solution)/shard_map/ppermute | solution.py:33
  212.3 9.4 %collective-permute-start.24 = (bf16[160,1024]{1,0:T(8,128)(2,1)S(1)}, bf16[160,1024]{1,0:T(8,128)(2,1)}, u32[]{:S(2)}, u32[]{:S(2)}) collective-permute-start(bf16[160,1024]{1,0:T(8,128)(2,1)S(1)} %get-tuple-element.56), channel_id=1, source_target_pairs={{0,32},{1,33},{2,34},{3,35},{4,36},{5,37},{6,38},{7,39},{8,40},{9,... | collective-permute-start | bytes 983048 | tf_op jit(solution)/shard_map/ppermute | solution.py:33
  226.7 10.8 %collective-permute-start.27 = (bf16[80,2048]{1,0:T(8,128)(2,1)S(1)}, bf16[80,2048]{1,0:T(8,128)(2,1)S(1)}, u32[]{:S(2)}, u32[]{:S(2)}) collective-permute-start(bf16[80,2048]{1,0:T(8,128)(2,1)S(1)} %get-tuple-element.90.refs_0_), channel_id=1, source_target_pairs={{0,48},{1,49},{2,50},{3,51},{4,52},{5,53},{6,54},{7,55},{8,24},{9,... | collective-permute-start | bytes 983048 | tf_op jit(solution)/shard_map/ppermute | solution.py:33
  227.6 16.2 %collective-permute-start.28 = (bf16[80,2048]{1,0:T(8,128)(2,1)S(1)}, bf16[80,2048]{1,0:T(8,128)(2,1)S(1)}, u32[]{:S(2)}, u32[]{:S(2)}) collective-permute-start(bf16[80,2048]{1,0:T(8,128)(2,1)S(1)} %get-tuple-element.90.refs_0_), channel_id=1, source_target_pairs={{0,32},{1,33},{2,34},{3,35},{4,36},{5,37},{6,38},{7,39},{8,56},{9,... | collective-permute-start | bytes 983048 | tf_op jit(solution)/shard_map/ppermute | solution.py:33
  230.0 18.1 %collective-permute-start.29 = (bf16[80,2048]{1,0:T(8,128)(2,1)S(1)}, bf16[80,2048]{1,0:T(8,128)(2,1)S(1)}, u32[]{:S(2)}, u32[]{:S(2)}) collective-permute-start(bf16[80,2048]{1,0:T(8,128)(2,1)S(1)} %get-tuple-element.90.refs_0_), channel_id=1, source_target_pairs={{0,64},{1,65},{2,66},{3,67},{4,68},{5,69},{6,70},{7,71},{8,40},{9,... | collective-permute-start | bytes 983048 | tf_op jit(solution)/shard_map/ppermute | solution.py:33
  230.1 18.0 %collective-permute-start.33 = (bf16[80,2048]{1,0:T(8,128)(2,1)S(1)}, bf16[80,2048]{1,0:T(8,128)(2,1)S(1)}, u32[]{:S(2)}, u32[]{:S(2)}) collective-permute-start(bf16[80,2048]{1,0:T(8,128)(2,1)S(1)} %get-tuple-element.90.refs_0_), channel_id=1, source_target_pairs={{0,8},{1,9},{2,10},{3,11},{4,12},{5,13},{6,14},{7,15},{8,0},{9,1},... | collective-permute-start | bytes 983048 | tf_op jit(solution)/shard_map/ppermute | solution.py:33
  243.8 11.2 %collective-permute-start.31 = (bf16[80,2048]{1,0:T(8,128)(2,1)S(1)}, bf16[80,2048]{1,0:T(8,128)(2,1)S(1)}, u32[]{:S(2)}, u32[]{:S(2)}) collective-permute-start(bf16[80,2048]{1,0:T(8,128)(2,1)S(1)} %get-tuple-element.89), channel_id=1, source_target_pairs={{0,64},{1,65},{2,66},{3,67},{4,68},{5,69},{6,70},{7,71},{8,56},{9,... | collective-permute-start | bytes 983048 | tf_op jit(solution)/shard_map/ppermute | solution.py:33
  247.4 10.6 %collective-permute-start.30 = (bf16[80,2048]{1,0:T(8,128)(2,1)S(1)}, bf16[80,2048]{1,0:T(8,128)(2,1)S(1)}, u32[]{:S(2)}, u32[]{:S(2)}) collective-permute-start(bf16[80,2048]{1,0:T(8,128)(2,1)S(1)} %collective-permute-done.26.refs_1_), channel_id=1, source_target_pairs={{0,64},{1,65},{2,66},{3,67},{4,68},{5,69},{6,70},{7,71},{8,24},{9,... | collective-permute-start | bytes 983048 | tf_op jit(solution)/shard_map/ppermute | solution.py:33
  248.1 10.7 %collective-permute-start.34 = (bf16[80,2048]{1,0:T(8,128)(2,1)S(1)}, bf16[80,2048]{1,0:T(8,128)(2,1)S(1)}, u32[]{:S(2)}, u32[]{:S(2)}) collective-permute-start(bf16[80,2048]{1,0:T(8,128)(2,1)S(1)} %collective-permute-done.26.refs_1_), channel_id=1, source_target_pairs={{0,8},{1,9},{2,10},{3,11},{4,12},{5,13},{6,14},{7,15},{8,0},{9,1},... | collective-permute-start | bytes 983048 | tf_op jit(solution)/shard_map/ppermute | solution.py:33
  248.2 10.8 %collective-permute-start.35 = (bf16[80,2048]{1,0:T(8,128)(2,1)S(1)}, bf16[80,2048]{1,0:T(8,128)(2,1)S(1)}, u32[]{:S(2)}, u32[]{:S(2)}) collective-permute-start(bf16[80,2048]{1,0:T(8,128)(2,1)S(1)} %collective-permute-done.27.refs_2_), channel_id=1, source_target_pairs={{0,8},{1,9},{2,10},{3,11},{4,12},{5,13},{6,14},{7,15},{8,0},{9,1},... | collective-permute-start | bytes 983048 | tf_op jit(solution)/shard_map/ppermute | solution.py:33
  255.0 7.8 %collective-permute-start.36 = (bf16[80,2048]{1,0:T(8,128)(2,1)S(1)}, bf16[80,2048]{1,0:T(8,128)(2,1)S(1)}, u32[]{:S(2)}, u32[]{:S(2)}) collective-permute-start(bf16[80,2048]{1,0:T(8,128)(2,1)S(1)} %collective-permute-done.28.refs_3_), channel_id=1, source_target_pairs={{0,8},{1,9},{2,10},{3,11},{4,12},{5,13},{6,14},{7,15},{8,0},{9,1},... | collective-permute-start | bytes 983048 | tf_op jit(solution)/shard_map/ppermute | solution.py:33
  255.0 7.7 %collective-permute-start.37 = (bf16[80,2048]{1,0:T(8,128)(2,1)S(1)}, bf16[80,2048]{1,0:T(8,128)(2,1)S(1)}, u32[]{:S(2)}, u32[]{:S(2)}) collective-permute-start(bf16[80,2048]{1,0:T(8,128)(2,1)S(1)} %collective-permute-done.29.refs_4_), channel_id=1, source_target_pairs={{0,8},{1,9},{2,10},{3,11},{4,12},{5,13},{6,14},{7,15},{8,0},{9,1},... | collective-permute-start | bytes 983048 | tf_op jit(solution)/shard_map/ppermute | solution.py:33
  (50 other events, 404.5 us)
Sparse Core Ops, SparseCore 0:
  153.9 43.2 all-gather.1

commit v4 on v3

--- a/solution.py
+++ b/solution.py
@@ -183,8 +183,8 @@
     return value.astype(jnp.bfloat16)
 
 
-def after(value, *others):
-    return lax.optimization_barrier((value, others))[0]
+def tie(*values):
+    return lax.optimization_barrier(values)
 
 
 def ring_send(plus, minus, along):
@@ -245,37 +245,27 @@
     first, second, half = first // 2, second // 2, columns // 2
 
     def kernel(places_ref, gathered_ref, *refs):
-        part_refs, out_ref, semaphores = refs[:-2], refs[-2], refs[-1]
-        copies = []
+        out_ref = refs[-1]
         for side in range(2):
-            copies.append((gathered_ref.at[:, pl.ds(side * first, first)], out_ref.at[:, pl.ds(side * half, first)]))
-            for place, ref in enumerate(part_refs):
-                start = pl.multiple_of(places_ref[place] * unit, unit)
-                copies.append(
-                    (
-                        ref.at[:, pl.ds(side * second, second)],
-                        out_ref.at[pl.ds(start, unit), pl.ds(side * half + first, second)],
-                    )
-                )
-        copies = [
-            pltpu.make_async_copy(source, target, semaphores.at[place]) for place, (source, target) in enumerate(copies)
-        ]
-        for copy in copies:
-            copy.start()
-        for copy in copies:
-            copy.wait()
-
-    anywhere = pl.BlockSpec(memory_space=pl.ANY)
+            out_ref[:, pl.ds(side * half, first)] = gathered_ref[:, pl.ds(side * first, first)]
+        for place, ref in enumerate(refs[:-1]):
+
+            @pl.when(pl.program_id(0) == place)
+            def _(ref=ref):
+                for side in range(2):
+                    out_ref[:, pl.ds(side * half + first, second)] = ref[:, pl.ds(side * second, second)]
+
     return pl.pallas_call(
         kernel,
         grid_spec=pltpu.PrefetchScalarGridSpec(
             num_scalar_prefetch=1,
-            grid=(1,),
-            in_specs=[anywhere] * (1 + len(parts)),
-            out_specs=anywhere,
-            scratch_shapes=[pltpu.SemaphoreType.DMA((2 * (1 + len(parts)),))],
+            grid=(len(parts),),
+            in_specs=[pl.BlockSpec((unit, 2 * first), lambda k, p: (p[k], 0))]
+            + [pl.BlockSpec((unit, 2 * second), lambda k, p: (0, 0))] * len(parts),
+            out_specs=pl.BlockSpec((unit, columns), lambda k, p: (p[k], 0)),
         ),
         out_shape=jax.ShapeDtypeStruct((rows, columns), jnp.bfloat16),
+        compiler_params=pltpu.CompilerParams(vmem_limit_bytes=32 * 1024 * 1024),
         name="assemble_copy",
     )(places, gathered, *parts)
 
@@ -303,7 +293,8 @@
     kept = jnp.where(c == 0, low, high)
     given = jnp.where(c == 0, high, low)
     chip_input = jnp.concatenate([kept, send(given, sibling)], axis=0)
-    other = send(after(up_cotangent, given), sibling)
+    chip_input, swapped = tie(chip_input, up_cotangent)
+    other = send(swapped, sibling)
 
     def spread(value):
         return [send(value, along_rows(step)) for step in (1, 3, 2)]
@@ -311,11 +302,15 @@
     starts = [sum(WIDTHS[:place]) for place in range(len(WIDTHS))]
     inputs = [chip_input[:, start : start + width] for start, width in zip(starts, WIDTHS)]
     inputs_0 = [inputs[0], *spread(inputs[0])]
+    (last,) = pack(where, up_cotangent, other, (2,))
+    last, where = tie(last, where)
+    last = send(last, along_rows(2))
     near, far = pack(where, up_cotangent, other, (1, 3))
-    near, far = after((near, far), inputs_0)
-    own, last = pack(after(where, near), up_cotangent, other, (0, 2))
-    blocks = [own, send(near, along_rows(1)), send(far, along_rows(3)), send(last, along_rows(2))]
-    inputs_1 = [inputs[1], *spread(after(inputs[1], blocks))]
+    near, far, inputs_0, where = tie(near, far, inputs_0, where)
+    (own,) = pack(where, up_cotangent, other, (0,))
+    blocks = [own, send(near, along_rows(1)), send(far, along_rows(3)), last]
+    blocks, waiting = tie(blocks, inputs[1])
+    inputs_1 = [inputs[1], *spread(waiting)]
 
     plus, minus, first, third, keep = partial_sums(where, blocks, inputs_0, True)
     sent_0 = ring_send(plus, minus, along_y)
@@ -323,6 +318,7 @@
     sent_0, pieces_1 = lax.optimization_barrier((sent_0, pieces_1))
     sent_1 = direct(pieces_1, along_sums)
     turned_0 = ring_turn(first, third, *sent_0, along_y)
+    turned_0, sent_1 = tie(turned_0, sent_1)
     again_0 = direct([ring_end(keep, *sent_0, *turned_0, place) for place in range(4)], along_sums)
     again_1 = direct([summed(sent_1, place) for place in range(4)], along_y)
 

time: 551 us -> 268 us (0.49)
  Pallas kernels: 311 us -> 44.7 us
  waiting for transfers between devices: 149 us -> 112 us
  starting transfers between devices: 52.5 us -> 64.8 us
  local copies, waits for them, and re-layouts: 11.5 us -> 19.4 us
    pallas_call x1, Pallas kernels: 280 us -> 8.12 us  [assemble(): pl.pallas_call(kernel, grid_spec=pltpu.PrefetchScalarGridSpec(num_scalar_...]
    ppermute x41, waiting for transfers between devices: 149 us -> 112 us  [send(): return lax.ppermute(value, AXES, permutation(move))]
    ppermute x41, starting transfers between devices: 52.5 us -> 64.7 us  [send(): return lax.ppermute(value, AXES, permutation(move))]
    unnamed x80 -> x58, local copies, waits for them, and re-layouts: 7.64 us -> 14.6 us
    pallas_call x2 -> x3, Pallas kernels: 11.5 us -> 15.5 us  [pack(): pl.pallas_call(kernel, grid_spec=pltpu.PrefetchScalarGridSpec(num_scalar_...]
  transfers between devices with their start and end apart: 42 -> 42, of which waited for: 23 -> 25; matrix products, arithmetic and copies ran while one was open for 2% -> 5% of each run, Pallas kernels for 6% -> 14%
where the time goes in v4:
time: 268 us; the launch traced here: 267 us
  waiting for transfers between devices  112 us (42%)
  starting transfers between devices  64.8 us (24%)
  Pallas kernels  44.7 us (17%)
  local copies, waits for them, and re-layouts  19.4 us (7%)
  between operations  14.4 us (5%)
  other arithmetic  11.8 us (4%)
    ppermute x41, waiting for transfers between devices, send(): return lax.ppermute(value, AXES, permutation(move))  112 us
    ppermute x41, starting transfers between devices, send(): return lax.ppermute(value, AXES, permutation(move))  64.7 us
    pallas_call x2, Pallas kernels, partial_sums(): pl.pallas_call(kernel, grid_spec=pltpu.PrefetchScalarGridSpec(num_scalar_...  21.1 us
    pallas_call x3, Pallas kernels, pack(): pl.pallas_call(kernel, grid_spec=pltpu.PrefetchScalarGridSpec(num_scalar_...  15.5 us
    unnamed x58, local copies, waits for them, and re-layouts  14.6 us
    pallas_call x1, Pallas kernels, assemble(): pl.pallas_call(kernel, grid_spec=pltpu.PrefetchScalarGridSpec(num_scalar_...  8.12 us
  transfers between devices with their start and end apart: 42, of which 25 were waited for; matrix products, arithmetic and copies ran while one was open for 5% of the time, Pallas kernels for 14%

profile of v4, /device:TPU:1, one launch (start us, length us, event | category | flops | bytes accessed | tf_op | source)
XLA Modules:
  0.0 266.7 jit_solution(12219827829477661158)
XLA Ops:
  19.2 4.9 %pack_cotangent.3 = bf16[2560,384]{1,0:T(8,128)(2,1)} custom-call(s32[4]{0:T(128)} %pad_add_fusion.where_ref, bf16[192,10240]{1,0:T(8,128)(2,1)} %refs_0_.5, bf16[192,10240]{1,0:T(8,128)(2,1)} %collective-permute-done.1.refs_1_.refs_2_.refs_3_), custom_call_target="tpu_custom_call" | custom-call | bytes 3932160 | tf_op jit(solution)/shard_map/pack_cotangent/pallas_call | solution.py:79
  24.1 5.8 %pack_cotangent.4 = (bf16[2560,384]{1,0:T(8,128)(2,1)}, bf16[2560,384]{1,0:T(8,128)(2,1)}) custom-call(s32[4]{0:T(128)} %pad_add_fusion.where_ref, bf16[192,10240]{1,0:T(8,128)(2,1)} %refs_0_.5, bf16[192,10240]{1,0:T(8,128)(2,1)} %refs_0_.5, bf16[192,10240]{1,0:T(8,128)(2,1)} %collective-permute-done.1.refs_1_.refs_2_.refs_3_, ...), custom_call_target="tpu_custom_call" | custom-call | bytes 7864320 | tf_op jit(solution)/shard_map/pack_cotangent/pallas_call | solution.py:79
  35.4 4.9 %pack_cotangent.5.refs_0_ = bf16[2560,384]{1,0:T(8,128)(2,1)} custom-call(s32[4]{0:T(128)} %pad_add_fusion.where_ref, bf16[192,10240]{1,0:T(8,128)(2,1)} %refs_0_.5, bf16[192,10240]{1,0:T(8,128)(2,1)} %collective-permute-done.1.refs_1_.refs_2_.refs_3_), custom_call_target="tpu_custom_call" | custom-call | bytes 3932160 | tf_op jit(solution)/shard_map/pack_cotangent/pallas_call | solution.py:79
  40.3 15.2 %collective-permute-done.5.refs_1_ = bf16[2560,384]{1,0:T(8,128)(2,1)} collective-permute-done((bf16[2560,384]{1,0:T(8,128)(2,1)}, bf16[2560,384]{1,0:T(8,128)(2,1)}, u32[]{:S(2)}, u32[]{:S(2)}) %collective-permute-start.5) | collective-permute-done | bytes 1966112 | tf_op jit(solution)/shard_map/ppermute | solution.py:33
  55.5 20.4 %collective-permute-done.6.refs_2_ = bf16[2560,384]{1,0:T(8,128)(2,1)} collective-permute-done((bf16[2560,384]{1,0:T(8,128)(2,1)}, bf16[2560,384]{1,0:T(8,128)(2,1)}, u32[]{:S(2)}, u32[]{:S(2)}) %collective-permute-start.6) | collective-permute-done | bytes 1966112 | tf_op jit(solution)/shard_map/ppermute | solution.py:33
  82.0 9.7 %partial_sums.2 = (bf16[2,4,80,768]{3,2,1,0:T(8,128)(2,1)S(1)}, bf16[2,4,80,768]{3,2,1,0:T(8,128)(2,1)S(1)}, bf16[4,80,768]{2,1,0:T(8,128)(2,1)S(1)}, bf16[4,80,...) custom-call(s32[4]{0:T(128)S(1)} %copy-done.14, bf16[2560,384]{1,0:T(8,128)(2,1)S(1)} %copy-done.1, ...), custom_call_target="tpu_custom_call" | custom-call | flops 6039797760 | bytes 14155776 | tf_op jit(solution)/shard_map/partial_sums/pallas_call | solution.py:154
  94.6 2.8 %collective-permute-done.11.refs_6_ = bf16[384,1024]{1,0:T(8,128)(2,1)S(1)} collective-permute-done((bf16[384,1024]{1,0:T(8,128)(2,1)S(1)}, bf16[384,1024]{1,0:T(8,128)(2,1)S(1)}, u32[]{:S(2)}, u32[]{:S(2)}) %collective-permute-start.11) | collective-permute-done | bytes 786464 | tf_op jit(solution)/shard_map/ppermute | solution.py:33
  98.5 11.4 %partial_sums.3 = (bf16[4,160,1024]{2,1,0:T(8,128)(2,1)S(1)}, bf16[4,160,1024]{2,1,0:T(8,128)(2,1)S(1)}, bf16[4,160,1024]{2,1,0:T(8,128)(2,1)S(1)}, bf16[4,160,1024]{2,1,0:T(8,128)(2,1)S(1)}) custom-call(s32[4]{0:T(128)S(1)} %copy-done.14, bf16[2560,384]{1,0:T(8,128)(2,1)S(1)} %copy-done.1, bf16[2560,384]{1,0:T(8,128)(2,1)} %collective-permute-done.5.refs_1_, ...), custom_call_target="tpu_custom_call" | custom-call | flops 8053063680 | bytes 16252928 | tf_op jit(solution)/shard_map/partial_sums/pallas_call | solution.py:154
  109.9 2.5 collective-permute-done.8
  113.9 3.8 %collective-permute-start.16 = (bf16[4,160,1024]{2,1,0:T(8,128)(2,1)S(1)}, bf16[4,160,1024]{2,1,0:T(8,128)(2,1)S(1)}, u32[]{:S(2)}, u32[]{:S(2)}) collective-permute-start(bf16[4,160,1024]{2,1,0:T(8,128)(2,1)S(1)} %get-tuple-element.74), channel_id=1, source_target_pairs={{0,6},{1,7},{2,0},{3,1},{4,2},{5,3},{6,4},{7,5},{8,73},{9,72},{10,... | collective-permute-start | bytes 3932168 | tf_op jit(solution)/shard_map/ppermute | solution.py:33
  119.0 2.6 collective-permute-start.14
  121.8 6.9 %collective-permute-done.14 = bf16[4,80,768]{2,1,0:T(8,128)(2,1)S(1)} collective-permute-done((bf16[4,80,768]{2,1,0:T(8,128)(2,1)S(1)}, bf16[4,80,768]{2,1,0:T(8,128)(2,1)S(1)}, u32[]{:S(2)}, u32[]{:S(2)}) %collective-permute-start.14) | collective-permute-done | bytes 491552 | tf_op jit(solution)/shard_map/ppermute | solution.py:33
  128.7 3.3 %collective-permute-done.13 = bf16[4,80,768]{2,1,0:T(8,128)(2,1)S(1)} collective-permute-done((bf16[4,80,768]{2,1,0:T(8,128)(2,1)S(1)}, bf16[4,80,768]{2,1,0:T(8,128)(2,1)S(1)}, u32[]{:S(2)}, u32[]{:S(2)}) %collective-permute-start.13) | collective-permute-done | bytes 491552 | tf_op jit(solution)/shard_map/ppermute | solution.py:33
  133.0 13.3 %collective-permute-done.16 = bf16[4,160,1024]{2,1,0:T(8,128)(2,1)S(1)} collective-permute-done((bf16[4,160,1024]{2,1,0:T(8,128)(2,1)S(1)}, bf16[4,160,1024]{2,1,0:T(8,128)(2,1)S(1)}, u32[]{:S(2)}, u32[]{:S(2)}) %collective-permute-start.16) | collective-permute-done | bytes 1310752 | tf_op jit(solution)/shard_map/ppermute | solution.py:33
  146.3 1.9 collective-permute-done.17
  150.4 1.9 collective-permute-start.19
  155.8 2.3 collective-permute-done.19
  159.1 4.5 %collective-permute-start.21 = (bf16[80,768]{1,0:T(8,128)(2,1)S(1)}, bf16[80,768]{1,0:T(8,128)(2,1)S(1)}, u32[]{:S(2)}, u32[]{:S(2)}) collective-permute-start(bf16[80,768]{1,0:T(8,128)(2,1)S(1)} %broadcast_select_fusion.10), channel_id=1, source_target_pairs={{0,8},{1,9},{2,10},{3,11},{4,12},{5,13},{6,14},{7,15},{8,0},{9,1},... | collective-permute-start | bytes 368648 | tf_op jit(solution)/shard_map/ppermute | solution.py:33
  166.1 2.6 fusion.28
  174.1 5.2 %collective-permute-done.22 = bf16[160,1024]{1,0:T(8,128)(2,1)} collective-permute-done((bf16[160,1024]{1,0:T(8,128)(2,1)S(1)}, bf16[160,1024]{1,0:T(8,128)(2,1)}, u32[]{:S(2)}, u32[]{:S(2)}) %collective-permute-start.22) | collective-permute-done | bytes 327712 | tf_op jit(solution)/shard_map/ppermute | solution.py:33
  179.6 15.5 %collective-permute-done.24 = bf16[160,1024]{1,0:T(8,128)(2,1)} collective-permute-done((bf16[160,1024]{1,0:T(8,128)(2,1)S(1)}, bf16[160,1024]{1,0:T(8,128)(2,1)}, u32[]{:S(2)}, u32[]{:S(2)}) %collective-permute-start.24) | collective-permute-done | bytes 327712 | tf_op jit(solution)/shard_map/ppermute | solution.py:33
  195.1 1.9 fusion.14
  197.0 2.4 collective-permute-start.25
  207.5 4.0 %collective-permute-done.26.refs_1_ = bf16[80,2048]{1,0:T(8,128)(2,1)S(1)} collective-permute-done((bf16[80,2048]{1,0:T(8,128)(2,1)S(1)}, bf16[80,2048]{1,0:T(8,128)(2,1)S(1)}, u32[]{:S(2)}, u32[]{:S(2)}) %collective-permute-start.26) | collective-permute-done | bytes 327712 | tf_op jit(solution)/shard_map/ppermute | solution.py:33
  217.6 4.1 %collective-permute-done.29.refs_4_ = bf16[80,2048]{1,0:T(8,128)(2,1)S(1)} collective-permute-done((bf16[80,2048]{1,0:T(8,128)(2,1)S(1)}, bf16[80,2048]{1,0:T(8,128)(2,1)S(1)}, u32[]{:S(2)}, u32[]{:S(2)}) %collective-permute-start.29) | collective-permute-done | bytes 327712 | tf_op jit(solution)/shard_map/ppermute | solution.py:33
  221.7 4.8 %collective-permute-start.34 = (bf16[80,2048]{1,0:T(8,128)(2,1)S(1)}, bf16[80,2048]{1,0:T(8,128)(2,1)S(1)}, u32[]{:S(2)}, u32[]{:S(2)}) collective-permute-start(bf16[80,2048]{1,0:T(8,128)(2,1)S(1)} %collective-permute-done.26.refs_1_), channel_id=1, source_target_pairs={{0,8},{1,9},{2,10},{3,11},{4,12},{5,13},{6,14},{7,15},{8,0},{9,1},... | collective-permute-start | bytes 983048 | tf_op jit(solution)/shard_map/ppermute | solution.py:33
  226.7 2.8 %collective-permute-start.36 = (bf16[80,2048]{1,0:T(8,128)(2,1)S(1)}, bf16[80,2048]{1,0:T(8,128)(2,1)S(1)}, u32[]{:S(2)}, u32[]{:S(2)}) collective-permute-start(bf16[80,2048]{1,0:T(8,128)(2,1)S(1)} %collective-permute-done.28.refs_3_), channel_id=1, source_target_pairs={{0,8},{1,9},{2,10},{3,11},{4,12},{5,13},{6,14},{7,15},{8,0},{9,1},... | collective-permute-start | bytes 983048 | tf_op jit(solution)/shard_map/ppermute | solution.py:33
  229.5 3.5 %collective-permute-start.37 = (bf16[80,2048]{1,0:T(8,128)(2,1)S(1)}, bf16[80,2048]{1,0:T(8,128)(2,1)S(1)}, u32[]{:S(2)}, u32[]{:S(2)}) collective-permute-start(bf16[80,2048]{1,0:T(8,128)(2,1)S(1)} %collective-permute-done.29.refs_4_), channel_id=1, source_target_pairs={{0,8},{1,9},{2,10},{3,11},{4,12},{5,13},{6,14},{7,15},{8,0},{9,1},... | collective-permute-start | bytes 983048 | tf_op jit(solution)/shard_map/ppermute | solution.py:33
  233.0 3.5 %collective-permute-start.39 = (bf16[80,2048]{1,0:T(8,128)(2,1)S(1)}, bf16[80,2048]{1,0:T(8,128)(2,1)S(1)}, u32[]{:S(2)}, u32[]{:S(2)}) collective-permute-start(bf16[80,2048]{1,0:T(8,128)(2,1)S(1)} %collective-permute-done.31.refs_6_), channel_id=1, source_target_pairs={{0,8},{1,9},{2,10},{3,11},{4,12},{5,13},{6,14},{7,15},{8,0},{9,1},... | collective-permute-start | bytes 983048 | tf_op jit(solution)/shard_map/ppermute | solution.py:33
  237.8 2.3 multiply_subtract_fusion
  243.8 2.1 copy-done
  251.7 8.1 %assemble_copy.1 = bf16[1280,3584]{1,0:T(8,128)(2,1)} custom-call(s32[16]{0:T(128)S(1)} %fusion.39.places_ref, bf16[1280,1536]{1,0:T(8,128)(2,1)S(1)} %copy-done, bf16[80,2048]{1,0:T(8,128)(2,1)S(1)} %get-tuple-element.120.refs_0_, bf16[80,2048]{1,0:T(8,128)(2,1)S(1)} %collective-permute-done.26.refs_1_, ...), custom_call_target="tpu_custom_call" | custom-call | tf_op jit(solution)/shard_map/assemble_copy/pallas_call | solution.py:258
  (148 shorter events, 71.5 us)
Async XLA Ops:
  7.2 236.6 %all-gather.2.cloned.1.call-start = ((), (), s32[]{:S(2)}) async-start(), calls=%async_computation | async-start | bytes 4177920 | tf_op jit(solution)/shard_map/all_gather | solution.py:348
  12.5 17.3 %collective-permute-start.2 = (bf16[384,768]{1,0:T(8,128)(2,1)S(1)}, bf16[384,768]{1,0:T(8,128)(2,1)S(1)}, u32[]{:S(2)}, u32[]{:S(2)}) collective-permute-start(bf16[384,768]{1,0:T(8,128)(2,1)S(1)} %slice.200.refs_4_), channel_id=1, source_target_pairs={{0,64},{1,65},{2,66},{3,67},{4,68},{5,69},{6,70},{7,71},{8,10},{9,... | collective-permute-start | bytes 1769480 | tf_op jit(solution)/shard_map/ppermute | solution.py:33
  13.9 16.0 %collective-permute-start.3 = (bf16[384,768]{1,0:T(8,128)(2,1)S(1)}, bf16[384,768]{1,0:T(8,128)(2,1)S(1)}, u32[]{:S(2)}, u32[]{:S(2)}) collective-permute-start(bf16[384,768]{1,0:T(8,128)(2,1)S(1)} %slice.200.refs_4_), channel_id=1, source_target_pairs={{0,65},{1,64},{2,67},{3,66},{4,69},{5,68},{6,71},{7,70},{8,14},{9,... | collective-permute-start | bytes 1769480 | tf_op jit(solution)/shard_map/ppermute | solution.py:33
  15.6 14.6 %collective-permute-start.4 = (bf16[384,768]{1,0:T(8,128)(2,1)S(1)}, bf16[384,768]{1,0:T(8,128)(2,1)S(1)}, u32[]{:S(2)}, u32[]{:S(2)}) collective-permute-start(bf16[384,768]{1,0:T(8,128)(2,1)S(1)} %slice.200.refs_4_), channel_id=1, source_target_pairs={{0,1},{1,0},{2,3},{3,2},{4,5},{5,4},{6,7},{7,6},{8,12},{9,13},{10,... | collective-permute-start | bytes 1769480 | tf_op jit(solution)/shard_map/ppermute | solution.py:33
  30.2 25.3 %collective-permute-start.5 = (bf16[2560,384]{1,0:T(8,128)(2,1)}, bf16[2560,384]{1,0:T(8,128)(2,1)}, u32[]{:S(2)}, u32[]{:S(2)}) collective-permute-start(bf16[2560,384]{1,0:T(8,128)(2,1)} %get-tuple-element.49), channel_id=1, source_target_pairs={{0,64},{1,65},{2,66},{3,67},{4,68},{5,69},{6,70},{7,71},{8,10},{9,... | collective-permute-start | bytes 5898248 | tf_op jit(solution)/shard_map/ppermute | solution.py:33
  31.2 44.6 %collective-permute-start.6 = (bf16[2560,384]{1,0:T(8,128)(2,1)}, bf16[2560,384]{1,0:T(8,128)(2,1)}, u32[]{:S(2)}, u32[]{:S(2)}) collective-permute-start(bf16[2560,384]{1,0:T(8,128)(2,1)} %get-tuple-element.50), channel_id=1, source_target_pairs={{0,65},{1,64},{2,67},{3,66},{4,69},{5,68},{6,71},{7,70},{8,14},{9,... | collective-permute-start | bytes 5898248 | tf_op jit(solution)/shard_map/ppermute | solution.py:33
  32.9 44.5 %collective-permute-start.7 = (bf16[2560,384]{1,0:T(8,128)(2,1)}, bf16[2560,384]{1,0:T(8,128)(2,1)}, u32[]{:S(2)}, u32[]{:S(2)}) collective-permute-start(bf16[2560,384]{1,0:T(8,128)(2,1)} %pack_cotangent.3), channel_id=1, source_target_pairs={{0,1},{1,0},{2,3},{3,2},{4,5},{5,4},{6,7},{7,6},{8,12},{9,13},{10,... | collective-permute-start | bytes 5898248 | tf_op jit(solution)/shard_map/ppermute | solution.py:33
  77.4 17.2 %collective-permute-start.10 = (bf16[384,1024]{1,0:T(8,128)(2,1)S(1)}, bf16[384,1024]{1,0:T(8,128)(2,1)S(1)}, u32[]{:S(2)}, u32[]{:S(2)}) collective-permute-start(bf16[384,1024]{1,0:T(8,128)(2,1)S(1)} %slice.201.refs_4_), channel_id=1, source_target_pairs={{0,64},{1,65},{2,66},{3,67},{4,68},{5,69},{6,70},{7,71},{8,10},{9,... | collective-permute-start | bytes 2359304 | tf_op jit(solution)/shard_map/ppermute | solution.py:33
  78.2 19.2 %collective-permute-start.11 = (bf16[384,1024]{1,0:T(8,128)(2,1)S(1)}, bf16[384,1024]{1,0:T(8,128)(2,1)S(1)}, u32[]{:S(2)}, u32[]{:S(2)}) collective-permute-start(bf16[384,1024]{1,0:T(8,128)(2,1)S(1)} %slice.201.refs_4_), channel_id=1, source_target_pairs={{0,65},{1,64},{2,67},{3,66},{4,69},{5,68},{6,71},{7,70},{8,14},{9,... | collective-permute-start | bytes 2359304 | tf_op jit(solution)/shard_map/ppermute | solution.py:33
  80.1 18.5 %collective-permute-start.12 = (bf16[384,1024]{1,0:T(8,128)(2,1)S(1)}, bf16[384,1024]{1,0:T(8,128)(2,1)S(1)}, u32[]{:S(2)}, u32[]{:S(2)}) collective-permute-start(bf16[384,1024]{1,0:T(8,128)(2,1)S(1)} %slice.201.refs_4_), channel_id=1, source_target_pairs={{0,1},{1,0},{2,3},{3,2},{4,5},{5,4},{6,7},{7,6},{8,12},{9,13},{10,... | collective-permute-start | bytes 2359304 | tf_op jit(solution)/shard_map/ppermute | solution.py:33
  91.7 20.7 %collective-permute-start.8 = (bf16[2,4,80,768]{3,2,1,0:T(8,128)(2,1)S(1)}, bf16[2,4,80,768]{3,2,1,0:T(8,128)(2,1)S(1)}, u32[]{:S(2)}, u32[]{:S(2)}) collective-permute-start(bf16[2,4,80,768]{3,2,1,0:T(8,128)(2,1)S(1)} %get-tuple-element.61), channel_id=1, source_target_pairs={{0,16},{1,17},{2,18},{3,19},{4,20},{5,21},{6,22},{7,23},{8,24},{9,... | collective-permute-start | bytes 2949128 | tf_op jit(solution)/shard_map/ppermute | solution.py:33
  93.1 19.4 %collective-permute-start.9 = (bf16[2,4,80,768]{3,2,1,0:T(8,128)(2,1)S(1)}, bf16[2,4,80,768]{3,2,1,0:T(8,128)(2,1)S(1)}, u32[]{:S(2)}, u32[]{:S(2)}) collective-permute-start(bf16[2,4,80,768]{3,2,1,0:T(8,128)(2,1)S(1)} %get-tuple-element.62), channel_id=1, source_target_pairs={{0,48},{1,49},{2,50},{3,51},{4,52},{5,53},{6,54},{7,55},{8,56},{9,... | collective-permute-start | bytes 2949128 | tf_op jit(solution)/shard_map/ppermute | solution.py:33
  112.5 20.6 %collective-permute-start.15 = (bf16[4,160,1024]{2,1,0:T(8,128)(2,1)S(1)}, bf16[4,160,1024]{2,1,0:T(8,128)(2,1)S(1)}, u32[]{:S(2)}, u32[]{:S(2)}) collective-permute-start(bf16[4,160,1024]{2,1,0:T(8,128)(2,1)S(1)} %get-tuple-element.73), channel_id=1, source_target_pairs={{0,2},{1,3},{2,4},{3,5},{4,6},{5,7},{6,0},{7,1},{8,72},{9,73},{10,... | collective-permute-start | bytes 3932168 | tf_op jit(solution)/shard_map/ppermute | solution.py:33
  113.9 32.4 %collective-permute-start.16 = (bf16[4,160,1024]{2,1,0:T(8,128)(2,1)S(1)}, bf16[4,160,1024]{2,1,0:T(8,128)(2,1)S(1)}, u32[]{:S(2)}, u32[]{:S(2)}) collective-permute-start(bf16[4,160,1024]{2,1,0:T(8,128)(2,1)S(1)} %get-tuple-element.74), channel_id=1, source_target_pairs={{0,6},{1,7},{2,0},{3,1},{4,2},{5,3},{6,4},{7,5},{8,73},{9,72},{10,... | collective-permute-start | bytes 3932168 | tf_op jit(solution)/shard_map/ppermute | solution.py:33
  117.7 30.5 %collective-permute-start.17 = (bf16[4,160,1024]{2,1,0:T(8,128)(2,1)S(1)}, bf16[4,160,1024]{2,1,0:T(8,128)(2,1)S(1)}, u32[]{:S(2)}, u32[]{:S(2)}) collective-permute-start(bf16[4,160,1024]{2,1,0:T(8,128)(2,1)S(1)} %get-tuple-element.75), channel_id=1, source_target_pairs={{0,4},{1,5},{2,6},{3,7},{4,0},{5,1},{6,2},{7,3},{8,9},{9,8},{10,11... | collective-permute-start | bytes 3932168 | tf_op jit(solution)/shard_map/ppermute | solution.py:33
  119.0 9.7 %collective-permute-start.14 = (bf16[4,80,768]{2,1,0:T(8,128)(2,1)S(1)}, bf16[4,80,768]{2,1,0:T(8,128)(2,1)S(1)}, u32[]{:S(2)}, u32[]{:S(2)}) collective-permute-start(bf16[4,80,768]{2,1,0:T(8,128)(2,1)S(1)} %fusion), channel_id=1, source_target_pairs={{0,48},{1,49},{2,50},{3,51},{4,52},{5,53},{6,54},{7,55},{8,56},{9,... | collective-permute-start | bytes 1474568 | tf_op jit(solution)/shard_map/ppermute | solution.py:33
  121.8 10.3 %collective-permute-start.13 = (bf16[4,80,768]{2,1,0:T(8,128)(2,1)S(1)}, bf16[4,80,768]{2,1,0:T(8,128)(2,1)S(1)}, u32[]{:S(2)}, u32[]{:S(2)}) collective-permute-start(bf16[4,80,768]{2,1,0:T(8,128)(2,1)S(1)} %fusion.1), channel_id=1, source_target_pairs={{0,16},{1,17},{2,18},{3,19},{4,20},{5,21},{6,22},{7,23},{8,24},{9,... | collective-permute-start | bytes 1474568 | tf_op jit(solution)/shard_map/ppermute | solution.py:33
  168.7 10.6 %collective-permute-start.22 = (bf16[160,1024]{1,0:T(8,128)(2,1)S(1)}, bf16[160,1024]{1,0:T(8,128)(2,1)}, u32[]{:S(2)}, u32[]{:S(2)}) collective-permute-start(bf16[160,1024]{1,0:T(8,128)(2,1)S(1)} %get-tuple-element.85), channel_id=1, source_target_pairs={{0,16},{1,17},{2,18},{3,19},{4,20},{5,21},{6,22},{7,23},{8,24},{9,... | collective-permute-start | bytes 983048 | tf_op jit(solution)/shard_map/ppermute | solution.py:33
  170.0 9.6 %collective-permute-start.23 = (bf16[160,1024]{1,0:T(8,128)(2,1)S(1)}, bf16[160,1024]{1,0:T(8,128)(2,1)}, u32[]{:S(2)}, u32[]{:S(2)}) collective-permute-start(bf16[160,1024]{1,0:T(8,128)(2,1)S(1)} %get-tuple-element.87), channel_id=1, source_target_pairs={{0,48},{1,49},{2,50},{3,51},{4,52},{5,53},{6,54},{7,55},{8,56},{9,... | collective-permute-start | bytes 983048 | tf_op jit(solution)/shard_map/ppermute | solution.py:33
  171.6 23.5 %collective-permute-start.24 = (bf16[160,1024]{1,0:T(8,128)(2,1)S(1)}, bf16[160,1024]{1,0:T(8,128)(2,1)}, u32[]{:S(2)}, u32[]{:S(2)}) collective-permute-start(bf16[160,1024]{1,0:T(8,128)(2,1)S(1)} %get-tuple-element.86), channel_id=1, source_target_pairs={{0,32},{1,33},{2,34},{3,35},{4,36},{5,37},{6,38},{7,39},{8,40},{9,... | collective-permute-start | bytes 983048 | tf_op jit(solution)/shard_map/ppermute | solution.py:33
  201.1 10.4 %collective-permute-start.26 = (bf16[80,2048]{1,0:T(8,128)(2,1)S(1)}, bf16[80,2048]{1,0:T(8,128)(2,1)S(1)}, u32[]{:S(2)}, u32[]{:S(2)}) collective-permute-start(bf16[80,2048]{1,0:T(8,128)(2,1)S(1)} %get-tuple-element.120.refs_0_), channel_id=1, source_target_pairs={{0,16},{1,17},{2,18},{3,19},{4,20},{5,21},{6,22},{7,23},{8,72},{9,... | collective-permute-start | bytes 983048 | tf_op jit(solution)/shard_map/ppermute | solution.py:33
  202.6 10.1 %collective-permute-start.27 = (bf16[80,2048]{1,0:T(8,128)(2,1)S(1)}, bf16[80,2048]{1,0:T(8,128)(2,1)S(1)}, u32[]{:S(2)}, u32[]{:S(2)}) collective-permute-start(bf16[80,2048]{1,0:T(8,128)(2,1)S(1)} %get-tuple-element.120.refs_0_), channel_id=1, source_target_pairs={{0,48},{1,49},{2,50},{3,51},{4,52},{5,53},{6,54},{7,55},{8,24},{9,... | collective-permute-start | bytes 983048 | tf_op jit(solution)/shard_map/ppermute | solution.py:33
  204.2 10.1 %collective-permute-start.28 = (bf16[80,2048]{1,0:T(8,128)(2,1)S(1)}, bf16[80,2048]{1,0:T(8,128)(2,1)S(1)}, u32[]{:S(2)}, u32[]{:S(2)}) collective-permute-start(bf16[80,2048]{1,0:T(8,128)(2,1)S(1)} %get-tuple-element.120.refs_0_), channel_id=1, source_target_pairs={{0,32},{1,33},{2,34},{3,35},{4,36},{5,37},{6,38},{7,39},{8,56},{9,... | collective-permute-start | bytes 983048 | tf_op jit(solution)/shard_map/ppermute | solution.py:33
  205.4 16.3 %collective-permute-start.29 = (bf16[80,2048]{1,0:T(8,128)(2,1)S(1)}, bf16[80,2048]{1,0:T(8,128)(2,1)S(1)}, u32[]{:S(2)}, u32[]{:S(2)}) collective-permute-start(bf16[80,2048]{1,0:T(8,128)(2,1)S(1)} %get-tuple-element.120.refs_0_), channel_id=1, source_target_pairs={{0,64},{1,65},{2,66},{3,67},{4,68},{5,69},{6,70},{7,71},{8,40},{9,... | collective-permute-start | bytes 983048 | tf_op jit(solution)/shard_map/ppermute | solution.py:33
  206.2 20.2 %collective-permute-start.33 = (bf16[80,2048]{1,0:T(8,128)(2,1)S(1)}, bf16[80,2048]{1,0:T(8,128)(2,1)S(1)}, u32[]{:S(2)}, u32[]{:S(2)}) collective-permute-start(bf16[80,2048]{1,0:T(8,128)(2,1)S(1)} %get-tuple-element.120.refs_0_), channel_id=1, source_target_pairs={{0,8},{1,9},{2,10},{3,11},{4,12},{5,13},{6,14},{7,15},{8,0},{9,1},... | collective-permute-start | bytes 983048 | tf_op jit(solution)/shard_map/ppermute | solution.py:33
  214.4 12.3 %collective-permute-start.31 = (bf16[80,2048]{1,0:T(8,128)(2,1)S(1)}, bf16[80,2048]{1,0:T(8,128)(2,1)S(1)}, u32[]{:S(2)}, u32[]{:S(2)}) collective-permute-start(bf16[80,2048]{1,0:T(8,128)(2,1)S(1)} %get-tuple-element.119), channel_id=1, source_target_pairs={{0,64},{1,65},{2,66},{3,67},{4,68},{5,69},{6,70},{7,71},{8,56},{9,... | collective-permute-start | bytes 983048 | tf_op jit(solution)/shard_map/ppermute | solution.py:33
  215.7 13.8 %collective-permute-start.32 = (bf16[80,2048]{1,0:T(8,128)(2,1)S(1)}, bf16[80,2048]{1,0:T(8,128)(2,1)S(1)}, u32[]{:S(2)}, u32[]{:S(2)}) collective-permute-start(bf16[80,2048]{1,0:T(8,128)(2,1)S(1)} %get-tuple-element.118), channel_id=1, source_target_pairs={{0,64},{1,65},{2,66},{3,67},{4,68},{5,69},{6,70},{7,71},{8,40},{9,... | collective-permute-start | bytes 983048 | tf_op jit(solution)/shard_map/ppermute | solution.py:33
  216.8 16.1 %collective-permute-start.30 = (bf16[80,2048]{1,0:T(8,128)(2,1)S(1)}, bf16[80,2048]{1,0:T(8,128)(2,1)S(1)}, u32[]{:S(2)}, u32[]{:S(2)}) collective-permute-start(bf16[80,2048]{1,0:T(8,128)(2,1)S(1)} %collective-permute-done.26.refs_1_), channel_id=1, source_target_pairs={{0,64},{1,65},{2,66},{3,67},{4,68},{5,69},{6,70},{7,71},{8,24},{9,... | collective-permute-start | bytes 983048 | tf_op jit(solution)/shard_map/ppermute | solution.py:33
  221.7 14.8 %collective-permute-start.34 = (bf16[80,2048]{1,0:T(8,128)(2,1)S(1)}, bf16[80,2048]{1,0:T(8,128)(2,1)S(1)}, u32[]{:S(2)}, u32[]{:S(2)}) collective-permute-start(bf16[80,2048]{1,0:T(8,128)(2,1)S(1)} %collective-permute-done.26.refs_1_), channel_id=1, source_target_pairs={{0,8},{1,9},{2,10},{3,11},{4,12},{5,13},{6,14},{7,15},{8,0},{9,1},... | collective-permute-start | bytes 983048 | tf_op jit(solution)/shard_map/ppermute | solution.py:33
  226.5 10.1 %collective-permute-start.35 = (bf16[80,2048]{1,0:T(8,128)(2,1)S(1)}, bf16[80,2048]{1,0:T(8,128)(2,1)S(1)}, u32[]{:S(2)}, u32[]{:S(2)}) collective-permute-start(bf16[80,2048]{1,0:T(8,128)(2,1)S(1)} %collective-permute-done.27.refs_2_), channel_id=1, source_target_pairs={{0,8},{1,9},{2,10},{3,11},{4,12},{5,13},{6,14},{7,15},{8,0},{9,1},... | collective-permute-start | bytes 983048 | tf_op jit(solution)/shard_map/ppermute | solution.py:33
  226.7 13.4 %collective-permute-start.36 = (bf16[80,2048]{1,0:T(8,128)(2,1)S(1)}, bf16[80,2048]{1,0:T(8,128)(2,1)S(1)}, u32[]{:S(2)}, u32[]{:S(2)}) collective-permute-start(bf16[80,2048]{1,0:T(8,128)(2,1)S(1)} %collective-permute-done.28.refs_3_), channel_id=1, source_target_pairs={{0,8},{1,9},{2,10},{3,11},{4,12},{5,13},{6,14},{7,15},{8,0},{9,1},... | collective-permute-start | bytes 983048 | tf_op jit(solution)/shard_map/ppermute | solution.py:33
  229.5 11.3 %collective-permute-start.37 = (bf16[80,2048]{1,0:T(8,128)(2,1)S(1)}, bf16[80,2048]{1,0:T(8,128)(2,1)S(1)}, u32[]{:S(2)}, u32[]{:S(2)}) collective-permute-start(bf16[80,2048]{1,0:T(8,128)(2,1)S(1)} %collective-permute-done.29.refs_4_), channel_id=1, source_target_pairs={{0,8},{1,9},{2,10},{3,11},{4,12},{5,13},{6,14},{7,15},{8,0},{9,1},... | collective-permute-start | bytes 983048 | tf_op jit(solution)/shard_map/ppermute | solution.py:33
  (39 other events, 240.8 us)
Sparse Core Ops, SparseCore 0:
  166.2 45.2 all-gather.1

commit v5 on v3

--- a/solution.py
+++ b/solution.py
@@ -58,38 +58,34 @@
     return move
 
 
-def pack(where, mine, other, steps):
+VMEM = pl.BlockSpec(memory_space=pltpu.VMEM)
+SMEM = pl.BlockSpec(memory_space=pltpu.SMEM)
+
+
+def pack(where, mine, other):
     tokens, hidden = mine.shape
     piece = hidden // 16
-    count = len(steps)
-
-    def kernel(where_ref, *refs):
-        for place in range(count):
-            both = jnp.concatenate([refs[place][...], refs[count + place][...]], axis=0)
-            refs[2 * count + place][...] = both.T
-
-    def source_map(step):
-        def index(g, w):
-            at = lax.rem(w[0] + step, 4)
-            return 0, jnp.where(w[3] == 0, g * 4 + at, at * 4 + g)
-
-        return index
-
-    maps = [pl.BlockSpec((tokens, piece), source_map(step)) for step in steps]
+
+    def kernel(where_ref, mine_ref, other_ref, *out_refs):
+        @pl.loop(0, 4)
+        def _(g):
+            rows = pl.ds(pl.multiple_of(g * piece, piece), piece)
+            for step, out_ref in enumerate(out_refs):
+                at = lax.rem(where_ref[0] + step, 4)
+                place = jnp.where(where_ref[3] == 0, g * 4 + at, at * 4 + g)
+                columns = pl.ds(pl.multiple_of(place * piece, piece), piece)
+                both = jnp.concatenate([mine_ref[:, columns], other_ref[:, columns]], axis=0)
+                out_ref[rows, :] = both.T
+
     return pl.pallas_call(
         kernel,
-        grid_spec=pltpu.PrefetchScalarGridSpec(
-            num_scalar_prefetch=1,
-            grid=(4,),
-            in_specs=maps + maps,
-            out_specs=[pl.BlockSpec((piece, 2 * tokens), lambda g, w: (g, 0))] * count,
-        ),
-        out_shape=[jax.ShapeDtypeStruct((hidden // 4, 2 * tokens), mine.dtype)] * count,
-        cost_estimate=pl.CostEstimate(
-            flops=0, bytes_accessed=count * 2 * tokens * hidden, transcendentals=0
-        ),
+        in_specs=[SMEM, VMEM, VMEM],
+        out_specs=[VMEM] * 4,
+        out_shape=[jax.ShapeDtypeStruct((hidden // 4, 2 * tokens), mine.dtype)] * 4,
+        compiler_params=pltpu.CompilerParams(vmem_limit_bytes=24 * 1024 * 1024),
+        cost_estimate=pl.CostEstimate(flops=0, bytes_accessed=8 * tokens * hidden, transcendentals=0),
         name="pack_cotangent",
-    )(where, *([mine] * count), *([other] * count))
+    )(where, mine, other)
 
 
 def partial_sums(where, blocks, inputs, y_first):
@@ -102,49 +98,45 @@
         block_refs, input_refs = refs[:4], refs[4:8]
         out_refs = refs[8:-2]
         held, total = refs[-2:]
-        g = pl.program_id(0)
-
-        @pl.when(g == 0)
-        def _():
-            for step in range(4):
-                held[pl.ds(step * tokens, tokens), :] = input_refs[step][...]
-
-        turned = jnp.concatenate([ref[...] for ref in block_refs], axis=1)
-        total[...] = jnp.dot(turned, held[...], preferred_element_type=jnp.float32).astype(jnp.bfloat16)
-
-        step_g = lax.rem(g - where_ref[1] + 4, 4)
-        if not y_first:
-            for distance, ref in enumerate(out_refs):
-
-                @pl.when(step_g == distance)
-                def _(ref=ref):
-                    for to_y in range(4):
-                        ref[lax.rem(to_y - where_ref[2] + 4, 4)] = total[pl.ds(to_y * 2 * unit, 2 * unit), :]
-
-            return
-        plus_ref, minus_ref, first_ref, third_ref, keep_ref = out_refs
-        for to_y in range(4):
-            step_y = lax.rem(to_y - where_ref[2] + 4, 4)
-            for half in range(2):
-                start = (to_y * 2 + half) * unit
-                places = {
-                    0: (keep_ref, half),
-                    1: (first_ref, None) if half == 0 else (plus_ref, 1),
-                    2: (plus_ref, 0) if half == 0 else (minus_ref, 0),
-                    3: (minus_ref, 1) if half == 0 else (third_ref, None),
-                }
-                for distance, (ref, slot) in places.items():
-
-                    @pl.when(step_y == distance)
-                    def _(ref=ref, slot=slot, start=start):
-                        value = total[pl.ds(start, unit), :]
-                        if slot is None:
-                            ref[step_g] = value
-                        else:
-                            ref[slot, step_g] = value
-
-    def whole(shape):
-        return pl.BlockSpec(shape, lambda g, w: (0,) * len(shape))
+        for step in range(4):
+            held[pl.ds(step * tokens, tokens), :] = input_refs[step][...]
+
+        @pl.loop(0, 4)
+        def _(g):
+            at = pl.ds(pl.multiple_of(g * piece, piece), piece)
+            turned = jnp.concatenate([ref[at, :] for ref in block_refs], axis=1)
+            total[...] = jnp.dot(turned, held[...], preferred_element_type=jnp.float32).astype(jnp.bfloat16)
+
+            step_g = lax.rem(g - where_ref[1] + 4, 4)
+            if not y_first:
+                for distance, ref in enumerate(out_refs):
+
+                    @pl.when(step_g == distance)
+                    def _(ref=ref):
+                        for to_y in range(4):
+                            ref[lax.rem(to_y - where_ref[2] + 4, 4)] = total[pl.ds(to_y * 2 * unit, 2 * unit), :]
+
+                return
+            plus_ref, minus_ref, first_ref, third_ref, keep_ref = out_refs
+            for to_y in range(4):
+                step_y = lax.rem(to_y - where_ref[2] + 4, 4)
+                for half in range(2):
+                    start = (to_y * 2 + half) * unit
+                    places = {
+                        0: (keep_ref, half),
+                        1: (first_ref, None) if half == 0 else (plus_ref, 1),
+                        2: (plus_ref, 0) if half == 0 else (minus_ref, 0),
+                        3: (minus_ref, 1) if half == 0 else (third_ref, None),
+                    }
+                    for distance, (ref, slot) in places.items():
+
+                        @pl.when(step_y == distance)
+                        def _(ref=ref, slot=slot, start=start):
+                            value = total[pl.ds(start, unit), :]
+                            if slot is None:
+                                ref[step_g] = value
+                            else:
+                                ref[slot, step_g] = value
 
     if y_first:
         two, one = (2, 4, unit, width), (4, unit, width)
@@ -153,19 +145,14 @@
         shapes = ((4, 2 * unit, width),) * 4
     return pl.pallas_call(
         kernel,
-        grid_spec=pltpu.PrefetchScalarGridSpec(
-            num_scalar_prefetch=1,
-            grid=(4,),
-            in_specs=[pl.BlockSpec((piece, tokens), lambda g, w: (g, 0))] * 4
-            + [whole(value.shape) for value in inputs],
-            out_specs=[whole(shape) for shape in shapes],
-            scratch_shapes=[
-                pltpu.VMEM((4 * tokens, width), jnp.bfloat16),
-                pltpu.VMEM((piece, width), jnp.bfloat16),
-            ],
-        ),
+        in_specs=[SMEM] + [VMEM] * 8,
+        out_specs=[VMEM] * len(shapes),
+        scratch_shapes=[
+            pltpu.VMEM((4 * tokens, width), jnp.bfloat16),
+            pltpu.VMEM((piece, width), jnp.bfloat16),
+        ],
         out_shape=[jax.ShapeDtypeStruct(shape, jnp.bfloat16) for shape in shapes],
-        compiler_params=pltpu.CompilerParams(vmem_limit_bytes=40 * 1024 * 1024),
+        compiler_params=pltpu.CompilerParams(vmem_limit_bytes=24 * 1024 * 1024),
         cost_estimate=pl.CostEstimate(
             flops=2 * 4 * tokens * rows * width,
             bytes_accessed=4 * tokens * (rows + width) * 2 + rows * width * 2,
@@ -183,8 +170,8 @@
     return value.astype(jnp.bfloat16)
 
 
-def after(value, *others):
-    return lax.optimization_barrier((value, others))[0]
+def tie(*values):
+    return lax.optimization_barrier(values)
 
 
 def ring_send(plus, minus, along):
@@ -219,7 +206,7 @@
     return move
 
 
-def gather_rows(value, c):
+def gather_rows(value, c, state):
     def choose(low, high):
         return jnp.where(c == 0, low, high)
 
@@ -227,6 +214,7 @@
     two = send(value, near_and_pair(-1, 1))
     three = send(value, near_and_pair(2, -1))
     four = send(value, near_and_pair(None, 2))
+    one, state = tie(one, state)
     five = send(one, near_and_pair(None, 1))
     six = send(choose(two, one), near_and_pair(None, -1))
     seven = send(choose(three, one), near_and_pair(None, 2))
@@ -236,7 +224,8 @@
     z_steps = jnp.where(c == 0, jnp.array([0, 0, 0, 0, 1, 1, 1, 1]), jnp.array([0, 1, 0, 0, 0, 1, 1, 1]))
     other_y = jnp.where(c == 1, jnp.array([0, 3, 1, 2, 0, 3, 1, 2]), jnp.array([0, 0, 3, 1, 2, 3, 1, 2]))
     other_z = jnp.where(c == 1, jnp.array([0, 0, 0, 0, 1, 1, 1, 1]), jnp.array([0, 1, 0, 0, 0, 1, 1, 1]))
-    return own + swapped, jnp.concatenate([y_steps, other_y]), jnp.concatenate([z_steps, other_z])
+    steps = jnp.concatenate([y_steps, other_y]), jnp.concatenate([z_steps, other_z])
+    return own + swapped, *steps, state
 
 
 def assemble(places, gathered, parts, columns):
@@ -265,17 +254,13 @@
         for copy in copies:
             copy.wait()
 
-    anywhere = pl.BlockSpec(memory_space=pl.ANY)
     return pl.pallas_call(
         kernel,
-        grid_spec=pltpu.PrefetchScalarGridSpec(
-            num_scalar_prefetch=1,
-            grid=(1,),
-            in_specs=[anywhere] * (1 + len(parts)),
-            out_specs=anywhere,
-            scratch_shapes=[pltpu.SemaphoreType.DMA((2 * (1 + len(parts)),))],
-        ),
+        in_specs=[SMEM] + [VMEM] * (1 + len(parts)),
+        out_specs=pl.BlockSpec(memory_space=pltpu.HBM),
+        scratch_shapes=[pltpu.SemaphoreType.DMA((2 * (1 + len(parts)),))],
         out_shape=jax.ShapeDtypeStruct((rows, columns), jnp.bfloat16),
+        compiler_params=pltpu.CompilerParams(vmem_limit_bytes=4 * 1024 * 1024),
         name="assemble_copy",
     )(places, gathered, *parts)
 
@@ -303,7 +288,8 @@
     kept = jnp.where(c == 0, low, high)
     given = jnp.where(c == 0, high, low)
     chip_input = jnp.concatenate([kept, send(given, sibling)], axis=0)
-    other = send(after(up_cotangent, given), sibling)
+    chip_input, swapped = tie(chip_input, up_cotangent)
+    other = send(swapped, sibling)
 
     def spread(value):
         return [send(value, along_rows(step)) for step in (1, 3, 2)]
@@ -311,11 +297,11 @@
     starts = [sum(WIDTHS[:place]) for place in range(len(WIDTHS))]
     inputs = [chip_input[:, start : start + width] for start, width in zip(starts, WIDTHS)]
     inputs_0 = [inputs[0], *spread(inputs[0])]
-    near, far = pack(where, up_cotangent, other, (1, 3))
-    near, far = after((near, far), inputs_0)
-    own, last = pack(after(where, near), up_cotangent, other, (0, 2))
+    own, near, last, far = pack(where, up_cotangent, other)
+    near, far, inputs_0 = tie(near, far, inputs_0)
     blocks = [own, send(near, along_rows(1)), send(far, along_rows(3)), send(last, along_rows(2))]
-    inputs_1 = [inputs[1], *spread(after(inputs[1], blocks))]
+    blocks, waiting = tie(blocks, inputs[1])
+    inputs_1 = [inputs[1], *spread(waiting)]
 
     plus, minus, first, third, keep = partial_sums(where, blocks, inputs_0, True)
     sent_0 = ring_send(plus, minus, along_y)
@@ -323,6 +309,7 @@
     sent_0, pieces_1 = lax.optimization_barrier((sent_0, pieces_1))
     sent_1 = direct(pieces_1, along_sums)
     turned_0 = ring_turn(first, third, *sent_0, along_y)
+    turned_0, sent_1[1] = tie(turned_0, sent_1[1])
     again_0 = direct([ring_end(keep, *sent_0, *turned_0, place) for place in range(4)], along_sums)
     again_1 = direct([summed(sent_1, place) for place in range(4)], along_y)
 
@@ -349,13 +336,12 @@
             axis=1,
         )
 
+    state = adamw(joined(grads), master, first_moment, second_moment)
     gathered = lax.all_gather(copies[0], "inter", axis=0, tiled=True)
-    parts, y_steps, z_steps = gather_rows(copies[1], c)
+    parts, y_steps, z_steps, state = gather_rows(copies[1], c, state)
     cores = jnp.array([0] * 8 + [1] * 8)
     places = (((z + z_steps) % 2) * 8 + ((y + y_steps) % 4) * 2 + (c + cores) % 2).astype(jnp.int32)
-    new_copy = assemble(places, gathered, parts, columns)
-    new_master, new_first, new_second = adamw(joined(grads), master, first_moment, second_moment)
-    return (new_master, new_first, new_second, new_copy)
+    return (*state, assemble(places, gathered, parts, columns))
 
 
 def solution(mesh):

time: 551 us -> 271 us (0.49)
  Pallas kernels: 311 us -> 28.8 us
    pallas_call x5 -> x4, Pallas kernels: 311 us -> 28.8 us  [the longest x2 18.4 us: partial_sums(): pl.pallas_call(kernel, in_specs=[SMEM] + [VMEM] * 8, out_specs=[VMEM] * l...]
    unnamed x80 -> x46, local copies, waits for them, and re-layouts: 7.64 us -> 11.4 us
  transfers between devices with their start and end apart: 42 -> 42, of which waited for: 23 -> 23; matrix products, arithmetic and copies ran while one was open for 2% -> 4% of each run, Pallas kernels for 6% -> 9%
where the time goes in v5:
time: 271 us; the launch traced here: 270 us
  waiting for transfers between devices  154 us (57%)
  starting transfers between devices  47.8 us (18%)
  Pallas kernels  28.8 us (11%)
  between operations  14.4 us (5%)
  local copies, waits for them, and re-layouts  14.3 us (5%)
  other arithmetic  10.9 us (4%)
    ppermute x41, waiting for transfers between devices, send(): return lax.ppermute(value, AXES, permutation(move))  154 us
    ppermute x41, starting transfers between devices, send(): return lax.ppermute(value, AXES, permutation(move))  47.8 us
    pallas_call x2, Pallas kernels, partial_sums(): pl.pallas_call(kernel, in_specs=[SMEM] + [VMEM] * 8, out_specs=[VMEM] * l...  18.4 us
    unnamed x46, local copies, waits for them, and re-layouts  11.4 us
    pallas_call x1, Pallas kernels, pack(): pl.pallas_call(kernel, in_specs=[SMEM, VMEM, VMEM], out_specs=[VMEM] * 4,...  5.66 us
  transfers between devices with their start and end apart: 42, of which 23 were waited for; matrix products, arithmetic and copies ran while one was open for 4% of the time, Pallas kernels for 9%

profile of v5, /device:TPU:1, one launch (start us, length us, event | category | flops | bytes accessed | tf_op | source)
XLA Modules:
  0.0 270.0 jit_solution(12970991554368504211)
XLA Ops:
  16.9 2.3 collective-permute-done.1.other_ref
  19.2 5.7 %pack_cotangent.1 = (bf16[2560,384]{1,0:T(8,128)(2,1)S(1)}, bf16[2560,384]{1,0:T(8,128)(2,1)S(1)}, bf16[2560,384]{1,0:T(8,128)(2,1)S(1)}, bf16[2560,384]{1,0:T(8,128)(2,1)S(1)}) custom-call(s32[4]{0:T(128)S(1)} %pad_add_fusion.where_ref, bf16[192,10240]{1,0:T(8,128)(2,1)} %mine_ref.1, bf16[192,10240]{1,0:T(8,128)(2,1)} %collective-permute-done.1.other_ref), custom_call_target="tpu_custom_call" | custom-call | bytes 15728640 | tf_op jit(solution)/shard_map/pack_cotangent/pallas_call | solution.py:80
  24.9 3.9 %collective-permute-done.3.refs_6_ = bf16[384,768]{1,0:T(8,128)(2,1)S(1)} collective-permute-done((bf16[384,768]{1,0:T(8,128)(2,1)S(1)}, bf16[384,768]{1,0:T(8,128)(2,1)S(1)}, u32[]{:S(2)}, u32[]{:S(2)}) %collective-permute-start.3) | collective-permute-done | bytes 589856 | tf_op jit(solution)/shard_map/ppermute | solution.py:33
  31.1 1.8 collective-permute-start.6
  33.5 21.7 %collective-permute-done.5.refs_1_ = bf16[2560,384]{1,0:T(8,128)(2,1)S(1)} collective-permute-done((bf16[2560,384]{1,0:T(8,128)(2,1)S(1)}, bf16[2560,384]{1,0:T(8,128)(2,1)S(1)}, u32[]{:S(2)}, u32[]{:S(2)}) %collective-permute-start.5) | collective-permute-done | bytes 1966112 | tf_op jit(solution)/shard_map/ppermute | solution.py:33
  55.2 20.3 %collective-permute-done.6.refs_2_ = bf16[2560,384]{1,0:T(8,128)(2,1)S(1)} collective-permute-done((bf16[2560,384]{1,0:T(8,128)(2,1)S(1)}, bf16[2560,384]{1,0:T(8,128)(2,1)S(1)}, u32[]{:S(2)}, u32[]{:S(2)}) %collective-permute-start.6) | collective-permute-done | bytes 1966112 | tf_op jit(solution)/shard_map/ppermute | solution.py:33
  77.6 1.8 collective-permute-start.11
  80.1 8.3 %partial_sums.2 = (bf16[2,4,80,768]{3,2,1,0:T(8,128)(2,1)S(1)}, bf16[2,4,80,768]{3,2,1,0:T(8,128)(2,1)S(1)}, bf16[4,80,768]{2,1,0:T(8,128)(2,1)S(1)}, bf16[4,80,...) custom-call(s32[4]{0:T(128)S(1)} %pad_add_fusion.where_ref, bf16[2560,384]{1,0:T(8,128)(2,1)S(1)} %get-tuple-element.51.refs_0_, ...), custom_call_target="tpu_custom_call" | custom-call | flops 6039797760 | bytes 14155776 | tf_op jit(solution)/shard_map/partial_sums/pallas_call | solution.py:146
  91.3 5.5 %collective-permute-done.11.refs_6_ = bf16[384,1024]{1,0:T(8,128)(2,1)S(1)} collective-permute-done((bf16[384,1024]{1,0:T(8,128)(2,1)S(1)}, bf16[384,1024]{1,0:T(8,128)(2,1)S(1)}, u32[]{:S(2)}, u32[]{:S(2)}) %collective-permute-start.11) | collective-permute-done | bytes 786464 | tf_op jit(solution)/shard_map/ppermute | solution.py:33
  98.2 10.1 %partial_sums.3 = (bf16[4,160,1024]{2,1,0:T(8,128)(2,1)S(1)}, bf16[4,160,1024]{2,1,0:T(8,128)(2,1)S(1)}, bf16[4,160,1024]{2,1,0:T(8,128)(2,1)S(1)}, bf16[4,160,1024]{2,1,0:T(8,128)(2,1)S(1)}) custom-call(s32[4]{0:T(128)S(1)} %pad_add_fusion.where_ref, bf16[2560,384]{1,0:T(8,128)(2,1)S(1)} %get-tuple-element.51.refs_0_, ...), custom_call_target="tpu_custom_call" | custom-call | flops 8053063680 | bytes 16252928 | tf_op jit(solution)/shard_map/partial_sums/pallas_call | solution.py:146
  111.7 1.8 collective-permute-start.14
  113.5 6.3 %collective-permute-done.13 = bf16[4,80,768]{2,1,0:T(8,128)(2,1)S(1)} collective-permute-done((bf16[4,80,768]{2,1,0:T(8,128)(2,1)S(1)}, bf16[4,80,768]{2,1,0:T(8,128)(2,1)S(1)}, u32[]{:S(2)}, u32[]{:S(2)}) %collective-permute-start.13) | collective-permute-done | bytes 491552 | tf_op jit(solution)/shard_map/ppermute | solution.py:33
  119.8 9.7 %collective-permute-done.15 = bf16[4,160,1024]{2,1,0:T(8,128)(2,1)S(1)} collective-permute-done((bf16[4,160,1024]{2,1,0:T(8,128)(2,1)S(1)}, bf16[4,160,1024]{2,1,0:T(8,128)(2,1)S(1)}, u32[]{:S(2)}, u32[]{:S(2)}) %collective-permute-start.15) | collective-permute-done | bytes 1310752 | tf_op jit(solution)/shard_map/ppermute | solution.py:33
  134.5 2.8 %collective-permute-done.25 = bf16[160,768]{1,0:T(8,128)(2,1)S(1)} collective-permute-done((bf16[160,768]{1,0:T(8,128)(2,1)S(1)}, bf16[160,768]{1,0:T(8,128)(2,1)S(1)}, u32[]{:S(2)}, u32[]{:S(2)}) %collective-permute-start.25) | collective-permute-done | bytes 245792 | tf_op jit(solution)/shard_map/ppermute | solution.py:33
  137.4 1.9 collective-permute-done.24
  140.3 4.3 %collective-permute-start.26 = (bf16[80,768]{1,0:T(8,128)(2,1)S(1)}, bf16[80,768]{1,0:T(8,128)(2,1)S(1)}, u32[]{:S(2)}, u32[]{:S(2)}) collective-permute-start(bf16[80,768]{1,0:T(8,128)(2,1)S(1)} %broadcast_select_fusion.10), channel_id=1, source_target_pairs={{0,8},{1,9},{2,10},{3,11},{4,12},{5,13},{6,14},{7,15},{8,0},{9,1},... | collective-permute-start | bytes 368648 | tf_op jit(solution)/shard_map/ppermute | solution.py:33
  146.9 3.2 %collective-permute-start.17 = (bf16[4,160,1024]{2,1,0:T(8,128)(2,1)}, bf16[4,160,1024]{2,1,0:T(8,128)(2,1)S(1)}, u32[]{:S(2)}, u32[]{:S(2)}) collective-permute-start(bf16[4,160,1024]{2,1,0:T(8,128)(2,1)} %copy-done.11), channel_id=1, source_target_pairs={{0,4},{1,5},{2,6},{3,7},{4,0},{5,1},{6,2},{7,3},{8,9},{9,8},{10,11... | collective-permute-start | bytes 3932168 | tf_op jit(solution)/shard_map/ppermute | solution.py:33
  150.6 30.6 %collective-permute-done.17 = bf16[4,160,1024]{2,1,0:T(8,128)(2,1)S(1)} collective-permute-done((bf16[4,160,1024]{2,1,0:T(8,128)(2,1)}, bf16[4,160,1024]{2,1,0:T(8,128)(2,1)S(1)}, u32[]{:S(2)}, u32[]{:S(2)}) %collective-permute-start.17) | collective-permute-done | bytes 1310752 | tf_op jit(solution)/shard_map/ppermute | solution.py:33
  181.1 17.6 %collective-permute-done.16 = bf16[4,160,1024]{2,1,0:T(8,128)(2,1)S(1)} collective-permute-done((bf16[4,160,1024]{2,1,0:T(8,128)(2,1)S(1)}, bf16[4,160,1024]{2,1,0:T(8,128)(2,1)S(1)}, u32[]{:S(2)}, u32[]{:S(2)}) %collective-permute-start.16) | collective-permute-done | bytes 1310752 | tf_op jit(solution)/shard_map/ppermute | solution.py:33
  198.7 2.1 fusion.28
  201.0 2.8 %collective-permute-start.19 = (bf16[160,1024]{1,0:T(8,128)(2,1)S(1)}, bf16[160,1024]{1,0:T(8,128)(2,1)S(1)}, u32[]{:S(2)}, u32[]{:S(2)}) collective-permute-start(bf16[160,1024]{1,0:T(8,128)(2,1)S(1)} %get-tuple-element.87), channel_id=1, source_target_pairs={{0,48},{1,49},{2,50},{3,51},{4,52},{5,53},{6,54},{7,55},{8,56},{9,... | collective-permute-start | bytes 983048 | tf_op jit(solution)/shard_map/ppermute | solution.py:33
  204.5 4.0 %collective-permute-done.20 = bf16[160,1024]{1,0:T(8,128)(2,1)S(1)} collective-permute-done((bf16[160,1024]{1,0:T(8,128)(2,1)S(1)}, bf16[160,1024]{1,0:T(8,128)(2,1)S(1)}, u32[]{:S(2)}, u32[]{:S(2)}) %collective-permute-start.20) | collective-permute-done | bytes 327712 | tf_op jit(solution)/shard_map/ppermute | solution.py:33
  208.5 3.8 %collective-permute-done.19 = bf16[160,1024]{1,0:T(8,128)(2,1)S(1)} collective-permute-done((bf16[160,1024]{1,0:T(8,128)(2,1)S(1)}, bf16[160,1024]{1,0:T(8,128)(2,1)S(1)}, u32[]{:S(2)}, u32[]{:S(2)}) %collective-permute-start.19) | collective-permute-done | bytes 327712 | tf_op jit(solution)/shard_map/ppermute | solution.py:33
  215.9 2.7 collective-permute-start.28
  219.9 2.3 multiply_subtract_fusion
  223.5 2.9 %collective-permute-done.27.refs_2_ = bf16[80,2048]{1,0:T(8,128)(2,1)S(1)} collective-permute-done((bf16[80,2048]{1,0:T(8,128)(2,1)S(1)}, bf16[80,2048]{1,0:T(8,128)(2,1)S(1)}, u32[]{:S(2)}, u32[]{:S(2)}) %collective-permute-start.27) | collective-permute-done | bytes 327712 | tf_op jit(solution)/shard_map/ppermute | solution.py:33
  226.4 5.8 %collective-permute-done.28.refs_3_ = bf16[80,2048]{1,0:T(8,128)(2,1)S(1)} collective-permute-done((bf16[80,2048]{1,0:T(8,128)(2,1)S(1)}, bf16[80,2048]{1,0:T(8,128)(2,1)S(1)}, u32[]{:S(2)}, u32[]{:S(2)}) %collective-permute-start.28) | collective-permute-done | bytes 327712 | tf_op jit(solution)/shard_map/ppermute | solution.py:33
  233.1 3.6 %collective-permute-start.31 = (bf16[80,2048]{1,0:T(8,128)(2,1)}, bf16[80,2048]{1,0:T(8,128)(2,1)S(1)}, u32[]{:S(2)}, u32[]{:S(2)}) collective-permute-start(bf16[80,2048]{1,0:T(8,128)(2,1)} %get-tuple-element.119), channel_id=1, source_target_pairs={{0,64},{1,65},{2,66},{3,67},{4,68},{5,69},{6,70},{7,71},{8,56},{9,... | collective-permute-start | bytes 983048 | tf_op jit(solution)/shard_map/ppermute | solution.py:33
  238.8 5.7 %collective-permute-done.31.refs_6_ = bf16[80,2048]{1,0:T(8,128)(2,1)S(1)} collective-permute-done((bf16[80,2048]{1,0:T(8,128)(2,1)}, bf16[80,2048]{1,0:T(8,128)(2,1)S(1)}, u32[]{:S(2)}, u32[]{:S(2)}) %collective-permute-start.31) | collective-permute-done | bytes 327712 | tf_op jit(solution)/shard_map/ppermute | solution.py:33
  244.5 2.6 collective-permute-start.38
  251.4 2.1 copy-done
  258.4 4.8 %assemble_copy.1 = bf16[1280,3584]{1,0:T(8,128)(2,1)} custom-call(s32[16]{0:T(128)S(1)} %fusion.39.places_ref, bf16[1280,1536]{1,0:T(8,128)(2,1)S(1)} %copy-done, bf16[80,2048]{1,0:T(8,128)(2,1)S(1)} %get-tuple-element.121.refs_0_, bf16[80,2048]{1,0:T(8,128)(2,1)S(1)} %collective-permute-done.22.refs_1_, ...), custom_call_target="tpu_custom_call" | custom-call | tf_op jit(solution)/shard_map/assemble_copy/pallas_call | solution.py:257
  (134 shorter events, 50.9 us)
Async XLA Ops:
  7.2 244.3 %all-gather.2.cloned.1.call-start = ((), (), s32[]{:S(2)}) async-start(), calls=%async_computation | async-start | bytes 4177920 | tf_op jit(solution)/shard_map/all_gather | solution.py:340
  12.5 12.4 %collective-permute-start.2 = (bf16[384,768]{1,0:T(8,128)(2,1)S(1)}, bf16[384,768]{1,0:T(8,128)(2,1)S(1)}, u32[]{:S(2)}, u32[]{:S(2)}) collective-permute-start(bf16[384,768]{1,0:T(8,128)(2,1)S(1)} %slice.204.refs_4_), channel_id=1, source_target_pairs={{0,64},{1,65},{2,66},{3,67},{4,68},{5,69},{6,70},{7,71},{8,10},{9,... | collective-permute-start | bytes 1769480 | tf_op jit(solution)/shard_map/ppermute | solution.py:33
  13.9 14.9 %collective-permute-start.3 = (bf16[384,768]{1,0:T(8,128)(2,1)S(1)}, bf16[384,768]{1,0:T(8,128)(2,1)S(1)}, u32[]{:S(2)}, u32[]{:S(2)}) collective-permute-start(bf16[384,768]{1,0:T(8,128)(2,1)S(1)} %slice.204.refs_4_), channel_id=1, source_target_pairs={{0,65},{1,64},{2,67},{3,66},{4,69},{5,68},{6,71},{7,70},{8,14},{9,... | collective-permute-start | bytes 1769480 | tf_op jit(solution)/shard_map/ppermute | solution.py:33
  15.6 14.6 %collective-permute-start.4 = (bf16[384,768]{1,0:T(8,128)(2,1)S(1)}, bf16[384,768]{1,0:T(8,128)(2,1)S(1)}, u32[]{:S(2)}, u32[]{:S(2)}) collective-permute-start(bf16[384,768]{1,0:T(8,128)(2,1)S(1)} %slice.204.refs_4_), channel_id=1, source_target_pairs={{0,1},{1,0},{2,3},{3,2},{4,5},{5,4},{6,7},{7,6},{8,12},{9,13},{10,... | collective-permute-start | bytes 1769480 | tf_op jit(solution)/shard_map/ppermute | solution.py:33
  30.2 25.0 %collective-permute-start.5 = (bf16[2560,384]{1,0:T(8,128)(2,1)S(1)}, bf16[2560,384]{1,0:T(8,128)(2,1)S(1)}, u32[]{:S(2)}, u32[]{:S(2)}) collective-permute-start(bf16[2560,384]{1,0:T(8,128)(2,1)S(1)} %get-tuple-element.48), channel_id=1, source_target_pairs={{0,64},{1,65},{2,66},{3,67},{4,68},{5,69},{6,70},{7,71},{8,10},{9,... | collective-permute-start | bytes 5898248 | tf_op jit(solution)/shard_map/ppermute | solution.py:33
  31.1 44.5 %collective-permute-start.6 = (bf16[2560,384]{1,0:T(8,128)(2,1)S(1)}, bf16[2560,384]{1,0:T(8,128)(2,1)S(1)}, u32[]{:S(2)}, u32[]{:S(2)}) collective-permute-start(bf16[2560,384]{1,0:T(8,128)(2,1)S(1)} %get-tuple-element.49), channel_id=1, source_target_pairs={{0,65},{1,64},{2,67},{3,66},{4,69},{5,68},{6,71},{7,70},{8,14},{9,... | collective-permute-start | bytes 5898248 | tf_op jit(solution)/shard_map/ppermute | solution.py:33
  32.9 43.9 %collective-permute-start.7 = (bf16[2560,384]{1,0:T(8,128)(2,1)S(1)}, bf16[2560,384]{1,0:T(8,128)(2,1)S(1)}, u32[]{:S(2)}, u32[]{:S(2)}) collective-permute-start(bf16[2560,384]{1,0:T(8,128)(2,1)S(1)} %get-tuple-element.50), channel_id=1, source_target_pairs={{0,1},{1,0},{2,3},{3,2},{4,5},{5,4},{6,7},{7,6},{8,12},{9,13},{10,... | collective-permute-start | bytes 5898248 | tf_op jit(solution)/shard_map/ppermute | solution.py:33
  76.8 14.6 %collective-permute-start.10 = (bf16[384,1024]{1,0:T(8,128)(2,1)S(1)}, bf16[384,1024]{1,0:T(8,128)(2,1)S(1)}, u32[]{:S(2)}, u32[]{:S(2)}) collective-permute-start(bf16[384,1024]{1,0:T(8,128)(2,1)S(1)} %slice.205.refs_4_), channel_id=1, source_target_pairs={{0,64},{1,65},{2,66},{3,67},{4,68},{5,69},{6,70},{7,71},{8,10},{9,... | collective-permute-start | bytes 2359304 | tf_op jit(solution)/shard_map/ppermute | solution.py:33
  77.6 19.2 %collective-permute-start.11 = (bf16[384,1024]{1,0:T(8,128)(2,1)S(1)}, bf16[384,1024]{1,0:T(8,128)(2,1)S(1)}, u32[]{:S(2)}, u32[]{:S(2)}) collective-permute-start(bf16[384,1024]{1,0:T(8,128)(2,1)S(1)} %slice.205.refs_4_), channel_id=1, source_target_pairs={{0,65},{1,64},{2,67},{3,66},{4,69},{5,68},{6,71},{7,70},{8,14},{9,... | collective-permute-start | bytes 2359304 | tf_op jit(solution)/shard_map/ppermute | solution.py:33
  79.4 18.8 %collective-permute-start.12 = (bf16[384,1024]{1,0:T(8,128)(2,1)S(1)}, bf16[384,1024]{1,0:T(8,128)(2,1)S(1)}, u32[]{:S(2)}, u32[]{:S(2)}) collective-permute-start(bf16[384,1024]{1,0:T(8,128)(2,1)S(1)} %slice.205.refs_4_), channel_id=1, source_target_pairs={{0,1},{1,0},{2,3},{3,2},{4,5},{5,4},{6,7},{7,6},{8,12},{9,13},{10,... | collective-permute-start | bytes 2359304 | tf_op jit(solution)/shard_map/ppermute | solution.py:33
  88.4 20.7 %collective-permute-start.8 = (bf16[2,4,80,768]{3,2,1,0:T(8,128)(2,1)S(1)}, bf16[2,4,80,768]{3,2,1,0:T(8,128)(2,1)S(1)}, u32[]{:S(2)}, u32[]{:S(2)}) collective-permute-start(bf16[2,4,80,768]{3,2,1,0:T(8,128)(2,1)S(1)} %get-tuple-element.59), channel_id=1, source_target_pairs={{0,16},{1,17},{2,18},{3,19},{4,20},{5,21},{6,22},{7,23},{8,24},{9,... | collective-permute-start | bytes 2949128 | tf_op jit(solution)/shard_map/ppermute | solution.py:33
  89.8 19.3 %collective-permute-start.9 = (bf16[2,4,80,768]{3,2,1,0:T(8,128)(2,1)S(1)}, bf16[2,4,80,768]{3,2,1,0:T(8,128)(2,1)S(1)}, u32[]{:S(2)}, u32[]{:S(2)}) collective-permute-start(bf16[2,4,80,768]{3,2,1,0:T(8,128)(2,1)S(1)} %get-tuple-element.60), channel_id=1, source_target_pairs={{0,48},{1,49},{2,50},{3,51},{4,52},{5,53},{6,54},{7,55},{8,56},{9,... | collective-permute-start | bytes 2949128 | tf_op jit(solution)/shard_map/ppermute | solution.py:33
  109.2 20.3 %collective-permute-start.15 = (bf16[4,160,1024]{2,1,0:T(8,128)(2,1)S(1)}, bf16[4,160,1024]{2,1,0:T(8,128)(2,1)S(1)}, u32[]{:S(2)}, u32[]{:S(2)}) collective-permute-start(bf16[4,160,1024]{2,1,0:T(8,128)(2,1)S(1)} %get-tuple-element.71), channel_id=1, source_target_pairs={{0,2},{1,3},{2,4},{3,5},{4,6},{5,7},{6,0},{7,1},{8,72},{9,73},{10,... | collective-permute-start | bytes 3932168 | tf_op jit(solution)/shard_map/ppermute | solution.py:33
  110.5 9.3 %collective-permute-start.13 = (bf16[4,80,768]{2,1,0:T(8,128)(2,1)S(1)}, bf16[4,80,768]{2,1,0:T(8,128)(2,1)S(1)}, u32[]{:S(2)}, u32[]{:S(2)}) collective-permute-start(bf16[4,80,768]{2,1,0:T(8,128)(2,1)S(1)} %fusion.1), channel_id=1, source_target_pairs={{0,16},{1,17},{2,18},{3,19},{4,20},{5,21},{6,22},{7,23},{8,24},{9,... | collective-permute-start | bytes 1474568 | tf_op jit(solution)/shard_map/ppermute | solution.py:33
  111.7 8.1 %collective-permute-start.14 = (bf16[4,80,768]{2,1,0:T(8,128)(2,1)S(1)}, bf16[4,80,768]{2,1,0:T(8,128)(2,1)S(1)}, u32[]{:S(2)}, u32[]{:S(2)}) collective-permute-start(bf16[4,80,768]{2,1,0:T(8,128)(2,1)S(1)} %fusion), channel_id=1, source_target_pairs={{0,48},{1,49},{2,50},{3,51},{4,52},{5,53},{6,54},{7,55},{8,56},{9,... | collective-permute-start | bytes 1474568 | tf_op jit(solution)/shard_map/ppermute | solution.py:33
  131.2 8.1 %collective-permute-start.24 = (bf16[160,768]{1,0:T(8,128)(2,1)S(1)}, bf16[160,768]{1,0:T(8,128)(2,1)S(1)}, u32[]{:S(2)}, u32[]{:S(2)}) collective-permute-start(bf16[160,768]{1,0:T(8,128)(2,1)S(1)} %pad_maximum_fusion.6), channel_id=1, source_target_pairs={{0,6},{1,7},{2,0},{3,1},{4,2},{5,3},{6,4},{7,5},{8,73},{9,72},{10,... | collective-permute-start | bytes 737288 | tf_op jit(solution)/shard_map/ppermute | solution.py:33
  132.3 7.9 %collective-permute-start.23 = (bf16[160,768]{1,0:T(8,128)(2,1)S(1)}, bf16[160,768]{1,0:T(8,128)(2,1)S(1)}, u32[]{:S(2)}, u32[]{:S(2)}) collective-permute-start(bf16[160,768]{1,0:T(8,128)(2,1)S(1)} %pad_maximum_fusion.5), channel_id=1, source_target_pairs={{0,2},{1,3},{2,4},{3,5},{4,6},{5,7},{6,0},{7,1},{8,72},{9,73},{10,... | collective-permute-start | bytes 737288 | tf_op jit(solution)/shard_map/ppermute | solution.py:33
  146.9 34.2 %collective-permute-start.17 = (bf16[4,160,1024]{2,1,0:T(8,128)(2,1)}, bf16[4,160,1024]{2,1,0:T(8,128)(2,1)S(1)}, u32[]{:S(2)}, u32[]{:S(2)}) collective-permute-start(bf16[4,160,1024]{2,1,0:T(8,128)(2,1)} %copy-done.11), channel_id=1, source_target_pairs={{0,4},{1,5},{2,6},{3,7},{4,0},{5,1},{6,2},{7,3},{8,9},{9,8},{10,11... | collective-permute-start | bytes 3932168 | tf_op jit(solution)/shard_map/ppermute | solution.py:33
  150.1 48.6 %collective-permute-start.16 = (bf16[4,160,1024]{2,1,0:T(8,128)(2,1)S(1)}, bf16[4,160,1024]{2,1,0:T(8,128)(2,1)S(1)}, u32[]{:S(2)}, u32[]{:S(2)}) collective-permute-start(bf16[4,160,1024]{2,1,0:T(8,128)(2,1)S(1)} %get-tuple-element.73), channel_id=1, source_target_pairs={{0,6},{1,7},{2,0},{3,1},{4,2},{5,3},{6,4},{7,5},{8,73},{9,72},{10,... | collective-permute-start | bytes 3932168 | tf_op jit(solution)/shard_map/ppermute | solution.py:33
  200.9 7.6 %collective-permute-start.20 = (bf16[160,1024]{1,0:T(8,128)(2,1)S(1)}, bf16[160,1024]{1,0:T(8,128)(2,1)S(1)}, u32[]{:S(2)}, u32[]{:S(2)}) collective-permute-start(bf16[160,1024]{1,0:T(8,128)(2,1)S(1)} %get-tuple-element.86), channel_id=1, source_target_pairs={{0,32},{1,33},{2,34},{3,35},{4,36},{5,37},{6,38},{7,39},{8,40},{9,... | collective-permute-start | bytes 983048 | tf_op jit(solution)/shard_map/ppermute | solution.py:33
  201.0 11.3 %collective-permute-start.19 = (bf16[160,1024]{1,0:T(8,128)(2,1)S(1)}, bf16[160,1024]{1,0:T(8,128)(2,1)S(1)}, u32[]{:S(2)}, u32[]{:S(2)}) collective-permute-start(bf16[160,1024]{1,0:T(8,128)(2,1)S(1)} %get-tuple-element.87), channel_id=1, source_target_pairs={{0,48},{1,49},{2,50},{3,51},{4,52},{5,53},{6,54},{7,55},{8,56},{9,... | collective-permute-start | bytes 983048 | tf_op jit(solution)/shard_map/ppermute | solution.py:33
  203.8 8.5 %collective-permute-start.18 = (bf16[160,1024]{1,0:T(8,128)(2,1)S(1)}, bf16[160,1024]{1,0:T(8,128)(2,1)S(1)}, u32[]{:S(2)}, u32[]{:S(2)}) collective-permute-start(bf16[160,1024]{1,0:T(8,128)(2,1)S(1)} %get-tuple-element.85), channel_id=1, source_target_pairs={{0,16},{1,17},{2,18},{3,19},{4,20},{5,21},{6,22},{7,23},{8,24},{9,... | collective-permute-start | bytes 983048 | tf_op jit(solution)/shard_map/ppermute | solution.py:33
  215.8 10.6 %collective-permute-start.27 = (bf16[80,2048]{1,0:T(8,128)(2,1)S(1)}, bf16[80,2048]{1,0:T(8,128)(2,1)S(1)}, u32[]{:S(2)}, u32[]{:S(2)}) collective-permute-start(bf16[80,2048]{1,0:T(8,128)(2,1)S(1)} %get-tuple-element.121.refs_0_), channel_id=1, source_target_pairs={{0,48},{1,49},{2,50},{3,51},{4,52},{5,53},{6,54},{7,55},{8,24},{9,... | collective-permute-start | bytes 983048 | tf_op jit(solution)/shard_map/ppermute | solution.py:33
  215.9 16.3 %collective-permute-start.28 = (bf16[80,2048]{1,0:T(8,128)(2,1)S(1)}, bf16[80,2048]{1,0:T(8,128)(2,1)S(1)}, u32[]{:S(2)}, u32[]{:S(2)}) collective-permute-start(bf16[80,2048]{1,0:T(8,128)(2,1)S(1)} %get-tuple-element.121.refs_0_), channel_id=1, source_target_pairs={{0,32},{1,33},{2,34},{3,35},{4,36},{5,37},{6,38},{7,39},{8,56},{9,... | collective-permute-start | bytes 983048 | tf_op jit(solution)/shard_map/ppermute | solution.py:33
  218.6 18.1 %collective-permute-start.29 = (bf16[80,2048]{1,0:T(8,128)(2,1)S(1)}, bf16[80,2048]{1,0:T(8,128)(2,1)S(1)}, u32[]{:S(2)}, u32[]{:S(2)}) collective-permute-start(bf16[80,2048]{1,0:T(8,128)(2,1)S(1)} %get-tuple-element.121.refs_0_), channel_id=1, source_target_pairs={{0,64},{1,65},{2,66},{3,67},{4,68},{5,69},{6,70},{7,71},{8,40},{9,... | collective-permute-start | bytes 983048 | tf_op jit(solution)/shard_map/ppermute | solution.py:33
  219.2 19.1 %collective-permute-start.33 = (bf16[80,2048]{1,0:T(8,128)(2,1)S(1)}, bf16[80,2048]{1,0:T(8,128)(2,1)S(1)}, u32[]{:S(2)}, u32[]{:S(2)}) collective-permute-start(bf16[80,2048]{1,0:T(8,128)(2,1)S(1)} %get-tuple-element.121.refs_0_), channel_id=1, source_target_pairs={{0,8},{1,9},{2,10},{3,11},{4,12},{5,13},{6,14},{7,15},{8,0},{9,1},... | collective-permute-start | bytes 983048 | tf_op jit(solution)/shard_map/ppermute | solution.py:33
  222.3 16.1 %collective-permute-start.30 = (bf16[80,2048]{1,0:T(8,128)(2,1)S(1)}, bf16[80,2048]{1,0:T(8,128)(2,1)S(1)}, u32[]{:S(2)}, u32[]{:S(2)}) collective-permute-start(bf16[80,2048]{1,0:T(8,128)(2,1)S(1)} %collective-permute-done.22.refs_1_), channel_id=1, source_target_pairs={{0,64},{1,65},{2,66},{3,67},{4,68},{5,69},{6,70},{7,71},{8,24},{9,... | collective-permute-start | bytes 983048 | tf_op jit(solution)/shard_map/ppermute | solution.py:33
  233.1 11.4 %collective-permute-start.31 = (bf16[80,2048]{1,0:T(8,128)(2,1)}, bf16[80,2048]{1,0:T(8,128)(2,1)S(1)}, u32[]{:S(2)}, u32[]{:S(2)}) collective-permute-start(bf16[80,2048]{1,0:T(8,128)(2,1)} %get-tuple-element.119), channel_id=1, source_target_pairs={{0,64},{1,65},{2,66},{3,67},{4,68},{5,69},{6,70},{7,71},{8,56},{9,... | collective-permute-start | bytes 983048 | tf_op jit(solution)/shard_map/ppermute | solution.py:33
  236.7 7.9 %collective-permute-start.32 = (bf16[80,2048]{1,0:T(8,128)(2,1)}, bf16[80,2048]{1,0:T(8,128)(2,1)S(1)}, u32[]{:S(2)}, u32[]{:S(2)}) collective-permute-start(bf16[80,2048]{1,0:T(8,128)(2,1)} %get-tuple-element.118), channel_id=1, source_target_pairs={{0,64},{1,65},{2,66},{3,67},{4,68},{5,69},{6,70},{7,71},{8,40},{9,... | collective-permute-start | bytes 983048 | tf_op jit(solution)/shard_map/ppermute | solution.py:33
  236.7 10.4 %collective-permute-start.34 = (bf16[80,2048]{1,0:T(8,128)(2,1)S(1)}, bf16[80,2048]{1,0:T(8,128)(2,1)S(1)}, u32[]{:S(2)}, u32[]{:S(2)}) collective-permute-start(bf16[80,2048]{1,0:T(8,128)(2,1)S(1)} %collective-permute-done.22.refs_1_), channel_id=1, source_target_pairs={{0,8},{1,9},{2,10},{3,11},{4,12},{5,13},{6,14},{7,15},{8,0},{9,1},... | collective-permute-start | bytes 983048 | tf_op jit(solution)/shard_map/ppermute | solution.py:33
  238.3 8.8 %collective-permute-start.35 = (bf16[80,2048]{1,0:T(8,128)(2,1)S(1)}, bf16[80,2048]{1,0:T(8,128)(2,1)}, u32[]{:S(2)}, u32[]{:S(2)}) collective-permute-start(bf16[80,2048]{1,0:T(8,128)(2,1)S(1)} %collective-permute-done.27.refs_2_), channel_id=1, source_target_pairs={{0,8},{1,9},{2,10},{3,11},{4,12},{5,13},{6,14},{7,15},{8,0},{9,1},... | collective-permute-start | bytes 983048 | tf_op jit(solution)/shard_map/ppermute | solution.py:33
  238.4 9.3 %collective-permute-start.36 = (bf16[80,2048]{1,0:T(8,128)(2,1)S(1)}, bf16[80,2048]{1,0:T(8,128)(2,1)S(1)}, u32[]{:S(2)}, u32[]{:S(2)}) collective-permute-start(bf16[80,2048]{1,0:T(8,128)(2,1)S(1)} %collective-permute-done.28.refs_3_), channel_id=1, source_target_pairs={{0,8},{1,9},{2,10},{3,11},{4,12},{5,13},{6,14},{7,15},{8,0},{9,1},... | collective-permute-start | bytes 983048 | tf_op jit(solution)/shard_map/ppermute | solution.py:33
  (33 other events, 272.5 us)
Sparse Core Ops, SparseCore 0:
  147.0 41.0 all-gather.1

commit v6 on v5

--- a/solution.py
+++ b/solution.py
@@ -107,16 +107,12 @@
             turned = jnp.concatenate([ref[at, :] for ref in block_refs], axis=1)
             total[...] = jnp.dot(turned, held[...], preferred_element_type=jnp.float32).astype(jnp.bfloat16)
 
+            if not y_first:
+                for to_y in range(4):
+                    step_y = lax.rem(to_y - where_ref[2] + 4, 4)
+                    out_refs[0][g, step_y] = total[pl.ds(to_y * 2 * unit, 2 * unit), :]
+                return
             step_g = lax.rem(g - where_ref[1] + 4, 4)
-            if not y_first:
-                for distance, ref in enumerate(out_refs):
-
-                    @pl.when(step_g == distance)
-                    def _(ref=ref):
-                        for to_y in range(4):
-                            ref[lax.rem(to_y - where_ref[2] + 4, 4)] = total[pl.ds(to_y * 2 * unit, 2 * unit), :]
-
-                return
             plus_ref, minus_ref, first_ref, third_ref, keep_ref = out_refs
             for to_y in range(4):
                 step_y = lax.rem(to_y - where_ref[2] + 4, 4)
@@ -142,7 +138,7 @@
         two, one = (2, 4, unit, width), (4, unit, width)
         shapes = (two, two, one, one, two)
     else:
-        shapes = ((4, 2 * unit, width),) * 4
+        shapes = ((4, 4, 2 * unit, width),)
     return pl.pallas_call(
         kernel,
         in_specs=[SMEM] + [VMEM] * 8,
@@ -194,8 +190,13 @@
     return [pieces[0]] + [send(pieces[step], along(step)) for step in (1, 3, 2)]
 
 
-def summed(received, place=None):
-    return narrow(sum(wide(value if place is None else value[place]) for value in received))
+def summed(received):
+    return narrow(sum(wide(value) for value in received))
+
+
+def sum_groups():
+    groups = [[device(place, y, z, 0) for place in range(4)] for y in range(4) for z in range(4)]
+    return groups + [[device(x, y, place, 1) for place in range(4)] for x in range(4) for y in range(4)]
 
 
 def near_and_pair(first, second):
@@ -220,34 +221,27 @@
     seven = send(choose(three, one), near_and_pair(None, 2))
     own = [value, one, two, three, four, five, six, seven]
     swapped = [send(part, sibling) for part in own]
+    return own, swapped, state
+
+
+def gathered_places(y, z, c):
     y_steps = jnp.where(c == 0, jnp.array([0, 3, 1, 2, 0, 3, 1, 2]), jnp.array([0, 0, 3, 1, 2, 3, 1, 2]))
     z_steps = jnp.where(c == 0, jnp.array([0, 0, 0, 0, 1, 1, 1, 1]), jnp.array([0, 1, 0, 0, 0, 1, 1, 1]))
-    other_y = jnp.where(c == 1, jnp.array([0, 3, 1, 2, 0, 3, 1, 2]), jnp.array([0, 0, 3, 1, 2, 3, 1, 2]))
-    other_z = jnp.where(c == 1, jnp.array([0, 0, 0, 0, 1, 1, 1, 1]), jnp.array([0, 1, 0, 0, 0, 1, 1, 1]))
-    steps = jnp.concatenate([y_steps, other_y]), jnp.concatenate([z_steps, other_z])
-    return own + swapped, *steps, state
-
-
-def assemble(places, gathered, parts, columns):
-    rows, first = gathered.shape
-    unit, second = parts[0].shape
-    first, second, half = first // 2, second // 2, columns // 2
-
-    def kernel(places_ref, gathered_ref, *refs):
-        part_refs, out_ref, semaphores = refs[:-2], refs[-2], refs[-1]
-        copies = []
-        for side in range(2):
-            copies.append((gathered_ref.at[:, pl.ds(side * first, first)], out_ref.at[:, pl.ds(side * half, first)]))
-            for place, ref in enumerate(part_refs):
-                start = pl.multiple_of(places_ref[place] * unit, unit)
-                copies.append(
-                    (
-                        ref.at[:, pl.ds(side * second, second)],
-                        out_ref.at[pl.ds(start, unit), pl.ds(side * half + first, second)],
-                    )
-                )
+    return (((z + z_steps) % 2) * 8 + ((y + y_steps) % 4) * 2 + c).astype(jnp.int32)
+
+
+def place_columns(gathered, columns, start):
+    rows, width = gathered.shape
+    width, half = width // 2, columns // 2
+
+    def kernel(gathered_ref, out_ref, semaphores):
         copies = [
-            pltpu.make_async_copy(source, target, semaphores.at[place]) for place, (source, target) in enumerate(copies)
+            pltpu.make_async_copy(
+                gathered_ref.at[:, pl.ds(side * width, width)],
+                out_ref.at[:, pl.ds(side * half + start, width)],
+                semaphores.at[side],
+            )
+            for side in range(2)
         ]
         for copy in copies:
             copy.start()
@@ -256,13 +250,49 @@
 
     return pl.pallas_call(
         kernel,
-        in_specs=[SMEM] + [VMEM] * (1 + len(parts)),
+        in_specs=[VMEM],
         out_specs=pl.BlockSpec(memory_space=pltpu.HBM),
-        scratch_shapes=[pltpu.SemaphoreType.DMA((2 * (1 + len(parts)),))],
+        scratch_shapes=[pltpu.SemaphoreType.DMA((2,))],
         out_shape=jax.ShapeDtypeStruct((rows, columns), jnp.bfloat16),
         compiler_params=pltpu.CompilerParams(vmem_limit_bytes=4 * 1024 * 1024),
-        name="assemble_copy",
-    )(places, gathered, *parts)
+        name="place_columns",
+    )(gathered)
+
+
+def place_rows(copy, parts, places, start):
+    rows, columns = copy.shape
+    unit, width = parts[0].shape
+    width, half = width // 2, columns // 2
+
+    def kernel(places_ref, copy_ref, *refs):
+        part_refs, out_ref, semaphores = refs[:-2], refs[-2], refs[-1]
+        copies = []
+        for place, ref in enumerate(part_refs):
+            at = pl.ds(pl.multiple_of(places_ref[place] * unit, unit), unit)
+            for side in range(2):
+                copies.append(
+                    pltpu.make_async_copy(
+                        ref.at[:, pl.ds(side * width, width)],
+                        out_ref.at[at, pl.ds(side * half + start, width)],
+                        semaphores.at[2 * place + side],
+                    )
+                )
+        for copy in copies:
+            copy.start()
+        for copy in copies:
+            copy.wait()
+
+    hbm = pl.BlockSpec(memory_space=pltpu.HBM)
+    return pl.pallas_call(
+        kernel,
+        in_specs=[SMEM, hbm] + [VMEM] * len(parts),
+        out_specs=hbm,
+        scratch_shapes=[pltpu.SemaphoreType.DMA((2 * len(parts),))],
+        out_shape=jax.ShapeDtypeStruct((rows, columns), jnp.bfloat16),
+        input_output_aliases={1: 0},
+        compiler_params=pltpu.CompilerParams(vmem_limit_bytes=4 * 1024 * 1024),
+        name="place_rows",
+    )(places, copy, *parts)
 
 
 def adamw(grad, master, first_moment, second_moment):
@@ -306,12 +336,11 @@
     plus, minus, first, third, keep = partial_sums(where, blocks, inputs_0, True)
     sent_0 = ring_send(plus, minus, along_y)
     pieces_1 = partial_sums(where, blocks, inputs_1, False)
-    sent_0, pieces_1 = lax.optimization_barrier((sent_0, pieces_1))
-    sent_1 = direct(pieces_1, along_sums)
+    sent_0, pieces_1 = tie(sent_0, pieces_1)
+    (part_1,) = lax.psum_scatter(pieces_1[0], AXES, scatter_dimension=0, axis_index_groups=sum_groups(), tiled=True)
     turned_0 = ring_turn(first, third, *sent_0, along_y)
-    turned_0, sent_1[1] = tie(turned_0, sent_1[1])
     again_0 = direct([ring_end(keep, *sent_0, *turned_0, place) for place in range(4)], along_sums)
-    again_1 = direct([summed(sent_1, place) for place in range(4)], along_y)
+    again_1 = direct([part_1[place] for place in range(4)], along_y)
 
     scale = 1.0 / math.sqrt(total_tokens)
     grads, copies = [], []
@@ -338,10 +367,12 @@
 
     state = adamw(joined(grads), master, first_moment, second_moment)
     gathered = lax.all_gather(copies[0], "inter", axis=0, tiled=True)
-    parts, y_steps, z_steps, state = gather_rows(copies[1], c, state)
-    cores = jnp.array([0] * 8 + [1] * 8)
-    places = (((z + z_steps) % 2) * 8 + ((y + y_steps) % 4) * 2 + (c + cores) % 2).astype(jnp.int32)
-    return (*state, assemble(places, gathered, parts, columns))
+    own_places, other_places = tie(gathered_places(y, z, c), gathered_places(y, z, 1 - c))
+    own_parts, other_parts, state = gather_rows(copies[1], c, state)
+    new_copy = place_columns(gathered, columns, starts[0])
+    new_copy = place_rows(new_copy, own_parts, own_places, starts[1])
+    new_copy = place_rows(new_copy, other_parts, other_places, starts[1])
+    return (*state, new_copy)
 
 
 def solution(mesh):

time: 271 us -> 245 us (0.904)
  waiting for transfers between devices: 154 us -> 112 us
  starting transfers between devices: 47.8 us -> 60.7 us
  local copies, waits for them, and re-layouts: 14.3 us -> 11 us
  Pallas kernels: 28.8 us -> 31.6 us
    ppermute x41 -> x38, waiting for transfers between devices: 154 us -> 105 us  [send(): return lax.ppermute(value, AXES, permutation(move))]
    ppermute x41 -> x38, starting transfers between devices: 47.8 us -> 60.6 us  [send(): return lax.ppermute(value, AXES, permutation(move))]
    reduce_scatter x0 -> x1, waiting for transfers between devices: none -> 6.77 us  [body(): lax.psum_scatter(pieces_1[0], AXES, scatter_dimension=0, axis_index_group...]
    unnamed x46 -> x40, local copies, waits for them, and re-layouts: 11.4 us -> 8.2 us
    pallas_call x1 -> x3, Pallas kernels: 4.77 us -> 7.1 us  [the longest x2 5.17 us: place_rows(): pl.pallas_call(kernel, in_specs=[SMEM, hbm] + [VMEM] * len(parts), out_sp...]
  transfers between devices with their start and end apart: 42 -> 40, of which waited for: 23 -> 21; matrix products, arithmetic and copies ran while one was open for 4% -> 5% of each run, Pallas kernels for 9% -> 12%
where the time goes in v6:
time: 245 us; the launch traced here: 243 us
  waiting for transfers between devices  112 us (46%)
  starting transfers between devices  60.7 us (25%)
  Pallas kernels  31.6 us (13%)
  between operations  15.9 us (6%)
  other arithmetic  12.1 us (5%)
  local copies, waits for them, and re-layouts  11 us (4%)
    ppermute x38, waiting for transfers between devices, send(): return lax.ppermute(value, AXES, permutation(move))  105 us
    ppermute x38, starting transfers between devices, send(): return lax.ppermute(value, AXES, permutation(move))  60.6 us
    pallas_call x2, Pallas kernels, partial_sums(): pl.pallas_call(kernel, in_specs=[SMEM] + [VMEM] * 8, out_specs=[VMEM] * l...  18.9 us
    unnamed x40, local copies, waits for them, and re-layouts  8.2 us
    reduce_scatter x1, waiting for transfers between devices, body(): lax.psum_scatter(pieces_1[0], AXES, scatter_dimension=0, axis_index_group...  6.77 us
    pallas_call x1, Pallas kernels, pack(): pl.pallas_call(kernel, in_specs=[SMEM, VMEM, VMEM], out_specs=[VMEM] * 4,...  5.66 us
    pallas_call x2, Pallas kernels, place_rows(): pl.pallas_call(kernel, in_specs=[SMEM, hbm] + [VMEM] * len(parts), out_sp...  5.17 us
  transfers between devices with their start and end apart: 40, of which 21 were waited for; matrix products, arithmetic and copies ran while one was open for 5% of the time, Pallas kernels for 12%

profile of v6, /device:TPU:1, one launch (start us, length us, event | category | flops | bytes accessed | tf_op | source)
XLA Modules:
  0.0 242.8 jit_solution(7821406796883876337)
XLA Ops:
  17.8 2.3 collective-permute-done.1.other_ref
  20.0 5.7 %pack_cotangent.1 = (bf16[2560,384]{1,0:T(8,128)(2,1)S(1)}, bf16[2560,384]{1,0:T(8,128)(2,1)S(1)}, bf16[2560,384]{1,0:T(8,128)(2,1)S(1)}, bf16[2560,384]{1,0:T(8,128)(2,1)S(1)}) custom-call(s32[4]{0:T(128)S(1)} %pad_add_fusion.where_ref, bf16[192,10240]{1,0:T(8,128)(2,1)} %mine_ref.1, bf16[192,10240]{1,0:T(8,128)(2,1)} %collective-permute-done.1.other_ref), custom_call_target="tpu_custom_call" | custom-call | bytes 15728640 | tf_op jit(solution)/shard_map/pack_cotangent/pallas_call | solution.py:80
  25.7 3.9 %collective-permute-done.3.refs_6_ = bf16[384,768]{1,0:T(8,128)(2,1)S(1)} collective-permute-done((bf16[384,768]{1,0:T(8,128)(2,1)S(1)}, bf16[384,768]{1,0:T(8,128)(2,1)S(1)}, u32[]{:S(2)}, u32[]{:S(2)}) %collective-permute-start.3) | collective-permute-done | bytes 589856 | tf_op jit(solution)/shard_map/ppermute | solution.py:33
  35.2 21.7 %collective-permute-done.5.refs_1_ = bf16[2560,384]{1,0:T(8,128)(2,1)S(1)} collective-permute-done((bf16[2560,384]{1,0:T(8,128)(2,1)S(1)}, bf16[2560,384]{1,0:T(8,128)(2,1)S(1)}, u32[]{:S(2)}, u32[]{:S(2)}) %collective-permute-start.5) | collective-permute-done | bytes 1966112 | tf_op jit(solution)/shard_map/ppermute | solution.py:33
  56.8 20.3 %collective-permute-done.6.refs_2_ = bf16[2560,384]{1,0:T(8,128)(2,1)S(1)} collective-permute-done((bf16[2560,384]{1,0:T(8,128)(2,1)S(1)}, bf16[2560,384]{1,0:T(8,128)(2,1)S(1)}, u32[]{:S(2)}, u32[]{:S(2)}) %collective-permute-start.6) | collective-permute-done | bytes 1966112 | tf_op jit(solution)/shard_map/ppermute | solution.py:33
  84.0 9.2 %partial_sums.2 = (bf16[2,4,80,768]{3,2,1,0:T(8,128)(2,1)}, bf16[2,4,80,768]{3,2,1,0:T(8,128)(2,1)S(1)}, bf16[4,80,768]{2,1,0:T(8,128)(2,1)S(1)}, bf16[4,80,768]...) custom-call(s32[4]{0:T(128)S(1)} %pad_add_fusion.where_ref, bf16[2560,384]{1,0:T(8,128)(2,1)S(1)} %get-tuple-element.43.refs_0_, ...), custom_call_target="tpu_custom_call" | custom-call | flops 6039797760 | bytes 14155776 | tf_op jit(solution)/shard_map/partial_sums/pallas_call | solution.py:142
  96.0 2.5 %collective-permute-done.11.refs_6_ = bf16[384,1024]{1,0:T(8,128)(2,1)S(1)} collective-permute-done((bf16[384,1024]{1,0:T(8,128)(2,1)S(1)}, bf16[384,1024]{1,0:T(8,128)(2,1)S(1)}, u32[]{:S(2)}, u32[]{:S(2)}) %collective-permute-start.11) | collective-permute-done | bytes 786464 | tf_op jit(solution)/shard_map/ppermute | solution.py:33
  99.9 9.6 %partial_sums.3 = bf16[4,4,160,1024]{3,2,1,0:T(8,128)(2,1)S(1)} custom-call(s32[4]{0:T(128)S(1)} %pad_add_fusion.where_ref, bf16[2560,384]{1,0:T(8,128)(2,1)S(1)} %get-tuple-element.43.refs_0_, bf16[2560,384]{1,0:T(8,128)(2,1)S(1)} %collective-permute-done.5.refs_1_, bf16[2560,384]{1,0:T(8,128)(2,1)S(1)} %collective-permute-done.6.refs_2_, ...), custom_call_target="tpu_custom_call" | custom-call | flops 8053063680 | bytes 16252928 | tf_op jit(solution)/shard_map/partial_sums/pallas_call | solution.py:142
  109.5 2.3 copy-done
  111.9 2.3 collective-permute-done.8
  115.4 2.3 collective-permute-start.19
  118.9 4.7 %collective-permute-done.19 = bf16[4,80,768]{2,1,0:T(8,128)(2,1)S(1)} collective-permute-done((bf16[4,80,768]{2,1,0:T(8,128)(2,1)S(1)}, bf16[4,80,768]{2,1,0:T(8,128)(2,1)S(1)}, u32[]{:S(2)}, u32[]{:S(2)}) %collective-permute-start.19) | collective-permute-done | bytes 491552 | tf_op jit(solution)/shard_map/ppermute | solution.py:33
  124.9 2.9 %collective-permute-done.18 = bf16[4,80,768]{2,1,0:T(8,128)(2,1)S(1)} collective-permute-done((bf16[4,80,768]{2,1,0:T(8,128)(2,1)S(1)}, bf16[4,80,768]{2,1,0:T(8,128)(2,1)S(1)}, u32[]{:S(2)}, u32[]{:S(2)}) %collective-permute-start.18) | collective-permute-done | bytes 491552 | tf_op jit(solution)/shard_map/ppermute | solution.py:33
  129.2 4.3 %collective-permute-start.22 = (bf16[160,768]{1,0:T(8,128)(2,1)S(1)}, bf16[160,768]{1,0:T(8,128)(2,1)S(1)}, u32[]{:S(2)}, u32[]{:S(2)}) collective-permute-start(bf16[160,768]{1,0:T(8,128)(2,1)S(1)} %pad_maximum_fusion.7), channel_id=1, source_target_pairs={{0,4},{1,5},{2,6},{3,7},{4,0},{5,1},{6,2},{7,3},{8,9},{9,8},{10,11... | collective-permute-start | bytes 737288 | tf_op jit(solution)/shard_map/ppermute | solution.py:33
  133.5 2.1 collective-permute-start.21
  137.5 2.2 collective-permute-done.22
  139.7 8.3 %collective-permute-done.21 = bf16[160,768]{1,0:T(8,128)(2,1)S(1)} collective-permute-done((bf16[160,768]{1,0:T(8,128)(2,1)S(1)}, bf16[160,768]{1,0:T(8,128)(2,1)S(1)}, u32[]{:S(2)}, u32[]{:S(2)}) %collective-permute-start.21) | collective-permute-done | bytes 245792 | tf_op jit(solution)/shard_map/ppermute | solution.py:33
  148.1 3.0 %collective-permute-start.23 = (bf16[80,768]{1,0:T(8,128)(2,1)S(1)}, bf16[80,768]{1,0:T(8,128)(2,1)S(1)}, u32[]{:S(2)}, u32[]{:S(2)}) collective-permute-start(bf16[80,768]{1,0:T(8,128)(2,1)S(1)} %broadcast_select_fusion.10), channel_id=1, source_target_pairs={{0,8},{1,9},{2,10},{3,11},{4,12},{5,13},{6,14},{7,15},{8,0},{9,1},... | collective-permute-start | bytes 368648 | tf_op jit(solution)/shard_map/ppermute | solution.py:33
  153.3 6.8 %reduce-scatter.2.cloned.1.call-done = bf16[1,4,160,1024]{3,2,1,0:T(8,128)(2,1)} async-done(((bf16[4,4,160,1024]{3,2,1,0:T(8,128)(2,1)}), bf16[1,4,160,1024]{3,2,1,0:T(8,128)(2,1)}) %reduce-scatter.2.cloned.1.call-update) | async-done | bytes 1310736 | tf_op jit(solution)/shard_map/reduce_scatter | solution.py:340
  163.0 2.0 collective-permute-start.14
  165.1 13.7 %collective-permute-done.15 = bf16[160,1024]{1,0:T(8,128)(2,1)S(1)} collective-permute-done((bf16[160,1024]{1,0:T(8,128)(2,1)S(1)}, bf16[160,1024]{1,0:T(8,128)(2,1)S(1)}, u32[]{:S(2)}, u32[]{:S(2)}) %collective-permute-start.15) | collective-permute-done | bytes 327712 | tf_op jit(solution)/shard_map/ppermute | solution.py:33
  178.9 8.4 %collective-permute-done.14 = bf16[160,1024]{1,0:T(8,128)(2,1)S(1)} collective-permute-done((bf16[160,1024]{1,0:T(8,128)(2,1)S(1)}, bf16[160,1024]{1,0:T(8,128)(2,1)S(1)}, u32[]{:S(2)}, u32[]{:S(2)}) %collective-permute-start.14) | collective-permute-done | bytes 327712 | tf_op jit(solution)/shard_map/ppermute | solution.py:33
  193.4 3.9 %collective-permute-start.25 = (bf16[80,2048]{1,0:T(8,128)(2,1)S(1)}, bf16[80,2048]{1,0:T(8,128)(2,1)S(1)}, u32[]{:S(2)}, u32[]{:S(2)}) collective-permute-start(bf16[80,2048]{1,0:T(8,128)(2,1)S(1)} %get-tuple-element.105.refs_0_), channel_id=1, source_target_pairs={{0,32},{1,33},{2,34},{3,35},{4,36},{5,37},{6,38},{7,39},{8,56},{9,... | collective-permute-start | bytes 983048 | tf_op jit(solution)/shard_map/ppermute | solution.py:33
  197.3 3.4 %collective-permute-start.26 = (bf16[80,2048]{1,0:T(8,128)(2,1)S(1)}, bf16[80,2048]{1,0:T(8,128)(2,1)S(1)}, u32[]{:S(2)}, u32[]{:S(2)}) collective-permute-start(bf16[80,2048]{1,0:T(8,128)(2,1)S(1)} %get-tuple-element.105.refs_0_), channel_id=1, source_target_pairs={{0,64},{1,65},{2,66},{3,67},{4,68},{5,69},{6,70},{7,71},{8,40},{9,... | collective-permute-start | bytes 983048 | tf_op jit(solution)/shard_map/ppermute | solution.py:33
  202.2 2.3 multiply_subtract_fusion
  204.7 2.9 %collective-permute-done.25.refs_3_ = bf16[80,2048]{1,0:T(8,128)(2,1)S(1)} collective-permute-done((bf16[80,2048]{1,0:T(8,128)(2,1)S(1)}, bf16[80,2048]{1,0:T(8,128)(2,1)S(1)}, u32[]{:S(2)}, u32[]{:S(2)}) %collective-permute-start.25) | collective-permute-done | bytes 327712 | tf_op jit(solution)/shard_map/ppermute | solution.py:33
  208.0 7.0 %collective-permute-start.29 = (bf16[80,2048]{1,0:T(8,128)(2,1)S(1)}, bf16[80,2048]{1,0:T(8,128)(2,1)S(1)}, u32[]{:S(2)}, u32[]{:S(2)}) collective-permute-start(bf16[80,2048]{1,0:T(8,128)(2,1)S(1)} %get-tuple-element.102), channel_id=1, source_target_pairs={{0,64},{1,65},{2,66},{3,67},{4,68},{5,69},{6,70},{7,71},{8,40},{9,... | collective-permute-start | bytes 983048 | tf_op jit(solution)/shard_map/ppermute | solution.py:33
  217.5 3.7 %collective-permute-start.34 = (bf16[80,2048]{1,0:T(8,128)(2,1)S(1)}, bf16[80,2048]{1,0:T(8,128)(2,1)}, u32[]{:S(2)}, u32[]{:S(2)}) collective-permute-start(bf16[80,2048]{1,0:T(8,128)(2,1)S(1)} %collective-permute-done.26.refs_4_), channel_id=1, source_target_pairs={{0,8},{1,9},{2,10},{3,11},{4,12},{5,13},{6,14},{7,15},{8,0},{9,1},... | collective-permute-start | bytes 983048 | tf_op jit(solution)/shard_map/ppermute | solution.py:33
  221.2 3.5 %collective-permute-start.35 = (bf16[80,2048]{1,0:T(8,128)(2,1)S(1)}, bf16[80,2048]{1,0:T(8,128)(2,1)}, u32[]{:S(2)}, u32[]{:S(2)}) collective-permute-start(bf16[80,2048]{1,0:T(8,128)(2,1)S(1)} %collective-permute-done.27.refs_5_), channel_id=1, source_target_pairs={{0,8},{1,9},{2,10},{3,11},{4,12},{5,13},{6,14},{7,15},{8,0},{9,1},... | collective-permute-start | bytes 983048 | tf_op jit(solution)/shard_map/ppermute | solution.py:33
  226.0 2.1 copy-done.1
  230.1 2.2 place_rows.2.copy_ref
  232.3 3.0 %place_rows.3 = bf16[1280,3584]{1,0:T(8,128)(2,1)} custom-call(s32[8]{0:T(128)S(1)} %get-tuple-element.63.places_ref, bf16[1280,3584]{1,0:T(8,128)(2,1)} %place_rows.2.copy_ref, bf16[80,2048]{1,0:T(8,128)(2,1)S(1)} %collective-permute-done.30.refs_0_, bf16[80,2048]{1,0:T(8,128)(2,1)S(1)} %collective-permute-done.31.refs_1_, ...), custom_call_target="tpu_custom_call", output_to_operand_aliasing={{}: (1, {})} | custom-call | tf_op jit(solution)/shard_map/place_rows/pallas_call | solution.py:286
  (126 shorter events, 52.4 us)
Async XLA Ops:
  8.0 152.0 %reduce-scatter.2.cloned.1.call-start = ((), (), s32[]{:S(2)}) async-start(), calls=%async_computation.1 | async-start | bytes 6553600 | tf_op jit(solution)/shard_map/reduce_scatter | solution.py:340
  13.3 12.4 %collective-permute-start.2 = (bf16[384,768]{1,0:T(8,128)(2,1)S(1)}, bf16[384,768]{1,0:T(8,128)(2,1)S(1)}, u32[]{:S(2)}, u32[]{:S(2)}) collective-permute-start(bf16[384,768]{1,0:T(8,128)(2,1)S(1)} %slice.172.refs_4_), channel_id=1, source_target_pairs={{0,64},{1,65},{2,66},{3,67},{4,68},{5,69},{6,70},{7,71},{8,10},{9,... | collective-permute-start | bytes 1769480 | tf_op jit(solution)/shard_map/ppermute | solution.py:33
  14.7 14.9 %collective-permute-start.3 = (bf16[384,768]{1,0:T(8,128)(2,1)S(1)}, bf16[384,768]{1,0:T(8,128)(2,1)S(1)}, u32[]{:S(2)}, u32[]{:S(2)}) collective-permute-start(bf16[384,768]{1,0:T(8,128)(2,1)S(1)} %slice.172.refs_4_), channel_id=1, source_target_pairs={{0,65},{1,64},{2,67},{3,66},{4,69},{5,68},{6,71},{7,70},{8,14},{9,... | collective-permute-start | bytes 1769480 | tf_op jit(solution)/shard_map/ppermute | solution.py:33
  16.5 14.6 %collective-permute-start.4 = (bf16[384,768]{1,0:T(8,128)(2,1)S(1)}, bf16[384,768]{1,0:T(8,128)(2,1)S(1)}, u32[]{:S(2)}, u32[]{:S(2)}) collective-permute-start(bf16[384,768]{1,0:T(8,128)(2,1)S(1)} %slice.172.refs_4_), channel_id=1, source_target_pairs={{0,1},{1,0},{2,3},{3,2},{4,5},{5,4},{6,7},{7,6},{8,12},{9,13},{10,... | collective-permute-start | bytes 1769480 | tf_op jit(solution)/shard_map/ppermute | solution.py:33
  31.9 25.0 %collective-permute-start.5 = (bf16[2560,384]{1,0:T(8,128)(2,1)S(1)}, bf16[2560,384]{1,0:T(8,128)(2,1)S(1)}, u32[]{:S(2)}, u32[]{:S(2)}) collective-permute-start(bf16[2560,384]{1,0:T(8,128)(2,1)S(1)} %get-tuple-element.40), channel_id=1, source_target_pairs={{0,64},{1,65},{2,66},{3,67},{4,68},{5,69},{6,70},{7,71},{8,10},{9,... | collective-permute-start | bytes 5898248 | tf_op jit(solution)/shard_map/ppermute | solution.py:33
  32.7 44.5 %collective-permute-start.6 = (bf16[2560,384]{1,0:T(8,128)(2,1)S(1)}, bf16[2560,384]{1,0:T(8,128)(2,1)S(1)}, u32[]{:S(2)}, u32[]{:S(2)}) collective-permute-start(bf16[2560,384]{1,0:T(8,128)(2,1)S(1)} %get-tuple-element.41), channel_id=1, source_target_pairs={{0,65},{1,64},{2,67},{3,66},{4,69},{5,68},{6,71},{7,70},{8,14},{9,... | collective-permute-start | bytes 5898248 | tf_op jit(solution)/shard_map/ppermute | solution.py:33
  34.5 43.9 %collective-permute-start.7 = (bf16[2560,384]{1,0:T(8,128)(2,1)S(1)}, bf16[2560,384]{1,0:T(8,128)(2,1)S(1)}, u32[]{:S(2)}, u32[]{:S(2)}) collective-permute-start(bf16[2560,384]{1,0:T(8,128)(2,1)S(1)} %get-tuple-element.42), channel_id=1, source_target_pairs={{0,1},{1,0},{2,3},{3,2},{4,5},{5,4},{6,7},{7,6},{8,12},{9,13},{10,... | collective-permute-start | bytes 5898248 | tf_op jit(solution)/shard_map/ppermute | solution.py:33
  78.5 17.5 %collective-permute-start.10 = (bf16[384,1024]{1,0:T(8,128)(2,1)S(1)}, bf16[384,1024]{1,0:T(8,128)(2,1)S(1)}, u32[]{:S(2)}, u32[]{:S(2)}) collective-permute-start(bf16[384,1024]{1,0:T(8,128)(2,1)S(1)} %slice.173.refs_4_), channel_id=1, source_target_pairs={{0,64},{1,65},{2,66},{3,67},{4,68},{5,69},{6,70},{7,71},{8,10},{9,... | collective-permute-start | bytes 2359304 | tf_op jit(solution)/shard_map/ppermute | solution.py:33
  79.3 19.2 %collective-permute-start.11 = (bf16[384,1024]{1,0:T(8,128)(2,1)S(1)}, bf16[384,1024]{1,0:T(8,128)(2,1)S(1)}, u32[]{:S(2)}, u32[]{:S(2)}) collective-permute-start(bf16[384,1024]{1,0:T(8,128)(2,1)S(1)} %slice.173.refs_4_), channel_id=1, source_target_pairs={{0,65},{1,64},{2,67},{3,66},{4,69},{5,68},{6,71},{7,70},{8,14},{9,... | collective-permute-start | bytes 2359304 | tf_op jit(solution)/shard_map/ppermute | solution.py:33
  81.1 18.7 %collective-permute-start.12 = (bf16[384,1024]{1,0:T(8,128)(2,1)S(1)}, bf16[384,1024]{1,0:T(8,128)(2,1)S(1)}, u32[]{:S(2)}, u32[]{:S(2)}) collective-permute-start(bf16[384,1024]{1,0:T(8,128)(2,1)S(1)} %slice.173.refs_4_), channel_id=1, source_target_pairs={{0,1},{1,0},{2,3},{3,2},{4,5},{5,4},{6,7},{7,6},{8,12},{9,13},{10,... | collective-permute-start | bytes 2359304 | tf_op jit(solution)/shard_map/ppermute | solution.py:33
  93.2 21.0 %collective-permute-start.8 = (bf16[2,4,80,768]{3,2,1,0:T(8,128)(2,1)}, bf16[2,4,80,768]{3,2,1,0:T(8,128)(2,1)}, u32[]{:S(2)}, u32[]{:S(2)}) collective-permute-start(bf16[2,4,80,768]{3,2,1,0:T(8,128)(2,1)} %get-tuple-element.51), channel_id=1, source_target_pairs={{0,16},{1,17},{2,18},{3,19},{4,20},{5,21},{6,22},{7,23},{8,24},{9,... | collective-permute-start | bytes 2949128 | tf_op jit(solution)/shard_map/ppermute | solution.py:33
  94.5 19.7 %collective-permute-start.9 = (bf16[2,4,80,768]{3,2,1,0:T(8,128)(2,1)S(1)}, bf16[2,4,80,768]{3,2,1,0:T(8,128)(2,1)}, u32[]{:S(2)}, u32[]{:S(2)}) collective-permute-start(bf16[2,4,80,768]{3,2,1,0:T(8,128)(2,1)S(1)} %get-tuple-element.52), channel_id=1, source_target_pairs={{0,48},{1,49},{2,50},{3,51},{4,52},{5,53},{6,54},{7,55},{8,56},{9,... | collective-permute-start | bytes 2949128 | tf_op jit(solution)/shard_map/ppermute | solution.py:33
  114.2 111.8 %all-gather.2.cloned.1.call-start = ((), (), s32[]{:S(2)}) async-start(), calls=%async_computation.2 | async-start | bytes 4177920 | tf_op jit(solution)/shard_map/all_gather | solution.py:369
  118.8 9.0 %collective-permute-start.18 = (bf16[4,80,768]{2,1,0:T(8,128)(2,1)S(1)}, bf16[4,80,768]{2,1,0:T(8,128)(2,1)S(1)}, u32[]{:S(2)}, u32[]{:S(2)}) collective-permute-start(bf16[4,80,768]{2,1,0:T(8,128)(2,1)S(1)} %fusion.1), channel_id=1, source_target_pairs={{0,16},{1,17},{2,18},{3,19},{4,20},{5,21},{6,22},{7,23},{8,24},{9,... | collective-permute-start | bytes 1474568 | tf_op jit(solution)/shard_map/ppermute | solution.py:33
  129.2 10.5 %collective-permute-start.22 = (bf16[160,768]{1,0:T(8,128)(2,1)S(1)}, bf16[160,768]{1,0:T(8,128)(2,1)S(1)}, u32[]{:S(2)}, u32[]{:S(2)}) collective-permute-start(bf16[160,768]{1,0:T(8,128)(2,1)S(1)} %pad_maximum_fusion.7), channel_id=1, source_target_pairs={{0,4},{1,5},{2,6},{3,7},{4,0},{5,1},{6,2},{7,3},{8,9},{9,8},{10,11... | collective-permute-start | bytes 737288 | tf_op jit(solution)/shard_map/ppermute | solution.py:33
  133.5 14.5 %collective-permute-start.21 = (bf16[160,768]{1,0:T(8,128)(2,1)S(1)}, bf16[160,768]{1,0:T(8,128)(2,1)S(1)}, u32[]{:S(2)}, u32[]{:S(2)}) collective-permute-start(bf16[160,768]{1,0:T(8,128)(2,1)S(1)} %pad_maximum_fusion.6), channel_id=1, source_target_pairs={{0,6},{1,7},{2,0},{3,1},{4,2},{5,3},{6,4},{7,5},{8,73},{9,72},{10,... | collective-permute-start | bytes 737288 | tf_op jit(solution)/shard_map/ppermute | solution.py:33
  135.7 12.3 %collective-permute-start.20 = (bf16[160,768]{1,0:T(8,128)(2,1)S(1)}, bf16[160,768]{1,0:T(8,128)(2,1)S(1)}, u32[]{:S(2)}, u32[]{:S(2)}) collective-permute-start(bf16[160,768]{1,0:T(8,128)(2,1)S(1)} %pad_maximum_fusion.5), channel_id=1, source_target_pairs={{0,2},{1,3},{2,4},{3,5},{4,6},{5,7},{6,0},{7,1},{8,72},{9,73},{10,... | collective-permute-start | bytes 737288 | tf_op jit(solution)/shard_map/ppermute | solution.py:33
  161.3 17.6 %collective-permute-start.15 = (bf16[160,1024]{1,0:T(8,128)(2,1)S(1)}, bf16[160,1024]{1,0:T(8,128)(2,1)S(1)}, u32[]{:S(2)}, u32[]{:S(2)}) collective-permute-start(bf16[160,1024]{1,0:T(8,128)(2,1)S(1)} %get-tuple-element.80), channel_id=1, source_target_pairs={{0,32},{1,33},{2,34},{3,35},{4,36},{5,37},{6,38},{7,39},{8,40},{9,... | collective-permute-start | bytes 983048 | tf_op jit(solution)/shard_map/ppermute | solution.py:33
  163.0 24.3 %collective-permute-start.14 = (bf16[160,1024]{1,0:T(8,128)(2,1)S(1)}, bf16[160,1024]{1,0:T(8,128)(2,1)S(1)}, u32[]{:S(2)}, u32[]{:S(2)}) collective-permute-start(bf16[160,1024]{1,0:T(8,128)(2,1)S(1)} %get-tuple-element.81), channel_id=1, source_target_pairs={{0,48},{1,49},{2,50},{3,51},{4,52},{5,53},{6,54},{7,55},{8,56},{9,... | collective-permute-start | bytes 983048 | tf_op jit(solution)/shard_map/ppermute | solution.py:33
  165.0 22.3 %collective-permute-start.13 = (bf16[160,1024]{1,0:T(8,128)(2,1)S(1)}, bf16[160,1024]{1,0:T(8,128)(2,1)S(1)}, u32[]{:S(2)}, u32[]{:S(2)}) collective-permute-start(bf16[160,1024]{1,0:T(8,128)(2,1)S(1)} %get-tuple-element.79), channel_id=1, source_target_pairs={{0,16},{1,17},{2,18},{3,19},{4,20},{5,21},{6,22},{7,23},{8,24},{9,... | collective-permute-start | bytes 983048 | tf_op jit(solution)/shard_map/ppermute | solution.py:33
  191.5 13.0 %collective-permute-start.17 = (bf16[80,2048]{1,0:T(8,128)(2,1)S(1)}, bf16[80,2048]{1,0:T(8,128)(2,1)S(1)}, u32[]{:S(2)}, u32[]{:S(2)}) collective-permute-start(bf16[80,2048]{1,0:T(8,128)(2,1)S(1)} %get-tuple-element.105.refs_0_), channel_id=1, source_target_pairs={{0,16},{1,17},{2,18},{3,19},{4,20},{5,21},{6,22},{7,23},{8,72},{9,... | collective-permute-start | bytes 983048 | tf_op jit(solution)/shard_map/ppermute | solution.py:33
  191.6 13.1 %collective-permute-start.24 = (bf16[80,2048]{1,0:T(8,128)(2,1)S(1)}, bf16[80,2048]{1,0:T(8,128)(2,1)S(1)}, u32[]{:S(2)}, u32[]{:S(2)}) collective-permute-start(bf16[80,2048]{1,0:T(8,128)(2,1)S(1)} %get-tuple-element.105.refs_0_), channel_id=1, source_target_pairs={{0,48},{1,49},{2,50},{3,51},{4,52},{5,53},{6,54},{7,55},{8,24},{9,... | collective-permute-start | bytes 983048 | tf_op jit(solution)/shard_map/ppermute | solution.py:33
  193.4 14.1 %collective-permute-start.25 = (bf16[80,2048]{1,0:T(8,128)(2,1)S(1)}, bf16[80,2048]{1,0:T(8,128)(2,1)S(1)}, u32[]{:S(2)}, u32[]{:S(2)}) collective-permute-start(bf16[80,2048]{1,0:T(8,128)(2,1)S(1)} %get-tuple-element.105.refs_0_), channel_id=1, source_target_pairs={{0,32},{1,33},{2,34},{3,35},{4,36},{5,37},{6,38},{7,39},{8,56},{9,... | collective-permute-start | bytes 983048 | tf_op jit(solution)/shard_map/ppermute | solution.py:33
  197.3 17.8 %collective-permute-start.26 = (bf16[80,2048]{1,0:T(8,128)(2,1)S(1)}, bf16[80,2048]{1,0:T(8,128)(2,1)S(1)}, u32[]{:S(2)}, u32[]{:S(2)}) collective-permute-start(bf16[80,2048]{1,0:T(8,128)(2,1)S(1)} %get-tuple-element.105.refs_0_), channel_id=1, source_target_pairs={{0,64},{1,65},{2,66},{3,67},{4,68},{5,69},{6,70},{7,71},{8,40},{9,... | collective-permute-start | bytes 983048 | tf_op jit(solution)/shard_map/ppermute | solution.py:33
  200.7 15.6 %collective-permute-start.30 = (bf16[80,2048]{1,0:T(8,128)(2,1)S(1)}, bf16[80,2048]{1,0:T(8,128)(2,1)S(1)}, u32[]{:S(2)}, u32[]{:S(2)}) collective-permute-start(bf16[80,2048]{1,0:T(8,128)(2,1)S(1)} %get-tuple-element.105.refs_0_), channel_id=1, source_target_pairs={{0,8},{1,9},{2,10},{3,11},{4,12},{5,13},{6,14},{7,15},{8,0},{9,1},... | collective-permute-start | bytes 983048 | tf_op jit(solution)/shard_map/ppermute | solution.py:33
  204.6 11.8 %collective-permute-start.27 = (bf16[80,2048]{1,0:T(8,128)(2,1)S(1)}, bf16[80,2048]{1,0:T(8,128)(2,1)S(1)}, u32[]{:S(2)}, u32[]{:S(2)}) collective-permute-start(bf16[80,2048]{1,0:T(8,128)(2,1)S(1)} %collective-permute-done.17.refs_1_), channel_id=1, source_target_pairs={{0,64},{1,65},{2,66},{3,67},{4,68},{5,69},{6,70},{7,71},{8,24},{9,... | collective-permute-start | bytes 983048 | tf_op jit(solution)/shard_map/ppermute | solution.py:33
  207.6 9.9 %collective-permute-start.28 = (bf16[80,2048]{1,0:T(8,128)(2,1)S(1)}, bf16[80,2048]{1,0:T(8,128)(2,1)S(1)}, u32[]{:S(2)}, u32[]{:S(2)}) collective-permute-start(bf16[80,2048]{1,0:T(8,128)(2,1)S(1)} %get-tuple-element.103), channel_id=1, source_target_pairs={{0,64},{1,65},{2,66},{3,67},{4,68},{5,69},{6,70},{7,71},{8,56},{9,... | collective-permute-start | bytes 983048 | tf_op jit(solution)/shard_map/ppermute | solution.py:33
  208.0 13.2 %collective-permute-start.29 = (bf16[80,2048]{1,0:T(8,128)(2,1)S(1)}, bf16[80,2048]{1,0:T(8,128)(2,1)S(1)}, u32[]{:S(2)}, u32[]{:S(2)}) collective-permute-start(bf16[80,2048]{1,0:T(8,128)(2,1)S(1)} %get-tuple-element.102), channel_id=1, source_target_pairs={{0,64},{1,65},{2,66},{3,67},{4,68},{5,69},{6,70},{7,71},{8,40},{9,... | collective-permute-start | bytes 983048 | tf_op jit(solution)/shard_map/ppermute | solution.py:33
  215.0 9.7 %collective-permute-start.31 = (bf16[80,2048]{1,0:T(8,128)(2,1)S(1)}, bf16[80,2048]{1,0:T(8,128)(2,1)S(1)}, u32[]{:S(2)}, u32[]{:S(2)}) collective-permute-start(bf16[80,2048]{1,0:T(8,128)(2,1)S(1)} %collective-permute-done.17.refs_1_), channel_id=1, source_target_pairs={{0,8},{1,9},{2,10},{3,11},{4,12},{5,13},{6,14},{7,15},{8,0},{9,1},... | collective-permute-start | bytes 983048 | tf_op jit(solution)/shard_map/ppermute | solution.py:33
  216.3 15.9 %collective-permute-start.33 = (bf16[80,2048]{1,0:T(8,128)(2,1)S(1)}, bf16[80,2048]{1,0:T(8,128)(2,1)}, u32[]{:S(2)}, u32[]{:S(2)}) collective-permute-start(bf16[80,2048]{1,0:T(8,128)(2,1)S(1)} %collective-permute-done.25.refs_3_), channel_id=1, source_target_pairs={{0,8},{1,9},{2,10},{3,11},{4,12},{5,13},{6,14},{7,15},{8,0},{9,1},... | collective-permute-start | bytes 983048 | tf_op jit(solution)/shard_map/ppermute | solution.py:33
  217.5 14.8 %collective-permute-start.34 = (bf16[80,2048]{1,0:T(8,128)(2,1)S(1)}, bf16[80,2048]{1,0:T(8,128)(2,1)}, u32[]{:S(2)}, u32[]{:S(2)}) collective-permute-start(bf16[80,2048]{1,0:T(8,128)(2,1)S(1)} %collective-permute-done.26.refs_4_), channel_id=1, source_target_pairs={{0,8},{1,9},{2,10},{3,11},{4,12},{5,13},{6,14},{7,15},{8,0},{9,1},... | collective-permute-start | bytes 983048 | tf_op jit(solution)/shard_map/ppermute | solution.py:33
  221.2 11.1 %collective-permute-start.35 = (bf16[80,2048]{1,0:T(8,128)(2,1)S(1)}, bf16[80,2048]{1,0:T(8,128)(2,1)}, u32[]{:S(2)}, u32[]{:S(2)}) collective-permute-start(bf16[80,2048]{1,0:T(8,128)(2,1)S(1)} %collective-permute-done.27.refs_5_), channel_id=1, source_target_pairs={{0,8},{1,9},{2,10},{3,11},{4,12},{5,13},{6,14},{7,15},{8,0},{9,1},... | collective-permute-start | bytes 983048 | tf_op jit(solution)/shard_map/ppermute | solution.py:33
  (28 other events, 355.4 us)
Sparse Core Ops, SparseCore 0:
  114.4 45.6 reduce-scatter.1
Sparse Core Ops, SparseCore 1:
  153.4 50.1 all-gather.1

commit v7 on v6

--- a/solution.py
+++ b/solution.py
@@ -9,7 +9,7 @@
 from jax.sharding import PartitionSpec as P
 
 AXES = ("inter", "intra")
-WIDTHS = (768, 1024)
+WIDTHS = (1024, 768)
 
 
 def device(x, y, z, c):
@@ -56,6 +56,18 @@
         return x, y + step, z, c
 
     return move
+
+
+def along_rest(step):
+    def move(x, y, z, c):
+        return (x, y + step, z, c) if c == 0 else (x, y, z + step, c)
+
+    return move
+
+
+def first_groups():
+    groups = [[device(place, y, z, 0) for place in range(4)] for y in range(4) for z in range(4)]
+    return groups + [[device(x, place, z, 1) for place in range(4)] for x in range(4) for z in range(4)]
 
 
 VMEM = pl.BlockSpec(memory_space=pltpu.VMEM)
@@ -88,7 +100,7 @@
     )(where, mine, other)
 
 
-def partial_sums(where, blocks, inputs, y_first):
+def partial_sums(where, blocks, inputs, ring):
     rows, tokens = blocks[0].shape
     width = inputs[0].shape[1]
     piece = rows // 4
@@ -96,45 +108,63 @@
 
     def kernel(where_ref, *refs):
         block_refs, input_refs = refs[:4], refs[4:8]
-        out_refs = refs[8:-2]
-        held, total = refs[-2:]
+        out_refs, mark_ref = refs[8:-4], refs[-4]
+        mark_ref[...] = jnp.zeros_like(mark_ref)
+        held, total, semaphores = refs[-3:]
         for step in range(4):
             held[pl.ds(step * tokens, tokens), :] = input_refs[step][...]
 
-        @pl.loop(0, 4)
-        def _(g):
-            at = pl.ds(pl.multiple_of(g * piece, piece), piece)
-            turned = jnp.concatenate([ref[at, :] for ref in block_refs], axis=1)
-            total[...] = jnp.dot(turned, held[...], preferred_element_type=jnp.float32).astype(jnp.bfloat16)
-
-            if not y_first:
-                for to_y in range(4):
-                    step_y = lax.rem(to_y - where_ref[2] + 4, 4)
-                    out_refs[0][g, step_y] = total[pl.ds(to_y * 2 * unit, 2 * unit), :]
-                return
+        def copies(g, slot):
+            step_g = lax.rem(g - where_ref[1] + 4, 4)
+            for to_y in range(4):
+                step_y = lax.rem(to_y - where_ref[2] + 4, 4)
+                first = jnp.where(where_ref[3] == 0, g, to_y)
+                second = jnp.where(where_ref[3] == 0, step_y, step_g)
+                yield pltpu.make_async_copy(
+                    total.at[slot, pl.ds(to_y * 2 * unit, 2 * unit), :],
+                    out_refs[0].at[first, second],
+                    semaphores.at[slot, to_y],
+                )
+
+        for g in range(4):
+            slot = g % 2
+            if not ring and g >= 2:
+                for copy in copies(g - 2, slot):
+                    copy.wait()
+            turned = jnp.concatenate([ref[pl.ds(g * piece, piece), :] for ref in block_refs], axis=1)
+            total[slot] = jnp.dot(turned, held[...], preferred_element_type=jnp.float32).astype(jnp.bfloat16)
+            if not ring:
+                for copy in copies(g, slot):
+                    copy.start()
+                continue
+
             step_g = lax.rem(g - where_ref[1] + 4, 4)
             plus_ref, minus_ref, first_ref, third_ref, keep_ref = out_refs
-            for to_y in range(4):
-                step_y = lax.rem(to_y - where_ref[2] + 4, 4)
-                for half in range(2):
-                    start = (to_y * 2 + half) * unit
-                    places = {
-                        0: (keep_ref, half),
-                        1: (first_ref, None) if half == 0 else (plus_ref, 1),
-                        2: (plus_ref, 0) if half == 0 else (minus_ref, 0),
-                        3: (minus_ref, 1) if half == 0 else (third_ref, None),
-                    }
-                    for distance, (ref, slot) in places.items():
-
-                        @pl.when(step_y == distance)
-                        def _(ref=ref, slot=slot, start=start):
-                            value = total[pl.ds(start, unit), :]
-                            if slot is None:
-                                ref[step_g] = value
+            places = [
+                [(keep_ref, 0), (keep_ref, 1)],
+                [(first_ref, None), (plus_ref, 1)],
+                [(plus_ref, 0), (minus_ref, 0)],
+                [(minus_ref, 1), (third_ref, None)],
+            ]
+            for distance, halves in enumerate(places):
+
+                @pl.when(step_g == distance)
+                def _(halves=halves, slot=slot):
+                    for to_y in range(4):
+                        step_y = lax.rem(to_y - where_ref[2] + 4, 4)
+                        for half, (ref, at) in enumerate(halves):
+                            value = total[slot, pl.ds((to_y * 2 + half) * unit, unit), :]
+                            if at is None:
+                                ref[step_y] = value
                             else:
-                                ref[slot, step_g] = value
-
-    if y_first:
+                                ref[at, step_y] = value
+
+        if not ring:
+            for g in (2, 3):
+                for copy in copies(g, g % 2):
+                    copy.wait()
+
+    if ring:
         two, one = (2, 4, unit, width), (4, unit, width)
         shapes = (two, two, one, one, two)
     else:
@@ -142,12 +172,14 @@
     return pl.pallas_call(
         kernel,
         in_specs=[SMEM] + [VMEM] * 8,
-        out_specs=[VMEM] * len(shapes),
+        out_specs=[VMEM if ring else pl.BlockSpec(memory_space=pltpu.HBM)] * len(shapes) + [VMEM],
         scratch_shapes=[
             pltpu.VMEM((4 * tokens, width), jnp.bfloat16),
-            pltpu.VMEM((piece, width), jnp.bfloat16),
+            pltpu.VMEM((2, piece, width), jnp.bfloat16),
+            pltpu.SemaphoreType.DMA((2, 4)),
         ],
-        out_shape=[jax.ShapeDtypeStruct(shape, jnp.bfloat16) for shape in shapes],
+        out_shape=[jax.ShapeDtypeStruct(shape, jnp.bfloat16) for shape in shapes]
+        + [jax.ShapeDtypeStruct((8, 128), jnp.float32)],
         compiler_params=pltpu.CompilerParams(vmem_limit_bytes=24 * 1024 * 1024),
         cost_estimate=pl.CostEstimate(
             flops=2 * 4 * tokens * rows * width,
@@ -192,11 +224,6 @@
 
 def summed(received):
     return narrow(sum(wide(value) for value in received))
-
-
-def sum_groups():
-    groups = [[device(place, y, z, 0) for place in range(4)] for y in range(4) for z in range(4)]
-    return groups + [[device(x, y, place, 1) for place in range(4)] for x in range(4) for y in range(4)]
 
 
 def near_and_pair(first, second):
@@ -230,11 +257,11 @@
     return (((z + z_steps) % 2) * 8 + ((y + y_steps) % 4) * 2 + c).astype(jnp.int32)
 
 
-def place_columns(gathered, columns, start):
+def place_columns(gathered, mark, columns, start):
     rows, width = gathered.shape
     width, half = width // 2, columns // 2
 
-    def kernel(gathered_ref, out_ref, semaphores):
+    def kernel(gathered_ref, mark_ref, out_ref, semaphores):
         copies = [
             pltpu.make_async_copy(
                 gathered_ref.at[:, pl.ds(side * width, width)],
@@ -250,13 +277,13 @@
 
     return pl.pallas_call(
         kernel,
-        in_specs=[VMEM],
+        in_specs=[VMEM, pl.BlockSpec(memory_space=pl.ANY)],
         out_specs=pl.BlockSpec(memory_space=pltpu.HBM),
         scratch_shapes=[pltpu.SemaphoreType.DMA((2,))],
         out_shape=jax.ShapeDtypeStruct((rows, columns), jnp.bfloat16),
         compiler_params=pltpu.CompilerParams(vmem_limit_bytes=4 * 1024 * 1024),
         name="place_columns",
-    )(gathered)
+    )(gathered, mark)
 
 
 def place_rows(copy, parts, places, start):
@@ -333,14 +360,15 @@
     blocks, waiting = tie(blocks, inputs[1])
     inputs_1 = [inputs[1], *spread(waiting)]
 
-    plus, minus, first, third, keep = partial_sums(where, blocks, inputs_0, True)
-    sent_0 = ring_send(plus, minus, along_y)
-    pieces_1 = partial_sums(where, blocks, inputs_1, False)
-    sent_0, pieces_1 = tie(sent_0, pieces_1)
-    (part_1,) = lax.psum_scatter(pieces_1[0], AXES, scatter_dimension=0, axis_index_groups=sum_groups(), tiled=True)
-    turned_0 = ring_turn(first, third, *sent_0, along_y)
-    again_0 = direct([ring_end(keep, *sent_0, *turned_0, place) for place in range(4)], along_sums)
-    again_1 = direct([part_1[place] for place in range(4)], along_y)
+    plus, minus, first, third, keep, _ = partial_sums(where, blocks, inputs_0, True)
+    plus, minus, inputs_1[1:] = tie(plus, minus, inputs_1[1:])
+    sent_0 = ring_send(plus, minus, along_sums)
+    pieces_1, mark = partial_sums(where, blocks, inputs_1, False)
+    sent_0, mark = tie(sent_0, mark)
+    (part_1,) = lax.psum_scatter(pieces_1, AXES, scatter_dimension=0, axis_index_groups=first_groups(), tiled=True)
+    turned_0 = ring_turn(first, third, *sent_0, along_sums)
+    again_0 = direct([ring_end(keep, *sent_0, *turned_0, place) for place in range(4)], along_y)
+    again_1 = direct([part_1[place] for place in range(4)], along_rest)
 
     scale = 1.0 / math.sqrt(total_tokens)
     grads, copies = [], []
@@ -369,7 +397,7 @@
     gathered = lax.all_gather(copies[0], "inter", axis=0, tiled=True)
     own_places, other_places = tie(gathered_places(y, z, c), gathered_places(y, z, 1 - c))
     own_parts, other_parts, state = gather_rows(copies[1], c, state)
-    new_copy = place_columns(gathered, columns, starts[0])
+    new_copy = place_columns(gathered, mark, columns, starts[0])
     new_copy = place_rows(new_copy, own_parts, own_places, starts[1])
     new_copy = place_rows(new_copy, other_parts, other_places, starts[1])
     return (*state, new_copy)

time: 245 us -> 252 us (1.029)
  Pallas kernels: 31.6 us -> 37.7 us
  waiting for transfers between devices: 112 us -> 116 us
  other arithmetic: 12.1 us -> 8.29 us
  local copies, waits for them, and re-layouts: 11 us -> 14.5 us
    ppermute x38, waiting for transfers between devices: 105 us -> 116 us  [send(): return lax.ppermute(value, AXES, permutation(move))]
    pallas_call x3, Pallas kernels: 20.8 us -> 27.6 us  [the longest x2 25.2 us: partial_sums(): pl.pallas_call(kernel, in_specs=[SMEM] + [VMEM] * 8, out_specs=[VMEM if r...]
    reduce_scatter x1, waiting for transfers between devices: 6.77 us -> 0.02 us  [body(): lax.psum_scatter(pieces_1, AXES, scatter_dimension=0, axis_index_groups=f...]
  transfers between devices with their start and end apart: 40 -> 40, of which waited for: 21 -> 25; matrix products, arithmetic and copies ran while one was open for 5% -> 4% of each run, Pallas kernels for 12% -> 8%
where the time goes in v7:
time: 252 us
  waiting for transfers between devices  116 us (46%)
  starting transfers between devices  59.6 us (24%)
  Pallas kernels  37.7 us (15%)
  between operations  15.9 us (6%)
  local copies, waits for them, and re-layouts  14.5 us (6%)
  other arithmetic  8.29 us (3%)
    ppermute x38, waiting for transfers between devices, send(): return lax.ppermute(value, AXES, permutation(move))  116 us
    ppermute x38, starting transfers between devices, send(): return lax.ppermute(value, AXES, permutation(move))  59.5 us
    pallas_call x2, Pallas kernels, partial_sums(): pl.pallas_call(kernel, in_specs=[SMEM] + [VMEM] * 8, out_specs=[VMEM if r...  25.2 us
    unnamed x40, local copies, waits for them, and re-layouts  10.6 us
    pallas_call x1, Pallas kernels, pack(): pl.pallas_call(kernel, in_specs=[SMEM, VMEM, VMEM], out_specs=[VMEM] * 4,...  5.66 us
  transfers between devices with their start and end apart: 40, of which 25 were waited for; matrix products, arithmetic and copies ran while one was open for 4% of the time, Pallas kernels for 8%

profile of v7, /device:TPU:1, one launch (start us, length us, event | category | flops | bytes accessed | tf_op | source)
XLA Modules:
  0.0 251.8 jit_solution(11105049757233084457)
XLA Ops:
  17.8 2.2 collective-permute-done.1.other_ref
  20.0 5.7 %pack_cotangent.1 = (bf16[2560,384]{1,0:T(8,128)(2,1)S(1)}, bf16[2560,384]{1,0:T(8,128)(2,1)S(1)}, bf16[2560,384]{1,0:T(8,128)(2,1)S(1)}, bf16[2560,384]{1,0:T(8,128)(2,1)S(1)}) custom-call(s32[4]{0:T(128)S(1)} %pad_add_fusion.where_ref, bf16[192,10240]{1,0:T(8,128)(2,1)} %mine_ref.1, bf16[192,10240]{1,0:T(8,128)(2,1)} %collective-permute-done.1.other_ref), custom_call_target="tpu_custom_call" | custom-call | bytes 15728640 | tf_op jit(solution)/shard_map/pack_cotangent/pallas_call | solution.py:92
  25.8 8.0 %collective-permute-done.3.refs_6_ = bf16[384,1024]{1,0:T(8,128)(2,1)S(1)} collective-permute-done((bf16[384,1024]{1,0:T(8,128)(2,1)S(1)}, bf16[384,1024]{1,0:T(8,128)(2,1)S(1)}, u32[]{:S(2)}, u32[]{:S(2)}) %collective-permute-start.3) | collective-permute-done | bytes 786464 | tf_op jit(solution)/shard_map/ppermute | solution.py:33
  37.0 2.0 collective-permute-start.6
  41.3 20.0 %collective-permute-done.5.refs_1_ = bf16[2560,384]{1,0:T(8,128)(2,1)S(1)} collective-permute-done((bf16[2560,384]{1,0:T(8,128)(2,1)S(1)}, bf16[2560,384]{1,0:T(8,128)(2,1)S(1)}, u32[]{:S(2)}, u32[]{:S(2)}) %collective-permute-start.5) | collective-permute-done | bytes 1966112 | tf_op jit(solution)/shard_map/ppermute | solution.py:33
  61.3 20.3 %collective-permute-done.6.refs_2_ = bf16[2560,384]{1,0:T(8,128)(2,1)S(1)} collective-permute-done((bf16[2560,384]{1,0:T(8,128)(2,1)S(1)}, bf16[2560,384]{1,0:T(8,128)(2,1)S(1)}, u32[]{:S(2)}, u32[]{:S(2)}) %collective-permute-start.6) | collective-permute-done | bytes 1966112 | tf_op jit(solution)/shard_map/ppermute | solution.py:33
  88.5 10.7 %partial_sums.2 = (bf16[2,4,80,1024]{3,2,1,0:T(8,128)(2,1)S(1)}, bf16[2,4,80,1024]{3,2,1,0:T(8,128)(2,1)S(1)}, bf16[4,80,1024]{2,1,0:T(8,128)(2,1)S(1)}, bf16[4,...) custom-call(s32[4]{0:T(128)S(1)} %pad_add_fusion.where_ref, ...), custom_call_target="tpu_custom_call" | custom-call | flops 8053063680 | bytes 16252928 | tf_op jit(solution)/shard_map/partial_sums/pallas_call | solution.py:172
  101.4 14.6 %partial_sums.3 = (bf16[4,4,160,768]{3,2,1,0:T(8,128)(2,1)S(1)}, f32[8,128]{1,0:T(8,128)S(1)}) custom-call(s32[4]{0:T(128)S(1)} %pad_add_fusion.where_ref, bf16[2560,384]{1,0:T(8,128)(2,1)S(1)} %get-tuple-element.50.refs_0_, bf16[2560,384]{1,0:T(8,128)(2,1)S(1)} %collective-permute-done.5.refs_1_, bf16[2560,384]{1,0:T(8,128)(2,1)S(1)} %collective-permute-done.6.refs_2_, ...), custom_call_target="tpu_custom_call" | custom-call | flops 6039797760 | bytes 14155776 | tf_op jit(solution)/shard_map/partial_sums/pallas_call | solution.py:172
  119.5 2.4 collective-permute-start.17
  121.9 15.5 %collective-permute-done.16 = bf16[2,4,80,1024]{3,2,1,0:T(8,128)(2,1)S(1)} collective-permute-done((bf16[2,4,80,1024]{3,2,1,0:T(8,128)(2,1)}, bf16[2,4,80,1024]{3,2,1,0:T(8,128)(2,1)S(1)}, u32[]{:S(2)}, u32[]{:S(2)}) %collective-permute-start.16) | collective-permute-done | bytes 1310752 | tf_op jit(solution)/shard_map/ppermute | solution.py:33
  137.6 2.8 %collective-permute-start.19 = (bf16[4,80,1024]{2,1,0:T(8,128)(2,1)S(1)}, bf16[4,80,1024]{2,1,0:T(8,128)(2,1)S(1)}, u32[]{:S(2)}, u32[]{:S(2)}) collective-permute-start(bf16[4,80,1024]{2,1,0:T(8,128)(2,1)S(1)} %fusion), channel_id=1, source_target_pairs={{0,6},{1,7},{2,0},{3,1},{4,2},{5,3},{6,4},{7,5},{8,73},{9,72},{10,... | collective-permute-start | bytes 1966088 | tf_op jit(solution)/shard_map/ppermute | solution.py:33
  140.8 7.2 %collective-permute-done.19 = bf16[4,80,1024]{2,1,0:T(8,128)(2,1)S(1)} collective-permute-done((bf16[4,80,1024]{2,1,0:T(8,128)(2,1)S(1)}, bf16[4,80,1024]{2,1,0:T(8,128)(2,1)S(1)}, u32[]{:S(2)}, u32[]{:S(2)}) %collective-permute-start.19) | collective-permute-done | bytes 655392 | tf_op jit(solution)/shard_map/ppermute | solution.py:33
  148.3 3.5 %collective-permute-done.18 = bf16[4,80,1024]{2,1,0:T(8,128)(2,1)S(1)} collective-permute-done((bf16[4,80,1024]{2,1,0:T(8,128)(2,1)S(1)}, bf16[4,80,1024]{2,1,0:T(8,128)(2,1)S(1)}, u32[]{:S(2)}, u32[]{:S(2)}) %collective-permute-start.18) | collective-permute-done | bytes 655392 | tf_op jit(solution)/shard_map/ppermute | solution.py:33
  152.2 3.0 %collective-permute-start.22 = (bf16[160,1024]{1,0:T(8,128)(2,1)S(1)}, bf16[160,1024]{1,0:T(8,128)(2,1)S(1)}, u32[]{:S(2)}, u32[]{:S(2)}) collective-permute-start(bf16[160,1024]{1,0:T(8,128)(2,1)S(1)} %pad_maximum_fusion.6), channel_id=1, source_target_pairs={{0,32},{1,33},{2,34},{3,35},{4,36},{5,37},{6,38},{7,39},{8,40},{9,... | collective-permute-start | bytes 983048 | tf_op jit(solution)/shard_map/ppermute | solution.py:33
  157.0 2.7 %collective-permute-done.22 = bf16[160,1024]{1,0:T(8,128)(2,1)S(1)} collective-permute-done((bf16[160,1024]{1,0:T(8,128)(2,1)S(1)}, bf16[160,1024]{1,0:T(8,128)(2,1)S(1)}, u32[]{:S(2)}, u32[]{:S(2)}) %collective-permute-start.22) | collective-permute-done | bytes 327712 | tf_op jit(solution)/shard_map/ppermute | solution.py:33
  159.7 4.2 %collective-permute-done.21 = bf16[160,1024]{1,0:T(8,128)(2,1)S(1)} collective-permute-done((bf16[160,1024]{1,0:T(8,128)(2,1)S(1)}, bf16[160,1024]{1,0:T(8,128)(2,1)S(1)}, u32[]{:S(2)}, u32[]{:S(2)}) %collective-permute-start.21) | collective-permute-done | bytes 327712 | tf_op jit(solution)/shard_map/ppermute | solution.py:33
  164.2 14.6 %collective-permute-start.23 = (bf16[80,1024]{1,0:T(8,128)(2,1)S(1)}, bf16[80,1024]{1,0:T(8,128)(2,1)S(1)}, u32[]{:S(2)}, u32[]{:S(2)}) collective-permute-start(bf16[80,1024]{1,0:T(8,128)(2,1)S(1)} %broadcast_select_fusion.6), channel_id=1, source_target_pairs={{0,8},{1,9},{2,10},{3,11},{4,12},{5,13},{6,14},{7,15},{8,0},{9,1},... | collective-permute-start | bytes 491528 | tf_op jit(solution)/shard_map/ppermute | solution.py:33
  182.4 3.1 %collective-permute-start.13 = (bf16[160,768]{1,0:T(8,128)(2,1)S(1)}, bf16[160,768]{1,0:T(8,128)(2,1)S(1)}, u32[]{:S(2)}, u32[]{:S(2)}) collective-permute-start(bf16[160,768]{1,0:T(8,128)(2,1)S(1)} %get-tuple-element.106), channel_id=1, source_target_pairs={{0,32},{1,33},{2,34},{3,35},{4,36},{5,37},{6,38},{7,39},{8,9},{9,8... | collective-permute-start | bytes 737288 | tf_op jit(solution)/shard_map/ppermute | solution.py:33
  189.4 2.6 %collective-permute-done.12 = bf16[160,768]{1,0:T(8,128)(2,1)S(1)} collective-permute-done((bf16[160,768]{1,0:T(8,128)(2,1)S(1)}, bf16[160,768]{1,0:T(8,128)(2,1)S(1)}, u32[]{:S(2)}, u32[]{:S(2)}) %collective-permute-start.12) | collective-permute-done | bytes 245792 | tf_op jit(solution)/shard_map/ppermute | solution.py:33
  198.6 2.5 collective-permute-start.25
  202.8 2.3 multiply_subtract_fusion
  205.1 2.8 %collective-permute-done.15.refs_1_ = bf16[80,1536]{1,0:T(8,128)(2,1)S(1)} collective-permute-done((bf16[80,1536]{1,0:T(8,128)(2,1)S(1)}, bf16[80,1536]{1,0:T(8,128)(2,1)S(1)}, u32[]{:S(2)}, u32[]{:S(2)}) %collective-permute-start.15) | collective-permute-done | bytes 245792 | tf_op jit(solution)/shard_map/ppermute | solution.py:33
  209.5 2.0 collective-permute-done.25.refs_3_
  214.4 7.7 %collective-permute-done.26.refs_4_ = bf16[80,1536]{1,0:T(8,128)(2,1)S(1)} collective-permute-done((bf16[80,1536]{1,0:T(8,128)(2,1)S(1)}, bf16[80,1536]{1,0:T(8,128)(2,1)S(1)}, u32[]{:S(2)}, u32[]{:S(2)}) %collective-permute-start.26) | collective-permute-done | bytes 245792 | tf_op jit(solution)/shard_map/ppermute | solution.py:33
  222.1 2.5 %collective-permute-start.31 = (bf16[80,1536]{1,0:T(8,128)(2,1)S(1)}, bf16[80,1536]{1,0:T(8,128)(2,1)S(1)}, u32[]{:S(2)}, u32[]{:S(2)}) collective-permute-start(bf16[80,1536]{1,0:T(8,128)(2,1)S(1)} %collective-permute-done.15.refs_1_), channel_id=1, source_target_pairs={{0,8},{1,9},{2,10},{3,11},{4,12},{5,13},{6,14},{7,15},{8,0},{9,1},... | collective-permute-start | bytes 737288 | tf_op jit(solution)/shard_map/ppermute | solution.py:33
  224.7 3.3 %collective-permute-done.27.refs_5_ = bf16[80,1536]{1,0:T(8,128)(2,1)S(1)} collective-permute-done((bf16[80,1536]{1,0:T(8,128)(2,1)S(1)}, bf16[80,1536]{1,0:T(8,128)(2,1)S(1)}, u32[]{:S(2)}, u32[]{:S(2)}) %collective-permute-start.27) | collective-permute-done | bytes 245792 | tf_op jit(solution)/shard_map/ppermute | solution.py:33
  228.5 2.5 collective-permute-start.34
  231.0 3.3 %collective-permute-done.29.refs_7_ = bf16[80,1536]{1,0:T(8,128)(2,1)S(1)} collective-permute-done((bf16[80,1536]{1,0:T(8,128)(2,1)S(1)}, bf16[80,1536]{1,0:T(8,128)(2,1)S(1)}, u32[]{:S(2)}, u32[]{:S(2)}) %collective-permute-start.29) | collective-permute-done | bytes 245792 | tf_op jit(solution)/shard_map/ppermute | solution.py:33
  235.0 2.5 copy-done
  237.5 2.4 place_columns.1.copy_ref
  239.9 1.9 place_rows.2.copy_ref
  241.9 2.5 place_rows.3
  (126 shorter events, 52.6 us)
Async XLA Ops:
  8.0 173.2 %reduce-scatter.2.cloned.1.call-start = ((), (), s32[]{:S(2)}) async-start(), calls=%async_computation.1 | async-start | bytes 4915200 | tf_op jit(solution)/shard_map/reduce_scatter | solution.py:368
  13.4 12.4 %collective-permute-start.2 = (bf16[384,1024]{1,0:T(8,128)(2,1)S(1)}, bf16[384,1024]{1,0:T(8,128)(2,1)S(1)}, u32[]{:S(2)}, u32[]{:S(2)}) collective-permute-start(bf16[384,1024]{1,0:T(8,128)(2,1)S(1)} %slice.172.refs_4_), channel_id=1, source_target_pairs={{0,64},{1,65},{2,66},{3,67},{4,68},{5,69},{6,70},{7,71},{8,10},{9,... | collective-permute-start | bytes 2359304 | tf_op jit(solution)/shard_map/ppermute | solution.py:33
  14.8 19.1 %collective-permute-start.3 = (bf16[384,1024]{1,0:T(8,128)(2,1)S(1)}, bf16[384,1024]{1,0:T(8,128)(2,1)S(1)}, u32[]{:S(2)}, u32[]{:S(2)}) collective-permute-start(bf16[384,1024]{1,0:T(8,128)(2,1)S(1)} %slice.172.refs_4_), channel_id=1, source_target_pairs={{0,65},{1,64},{2,67},{3,66},{4,69},{5,68},{6,71},{7,70},{8,14},{9,... | collective-permute-start | bytes 2359304 | tf_op jit(solution)/shard_map/ppermute | solution.py:33
  16.5 18.8 %collective-permute-start.4 = (bf16[384,1024]{1,0:T(8,128)(2,1)S(1)}, bf16[384,1024]{1,0:T(8,128)(2,1)S(1)}, u32[]{:S(2)}, u32[]{:S(2)}) collective-permute-start(bf16[384,1024]{1,0:T(8,128)(2,1)S(1)} %slice.172.refs_4_), channel_id=1, source_target_pairs={{0,1},{1,0},{2,3},{3,2},{4,5},{5,4},{6,7},{7,6},{8,12},{9,13},{10,... | collective-permute-start | bytes 2359304 | tf_op jit(solution)/shard_map/ppermute | solution.py:33
  36.2 25.1 %collective-permute-start.5 = (bf16[2560,384]{1,0:T(8,128)(2,1)S(1)}, bf16[2560,384]{1,0:T(8,128)(2,1)S(1)}, u32[]{:S(2)}, u32[]{:S(2)}) collective-permute-start(bf16[2560,384]{1,0:T(8,128)(2,1)S(1)} %get-tuple-element.47), channel_id=1, source_target_pairs={{0,64},{1,65},{2,66},{3,67},{4,68},{5,69},{6,70},{7,71},{8,10},{9,... | collective-permute-start | bytes 5898248 | tf_op jit(solution)/shard_map/ppermute | solution.py:33
  37.0 44.6 %collective-permute-start.6 = (bf16[2560,384]{1,0:T(8,128)(2,1)S(1)}, bf16[2560,384]{1,0:T(8,128)(2,1)S(1)}, u32[]{:S(2)}, u32[]{:S(2)}) collective-permute-start(bf16[2560,384]{1,0:T(8,128)(2,1)S(1)} %get-tuple-element.48), channel_id=1, source_target_pairs={{0,65},{1,64},{2,67},{3,66},{4,69},{5,68},{6,71},{7,70},{8,14},{9,... | collective-permute-start | bytes 5898248 | tf_op jit(solution)/shard_map/ppermute | solution.py:33
  39.0 44.6 %collective-permute-start.7 = (bf16[2560,384]{1,0:T(8,128)(2,1)S(1)}, bf16[2560,384]{1,0:T(8,128)(2,1)S(1)}, u32[]{:S(2)}, u32[]{:S(2)}) collective-permute-start(bf16[2560,384]{1,0:T(8,128)(2,1)S(1)} %get-tuple-element.49), channel_id=1, source_target_pairs={{0,1},{1,0},{2,3},{3,2},{4,5},{5,4},{6,7},{7,6},{8,12},{9,13},{10,... | collective-permute-start | bytes 5898248 | tf_op jit(solution)/shard_map/ppermute | solution.py:33
  83.6 17.8 %collective-permute-start.8 = (bf16[384,768]{1,0:T(8,128)(2,1)S(1)}, bf16[384,768]{1,0:T(8,128)(2,1)S(1)}, u32[]{:S(2)}, u32[]{:S(2)}) collective-permute-start(bf16[384,768]{1,0:T(8,128)(2,1)S(1)} %slice.173.refs_4_), channel_id=1, source_target_pairs={{0,64},{1,65},{2,66},{3,67},{4,68},{5,69},{6,70},{7,71},{8,10},{9,... | collective-permute-start | bytes 1769480 | tf_op jit(solution)/shard_map/ppermute | solution.py:33
  84.4 16.9 %collective-permute-start.9 = (bf16[384,768]{1,0:T(8,128)(2,1)S(1)}, bf16[384,768]{1,0:T(8,128)(2,1)S(1)}, u32[]{:S(2)}, u32[]{:S(2)}) collective-permute-start(bf16[384,768]{1,0:T(8,128)(2,1)S(1)} %slice.173.refs_4_), channel_id=1, source_target_pairs={{0,65},{1,64},{2,67},{3,66},{4,69},{5,68},{6,71},{7,70},{8,14},{9,... | collective-permute-start | bytes 1769480 | tf_op jit(solution)/shard_map/ppermute | solution.py:33
  86.2 15.1 %collective-permute-start.10 = (bf16[384,768]{1,0:T(8,128)(2,1)S(1)}, bf16[384,768]{1,0:T(8,128)(2,1)S(1)}, u32[]{:S(2)}, u32[]{:S(2)}) collective-permute-start(bf16[384,768]{1,0:T(8,128)(2,1)S(1)} %slice.173.refs_4_), channel_id=1, source_target_pairs={{0,1},{1,0},{2,3},{3,2},{4,5},{5,4},{6,7},{7,6},{8,12},{9,13},{10,... | collective-permute-start | bytes 1769480 | tf_op jit(solution)/shard_map/ppermute | solution.py:33
  117.9 117.1 %all-gather.2.cloned.1.call-start = ((), (), s32[]{:S(2)}) async-start(), calls=%async_computation.2 | async-start | bytes 5570560 | tf_op jit(solution)/shard_map/all_gather | solution.py:397
  118.0 19.4 %collective-permute-start.16 = (bf16[2,4,80,1024]{3,2,1,0:T(8,128)(2,1)}, bf16[2,4,80,1024]{3,2,1,0:T(8,128)(2,1)S(1)}, u32[]{:S(2)}, u32[]{:S(2)}) collective-permute-start(bf16[2,4,80,1024]{3,2,1,0:T(8,128)(2,1)} %copy-done.3), channel_id=1, source_target_pairs={{0,2},{1,3},{2,4},{3,5},{4,6},{5,7},{6,0},{7,1},{8,72},{9,73},{10,... | collective-permute-start | bytes 3932168 | tf_op jit(solution)/shard_map/ppermute | solution.py:33
  119.5 17.9 %collective-permute-start.17 = (bf16[2,4,80,1024]{3,2,1,0:T(8,128)(2,1)}, bf16[2,4,80,1024]{3,2,1,0:T(8,128)(2,1)S(1)}, u32[]{:S(2)}, u32[]{:S(2)}) collective-permute-start(bf16[2,4,80,1024]{3,2,1,0:T(8,128)(2,1)} %copy-done.2), channel_id=1, source_target_pairs={{0,6},{1,7},{2,0},{3,1},{4,2},{5,3},{6,4},{7,5},{8,73},{9,72},{10,... | collective-permute-start | bytes 3932168 | tf_op jit(solution)/shard_map/ppermute | solution.py:33
  137.6 10.3 %collective-permute-start.19 = (bf16[4,80,1024]{2,1,0:T(8,128)(2,1)S(1)}, bf16[4,80,1024]{2,1,0:T(8,128)(2,1)S(1)}, u32[]{:S(2)}, u32[]{:S(2)}) collective-permute-start(bf16[4,80,1024]{2,1,0:T(8,128)(2,1)S(1)} %fusion), channel_id=1, source_target_pairs={{0,6},{1,7},{2,0},{3,1},{4,2},{5,3},{6,4},{7,5},{8,73},{9,72},{10,... | collective-permute-start | bytes 1966088 | tf_op jit(solution)/shard_map/ppermute | solution.py:33
  140.7 11.1 %collective-permute-start.18 = (bf16[4,80,1024]{2,1,0:T(8,128)(2,1)S(1)}, bf16[4,80,1024]{2,1,0:T(8,128)(2,1)S(1)}, u32[]{:S(2)}, u32[]{:S(2)}) collective-permute-start(bf16[4,80,1024]{2,1,0:T(8,128)(2,1)S(1)} %fusion.1), channel_id=1, source_target_pairs={{0,2},{1,3},{2,4},{3,5},{4,6},{5,7},{6,0},{7,1},{8,72},{9,73},{10,... | collective-permute-start | bytes 1966088 | tf_op jit(solution)/shard_map/ppermute | solution.py:33
  155.2 8.7 %collective-permute-start.21 = (bf16[160,1024]{1,0:T(8,128)(2,1)S(1)}, bf16[160,1024]{1,0:T(8,128)(2,1)S(1)}, u32[]{:S(2)}, u32[]{:S(2)}) collective-permute-start(bf16[160,1024]{1,0:T(8,128)(2,1)S(1)} %pad_maximum_fusion.5), channel_id=1, source_target_pairs={{0,48},{1,49},{2,50},{3,51},{4,52},{5,53},{6,54},{7,55},{8,56},{9,... | collective-permute-start | bytes 983048 | tf_op jit(solution)/shard_map/ppermute | solution.py:33
  156.1 7.8 %collective-permute-start.20 = (bf16[160,1024]{1,0:T(8,128)(2,1)S(1)}, bf16[160,1024]{1,0:T(8,128)(2,1)S(1)}, u32[]{:S(2)}, u32[]{:S(2)}) collective-permute-start(bf16[160,1024]{1,0:T(8,128)(2,1)S(1)} %pad_maximum_fusion.4), channel_id=1, source_target_pairs={{0,16},{1,17},{2,18},{3,19},{4,20},{5,21},{6,22},{7,23},{8,24},{9,... | collective-permute-start | bytes 983048 | tf_op jit(solution)/shard_map/ppermute | solution.py:33
  164.2 15.7 %collective-permute-start.23 = (bf16[80,1024]{1,0:T(8,128)(2,1)S(1)}, bf16[80,1024]{1,0:T(8,128)(2,1)S(1)}, u32[]{:S(2)}, u32[]{:S(2)}) collective-permute-start(bf16[80,1024]{1,0:T(8,128)(2,1)S(1)} %broadcast_select_fusion.6), channel_id=1, source_target_pairs={{0,8},{1,9},{2,10},{3,11},{4,12},{5,13},{6,14},{7,15},{8,0},{9,1},... | collective-permute-start | bytes 491528 | tf_op jit(solution)/shard_map/ppermute | solution.py:33
  196.9 11.0 %collective-permute-start.15 = (bf16[80,1536]{1,0:T(8,128)(2,1)S(1)}, bf16[80,1536]{1,0:T(8,128)(2,1)S(1)}, u32[]{:S(2)}, u32[]{:S(2)}) collective-permute-start(bf16[80,1536]{1,0:T(8,128)(2,1)S(1)} %get-tuple-element.121.refs_0_), channel_id=1, source_target_pairs={{0,16},{1,17},{2,18},{3,19},{4,20},{5,21},{6,22},{7,23},{8,72},{9,... | collective-permute-start | bytes 737288 | tf_op jit(solution)/shard_map/ppermute | solution.py:33
  198.4 11.1 %collective-permute-start.24 = (bf16[80,1536]{1,0:T(8,128)(2,1)S(1)}, bf16[80,1536]{1,0:T(8,128)(2,1)S(1)}, u32[]{:S(2)}, u32[]{:S(2)}) collective-permute-start(bf16[80,1536]{1,0:T(8,128)(2,1)S(1)} %get-tuple-element.121.refs_0_), channel_id=1, source_target_pairs={{0,48},{1,49},{2,50},{3,51},{4,52},{5,53},{6,54},{7,55},{8,24},{9,... | collective-permute-start | bytes 737288 | tf_op jit(solution)/shard_map/ppermute | solution.py:33
  198.6 12.9 %collective-permute-start.25 = (bf16[80,1536]{1,0:T(8,128)(2,1)S(1)}, bf16[80,1536]{1,0:T(8,128)(2,1)S(1)}, u32[]{:S(2)}, u32[]{:S(2)}) collective-permute-start(bf16[80,1536]{1,0:T(8,128)(2,1)S(1)} %get-tuple-element.121.refs_0_), channel_id=1, source_target_pairs={{0,32},{1,33},{2,34},{3,35},{4,36},{5,37},{6,38},{7,39},{8,56},{9,... | collective-permute-start | bytes 737288 | tf_op jit(solution)/shard_map/ppermute | solution.py:33
  201.1 21.1 %collective-permute-start.26 = (bf16[80,1536]{1,0:T(8,128)(2,1)S(1)}, bf16[80,1536]{1,0:T(8,128)(2,1)S(1)}, u32[]{:S(2)}, u32[]{:S(2)}) collective-permute-start(bf16[80,1536]{1,0:T(8,128)(2,1)S(1)} %get-tuple-element.121.refs_0_), channel_id=1, source_target_pairs={{0,64},{1,65},{2,66},{3,67},{4,68},{5,69},{6,70},{7,71},{8,40},{9,... | collective-permute-start | bytes 737288 | tf_op jit(solution)/shard_map/ppermute | solution.py:33
  201.2 23.4 %collective-permute-start.30 = (bf16[80,1536]{1,0:T(8,128)(2,1)S(1)}, bf16[80,1536]{1,0:T(8,128)(2,1)S(1)}, u32[]{:S(2)}, u32[]{:S(2)}) collective-permute-start(bf16[80,1536]{1,0:T(8,128)(2,1)S(1)} %get-tuple-element.121.refs_0_), channel_id=1, source_target_pairs={{0,8},{1,9},{2,10},{3,11},{4,12},{5,13},{6,14},{7,15},{8,0},{9,1},... | collective-permute-start | bytes 737288 | tf_op jit(solution)/shard_map/ppermute | solution.py:33
  207.9 20.1 %collective-permute-start.27 = (bf16[80,1536]{1,0:T(8,128)(2,1)S(1)}, bf16[80,1536]{1,0:T(8,128)(2,1)S(1)}, u32[]{:S(2)}, u32[]{:S(2)}) collective-permute-start(bf16[80,1536]{1,0:T(8,128)(2,1)S(1)} %collective-permute-done.15.refs_1_), channel_id=1, source_target_pairs={{0,64},{1,65},{2,66},{3,67},{4,68},{5,69},{6,70},{7,71},{8,24},{9,... | collective-permute-start | bytes 737288 | tf_op jit(solution)/shard_map/ppermute | solution.py:33
  211.6 16.9 %collective-permute-start.28 = (bf16[80,1536]{1,0:T(8,128)(2,1)S(1)}, bf16[80,1536]{1,0:T(8,128)(2,1)S(1)}, u32[]{:S(2)}, u32[]{:S(2)}) collective-permute-start(bf16[80,1536]{1,0:T(8,128)(2,1)S(1)} %get-tuple-element.119), channel_id=1, source_target_pairs={{0,64},{1,65},{2,66},{3,67},{4,68},{5,69},{6,70},{7,71},{8,56},{9,... | collective-permute-start | bytes 737288 | tf_op jit(solution)/shard_map/ppermute | solution.py:33
  212.5 21.8 %collective-permute-start.29 = (bf16[80,1536]{1,0:T(8,128)(2,1)S(1)}, bf16[80,1536]{1,0:T(8,128)(2,1)S(1)}, u32[]{:S(2)}, u32[]{:S(2)}) collective-permute-start(bf16[80,1536]{1,0:T(8,128)(2,1)S(1)} %get-tuple-element.118), channel_id=1, source_target_pairs={{0,64},{1,65},{2,66},{3,67},{4,68},{5,69},{6,70},{7,71},{8,40},{9,... | collective-permute-start | bytes 737288 | tf_op jit(solution)/shard_map/ppermute | solution.py:33
  222.1 12.2 %collective-permute-start.31 = (bf16[80,1536]{1,0:T(8,128)(2,1)S(1)}, bf16[80,1536]{1,0:T(8,128)(2,1)S(1)}, u32[]{:S(2)}, u32[]{:S(2)}) collective-permute-start(bf16[80,1536]{1,0:T(8,128)(2,1)S(1)} %collective-permute-done.15.refs_1_), channel_id=1, source_target_pairs={{0,8},{1,9},{2,10},{3,11},{4,12},{5,13},{6,14},{7,15},{8,0},{9,1},... | collective-permute-start | bytes 737288 | tf_op jit(solution)/shard_map/ppermute | solution.py:33
  224.7 10.2 %collective-permute-start.32 = (bf16[80,1536]{1,0:T(8,128)(2,1)S(1)}, bf16[80,1536]{1,0:T(8,128)(2,1)S(1)}, u32[]{:S(2)}, u32[]{:S(2)}) collective-permute-start(bf16[80,1536]{1,0:T(8,128)(2,1)S(1)} %collective-permute-done.24.refs_2_), channel_id=1, source_target_pairs={{0,8},{1,9},{2,10},{3,11},{4,12},{5,13},{6,14},{7,15},{8,0},{9,1},... | collective-permute-start | bytes 737288 | tf_op jit(solution)/shard_map/ppermute | solution.py:33
  228.1 13.8 %collective-permute-start.33 = (bf16[80,1536]{1,0:T(8,128)(2,1)S(1)}, bf16[80,1536]{1,0:T(8,128)(2,1)S(1)}, u32[]{:S(2)}, u32[]{:S(2)}) collective-permute-start(bf16[80,1536]{1,0:T(8,128)(2,1)S(1)} %collective-permute-done.25.refs_3_), channel_id=1, source_target_pairs={{0,8},{1,9},{2,10},{3,11},{4,12},{5,13},{6,14},{7,15},{8,0},{9,1},... | collective-permute-start | bytes 737288 | tf_op jit(solution)/shard_map/ppermute | solution.py:33
  228.5 13.3 %collective-permute-start.34 = (bf16[80,1536]{1,0:T(8,128)(2,1)S(1)}, bf16[80,1536]{1,0:T(8,128)(2,1)S(1)}, u32[]{:S(2)}, u32[]{:S(2)}) collective-permute-start(bf16[80,1536]{1,0:T(8,128)(2,1)S(1)} %collective-permute-done.26.refs_4_), channel_id=1, source_target_pairs={{0,8},{1,9},{2,10},{3,11},{4,12},{5,13},{6,14},{7,15},{8,0},{9,1},... | collective-permute-start | bytes 737288 | tf_op jit(solution)/shard_map/ppermute | solution.py:33
  234.3 7.5 %collective-permute-start.35 = (bf16[80,1536]{1,0:T(8,128)(2,1)S(1)}, bf16[80,1536]{1,0:T(8,128)(2,1)S(1)}, u32[]{:S(2)}, u32[]{:S(2)}) collective-permute-start(bf16[80,1536]{1,0:T(8,128)(2,1)S(1)} %collective-permute-done.27.refs_5_), channel_id=1, source_target_pairs={{0,8},{1,9},{2,10},{3,11},{4,12},{5,13},{6,14},{7,15},{8,0},{9,1},... | collective-permute-start | bytes 737288 | tf_op jit(solution)/shard_map/ppermute | solution.py:33
  234.3 7.5 %collective-permute-start.36 = (bf16[80,1536]{1,0:T(8,128)(2,1)S(1)}, bf16[80,1536]{1,0:T(8,128)(2,1)}, u32[]{:S(2)}, u32[]{:S(2)}) collective-permute-start(bf16[80,1536]{1,0:T(8,128)(2,1)S(1)} %collective-permute-done.28.refs_6_), channel_id=1, source_target_pairs={{0,8},{1,9},{2,10},{3,11},{4,12},{5,13},{6,14},{7,15},{8,0},{9,1},... | collective-permute-start | bytes 737288 | tf_op jit(solution)/shard_map/ppermute | solution.py:33
  (28 other events, 334.3 us)
Sparse Core Ops, SparseCore 0:
  118.0 34.2 reduce-scatter.1
Sparse Core Ops, SparseCore 1:
  181.3 53.1 all-gather.1

commit v8 on v7

--- a/solution.py
+++ b/solution.py
@@ -63,6 +63,11 @@
         return (x, y + step, z, c) if c == 0 else (x, y, z + step, c)
 
     return move
+
+
+def row_groups():
+    groups = [[device(x, y, place, 0) for place in range(4)] for x in range(4) for y in range(4)]
+    return groups + [[device(place, y, z, 1) for place in range(4)] for y in range(4) for z in range(4)]
 
 
 def first_groups():
@@ -100,19 +105,26 @@
     )(where, mine, other)
 
 
-def partial_sums(where, blocks, inputs, ring):
+def partial_sums(where, blocks, inputs, start, width, ring):
     rows, tokens = blocks[0].shape
-    width = inputs[0].shape[1]
     piece = rows // 4
     unit = piece // 8
 
     def kernel(where_ref, *refs):
-        block_refs, input_refs = refs[:4], refs[4:8]
-        out_refs, mark_ref = refs[8:-4], refs[-4]
-        mark_ref[...] = jnp.zeros_like(mark_ref)
-        held, total, semaphores = refs[-3:]
+        block_refs, input_ref = refs[:4], refs[4]
+        out_refs = refs[5:-4]
+        held, total, semaphores, input_semaphores = refs[-4:]
+
+        loads = []
         for step in range(4):
-            held[pl.ds(step * tokens, tokens), :] = input_refs[step][...]
+            at = lax.rem(where_ref[0] + step, 4) * tokens
+            source = input_ref.at[pl.ds(pl.multiple_of(at, tokens), tokens), pl.ds(start, width)]
+            target = held.at[pl.ds(step * tokens, tokens), :]
+            loads.append(pltpu.make_async_copy(source, target, input_semaphores.at[step]))
+        for load in loads:
+            load.start()
+        for load in loads:
+            load.wait()
 
         def copies(g, slot):
             step_g = lax.rem(g - where_ref[1] + 4, 4)
@@ -126,17 +138,23 @@
                     semaphores.at[slot, to_y],
                 )
 
-        for g in range(4):
-            slot = g % 2
-            if not ring and g >= 2:
-                for copy in copies(g - 2, slot):
-                    copy.wait()
-            turned = jnp.concatenate([ref[pl.ds(g * piece, piece), :] for ref in block_refs], axis=1)
+        @pl.loop(0, 4)
+        def _(g):
+            slot = lax.rem(g, 2)
+            if not ring:
+
+                @pl.when(g >= 2)
+                def _():
+                    for copy in copies(g - 2, slot):
+                        copy.wait()
+
+            at = pl.ds(pl.multiple_of(g * piece, piece), piece)
+            turned = jnp.concatenate([ref[at, :] for ref in block_refs], axis=1)
             total[slot] = jnp.dot(turned, held[...], preferred_element_type=jnp.float32).astype(jnp.bfloat16)
             if not ring:
                 for copy in copies(g, slot):
                     copy.start()
-                continue
+                return
 
             step_g = lax.rem(g - where_ref[1] + 4, 4)
             plus_ref, minus_ref, first_ref, third_ref, keep_ref = out_refs
@@ -149,7 +167,7 @@
             for distance, halves in enumerate(places):
 
                 @pl.when(step_g == distance)
-                def _(halves=halves, slot=slot):
+                def _(halves=halves):
                     for to_y in range(4):
                         step_y = lax.rem(to_y - where_ref[2] + 4, 4)
                         for half, (ref, at) in enumerate(halves):
@@ -164,6 +182,7 @@
                 for copy in copies(g, g % 2):
                     copy.wait()
 
+    hbm = pl.BlockSpec(memory_space=pltpu.HBM)
     if ring:
         two, one = (2, 4, unit, width), (4, unit, width)
         shapes = (two, two, one, one, two)
@@ -171,15 +190,15 @@
         shapes = ((4, 4, 2 * unit, width),)
     return pl.pallas_call(
         kernel,
-        in_specs=[SMEM] + [VMEM] * 8,
-        out_specs=[VMEM if ring else pl.BlockSpec(memory_space=pltpu.HBM)] * len(shapes) + [VMEM],
+        in_specs=[SMEM] + [VMEM] * 4 + [hbm],
+        out_specs=[VMEM if ring else hbm] * len(shapes),
         scratch_shapes=[
             pltpu.VMEM((4 * tokens, width), jnp.bfloat16),
             pltpu.VMEM((2, piece, width), jnp.bfloat16),
             pltpu.SemaphoreType.DMA((2, 4)),
+            pltpu.SemaphoreType.DMA((4,)),
         ],
-        out_shape=[jax.ShapeDtypeStruct(shape, jnp.bfloat16) for shape in shapes]
-        + [jax.ShapeDtypeStruct((8, 128), jnp.float32)],
+        out_shape=[jax.ShapeDtypeStruct(shape, jnp.bfloat16) for shape in shapes],
         compiler_params=pltpu.CompilerParams(vmem_limit_bytes=24 * 1024 * 1024),
         cost_estimate=pl.CostEstimate(
             flops=2 * 4 * tokens * rows * width,
@@ -187,7 +206,7 @@
             transcendentals=0,
         ),
         name="partial_sums",
-    )(where, *blocks, *inputs)
+    )(where, *blocks, inputs)
 
 
 def wide(value):
@@ -226,42 +245,27 @@
     return narrow(sum(wide(value) for value in received))
 
 
-def near_and_pair(first, second):
-    def move(x, y, z, c):
-        steps = first if c == 0 else second
-        return (x, y, z ^ 1, c) if steps is None else (x, y + steps, z, c)
-
-    return move
-
-
-def gather_rows(value, c, state):
-    def choose(low, high):
-        return jnp.where(c == 0, low, high)
-
-    one = send(value, near_and_pair(1, None))
-    two = send(value, near_and_pair(-1, 1))
-    three = send(value, near_and_pair(2, -1))
-    four = send(value, near_and_pair(None, 2))
-    one, state = tie(one, state)
-    five = send(one, near_and_pair(None, 1))
-    six = send(choose(two, one), near_and_pair(None, -1))
-    seven = send(choose(three, one), near_and_pair(None, 2))
-    own = [value, one, two, three, four, five, six, seven]
-    swapped = [send(part, sibling) for part in own]
-    return own, swapped, state
+def gather_rows(value):
+    def to(y_step, z_bit):
+        def move(x, y, z, c):
+            return x, y + y_step, z ^ z_bit, c
+
+        return move
+
+    own = [send(value, to(y_step, z_bit)) if y_step or z_bit else value for z_bit in range(2) for y_step in range(4)]
+    return own, [send(part, sibling) for part in own]
 
 
 def gathered_places(y, z, c):
-    y_steps = jnp.where(c == 0, jnp.array([0, 3, 1, 2, 0, 3, 1, 2]), jnp.array([0, 0, 3, 1, 2, 3, 1, 2]))
-    z_steps = jnp.where(c == 0, jnp.array([0, 0, 0, 0, 1, 1, 1, 1]), jnp.array([0, 1, 0, 0, 0, 1, 1, 1]))
-    return (((z + z_steps) % 2) * 8 + ((y + y_steps) % 4) * 2 + c).astype(jnp.int32)
-
-
-def place_columns(gathered, mark, columns, start):
+    steps = jnp.arange(8, dtype=jnp.int32)
+    return ((z + steps // 4) % 2) * 8 + ((y - steps % 4 + 4) % 4) * 2 + c
+
+
+def place_columns(gathered, columns, start):
     rows, width = gathered.shape
     width, half = width // 2, columns // 2
 
-    def kernel(gathered_ref, mark_ref, out_ref, semaphores):
+    def kernel(gathered_ref, out_ref, semaphores):
         copies = [
             pltpu.make_async_copy(
                 gathered_ref.at[:, pl.ds(side * width, width)],
@@ -277,13 +281,13 @@
 
     return pl.pallas_call(
         kernel,
-        in_specs=[VMEM, pl.BlockSpec(memory_space=pl.ANY)],
+        in_specs=[VMEM],
         out_specs=pl.BlockSpec(memory_space=pltpu.HBM),
         scratch_shapes=[pltpu.SemaphoreType.DMA((2,))],
         out_shape=jax.ShapeDtypeStruct((rows, columns), jnp.bfloat16),
         compiler_params=pltpu.CompilerParams(vmem_limit_bytes=4 * 1024 * 1024),
         name="place_columns",
-    )(gathered, mark)
+    )(gathered)
 
 
 def place_rows(copy, parts, places, start):
@@ -347,25 +351,18 @@
     chip_input = jnp.concatenate([kept, send(given, sibling)], axis=0)
     chip_input, swapped = tie(chip_input, up_cotangent)
     other = send(swapped, sibling)
-
-    def spread(value):
-        return [send(value, along_rows(step)) for step in (1, 3, 2)]
+    inputs = lax.all_gather(chip_input, AXES, axis=0, axis_index_groups=row_groups(), tiled=True)
+
+    blocks = pack(where, up_cotangent, other)
+    blocks = [blocks[0]] + [send(blocks[step], along_rows(step)) for step in (1, 3, 2)]
+    blocks = [blocks[0], blocks[2], blocks[3], blocks[1]]
 
     starts = [sum(WIDTHS[:place]) for place in range(len(WIDTHS))]
-    inputs = [chip_input[:, start : start + width] for start, width in zip(starts, WIDTHS)]
-    inputs_0 = [inputs[0], *spread(inputs[0])]
-    own, near, last, far = pack(where, up_cotangent, other)
-    near, far, inputs_0 = tie(near, far, inputs_0)
-    blocks = [own, send(near, along_rows(1)), send(far, along_rows(3)), send(last, along_rows(2))]
-    blocks, waiting = tie(blocks, inputs[1])
-    inputs_1 = [inputs[1], *spread(waiting)]
-
-    plus, minus, first, third, keep, _ = partial_sums(where, blocks, inputs_0, True)
-    plus, minus, inputs_1[1:] = tie(plus, minus, inputs_1[1:])
+    plus, minus, first, third, keep = partial_sums(where, blocks, inputs, starts[0], WIDTHS[0], True)
     sent_0 = ring_send(plus, minus, along_sums)
-    pieces_1, mark = partial_sums(where, blocks, inputs_1, False)
-    sent_0, mark = tie(sent_0, mark)
-    (part_1,) = lax.psum_scatter(pieces_1, AXES, scatter_dimension=0, axis_index_groups=first_groups(), tiled=True)
+    pieces_1 = partial_sums(where, blocks, inputs, starts[1], WIDTHS[1], False)
+    sent_0, pieces_1 = tie(sent_0, pieces_1)
+    (part_1,) = lax.psum_scatter(pieces_1[0], AXES, scatter_dimension=0, axis_index_groups=first_groups(), tiled=True)
     turned_0 = ring_turn(first, third, *sent_0, along_sums)
     again_0 = direct([ring_end(keep, *sent_0, *turned_0, place) for place in range(4)], along_y)
     again_1 = direct([part_1[place] for place in range(4)], along_rest)
@@ -395,11 +392,11 @@
 
     state = adamw(joined(grads), master, first_moment, second_moment)
     gathered = lax.all_gather(copies[0], "inter", axis=0, tiled=True)
-    own_places, other_places = tie(gathered_places(y, z, c), gathered_places(y, z, 1 - c))
-    own_parts, other_parts, state = gather_rows(copies[1], c, state)
-    new_copy = place_columns(gathered, mark, columns, starts[0])
-    new_copy = place_rows(new_copy, own_parts, own_places, starts[1])
-    new_copy = place_rows(new_copy, other_parts, other_places, starts[1])
+    own_parts, other_parts = gather_rows(copies[1])
+    own_parts[4], state = tie(own_parts[4], state)
+    new_copy = place_columns(gathered, columns, starts[0])
+    new_copy = place_rows(new_copy, own_parts, gathered_places(y, z, c), starts[1])
+    new_copy = place_rows(new_copy, other_parts, gathered_places(y, z, 1 - c), starts[1])
     return (*state, new_copy)
 
 

time: 252 us -> 266 us (1.056)
  waiting for transfers between devices: 116 us -> 141 us
  starting transfers between devices: 59.6 us -> 34.8 us
  local copies, waits for them, and re-layouts: 14.5 us -> 23.3 us
  other arithmetic: 8.29 us -> 16.5 us
    ppermute x38 -> x32, starting transfers between devices: 59.5 us -> 34.7 us  [send(): return lax.ppermute(value, AXES, permutation(move))]
    ppermute x38 -> x32, waiting for transfers between devices: 116 us -> 140 us  [send(): return lax.ppermute(value, AXES, permutation(move))]
    unnamed x40, local copies, waits for them, and re-layouts: 10.6 us -> 20.5 us
    another operation x2, other arithmetic: 0.67 us -> 3.38 us
  transfers between devices with their start and end apart: 40 -> 35, of which waited for: 25 -> 19; matrix products, arithmetic and copies ran while one was open for 4% -> 6% of each run, Pallas kernels for 8% -> 8%
where the time goes in v8:
time: 266 us
  waiting for transfers between devices  141 us (53%)
  Pallas kernels  35.8 us (13%)
  starting transfers between devices  34.8 us (13%)
  local copies, waits for them, and re-layouts  23.3 us (9%)
  other arithmetic  16.5 us (6%)
  between operations  14.1 us (5%)
    ppermute x32, waiting for transfers between devices, send(): return lax.ppermute(value, AXES, permutation(move))  140 us
    ppermute x32, starting transfers between devices, send(): return lax.ppermute(value, AXES, permutation(move))  34.7 us
    pallas_call x2, Pallas kernels, partial_sums(): pl.pallas_call(kernel, in_specs=[SMEM] + [VMEM] * 4 + [hbm], out_specs=[V...  24.4 us
    unnamed x40, local copies, waits for them, and re-layouts  20.5 us
    convert_element_type x5, other arithmetic, narrow(): return value.astype(jnp.bfloat16)  5.39 us
  transfers between devices with their start and end apart: 35, of which 19 were waited for; matrix products, arithmetic and copies ran while one was open for 6% of the time, Pallas kernels for 8%

profile of v8, /device:TPU:1, one launch (start us, length us, event | category | flops | bytes accessed | tf_op | source)
XLA Modules:
  0.0 265.6 jit_solution(8640187202780384408)
XLA Ops:
  13.7 6.7 %collective-permute-done.1.other_ref = bf16[192,10240]{1,0:T(8,128)(2,1)} collective-permute-done((bf16[192,10240]{1,0:T(8,128)(2,1)}, bf16[192,10240]{1,0:T(8,128)(2,1)}, u32[]{:S(2)}, u32[]{:S(2)}) %collective-permute-start.1) | collective-permute-done | bytes 3932192 | tf_op jit(solution)/shard_map/ppermute | solution.py:33
  20.4 2.1 copy-done.1
  22.5 4.6 %pack_cotangent.1 = (bf16[2560,384]{1,0:T(8,128)(2,1)S(1)}, bf16[2560,384]{1,0:T(8,128)(2,1)S(1)}, bf16[2560,384]{1,0:T(8,128)(2,1)S(1)}, bf16[2560,384]{1,0:T(8,128)(2,1)S(1)}) custom-call(s32[4]{0:T(128)S(1)} %pad_add_fusion.where_ref, bf16[192,10240]{1,0:T(8,128)(2,1)S(1)} %copy-done.1, bf16[192,10240]{1,0:T(8,128)(2,1)} %collective-permute-done.1.other_ref), custom_call_target="tpu_custom_call" | custom-call | bytes 15728640 | tf_op jit(solution)/shard_map/pack_cotangent/pallas_call | solution.py:97
  28.4 2.5 collective-permute-start.2
  32.1 41.1 %collective-permute-done.2.refs_1_ = bf16[2560,384]{1,0:T(8,128)(2,1)S(1)} collective-permute-done((bf16[2560,384]{1,0:T(8,128)(2,1)S(1)}, bf16[2560,384]{1,0:T(8,128)(2,1)S(1)}, u32[]{:S(2)}, u32[]{:S(2)}) %collective-permute-start.2) | collective-permute-done | bytes 1966112 | tf_op jit(solution)/shard_map/ppermute | solution.py:33
  75.8 18.7 %collective-permute-done.4.refs_3_ = bf16[2560,384]{1,0:T(8,128)(2,1)S(1)} collective-permute-done((bf16[2560,384]{1,0:T(8,128)(2,1)S(1)}, bf16[2560,384]{1,0:T(8,128)(2,1)S(1)}, u32[]{:S(2)}, u32[]{:S(2)}) %collective-permute-start.4) | collective-permute-done | bytes 1966112 | tf_op jit(solution)/shard_map/ppermute | solution.py:33
  96.9 2.6 copy-done.3
  105.6 11.6 %partial_sums.2 = (bf16[2,4,80,1024]{3,2,1,0:T(8,128)(2,1)}, bf16[2,4,80,1024]{3,2,1,0:T(8,128)(2,1)}, bf16[4,80,1024]{2,1,0:T(8,128)(2,1)S(1)}, bf16[4,80,1024]...) custom-call(s32[4]{0:T(128)S(1)} %pad_add_fusion.where_ref, bf16[2560,384]{1,0:T(8,128)(2,1)S(1)} %copy-done.5, ...), custom_call_target="tpu_custom_call" | custom-call | flops 8053063680 | bytes 16252928 | tf_op jit(solution)/shard_map/partial_sums/pallas_call | solution.py:191
  119.9 12.8 %partial_sums.3 = bf16[4,4,160,768]{3,2,1,0:T(8,128)(2,1)S(1)} custom-call(s32[4]{0:T(128)S(1)} %pad_add_fusion.where_ref, bf16[2560,384]{1,0:T(8,128)(2,1)S(1)} %copy-done.6, bf16[2560,384]{1,0:T(8,128)(2,1)S(1)} %copy-done.9, bf16[2560,384]{1,0:T(8,128)(2,1)S(1)} %copy-done.11, bf16[2560,384]{1,0:T(8,128)(2,1)S(1)} %copy-done.13, ...), custom_call_target="tpu_custom_call" | custom-call | flops 6039797760 | bytes 14155776 | tf_op jit(solution)/shard_map/partial_sums/pallas_call | solution.py:191
  132.8 1.9 copy-done.2
  137.0 2.7 %collective-permute-start.13 = (bf16[4,80,1024]{2,1,0:T(8,128)(2,1)S(1)}, bf16[4,80,1024]{2,1,0:T(8,128)(2,1)S(1)}, u32[]{:S(2)}, u32[]{:S(2)}) collective-permute-start(bf16[4,80,1024]{2,1,0:T(8,128)(2,1)S(1)} %fusion), channel_id=1, source_target_pairs={{0,6},{1,7},{2,0},{3,1},{4,2},{5,3},{6,4},{7,5},{8,73},{9,72},{10,... | collective-permute-start | bytes 1966088 | tf_op jit(solution)/shard_map/ppermute | solution.py:33
  141.1 6.1 %collective-permute-done.13 = bf16[4,80,1024]{2,1,0:T(8,128)(2,1)S(1)} collective-permute-done((bf16[4,80,1024]{2,1,0:T(8,128)(2,1)S(1)}, bf16[4,80,1024]{2,1,0:T(8,128)(2,1)S(1)}, u32[]{:S(2)}, u32[]{:S(2)}) %collective-permute-start.13) | collective-permute-done | bytes 655392 | tf_op jit(solution)/shard_map/ppermute | solution.py:33
  147.2 1.8 fusion.33
  149.0 3.1 %collective-permute-done.12 = bf16[4,80,1024]{2,1,0:T(8,128)(2,1)S(1)} collective-permute-done((bf16[4,80,1024]{2,1,0:T(8,128)(2,1)S(1)}, bf16[4,80,1024]{2,1,0:T(8,128)(2,1)S(1)}, u32[]{:S(2)}, u32[]{:S(2)}) %collective-permute-start.12) | collective-permute-done | bytes 655392 | tf_op jit(solution)/shard_map/ppermute | solution.py:33
  153.8 2.8 %collective-permute-start.16 = (bf16[160,1024]{1,0:T(8,128)(2,1)S(1)}, bf16[160,1024]{1,0:T(8,128)(2,1)S(1)}, u32[]{:S(2)}, u32[]{:S(2)}) collective-permute-start(bf16[160,1024]{1,0:T(8,128)(2,1)S(1)} %pad_maximum_fusion.6), channel_id=1, source_target_pairs={{0,32},{1,33},{2,34},{3,35},{4,36},{5,37},{6,38},{7,39},{8,40},{9,... | collective-permute-start | bytes 983048 | tf_op jit(solution)/shard_map/ppermute | solution.py:33
  158.4 6.8 %collective-permute-done.16 = bf16[160,1024]{1,0:T(8,128)(2,1)S(1)} collective-permute-done((bf16[160,1024]{1,0:T(8,128)(2,1)S(1)}, bf16[160,1024]{1,0:T(8,128)(2,1)S(1)}, u32[]{:S(2)}, u32[]{:S(2)}) %collective-permute-start.16) | collective-permute-done | bytes 327712 | tf_op jit(solution)/shard_map/ppermute | solution.py:33
  165.2 11.6 %collective-permute-done.15 = bf16[160,1024]{1,0:T(8,128)(2,1)S(1)} collective-permute-done((bf16[160,1024]{1,0:T(8,128)(2,1)S(1)}, bf16[160,1024]{1,0:T(8,128)(2,1)S(1)}, u32[]{:S(2)}, u32[]{:S(2)}) %collective-permute-start.15) | collective-permute-done | bytes 327712 | tf_op jit(solution)/shard_map/ppermute | solution.py:33
  177.1 3.4 %collective-permute-start.17 = (bf16[80,1024]{1,0:T(8,128)(2,1)S(1)}, bf16[80,1024]{1,0:T(8,128)(2,1)S(1)}, u32[]{:S(2)}, u32[]{:S(2)}) collective-permute-start(bf16[80,1024]{1,0:T(8,128)(2,1)S(1)} %broadcast_select_fusion.4), channel_id=1, source_target_pairs={{0,8},{1,9},{2,10},{3,11},{4,12},{5,13},{6,14},{7,15},{8,0},{9,1},... | collective-permute-start | bytes 491528 | tf_op jit(solution)/shard_map/ppermute | solution.py:33
  184.3 1.9 collective-permute-start.9
  186.2 1.8 collective-permute-start.8
  188.2 3.0 %collective-permute-done.9 = bf16[160,768]{1,0:T(8,128)(2,1)S(1)} collective-permute-done((bf16[160,768]{1,0:T(8,128)(2,1)S(1)}, bf16[160,768]{1,0:T(8,128)(2,1)S(1)}, u32[]{:S(2)}, u32[]{:S(2)}) %collective-permute-start.9) | collective-permute-done | bytes 245792 | tf_op jit(solution)/shard_map/ppermute | solution.py:33
  191.2 3.5 %collective-permute-done.8 = bf16[160,768]{1,0:T(8,128)(2,1)S(1)} collective-permute-done((bf16[160,768]{1,0:T(8,128)(2,1)S(1)}, bf16[160,768]{1,0:T(8,128)(2,1)S(1)}, u32[]{:S(2)}, u32[]{:S(2)}) %collective-permute-start.8) | collective-permute-done | bytes 245792 | tf_op jit(solution)/shard_map/ppermute | solution.py:33
  203.2 2.1 collective-permute-start.20
  205.3 11.6 %collective-permute-done.11.refs_4_ = bf16[80,1536]{1,0:T(8,128)(2,1)S(1)} collective-permute-done((bf16[80,1536]{1,0:T(8,128)(2,1)S(1)}, bf16[80,1536]{1,0:T(8,128)(2,1)S(1)}, u32[]{:S(2)}, u32[]{:S(2)}) %collective-permute-start.11) | collective-permute-done | bytes 245792 | tf_op jit(solution)/shard_map/ppermute | solution.py:33
  216.9 6.9 %collective-permute-done.19.refs_2_ = bf16[80,1536]{1,0:T(8,128)(2,1)S(1)} collective-permute-done((bf16[80,1536]{1,0:T(8,128)(2,1)S(1)}, bf16[80,1536]{1,0:T(8,128)(2,1)S(1)}, u32[]{:S(2)}, u32[]{:S(2)}) %collective-permute-start.19) | collective-permute-done | bytes 245792 | tf_op jit(solution)/shard_map/ppermute | solution.py:33
  224.8 3.7 %collective-permute-done.21.refs_5_ = bf16[80,1536]{1,0:T(8,128)(2,1)S(1)} collective-permute-done((bf16[80,1536]{1,0:T(8,128)(2,1)S(1)}, bf16[80,1536]{1,0:T(8,128)(2,1)S(1)}, u32[]{:S(2)}, u32[]{:S(2)}) %collective-permute-start.21) | collective-permute-done | bytes 245792 | tf_op jit(solution)/shard_map/ppermute | solution.py:33
  231.5 12.6 %collective-permute-done.22.refs_6_ = bf16[80,1536]{1,0:T(8,128)(2,1)S(1)} collective-permute-done((bf16[80,1536]{1,0:T(8,128)(2,1)S(1)}, bf16[80,1536]{1,0:T(8,128)(2,1)S(1)}, u32[]{:S(2)}, u32[]{:S(2)}) %collective-permute-start.22) | collective-permute-done | bytes 245792 | tf_op jit(solution)/shard_map/ppermute | solution.py:33
  246.1 3.6 %multiply_subtract_fusion = (f32[80,3584]{1,0:T(8,128)}, f32[80,3584]{1,0:T(8,128)}, f32[80,3584]{1,0:T(8,128)}) fusion(f32[80,3584]{1,0:T(8,128)S(1)} %copy-done.15, f32[80,768]{1,0:T(8,128)S(1)} %get-tuple-element.71, f32[80,1024]{1,0:T(8,128)S(1)} %get-tuple-element.69, f32[80,768]{1,0:T(8,128)S(1)} %get-tuple-element.70, ...), kind=kLoop, calls=%fused_computation.6 | loop fusion | flops 5160960 | bytes 8028160 | tf_op jit(solution)/shard_map/sub | solution.py:335
  249.7 2.5 copy-done
  252.2 2.4 place_columns.1.copy_ref
  254.6 1.9 place_rows.2.copy_ref
  256.6 2.5 place_rows.3
  (115 shorter events, 48.7 us)
Async XLA Ops:
  7.2 89.7 %all-gather.3.cloned.1.call-start = ((), (), s32[]{:S(2)}) async-start(), calls=%async_computation.1 | async-start | bytes 6881280 | tf_op jit(solution)/shard_map/all_gather | solution.py:354
  13.2 169.9 %reduce-scatter.2.cloned.1.call-start = ((), (), s32[]{:S(2)}) async-start(), calls=%async_computation.2 | async-start | bytes 4915200 | tf_op jit(solution)/shard_map/reduce_scatter | solution.py:365
  13.2 7.2 %collective-permute-start.1 = (bf16[192,10240]{1,0:T(8,128)(2,1)}, bf16[192,10240]{1,0:T(8,128)(2,1)}, u32[]{:S(2)}, u32[]{:S(2)}) collective-permute-start(bf16[192,10240]{1,0:T(8,128)(2,1)} %mine_ref.1), channel_id=1, source_target_pairs={{0,8},{1,9},{2,10},{3,11},{4,12},{5,13},{6,14},{7,15},{8,0},{9,1},... | collective-permute-start | bytes 11796488 | tf_op jit(solution)/shard_map/ppermute | solution.py:33
  28.4 44.7 %collective-permute-start.2 = (bf16[2560,384]{1,0:T(8,128)(2,1)S(1)}, bf16[2560,384]{1,0:T(8,128)(2,1)S(1)}, u32[]{:S(2)}, u32[]{:S(2)}) collective-permute-start(bf16[2560,384]{1,0:T(8,128)(2,1)S(1)} %get-tuple-element.24), channel_id=1, source_target_pairs={{0,65},{1,64},{2,67},{3,66},{4,69},{5,68},{6,71},{7,70},{8,14},{9,... | collective-permute-start | bytes 5898248 | tf_op jit(solution)/shard_map/ppermute | solution.py:33
  30.9 43.5 %collective-permute-start.3 = (bf16[2560,384]{1,0:T(8,128)(2,1)S(1)}, bf16[2560,384]{1,0:T(8,128)(2,1)S(1)}, u32[]{:S(2)}, u32[]{:S(2)}) collective-permute-start(bf16[2560,384]{1,0:T(8,128)(2,1)S(1)} %get-tuple-element.25), channel_id=1, source_target_pairs={{0,1},{1,0},{2,3},{3,2},{4,5},{5,4},{6,7},{7,6},{8,12},{9,13},{10,... | collective-permute-start | bytes 5898248 | tf_op jit(solution)/shard_map/ppermute | solution.py:33
  31.4 63.1 %collective-permute-start.4 = (bf16[2560,384]{1,0:T(8,128)(2,1)S(1)}, bf16[2560,384]{1,0:T(8,128)(2,1)S(1)}, u32[]{:S(2)}, u32[]{:S(2)}) collective-permute-start(bf16[2560,384]{1,0:T(8,128)(2,1)S(1)} %get-tuple-element.26), channel_id=1, source_target_pairs={{0,64},{1,65},{2,66},{3,67},{4,68},{5,69},{6,70},{7,71},{8,10},{9,... | collective-permute-start | bytes 5898248 | tf_op jit(solution)/shard_map/ppermute | solution.py:33
  117.2 18.3 %collective-permute-start.5 = (bf16[2,4,80,1024]{3,2,1,0:T(8,128)(2,1)}, bf16[2,4,80,1024]{3,2,1,0:T(8,128)(2,1)}, u32[]{:S(2)}, u32[]{:S(2)}) collective-permute-start(bf16[2,4,80,1024]{3,2,1,0:T(8,128)(2,1)} %get-tuple-element.28), channel_id=1, source_target_pairs={{0,2},{1,3},{2,4},{3,5},{4,6},{5,7},{6,0},{7,1},{8,72},{9,73},{10,... | collective-permute-start | bytes 3932168 | tf_op jit(solution)/shard_map/ppermute | solution.py:33
  118.5 17.1 %collective-permute-start.6 = (bf16[2,4,80,1024]{3,2,1,0:T(8,128)(2,1)}, bf16[2,4,80,1024]{3,2,1,0:T(8,128)(2,1)}, u32[]{:S(2)}, u32[]{:S(2)}) collective-permute-start(bf16[2,4,80,1024]{3,2,1,0:T(8,128)(2,1)} %get-tuple-element.29), channel_id=1, source_target_pairs={{0,6},{1,7},{2,0},{3,1},{4,2},{5,3},{6,4},{7,5},{8,73},{9,72},{10,... | collective-permute-start | bytes 3932168 | tf_op jit(solution)/shard_map/ppermute | solution.py:33
  135.6 114.1 %all-gather.5.cloned.1.call-start = ((), (), s32[]{:S(2)}) async-start(), calls=%async_computation.3 | async-start | bytes 5570560 | tf_op jit(solution)/shard_map/all_gather | solution.py:394
  137.0 10.2 %collective-permute-start.13 = (bf16[4,80,1024]{2,1,0:T(8,128)(2,1)S(1)}, bf16[4,80,1024]{2,1,0:T(8,128)(2,1)S(1)}, u32[]{:S(2)}, u32[]{:S(2)}) collective-permute-start(bf16[4,80,1024]{2,1,0:T(8,128)(2,1)S(1)} %fusion), channel_id=1, source_target_pairs={{0,6},{1,7},{2,0},{3,1},{4,2},{5,3},{6,4},{7,5},{8,73},{9,72},{10,... | collective-permute-start | bytes 1966088 | tf_op jit(solution)/shard_map/ppermute | solution.py:33
  141.0 11.1 %collective-permute-start.12 = (bf16[4,80,1024]{2,1,0:T(8,128)(2,1)S(1)}, bf16[4,80,1024]{2,1,0:T(8,128)(2,1)S(1)}, u32[]{:S(2)}, u32[]{:S(2)}) collective-permute-start(bf16[4,80,1024]{2,1,0:T(8,128)(2,1)S(1)} %fusion.1), channel_id=1, source_target_pairs={{0,2},{1,3},{2,4},{3,5},{4,6},{5,7},{6,0},{7,1},{8,72},{9,73},{10,... | collective-permute-start | bytes 1966088 | tf_op jit(solution)/shard_map/ppermute | solution.py:33
  153.8 11.5 %collective-permute-start.16 = (bf16[160,1024]{1,0:T(8,128)(2,1)S(1)}, bf16[160,1024]{1,0:T(8,128)(2,1)S(1)}, u32[]{:S(2)}, u32[]{:S(2)}) collective-permute-start(bf16[160,1024]{1,0:T(8,128)(2,1)S(1)} %pad_maximum_fusion.6), channel_id=1, source_target_pairs={{0,32},{1,33},{2,34},{3,35},{4,36},{5,37},{6,38},{7,39},{8,40},{9,... | collective-permute-start | bytes 983048 | tf_op jit(solution)/shard_map/ppermute | solution.py:33
  156.6 20.2 %collective-permute-start.15 = (bf16[160,1024]{1,0:T(8,128)(2,1)S(1)}, bf16[160,1024]{1,0:T(8,128)(2,1)S(1)}, u32[]{:S(2)}, u32[]{:S(2)}) collective-permute-start(bf16[160,1024]{1,0:T(8,128)(2,1)S(1)} %pad_maximum_fusion.5), channel_id=1, source_target_pairs={{0,48},{1,49},{2,50},{3,51},{4,52},{5,53},{6,54},{7,55},{8,56},{9,... | collective-permute-start | bytes 983048 | tf_op jit(solution)/shard_map/ppermute | solution.py:33
  157.6 19.2 %collective-permute-start.14 = (bf16[160,1024]{1,0:T(8,128)(2,1)S(1)}, bf16[160,1024]{1,0:T(8,128)(2,1)S(1)}, u32[]{:S(2)}, u32[]{:S(2)}) collective-permute-start(bf16[160,1024]{1,0:T(8,128)(2,1)S(1)} %pad_maximum_fusion.4), channel_id=1, source_target_pairs={{0,16},{1,17},{2,18},{3,19},{4,20},{5,21},{6,22},{7,23},{8,24},{9,... | collective-permute-start | bytes 983048 | tf_op jit(solution)/shard_map/ppermute | solution.py:33
  184.3 6.9 %collective-permute-start.9 = (bf16[160,768]{1,0:T(8,128)(2,1)S(1)}, bf16[160,768]{1,0:T(8,128)(2,1)S(1)}, u32[]{:S(2)}, u32[]{:S(2)}) collective-permute-start(bf16[160,768]{1,0:T(8,128)(2,1)S(1)} %get-tuple-element.66), channel_id=1, source_target_pairs={{0,32},{1,33},{2,34},{3,35},{4,36},{5,37},{6,38},{7,39},{8,9},{9,8... | collective-permute-start | bytes 737288 | tf_op jit(solution)/shard_map/ppermute | solution.py:33
  186.2 8.5 %collective-permute-start.8 = (bf16[160,768]{1,0:T(8,128)(2,1)S(1)}, bf16[160,768]{1,0:T(8,128)(2,1)S(1)}, u32[]{:S(2)}, u32[]{:S(2)}) collective-permute-start(bf16[160,768]{1,0:T(8,128)(2,1)S(1)} %get-tuple-element.67), channel_id=1, source_target_pairs={{0,48},{1,49},{2,50},{3,51},{4,52},{5,53},{6,54},{7,55},{8,73},{9,... | collective-permute-start | bytes 737288 | tf_op jit(solution)/shard_map/ppermute | solution.py:33
  188.0 6.7 %collective-permute-start.7 = (bf16[160,768]{1,0:T(8,128)(2,1)S(1)}, bf16[160,768]{1,0:T(8,128)(2,1)S(1)}, u32[]{:S(2)}, u32[]{:S(2)}) collective-permute-start(bf16[160,768]{1,0:T(8,128)(2,1)S(1)} %get-tuple-element.65), channel_id=1, source_target_pairs={{0,16},{1,17},{2,18},{3,19},{4,20},{5,21},{6,22},{7,23},{8,72},{9,... | collective-permute-start | bytes 737288 | tf_op jit(solution)/shard_map/ppermute | solution.py:33
  198.9 18.0 %collective-permute-start.11 = (bf16[80,1536]{1,0:T(8,128)(2,1)S(1)}, bf16[80,1536]{1,0:T(8,128)(2,1)S(1)}, u32[]{:S(2)}, u32[]{:S(2)}) collective-permute-start(bf16[80,1536]{1,0:T(8,128)(2,1)S(1)} %get-tuple-element.79.refs_0_), channel_id=1, source_target_pairs={{0,64},{1,65},{2,66},{3,67},{4,68},{5,69},{6,70},{7,71},{8,72},{9,... | collective-permute-start | bytes 737288 | tf_op jit(solution)/shard_map/ppermute | solution.py:33
  200.1 16.8 %collective-permute-start.18 = (bf16[80,1536]{1,0:T(8,128)(2,1)S(1)}, bf16[80,1536]{1,0:T(8,128)(2,1)S(1)}, u32[]{:S(2)}, u32[]{:S(2)}) collective-permute-start(bf16[80,1536]{1,0:T(8,128)(2,1)S(1)} %get-tuple-element.79.refs_0_), channel_id=1, source_target_pairs={{0,16},{1,17},{2,18},{3,19},{4,20},{5,21},{6,22},{7,23},{8,24},{9,... | collective-permute-start | bytes 737288 | tf_op jit(solution)/shard_map/ppermute | solution.py:33
  201.9 22.0 %collective-permute-start.19 = (bf16[80,1536]{1,0:T(8,128)(2,1)S(1)}, bf16[80,1536]{1,0:T(8,128)(2,1)S(1)}, u32[]{:S(2)}, u32[]{:S(2)}) collective-permute-start(bf16[80,1536]{1,0:T(8,128)(2,1)S(1)} %get-tuple-element.79.refs_0_), channel_id=1, source_target_pairs={{0,32},{1,33},{2,34},{3,35},{4,36},{5,37},{6,38},{7,39},{8,40},{9,... | collective-permute-start | bytes 737288 | tf_op jit(solution)/shard_map/ppermute | solution.py:33
  203.2 21.6 %collective-permute-start.20 = (bf16[80,1536]{1,0:T(8,128)(2,1)S(1)}, bf16[80,1536]{1,0:T(8,128)(2,1)S(1)}, u32[]{:S(2)}, u32[]{:S(2)}) collective-permute-start(bf16[80,1536]{1,0:T(8,128)(2,1)S(1)} %get-tuple-element.79.refs_0_), channel_id=1, source_target_pairs={{0,48},{1,49},{2,50},{3,51},{4,52},{5,53},{6,54},{7,55},{8,56},{9,... | collective-permute-start | bytes 737288 | tf_op jit(solution)/shard_map/ppermute | solution.py:33
  205.3 23.2 %collective-permute-start.21 = (bf16[80,1536]{1,0:T(8,128)(2,1)S(1)}, bf16[80,1536]{1,0:T(8,128)(2,1)S(1)}, u32[]{:S(2)}, u32[]{:S(2)}) collective-permute-start(bf16[80,1536]{1,0:T(8,128)(2,1)S(1)} %get-tuple-element.79.refs_0_), channel_id=1, source_target_pairs={{0,80},{1,81},{2,82},{3,83},{4,84},{5,85},{6,86},{7,87},{8,88},{9,... | collective-permute-start | bytes 737288 | tf_op jit(solution)/shard_map/ppermute | solution.py:33
  216.9 27.1 %collective-permute-start.22 = (bf16[80,1536]{1,0:T(8,128)(2,1)S(1)}, bf16[80,1536]{1,0:T(8,128)(2,1)S(1)}, u32[]{:S(2)}, u32[]{:S(2)}) collective-permute-start(bf16[80,1536]{1,0:T(8,128)(2,1)S(1)} %get-tuple-element.79.refs_0_), channel_id=1, source_target_pairs={{0,96},{1,97},{2,98},{3,99},{4,100},{5,101},{6,102},{7,103},{8,104... | collective-permute-start | bytes 737288 | tf_op jit(solution)/shard_map/ppermute | solution.py:33
  216.9 28.2 %collective-permute-start.23 = (bf16[80,1536]{1,0:T(8,128)(2,1)S(1)}, bf16[80,1536]{1,0:T(8,128)(2,1)S(1)}, u32[]{:S(2)}, u32[]{:S(2)}) collective-permute-start(bf16[80,1536]{1,0:T(8,128)(2,1)S(1)} %get-tuple-element.79.refs_0_), channel_id=1, source_target_pairs={{0,112},{1,113},{2,114},{3,115},{4,116},{5,117},{6,118},{7,119},{8... | collective-permute-start | bytes 737288 | tf_op jit(solution)/shard_map/ppermute | solution.py:33
  223.9 21.2 %collective-permute-start.24 = (bf16[80,1536]{1,0:T(8,128)(2,1)S(1)}, bf16[80,1536]{1,0:T(8,128)(2,1)S(1)}, u32[]{:S(2)}, u32[]{:S(2)}) collective-permute-start(bf16[80,1536]{1,0:T(8,128)(2,1)S(1)} %get-tuple-element.79.refs_0_), channel_id=1, source_target_pairs={{0,8},{1,9},{2,10},{3,11},{4,12},{5,13},{6,14},{7,15},{8,0},{9,1},... | collective-permute-start | bytes 737288 | tf_op jit(solution)/shard_map/ppermute | solution.py:33
  224.8 20.8 %collective-permute-start.25 = (bf16[80,1536]{1,0:T(8,128)(2,1)S(1)}, bf16[80,1536]{1,0:T(8,128)(2,1)S(1)}, u32[]{:S(2)}, u32[]{:S(2)}) collective-permute-start(bf16[80,1536]{1,0:T(8,128)(2,1)S(1)} %collective-permute-done.18.refs_1_), channel_id=1, source_target_pairs={{0,8},{1,9},{2,10},{3,11},{4,12},{5,13},{6,14},{7,15},{8,0},{9,1},... | collective-permute-start | bytes 737288 | tf_op jit(solution)/shard_map/ppermute | solution.py:33
  228.6 17.1 %collective-permute-start.26 = (bf16[80,1536]{1,0:T(8,128)(2,1)S(1)}, bf16[80,1536]{1,0:T(8,128)(2,1)S(1)}, u32[]{:S(2)}, u32[]{:S(2)}) collective-permute-start(bf16[80,1536]{1,0:T(8,128)(2,1)S(1)} %collective-permute-done.19.refs_2_), channel_id=1, source_target_pairs={{0,8},{1,9},{2,10},{3,11},{4,12},{5,13},{6,14},{7,15},{8,0},{9,1},... | collective-permute-start | bytes 737288 | tf_op jit(solution)/shard_map/ppermute | solution.py:33
  244.0 12.5 %collective-permute-start.27 = (bf16[80,1536]{1,0:T(8,128)(2,1)S(1)}, bf16[80,1536]{1,0:T(8,128)(2,1)S(1)}, u32[]{:S(2)}, u32[]{:S(2)}) collective-permute-start(bf16[80,1536]{1,0:T(8,128)(2,1)S(1)} %collective-permute-done.20.refs_3_), channel_id=1, source_target_pairs={{0,8},{1,9},{2,10},{3,11},{4,12},{5,13},{6,14},{7,15},{8,0},{9,1},... | collective-permute-start | bytes 737288 | tf_op jit(solution)/shard_map/ppermute | solution.py:33
  245.1 11.5 %collective-permute-start.28 = (bf16[80,1536]{1,0:T(8,128)(2,1)S(1)}, bf16[80,1536]{1,0:T(8,128)(2,1)S(1)}, u32[]{:S(2)}, u32[]{:S(2)}) collective-permute-start(bf16[80,1536]{1,0:T(8,128)(2,1)S(1)} %collective-permute-done.11.refs_4_), channel_id=1, source_target_pairs={{0,8},{1,9},{2,10},{3,11},{4,12},{5,13},{6,14},{7,15},{8,0},{9,1},... | collective-permute-start | bytes 737288 | tf_op jit(solution)/shard_map/ppermute | solution.py:33
  245.1 11.5 %collective-permute-start.29 = (bf16[80,1536]{1,0:T(8,128)(2,1)S(1)}, bf16[80,1536]{1,0:T(8,128)(2,1)S(1)}, u32[]{:S(2)}, u32[]{:S(2)}) collective-permute-start(bf16[80,1536]{1,0:T(8,128)(2,1)S(1)} %collective-permute-done.21.refs_5_), channel_id=1, source_target_pairs={{0,8},{1,9},{2,10},{3,11},{4,12},{5,13},{6,14},{7,15},{8,0},{9,1},... | collective-permute-start | bytes 737288 | tf_op jit(solution)/shard_map/ppermute | solution.py:33
  245.6 11.0 %collective-permute-start.30 = (bf16[80,1536]{1,0:T(8,128)(2,1)S(1)}, bf16[80,1536]{1,0:T(8,128)(2,1)}, u32[]{:S(2)}, u32[]{:S(2)}) collective-permute-start(bf16[80,1536]{1,0:T(8,128)(2,1)S(1)} %collective-permute-done.22.refs_6_), channel_id=1, source_target_pairs={{0,8},{1,9},{2,10},{3,11},{4,12},{5,13},{6,14},{7,15},{8,0},{9,1},... | collective-permute-start | bytes 737288 | tf_op jit(solution)/shard_map/ppermute | solution.py:33
  245.7 10.9 %collective-permute-start.31 = (bf16[80,1536]{1,0:T(8,128)(2,1)S(1)}, bf16[80,1536]{1,0:T(8,128)(2,1)}, u32[]{:S(2)}, u32[]{:S(2)}) collective-permute-start(bf16[80,1536]{1,0:T(8,128)(2,1)S(1)} %collective-permute-done.23.refs_7_), channel_id=1, source_target_pairs={{0,8},{1,9},{2,10},{3,11},{4,12},{5,13},{6,14},{7,15},{8,0},{9,1},... | collective-permute-start | bytes 737288 | tf_op jit(solution)/shard_map/ppermute | solution.py:33
  (23 other events, 155.7 us)
Sparse Core Ops, SparseCore 0:
  13.3 83.5 all-gather.2
  135.8 46.2 reduce-scatter.1
  183.7 62.9 all-gather.4

commit v9 on v6

v9 whole, which is shorter than its diff:
```python
import functools
import math

import jax
import jax.numpy as jnp
from jax import lax
from jax.experimental import pallas as pl
from jax.experimental.pallas import tpu as pltpu
from jax.sharding import PartitionSpec as P

AXES = ("inter", "intra")
WIDTHS = (1024, 768)
SPLIT = 2048


def device(x, y, z, c):
    inter = (z % 2) * 8 + y * 2 + c
    intra = x * 2 + z // 2
    return inter * 8 + intra


def permutation(move):
    pairs = []
    for x in range(4):
        for y in range(4):
            for z in range(4):
                for c in range(2):
                    a, b, d, e = move(x, y, z, c)
                    pairs.append((device(x, y, z, c), device(a % 4, b % 4, d % 4, e)))
    return sorted(pairs)


def send(value, move):
    return lax.ppermute(value, AXES, permutation(move))


def sibling(x, y, z, c):
    return x, y, z, 1 - c


def along_rows(step):
    def move(x, y, z, c):
        return (x, y, z + step, c) if c == 0 else (x + step, y, z, c)

    return move


def along_sums(step):
    def move(x, y, z, c):
        return (x + step, y, z, c) if c == 0 else (x, y, z + step, c)

    return move


def along_y(step):
    def move(x, y, z, c):
        return x, y + step, z, c

    return move


def sum_groups():
    groups = [[device(place, y, z, 0) for place in range(4)] for y in range(4) for z in range(4)]
    return groups + [[device(x, y, place, 1) for place in range(4)] for x in range(4) for y in range(4)]


VMEM = pl.BlockSpec(memory_space=pltpu.VMEM)
SMEM = pl.BlockSpec(memory_space=pltpu.SMEM)


def pack(where, mine, other):
    tokens, hidden = mine.shape
    piece = hidden // 16

    def kernel(where_ref, mine_ref, other_ref, *out_refs):
        @pl.loop(0, 4)
        def _(g):
            rows = pl.ds(pl.multiple_of(g * piece, piece), piece)
            for step, out_ref in enumerate(out_refs):
                at = lax.rem(where_ref[0] + step, 4)
                place = jnp.where(where_ref[3] == 0, g * 4 + at, at * 4 + g)
                columns = pl.ds(pl.multiple_of(place * piece, piece), piece)
                both = jnp.concatenate([mine_ref[:, columns], other_ref[:, columns]], axis=0)
                out_ref[rows, :] = both.T

    return pl.pallas_call(
        kernel,
        in_specs=[SMEM, VMEM, VMEM],
        out_specs=[VMEM] * 4,
        out_shape=[jax.ShapeDtypeStruct((hidden // 4, 2 * tokens), mine.dtype)] * 4,
        compiler_params=pltpu.CompilerParams(vmem_limit_bytes=10 * 1024 * 1024),
        cost_estimate=pl.CostEstimate(flops=0, bytes_accessed=8 * tokens * hidden, transcendentals=0),
        name="pack_cotangent",
    )(where, mine, other)


def partial_sums(where, blocks, inputs, ring):
    rows, tokens = blocks[0].shape
    width = inputs[0].shape[1]
    piece = rows // 4
    unit = piece // 8

    def kernel(where_ref, *refs):
        block_refs, input_refs = refs[:4], refs[4:8]
        out_refs = refs[8:-4]
        held, total, turned, semaphores = refs[-4:]

        def loads(g, slot):
            for step, ref in enumerate(block_refs):
                source = ref.at[pl.ds(pl.multiple_of(g * piece, piece), piece), :]
                target = turned.at[slot, :, pl.ds(step * tokens, tokens)]
                yield pltpu.make_async_copy(source, target, semaphores.at[slot, step])

        for load in loads(0, 0):
            load.start()
        for step in range(4):
            held[pl.ds(step * tokens, tokens), :] = input_refs[step][...]

        @pl.loop(0, 4)
        def _(g):
            slot = lax.rem(g, 2)

            @pl.when(g < 3)
            def _():
                for load in loads(g + 1, 1 - slot):
                    load.start()

            for load in loads(g, slot):
                load.wait()
            total[...] = jnp.dot(turned[slot], held[...], preferred_element_type=jnp.float32).astype(jnp.bfloat16)

            step_g = lax.rem(g - where_ref[1] + 4, 4)
            for to_y in range(4):
                step_y = lax.rem(to_y - where_ref[2] + 4, 4)
                if not ring:
                    out_refs[0][g, step_y] = total[pl.ds(to_y * 2 * unit, 2 * unit), :]
                    continue
                plus_ref, minus_ref, first_ref, third_ref, keep_ref = out_refs
                places = [
                    [(keep_ref, 0), (keep_ref, 1)],
                    [(first_ref, None), (plus_ref, 1)],
                    [(plus_ref, 0), (minus_ref, 0)],
                    [(minus_ref, 1), (third_ref, None)],
                ]
                for distance, halves in enumerate(places):

                    @pl.when(step_y == distance)
                    def _(halves=halves, to_y=to_y):
                        for half, (ref, at) in enumerate(halves):
                            value = total[pl.ds((to_y * 2 + half) * unit, unit), :]
                            if at is None:
                                ref[step_g] = value
                            else:
                                ref[at, step_g] = value

    if ring:
        two, one = (2, 4, unit, width), (4, unit, width)
        shapes = (two, two, one, one, two)
    else:
        shapes = ((4, 4, 2 * unit, width),)
    return pl.pallas_call(
        kernel,
        in_specs=[SMEM] + [pl.BlockSpec(memory_space=pltpu.HBM)] * 4 + [VMEM] * 4,
        out_specs=[VMEM] * len(shapes),
        scratch_shapes=[
            pltpu.VMEM((4 * tokens, width), jnp.bfloat16),
            pltpu.VMEM((piece, width), jnp.bfloat16),
            pltpu.VMEM((2, piece, 4 * tokens), jnp.bfloat16),
            pltpu.SemaphoreType.DMA((2, 4)),
        ],
        out_shape=[jax.ShapeDtypeStruct(shape, jnp.bfloat16) for shape in shapes],
        compiler_params=pltpu.CompilerParams(vmem_limit_bytes=16 * 1024 * 1024),
        cost_estimate=pl.CostEstimate(
            flops=2 * 4 * tokens * rows * width,
            bytes_accessed=4 * tokens * (rows + width) * 2 + rows * width * 2,
            transcendentals=0,
        ),
        name="partial_sums",
    )(where, *[pltpu.with_memory_space_constraint(block, pltpu.HBM) for block in blocks], *inputs)


def wide(value):
    return value.astype(jnp.float32)


def narrow(value):
    return value.astype(jnp.bfloat16)


def tie(*values):
    return lax.optimization_barrier(values)


def ring_send(plus, minus, along):
    return send(plus, along(1)), send(minus, along(-1))


def ring_turn(first, third, from_left, from_right, along):
    left = send(narrow(wide(first) + wide(from_left[0])), along(1))
    right = send(narrow(wide(third) + wide(from_right[0])), along(-1))
    return left, right


def ring_end(keep, from_left, from_right, left, right, place):
    low = wide(keep[0, place]) + wide(from_right[1, place]) + wide(left[place])
    high = wide(keep[1, place]) + wide(from_left[1, place]) + wide(right[place])
    return narrow(jnp.concatenate([low, high], axis=0))


def direct(pieces, along):
    return [pieces[0]] + [send(pieces[step], along(step)) for step in (1, 3, 2)]


def summed(received):
    return narrow(sum(wide(value) for value in received))


def near_and_pair(first, second):
    def move(x, y, z, c):
        steps = first if c == 0 else second
        return (x, y, z ^ 1, c) if steps is None else (x, y + steps, z, c)

    return move


def gather_rows(value, c, grad):
    def choose(low, high):
        return jnp.where(c == 0, low, high)

    one = send(value, near_and_pair(1, None))
    two = send(value, near_and_pair(-1, 1))
    three = send(value, near_and_pair(2, -1))
    four = send(value, near_and_pair(None, 2))
    one, grad = tie(one, grad)
    five = send(one, near_and_pair(None, 1))
    six = send(choose(two, one), near_and_pair(None, -1))
    seven = send(choose(three, one), near_and_pair(None, 2))
    own = [value, one, two, three, four, five, six, seven]
    swapped = [send(part, sibling) for part in own]
    return own, swapped, grad


def gathered_places(y, z, c):
    y_steps = jnp.where(c == 0, jnp.array([0, 3, 1, 2, 0, 3, 1, 2]), jnp.array([0, 0, 3, 1, 2, 3, 1, 2]))
    z_steps = jnp.where(c == 0, jnp.array([0, 0, 0, 0, 1, 1, 1, 1]), jnp.array([0, 1, 0, 0, 0, 1, 1, 1]))
    return (((z + z_steps) % 2) * 8 + ((y + y_steps) % 4) * 2 + c).astype(jnp.int32)


def place_columns(copy, gathered):
    rows, columns = copy.shape
    width = gathered.shape[1]

    def kernel(copy_ref, gathered_ref, out_ref, semaphore):
        copy = pltpu.make_async_copy(gathered_ref, out_ref.at[:, pl.ds(0, width)], semaphore.at[0])
        copy.start()
        copy.wait()

    hbm = pl.BlockSpec(memory_space=pltpu.HBM)
    return pl.pallas_call(
        kernel,
        in_specs=[hbm, VMEM],
        out_specs=hbm,
        scratch_shapes=[pltpu.SemaphoreType.DMA((1,))],
        out_shape=jax.ShapeDtypeStruct((rows, columns), jnp.bfloat16),
        input_output_aliases={0: 0},
        compiler_params=pltpu.CompilerParams(vmem_limit_bytes=4 * 1024 * 1024),
        name="place_columns",
    )(copy, gathered)


def place_rows(copy, parts, places, rows, columns):
    unit, width = parts[0].shape
    count = len(parts)

    def kernel(places_ref, *refs):
        out_ref, semaphores = refs[-2:]
        copies = []
        for place, ref in enumerate(refs[:count]):
            at = pl.ds(pl.multiple_of(places_ref[place] * unit, unit), unit)
            target = out_ref.at[at, pl.ds(columns - width, width)]
            copies.append(pltpu.make_async_copy(ref, target, semaphores.at[place]))
        for copy in copies:
            copy.start()
        for copy in copies:
            copy.wait()

    hbm = pl.BlockSpec(memory_space=pltpu.HBM)
    old = [] if copy is None else [copy]
    return pl.pallas_call(
        kernel,
        in_specs=[SMEM] + [VMEM] * count + [hbm] * len(old),
        out_specs=hbm,
        scratch_shapes=[pltpu.SemaphoreType.DMA((count,))],
        out_shape=jax.ShapeDtypeStruct((rows, columns), jnp.bfloat16),
        input_output_aliases={1 + count: 0} if old else {},
        compiler_params=pltpu.CompilerParams(vmem_limit_bytes=4 * 1024 * 1024),
        name="place_rows",
    )(places, *parts, *old)


def adamw(grad, master, first_moment, second_moment):
    new_first = 0.9 * first_moment + 0.1 * grad
    new_second = 0.95 * second_moment + 0.05 * (grad * grad)
    first_hat = new_first / (1.0 - 0.9**10)
    second_hat = new_second / (1.0 - 0.95**10)
    step_dir = first_hat / (jnp.sqrt(second_hat) + 1e-08) + 0.1 * master
    new_master = master - 0.02 * step_dir
    return (new_master, new_first, new_second)


def body(layer_input, up_cotangent, master, first_moment, second_moment):
    tokens, columns = layer_input.shape
    total_tokens = tokens * 128
    inter, intra = lax.axis_index("inter"), lax.axis_index("intra")
    c = inter % 2
    x, y, z = intra // 2, (inter // 2) % 4, (intra % 2) * 2 + inter // 8
    where = jnp.stack([jnp.where(c == 0, z, x), jnp.where(c == 0, x, z), y, c]).astype(jnp.int32)
    half = columns // 2

    low, high = layer_input[:, :half], layer_input[:, half:]
    kept = jnp.where(c == 0, low, high)
    given = jnp.where(c == 0, high, low)
    chip_input = jnp.concatenate([kept, send(given, sibling)], axis=0)
    chip_input, swapped = tie(chip_input, up_cotangent)
    other = send(swapped, sibling)

    def spread(value):
        return [send(value, along_rows(step)) for step in (1, 3, 2)]

    starts = [sum(WIDTHS[:place]) for place in range(len(WIDTHS))]
    inputs = [chip_input[:, start : start + width] for start, width in zip(starts, WIDTHS)]
    inputs_0 = [inputs[0], *spread(inputs[0])]
    own, near, last, far = pack(where, up_cotangent, other)
    near, far, inputs_0 = tie(near, far, inputs_0)
    blocks = [own, send(near, along_rows(1)), send(far, along_rows(3)), send(last, along_rows(2))]
    blocks, waiting = tie(blocks, inputs[1])
    inputs_1 = [inputs[1], *spread(waiting)]

    (pieces_0,) = partial_sums(where, blocks, inputs_0, False)
    pieces_0, inputs_1[1:] = tie(pieces_0, inputs_1[1:])
    (part_0,) = lax.psum_scatter(pieces_0, AXES, scatter_dimension=0, axis_index_groups=sum_groups(), tiled=True)
    plus, minus, first, third, keep = partial_sums(where, blocks, inputs_1, True)
    sent_1 = ring_send(plus, minus, along_y)
    turned_1 = ring_turn(first, third, *sent_1, along_y)
    part_0, turned_1 = tie(part_0, turned_1)
    again_0 = direct([part_0[place] for place in range(4)], along_y)
    again_1 = direct([ring_end(keep, *sent_1, *turned_1, place) for place in range(4)], along_sums)
    again_0, again_1 = tie(again_0, again_1)

    rows = jnp.concatenate([summed(again_0), summed(again_1)], axis=1)
    low, high = rows[: rows.shape[0] // 2], rows[rows.shape[0] // 2 :]
    ours = jnp.where(c == 0, low, high)
    theirs = send(jnp.where(c == 0, high, low), sibling)
    scale = 1.0 / math.sqrt(total_tokens)
    grad = wide(jnp.concatenate([jnp.where(c == 0, ours, theirs), jnp.where(c == 0, theirs, ours)], axis=1)) * scale
    fresh = narrow(adamw(grad, master, first_moment, second_moment)[0])

    gathered = lax.all_gather(fresh[:, :SPLIT], "inter", axis=0, tiled=True)
    own_places, other_places = tie(gathered_places(y, z, c), gathered_places(y, z, 1 - c))
    own_parts, other_parts, grad = gather_rows(fresh[:, SPLIT:], c, grad)
    new_copy = place_rows(None, own_parts, own_places, gathered.shape[0], columns)
    new_copy = place_rows(new_copy, other_parts, other_places, gathered.shape[0], columns)
    new_copy = place_columns(new_copy, gathered)
    return (*adamw(grad, master, first_moment, second_moment), new_copy)


def solution(mesh):
    in_specs = (
        P(("inter", "intra"), None),
        P(("inter", "intra"), None),
        P(("intra", "inter"), None),
        P(("intra", "inter"), None),
        P(("intra", "inter"), None),
    )
    out_specs = (
        P(("intra", "inter"), None),
        P(("intra", "inter"), None),
        P(("intra", "inter"), None),
        P("intra", None),
    )
    return jax.shard_map(body, mesh=mesh, in_specs=in_specs, out_specs=out_specs, check_vma=False)
```

time: 245 us -> 239 us (0.976)
  waiting for transfers between devices: 112 us -> 102 us
  starting transfers between devices: 60.7 us -> 70.2 us
    ppermute x38 -> x37, starting transfers between devices: 60.6 us -> 70.1 us  [send(): return lax.ppermute(value, AXES, permutation(move))]
    reduce_scatter x1, waiting for transfers between devices: 6.77 us -> 0.01 us  [body(): lax.psum_scatter(pieces_0, AXES, scatter_dimension=0, axis_index_groups=s...]
    convert_element_type x5 -> x4, other arithmetic: 4.74 us -> 0.57 us  [narrow(): return value.astype(jnp.bfloat16)]
    ppermute x38 -> x37, waiting for transfers between devices: 105 us -> 101 us  [send(): return lax.ppermute(value, AXES, permutation(move))]
    unnamed x40 -> x36, local copies, waits for them, and re-layouts: 8.2 us -> 7.09 us
  transfers between devices with their start and end apart: 40 -> 39, of which waited for: 21 -> 21; matrix products, arithmetic and copies ran while one was open for 5% -> 3% of each run, Pallas kernels for 12% -> 13%
where the time goes in v9:
time: 239 us
  waiting for transfers between devices  102 us (43%)
  starting transfers between devices  70.2 us (29%)
  Pallas kernels  33 us (14%)
  between operations  14.4 us (6%)
  other arithmetic  10.5 us (4%)
  local copies, waits for them, and re-layouts  9.14 us (4%)
    ppermute x37, waiting for transfers between devices, send(): return lax.ppermute(value, AXES, permutation(move))  101 us
    ppermute x37, starting transfers between devices, send(): return lax.ppermute(value, AXES, permutation(move))  70.1 us
    pallas_call x2, Pallas kernels, partial_sums(): pl.pallas_call(kernel, in_specs=[SMEM] + [pl.BlockSpec(memory_space=pltpu...  21.2 us
    unnamed x36, local copies, waits for them, and re-layouts  7.09 us
    pallas_call x1, Pallas kernels, pack(): pl.pallas_call(kernel, in_specs=[SMEM, VMEM, VMEM], out_specs=[VMEM] * 4,...  5.66 us
  transfers between devices with their start and end apart: 39, of which 21 were waited for; matrix products, arithmetic and copies ran while one was open for 3% of the time, Pallas kernels for 13%

profile of v9, /device:TPU:1, one launch (start us, length us, event | category | flops | bytes accessed | tf_op | source)
XLA Modules:
  0.0 238.8 jit_solution(7903124136483445045)
XLA Ops:
  17.0 2.2 collective-permute-done.1.other_ref
  19.2 5.7 %pack_cotangent.1 = (bf16[2560,384]{1,0:T(8,128)(2,1)S(1)}, bf16[2560,384]{1,0:T(8,128)(2,1)S(1)}, bf16[2560,384]{1,0:T(8,128)(2,1)S(1)}, bf16[2560,384]{1,0:T(8,128)(2,1)S(1)}) custom-call(s32[4]{0:T(128)S(1)} %pad_add_fusion.where_ref, bf16[192,10240]{1,0:T(8,128)(2,1)} %mine_ref.1, bf16[192,10240]{1,0:T(8,128)(2,1)} %collective-permute-done.1.other_ref), custom_call_target="tpu_custom_call" | custom-call | bytes 15728640 | tf_op jit(solution)/shard_map/pack_cotangent/pallas_call | solution.py:86
  26.2 6.8 %collective-permute-done.3.refs_6_ = bf16[384,1024]{1,0:T(8,128)(2,1)S(1)} collective-permute-done((bf16[384,1024]{1,0:T(8,128)(2,1)S(1)}, bf16[384,1024]{1,0:T(8,128)(2,1)S(1)}, u32[]{:S(2)}, u32[]{:S(2)}) %collective-permute-start.3) | collective-permute-done | bytes 786464 | tf_op jit(solution)/shard_map/ppermute | solution.py:34
  39.6 20.7 %collective-permute-done.5.refs_1_ = bf16[2560,384]{1,0:T(8,128)(2,1)S(1)} collective-permute-done((bf16[2560,384]{1,0:T(8,128)(2,1)S(1)}, bf16[2560,384]{1,0:T(8,128)(2,1)S(1)}, u32[]{:S(2)}, u32[]{:S(2)}) %collective-permute-start.5) | collective-permute-done | bytes 1966112 | tf_op jit(solution)/shard_map/ppermute | solution.py:34
  60.3 20.3 %collective-permute-done.6.refs_2_ = bf16[2560,384]{1,0:T(8,128)(2,1)S(1)} collective-permute-done((bf16[2560,384]{1,0:T(8,128)(2,1)S(1)}, bf16[2560,384]{1,0:T(8,128)(2,1)S(1)}, u32[]{:S(2)}, u32[]{:S(2)}) %collective-permute-start.6) | collective-permute-done | bytes 1966112 | tf_op jit(solution)/shard_map/ppermute | solution.py:34
  82.6 2.2 collective-permute-start.8
  85.3 10.9 %partial_sums.2 = bf16[4,4,160,1024]{3,2,1,0:T(8,128)(2,1)S(1)} custom-call(s32[4]{0:T(128)S(1)} %pad_add_fusion.where_ref, bf16[2560,384]{1,0:T(8,128)(2,1)} %copy-done.2, bf16[2560,384]{1,0:T(8,128)(2,1)} %copy-done.15, bf16[2560,384]{1,0:T(8,128)(2,1)} %copy-done.16, bf16[2560,384]{1,0:T(8,128)(2,1)} %copy-done.17, bf16[384,1024]{1,0:T(8,128)(2,1)S(1)} %slice.116.refs_4_, ...), custom_call_target="tpu_custom_call" | custom-call | flops 8053063680 | bytes 16252928 | tf_op jit(solution)/shard_map/partial_sums/pallas_call | solution.py:161
  96.2 2.3 copy-done
  98.9 10.3 %partial_sums.3 = (bf16[2,4,80,768]{3,2,1,0:T(8,128)(2,1)S(1)}, bf16[2,4,80,768]{3,2,1,0:T(8,128)(2,1)S(1)}, bf16[4,80,768]{2,1,0:T(8,128)(2,1)S(1)}, bf16[4,80,...) custom-call(s32[4]{0:T(128)S(1)} %pad_add_fusion.where_ref, bf16[2560,384]{1,0:T(8,128)(2,1)} %copy-done.2, ...), custom_call_target="tpu_custom_call" | custom-call | flops 6039797760 | bytes 14155776 | tf_op jit(solution)/shard_map/partial_sums/pallas_call | solution.py:161
  109.2 2.9 %collective-permute-start.13 = (bf16[2,4,80,768]{3,2,1,0:T(8,128)(2,1)S(1)}, bf16[2,4,80,768]{3,2,1,0:T(8,128)(2,1)S(1)}, u32[]{:S(2)}, u32[]{:S(2)}) collective-permute-start(bf16[2,4,80,768]{3,2,1,0:T(8,128)(2,1)S(1)} %get-tuple-element.69), channel_id=1, source_target_pairs={{0,48},{1,49},{2,50},{3,51},{4,52},{5,53},{6,54},{7,55},{8,56},{9,... | collective-permute-start | bytes 2949128 | tf_op jit(solution)/shard_map/ppermute | solution.py:34
  112.1 16.8 %collective-permute-done.13 = bf16[2,4,80,768]{3,2,1,0:T(8,128)(2,1)S(1)} collective-permute-done((bf16[2,4,80,768]{3,2,1,0:T(8,128)(2,1)S(1)}, bf16[2,4,80,768]{3,2,1,0:T(8,128)(2,1)S(1)}, u32[]{:S(2)}, u32[]{:S(2)}) %collective-permute-start.13) | collective-permute-done | bytes 983072 | tf_op jit(solution)/shard_map/ppermute | solution.py:34
  129.1 3.6 %collective-permute-start.14 = (bf16[4,80,768]{2,1,0:T(8,128)(2,1)S(1)}, bf16[4,80,768]{2,1,0:T(8,128)(2,1)S(1)}, u32[]{:S(2)}, u32[]{:S(2)}) collective-permute-start(bf16[4,80,768]{2,1,0:T(8,128)(2,1)S(1)} %fusion.7), channel_id=1, source_target_pairs={{0,48},{1,49},{2,50},{3,51},{4,52},{5,53},{6,54},{7,55},{8,56},{9,... | collective-permute-start | bytes 1474568 | tf_op jit(solution)/shard_map/ppermute | solution.py:34
  132.9 6.1 %collective-permute-done.14 = bf16[4,80,768]{2,1,0:T(8,128)(2,1)S(1)} collective-permute-done((bf16[4,80,768]{2,1,0:T(8,128)(2,1)S(1)}, bf16[4,80,768]{2,1,0:T(8,128)(2,1)S(1)}, u32[]{:S(2)}, u32[]{:S(2)}) %collective-permute-start.14) | collective-permute-done | bytes 491552 | tf_op jit(solution)/shard_map/ppermute | solution.py:34
  139.0 3.1 %collective-permute-done.12 = bf16[4,80,768]{2,1,0:T(8,128)(2,1)S(1)} collective-permute-done((bf16[4,80,768]{2,1,0:T(8,128)(2,1)S(1)}, bf16[4,80,768]{2,1,0:T(8,128)(2,1)S(1)}, u32[]{:S(2)}, u32[]{:S(2)}) %collective-permute-start.12) | collective-permute-done | bytes 491552 | tf_op jit(solution)/shard_map/ppermute | solution.py:34
  143.6 5.2 %collective-permute-start.20 = (bf16[160,768]{1,0:T(8,128)(2,1)S(1)}, bf16[160,768]{1,0:T(8,128)(2,1)S(1)}, u32[]{:S(2)}, u32[]{:S(2)}) collective-permute-start(bf16[160,768]{1,0:T(8,128)(2,1)S(1)} %pad_maximum_fusion.6), channel_id=1, source_target_pairs={{0,4},{1,5},{2,6},{3,7},{4,0},{5,1},{6,2},{7,3},{8,9},{9,8},{10,11... | collective-permute-start | bytes 737288 | tf_op jit(solution)/shard_map/ppermute | solution.py:34
  149.9 2.7 %collective-permute-start.16 = (bf16[160,1024]{1,0:T(8,128)(2,1)S(1)}, bf16[160,1024]{1,0:T(8,128)(2,1)S(1)}, u32[]{:S(2)}, u32[]{:S(2)}) collective-permute-start(bf16[160,1024]{1,0:T(8,128)(2,1)S(1)} %get-tuple-element.100), channel_id=1, source_target_pairs={{0,48},{1,49},{2,50},{3,51},{4,52},{5,53},{6,54},{7,55},{8,56},{9,... | collective-permute-start | bytes 983048 | tf_op jit(solution)/shard_map/ppermute | solution.py:34
  153.9 2.8 %collective-permute-done.19 = bf16[160,768]{1,0:T(8,128)(2,1)S(1)} collective-permute-done((bf16[160,768]{1,0:T(8,128)(2,1)S(1)}, bf16[160,768]{1,0:T(8,128)(2,1)S(1)}, u32[]{:S(2)}, u32[]{:S(2)}) %collective-permute-start.19) | collective-permute-done | bytes 245792 | tf_op jit(solution)/shard_map/ppermute | solution.py:34
  156.7 3.4 %collective-permute-done.18 = bf16[160,768]{1,0:T(8,128)(2,1)S(1)} collective-permute-done((bf16[160,768]{1,0:T(8,128)(2,1)S(1)}, bf16[160,768]{1,0:T(8,128)(2,1)S(1)}, u32[]{:S(2)}, u32[]{:S(2)}) %collective-permute-start.18) | collective-permute-done | bytes 245792 | tf_op jit(solution)/shard_map/ppermute | solution.py:34
  160.3 3.0 %collective-permute-done.17 = bf16[160,1024]{1,0:T(8,128)(2,1)S(1)} collective-permute-done((bf16[160,1024]{1,0:T(8,128)(2,1)S(1)}, bf16[160,1024]{1,0:T(8,128)(2,1)S(1)}, u32[]{:S(2)}, u32[]{:S(2)}) %collective-permute-start.17) | collective-permute-done | bytes 327712 | tf_op jit(solution)/shard_map/ppermute | solution.py:34
  163.7 5.6 %collective-permute-start.21 = (bf16[80,1792]{1,0:T(8,128)(2,1)S(1)}, bf16[80,1792]{1,0:T(8,128)(2,1)S(1)}, u32[]{:S(2)}, u32[]{:S(2)}) collective-permute-start(bf16[80,1792]{1,0:T(8,128)(2,1)S(1)} %broadcast_select_fusion.4), channel_id=1, source_target_pairs={{0,8},{1,9},{2,10},{3,11},{4,12},{5,13},{6,14},{7,15},{8,0},{9,1},... | collective-permute-start | bytes 860168 | tf_op jit(solution)/shard_map/ppermute | solution.py:34
  170.7 1.9 convert_multiply_fusion
  174.2 2.5 %collective-permute-start.27 = (bf16[80,1536]{1,0:T(8,128)(2,1)S(1)}, bf16[80,1536]{1,0:T(8,128)(2,1)S(1)}, u32[]{:S(2)}, u32[]{:S(2)}) collective-permute-start(bf16[80,1536]{1,0:T(8,128)(2,1)S(1)} %slice.164.refs_0_), channel_id=1, source_target_pairs={{0,32},{1,33},{2,34},{3,35},{4,36},{5,37},{6,38},{7,39},{8,56},{9,... | collective-permute-start | bytes 737288 | tf_op jit(solution)/shard_map/ppermute | solution.py:34
  178.8 4.1 %collective-permute-done.25.refs_2_ = bf16[80,1536]{1,0:T(8,128)(2,1)S(1)} collective-permute-done((bf16[80,1536]{1,0:T(8,128)(2,1)S(1)}, bf16[80,1536]{1,0:T(8,128)(2,1)S(1)}, u32[]{:S(2)}, u32[]{:S(2)}) %collective-permute-start.25) | collective-permute-done | bytes 245792 | tf_op jit(solution)/shard_map/ppermute | solution.py:34
  183.5 4.0 %collective-permute-start.33 = (bf16[80,1536]{1,0:T(8,128)(2,1)S(1)}, bf16[80,1536]{1,0:T(8,128)(2,1)S(1)}, u32[]{:S(2)}, u32[]{:S(2)}) collective-permute-start(bf16[80,1536]{1,0:T(8,128)(2,1)S(1)} %get-tuple-element.108), channel_id=1, source_target_pairs={{0,64},{1,65},{2,66},{3,67},{4,68},{5,69},{6,70},{7,71},{8,56},{9,... | collective-permute-start | bytes 737288 | tf_op jit(solution)/shard_map/ppermute | solution.py:34
  188.2 5.0 %collective-permute-done.29.refs_4_ = bf16[80,1536]{1,0:T(8,128)(2,1)S(1)} collective-permute-done((bf16[80,1536]{1,0:T(8,128)(2,1)S(1)}, bf16[80,1536]{1,0:T(8,128)(2,1)S(1)}, u32[]{:S(2)}, u32[]{:S(2)}) %collective-permute-start.29) | collective-permute-done | bytes 245792 | tf_op jit(solution)/shard_map/ppermute | solution.py:34
  193.2 3.6 %collective-permute-start.24 = (bf16[80,1536]{1,0:T(8,128)(2,1)S(1)}, bf16[80,1536]{1,0:T(8,128)(2,1)S(1)}, u32[]{:S(2)}, u32[]{:S(2)}) collective-permute-start(bf16[80,1536]{1,0:T(8,128)(2,1)S(1)} %collective-permute-done.22.refs_1_), channel_id=1, source_target_pairs={{0,8},{1,9},{2,10},{3,11},{4,12},{5,13},{6,14},{7,15},{8,0},{9,1},... | collective-permute-start | bytes 737288 | tf_op jit(solution)/shard_map/ppermute | solution.py:34
  197.2 5.1 %collective-permute-start.28 = (bf16[80,1536]{1,0:T(8,128)(2,1)S(1)}, bf16[80,1536]{1,0:T(8,128)(2,1)S(1)}, u32[]{:S(2)}, u32[]{:S(2)}) collective-permute-start(bf16[80,1536]{1,0:T(8,128)(2,1)S(1)} %collective-permute-done.27.refs_3_), channel_id=1, source_target_pairs={{0,8},{1,9},{2,10},{3,11},{4,12},{5,13},{6,14},{7,15},{8,0},{9,1},... | collective-permute-start | bytes 737288 | tf_op jit(solution)/shard_map/ppermute | solution.py:34
  202.3 7.9 %collective-permute-start.30 = (bf16[80,1536]{1,0:T(8,128)(2,1)S(1)}, bf16[80,1536]{1,0:T(8,128)(2,1)S(1)}, u32[]{:S(2)}, u32[]{:S(2)}) collective-permute-start(bf16[80,1536]{1,0:T(8,128)(2,1)S(1)} %collective-permute-done.29.refs_4_), channel_id=1, source_target_pairs={{0,8},{1,9},{2,10},{3,11},{4,12},{5,13},{6,14},{7,15},{8,0},{9,1},... | collective-permute-start | bytes 737288 | tf_op jit(solution)/shard_map/ppermute | solution.py:34
  210.2 7.9 %collective-permute-start.34 = (bf16[80,1536]{1,0:T(8,128)(2,1)S(1)}, bf16[80,1536]{1,0:T(8,128)(2,1)S(1)}, u32[]{:S(2)}, u32[]{:S(2)}) collective-permute-start(bf16[80,1536]{1,0:T(8,128)(2,1)S(1)} %collective-permute-done.33.refs_6_), channel_id=1, source_target_pairs={{0,8},{1,9},{2,10},{3,11},{4,12},{5,13},{6,14},{7,15},{8,0},{9,1},... | collective-permute-start | bytes 737288 | tf_op jit(solution)/shard_map/ppermute | solution.py:34
  218.6 4.7 %multiply_subtract_fusion = (f32[80,3584]{1,0:T(8,128)}, f32[80,3584]{1,0:T(8,128)}, f32[80,3584]{1,0:T(8,128)}) fusion(f32[80,3584]{1,0:T(8,128)} %param.15, f32[80,3584]{1,0:T(8,128)} %get-tuple-element.82, f32[80,3584]{1,0:T(8,128)} %param.16, f32[80,3584]{1,0:T(8,128)} %param.17), kind=kLoop, calls=%fused_computation.9 | loop fusion | flops 4300800 | bytes 8028160 | tf_op jit(solution)/shard_map/sub | solution.py:307
  227.1 2.5 %copy-done.1 = bf16[1280,2048]{1,0:T(8,128)(2,1)S(1)} copy-done((bf16[1280,2048]{1,0:T(8,128)(2,1)S(1)}, bf16[1280,2048]{1,0:T(8,128)(2,1)}, u32[]{:S(2)}) %copy-start.1) | copy-done | bytes 5242904
  229.6 2.4 place_columns.1
  (114 shorter events, 36.2 us)
Async XLA Ops:
  7.2 134.9 %reduce-scatter.2.cloned.1.call-start = ((), (), s32[]{:S(2)}) async-start(), calls=%async_computation.1 | async-start | bytes 6553600 | tf_op jit(solution)/shard_map/reduce_scatter | solution.py:341
  12.6 13.6 %collective-permute-start.2 = (bf16[384,1024]{1,0:T(8,128)(2,1)S(1)}, bf16[384,1024]{1,0:T(8,128)(2,1)S(1)}, u32[]{:S(2)}, u32[]{:S(2)}) collective-permute-start(bf16[384,1024]{1,0:T(8,128)(2,1)S(1)} %slice.116.refs_4_), channel_id=1, source_target_pairs={{0,64},{1,65},{2,66},{3,67},{4,68},{5,69},{6,70},{7,71},{8,10},{9,... | collective-permute-start | bytes 2359304 | tf_op jit(solution)/shard_map/ppermute | solution.py:34
  13.9 19.1 %collective-permute-start.3 = (bf16[384,1024]{1,0:T(8,128)(2,1)S(1)}, bf16[384,1024]{1,0:T(8,128)(2,1)S(1)}, u32[]{:S(2)}, u32[]{:S(2)}) collective-permute-start(bf16[384,1024]{1,0:T(8,128)(2,1)S(1)} %slice.116.refs_4_), channel_id=1, source_target_pairs={{0,65},{1,64},{2,67},{3,66},{4,69},{5,68},{6,71},{7,70},{8,14},{9,... | collective-permute-start | bytes 2359304 | tf_op jit(solution)/shard_map/ppermute | solution.py:34
  15.6 18.8 %collective-permute-start.4 = (bf16[384,1024]{1,0:T(8,128)(2,1)S(1)}, bf16[384,1024]{1,0:T(8,128)(2,1)S(1)}, u32[]{:S(2)}, u32[]{:S(2)}) collective-permute-start(bf16[384,1024]{1,0:T(8,128)(2,1)S(1)} %slice.116.refs_4_), channel_id=1, source_target_pairs={{0,1},{1,0},{2,3},{3,2},{4,5},{5,4},{6,7},{7,6},{8,12},{9,13},{10,... | collective-permute-start | bytes 2359304 | tf_op jit(solution)/shard_map/ppermute | solution.py:34
  35.3 25.0 %collective-permute-start.5 = (bf16[2560,384]{1,0:T(8,128)(2,1)S(1)}, bf16[2560,384]{1,0:T(8,128)(2,1)S(1)}, u32[]{:S(2)}, u32[]{:S(2)}) collective-permute-start(bf16[2560,384]{1,0:T(8,128)(2,1)S(1)} %get-tuple-element.50), channel_id=1, source_target_pairs={{0,64},{1,65},{2,66},{3,67},{4,68},{5,69},{6,70},{7,71},{8,10},{9,... | collective-permute-start | bytes 5898248 | tf_op jit(solution)/shard_map/ppermute | solution.py:34
  36.2 44.5 %collective-permute-start.6 = (bf16[2560,384]{1,0:T(8,128)(2,1)S(1)}, bf16[2560,384]{1,0:T(8,128)(2,1)S(1)}, u32[]{:S(2)}, u32[]{:S(2)}) collective-permute-start(bf16[2560,384]{1,0:T(8,128)(2,1)S(1)} %get-tuple-element.51), channel_id=1, source_target_pairs={{0,65},{1,64},{2,67},{3,66},{4,69},{5,68},{6,71},{7,70},{8,14},{9,... | collective-permute-start | bytes 5898248 | tf_op jit(solution)/shard_map/ppermute | solution.py:34
  38.0 43.8 %collective-permute-start.7 = (bf16[2560,384]{1,0:T(8,128)(2,1)S(1)}, bf16[2560,384]{1,0:T(8,128)(2,1)S(1)}, u32[]{:S(2)}, u32[]{:S(2)}) collective-permute-start(bf16[2560,384]{1,0:T(8,128)(2,1)S(1)} %get-tuple-element.52), channel_id=1, source_target_pairs={{0,1},{1,0},{2,3},{3,2},{4,5},{5,4},{6,7},{7,6},{8,12},{9,13},{10,... | collective-permute-start | bytes 5898248 | tf_op jit(solution)/shard_map/ppermute | solution.py:34
  81.9 16.7 %collective-permute-start.10 = (bf16[384,768]{1,0:T(8,128)(2,1)S(1)}, bf16[384,768]{1,0:T(8,128)(2,1)}, u32[]{:S(2)}, u32[]{:S(2)}) collective-permute-start(bf16[384,768]{1,0:T(8,128)(2,1)S(1)} %slice.117.refs_4_), channel_id=1, source_target_pairs={{0,1},{1,0},{2,3},{3,2},{4,5},{5,4},{6,7},{7,6},{8,12},{9,13},{10,... | collective-permute-start | bytes 1769480 | tf_op jit(solution)/shard_map/ppermute | solution.py:34
  82.6 16.3 %collective-permute-start.8 = (bf16[384,768]{1,0:T(8,128)(2,1)S(1)}, bf16[384,768]{1,0:T(8,128)(2,1)}, u32[]{:S(2)}, u32[]{:S(2)}) collective-permute-start(bf16[384,768]{1,0:T(8,128)(2,1)S(1)} %slice.117.refs_4_), channel_id=1, source_target_pairs={{0,64},{1,65},{2,66},{3,67},{4,68},{5,69},{6,70},{7,71},{8,10},{9,... | collective-permute-start | bytes 1769480 | tf_op jit(solution)/shard_map/ppermute | solution.py:34
  84.7 14.1 %collective-permute-start.9 = (bf16[384,768]{1,0:T(8,128)(2,1)S(1)}, bf16[384,768]{1,0:T(8,128)(2,1)}, u32[]{:S(2)}, u32[]{:S(2)}) collective-permute-start(bf16[384,768]{1,0:T(8,128)(2,1)S(1)} %slice.117.refs_4_), channel_id=1, source_target_pairs={{0,65},{1,64},{2,67},{3,66},{4,69},{5,68},{6,71},{7,70},{8,14},{9,... | collective-permute-start | bytes 1769480 | tf_op jit(solution)/shard_map/ppermute | solution.py:34
  98.8 128.3 %all-gather.2.cloned.1.call-start = ((), (), s32[]{:S(2)}) async-start(), calls=%async_computation.2 | async-start | bytes 5570560 | tf_op jit(solution)/shard_map/all_gather | solution.py:358
  109.2 19.7 %collective-permute-start.13 = (bf16[2,4,80,768]{3,2,1,0:T(8,128)(2,1)S(1)}, bf16[2,4,80,768]{3,2,1,0:T(8,128)(2,1)S(1)}, u32[]{:S(2)}, u32[]{:S(2)}) collective-permute-start(bf16[2,4,80,768]{3,2,1,0:T(8,128)(2,1)S(1)} %get-tuple-element.69), channel_id=1, source_target_pairs={{0,48},{1,49},{2,50},{3,51},{4,52},{5,53},{6,54},{7,55},{8,56},{9,... | collective-permute-start | bytes 2949128 | tf_op jit(solution)/shard_map/ppermute | solution.py:34
  112.1 20.5 %collective-permute-start.11 = (bf16[2,4,80,768]{3,2,1,0:T(8,128)(2,1)S(1)}, bf16[2,4,80,768]{3,2,1,0:T(8,128)(2,1)S(1)}, u32[]{:S(2)}, u32[]{:S(2)}) collective-permute-start(bf16[2,4,80,768]{3,2,1,0:T(8,128)(2,1)S(1)} %get-tuple-element.67), channel_id=1, source_target_pairs={{0,16},{1,17},{2,18},{3,19},{4,20},{5,21},{6,22},{7,23},{8,24},{9,... | collective-permute-start | bytes 2949128 | tf_op jit(solution)/shard_map/ppermute | solution.py:34
  129.1 9.9 %collective-permute-start.14 = (bf16[4,80,768]{2,1,0:T(8,128)(2,1)S(1)}, bf16[4,80,768]{2,1,0:T(8,128)(2,1)S(1)}, u32[]{:S(2)}, u32[]{:S(2)}) collective-permute-start(bf16[4,80,768]{2,1,0:T(8,128)(2,1)S(1)} %fusion.7), channel_id=1, source_target_pairs={{0,48},{1,49},{2,50},{3,51},{4,52},{5,53},{6,54},{7,55},{8,56},{9,... | collective-permute-start | bytes 1474568 | tf_op jit(solution)/shard_map/ppermute | solution.py:34
  132.8 9.3 %collective-permute-start.12 = (bf16[4,80,768]{2,1,0:T(8,128)(2,1)S(1)}, bf16[4,80,768]{2,1,0:T(8,128)(2,1)S(1)}, u32[]{:S(2)}, u32[]{:S(2)}) collective-permute-start(bf16[4,80,768]{2,1,0:T(8,128)(2,1)S(1)} %fusion.8), channel_id=1, source_target_pairs={{0,16},{1,17},{2,18},{3,19},{4,20},{5,21},{6,22},{7,23},{8,24},{9,... | collective-permute-start | bytes 1474568 | tf_op jit(solution)/shard_map/ppermute | solution.py:34
  143.6 9.0 %collective-permute-start.20 = (bf16[160,768]{1,0:T(8,128)(2,1)S(1)}, bf16[160,768]{1,0:T(8,128)(2,1)S(1)}, u32[]{:S(2)}, u32[]{:S(2)}) collective-permute-start(bf16[160,768]{1,0:T(8,128)(2,1)S(1)} %pad_maximum_fusion.6), channel_id=1, source_target_pairs={{0,4},{1,5},{2,6},{3,7},{4,0},{5,1},{6,2},{7,3},{8,9},{9,8},{10,11... | collective-permute-start | bytes 737288 | tf_op jit(solution)/shard_map/ppermute | solution.py:34
  148.8 8.0 %collective-permute-start.19 = (bf16[160,768]{1,0:T(8,128)(2,1)S(1)}, bf16[160,768]{1,0:T(8,128)(2,1)S(1)}, u32[]{:S(2)}, u32[]{:S(2)}) collective-permute-start(bf16[160,768]{1,0:T(8,128)(2,1)S(1)} %pad_maximum_fusion.5), channel_id=1, source_target_pairs={{0,6},{1,7},{2,0},{3,1},{4,2},{5,3},{6,4},{7,5},{8,73},{9,72},{10,... | collective-permute-start | bytes 737288 | tf_op jit(solution)/shard_map/ppermute | solution.py:34
  149.8 10.3 %collective-permute-start.15 = (bf16[160,1024]{1,0:T(8,128)(2,1)S(1)}, bf16[160,1024]{1,0:T(8,128)(2,1)S(1)}, u32[]{:S(2)}, u32[]{:S(2)}) collective-permute-start(bf16[160,1024]{1,0:T(8,128)(2,1)S(1)} %get-tuple-element.101), channel_id=1, source_target_pairs={{0,16},{1,17},{2,18},{3,19},{4,20},{5,21},{6,22},{7,23},{8,24},{9,... | collective-permute-start | bytes 983048 | tf_op jit(solution)/shard_map/ppermute | solution.py:34
  149.9 10.4 %collective-permute-start.16 = (bf16[160,1024]{1,0:T(8,128)(2,1)S(1)}, bf16[160,1024]{1,0:T(8,128)(2,1)S(1)}, u32[]{:S(2)}, u32[]{:S(2)}) collective-permute-start(bf16[160,1024]{1,0:T(8,128)(2,1)S(1)} %get-tuple-element.100), channel_id=1, source_target_pairs={{0,48},{1,49},{2,50},{3,51},{4,52},{5,53},{6,54},{7,55},{8,56},{9,... | collective-permute-start | bytes 983048 | tf_op jit(solution)/shard_map/ppermute | solution.py:34
  152.6 10.6 %collective-permute-start.17 = (bf16[160,1024]{1,0:T(8,128)(2,1)S(1)}, bf16[160,1024]{1,0:T(8,128)(2,1)S(1)}, u32[]{:S(2)}, u32[]{:S(2)}) collective-permute-start(bf16[160,1024]{1,0:T(8,128)(2,1)S(1)} %get-tuple-element.99), channel_id=1, source_target_pairs={{0,32},{1,33},{2,34},{3,35},{4,36},{5,37},{6,38},{7,39},{8,40},{9,... | collective-permute-start | bytes 983048 | tf_op jit(solution)/shard_map/ppermute | solution.py:34
  174.0 8.9 %collective-permute-start.25 = (bf16[80,1536]{1,0:T(8,128)(2,1)S(1)}, bf16[80,1536]{1,0:T(8,128)(2,1)S(1)}, u32[]{:S(2)}, u32[]{:S(2)}) collective-permute-start(bf16[80,1536]{1,0:T(8,128)(2,1)S(1)} %slice.164.refs_0_), channel_id=1, source_target_pairs={{0,48},{1,49},{2,50},{3,51},{4,52},{5,53},{6,54},{7,55},{8,24},{9,... | collective-permute-start | bytes 737288 | tf_op jit(solution)/shard_map/ppermute | solution.py:34
  174.2 9.3 %collective-permute-start.27 = (bf16[80,1536]{1,0:T(8,128)(2,1)S(1)}, bf16[80,1536]{1,0:T(8,128)(2,1)S(1)}, u32[]{:S(2)}, u32[]{:S(2)}) collective-permute-start(bf16[80,1536]{1,0:T(8,128)(2,1)S(1)} %slice.164.refs_0_), channel_id=1, source_target_pairs={{0,32},{1,33},{2,34},{3,35},{4,36},{5,37},{6,38},{7,39},{8,56},{9,... | collective-permute-start | bytes 737288 | tf_op jit(solution)/shard_map/ppermute | solution.py:34
  176.7 16.4 %collective-permute-start.29 = (bf16[80,1536]{1,0:T(8,128)(2,1)S(1)}, bf16[80,1536]{1,0:T(8,128)(2,1)S(1)}, u32[]{:S(2)}, u32[]{:S(2)}) collective-permute-start(bf16[80,1536]{1,0:T(8,128)(2,1)S(1)} %slice.164.refs_0_), channel_id=1, source_target_pairs={{0,64},{1,65},{2,66},{3,67},{4,68},{5,69},{6,70},{7,71},{8,40},{9,... | collective-permute-start | bytes 737288 | tf_op jit(solution)/shard_map/ppermute | solution.py:34
  177.4 19.4 %collective-permute-start.23 = (bf16[80,1536]{1,0:T(8,128)(2,1)S(1)}, bf16[80,1536]{1,0:T(8,128)(2,1)S(1)}, u32[]{:S(2)}, u32[]{:S(2)}) collective-permute-start(bf16[80,1536]{1,0:T(8,128)(2,1)S(1)} %slice.164.refs_0_), channel_id=1, source_target_pairs={{0,8},{1,9},{2,10},{3,11},{4,12},{5,13},{6,14},{7,15},{8,0},{9,1},... | collective-permute-start | bytes 737288 | tf_op jit(solution)/shard_map/ppermute | solution.py:34
  183.5 13.7 %collective-permute-start.33 = (bf16[80,1536]{1,0:T(8,128)(2,1)S(1)}, bf16[80,1536]{1,0:T(8,128)(2,1)S(1)}, u32[]{:S(2)}, u32[]{:S(2)}) collective-permute-start(bf16[80,1536]{1,0:T(8,128)(2,1)S(1)} %get-tuple-element.108), channel_id=1, source_target_pairs={{0,64},{1,65},{2,66},{3,67},{4,68},{5,69},{6,70},{7,71},{8,56},{9,... | collective-permute-start | bytes 737288 | tf_op jit(solution)/shard_map/ppermute | solution.py:34
  187.5 14.8 %collective-permute-start.35 = (bf16[80,1536]{1,0:T(8,128)(2,1)S(1)}, bf16[80,1536]{1,0:T(8,128)(2,1)S(1)}, u32[]{:S(2)}, u32[]{:S(2)}) collective-permute-start(bf16[80,1536]{1,0:T(8,128)(2,1)S(1)} %get-tuple-element.107), channel_id=1, source_target_pairs={{0,64},{1,65},{2,66},{3,67},{4,68},{5,69},{6,70},{7,71},{8,40},{9,... | collective-permute-start | bytes 737288 | tf_op jit(solution)/shard_map/ppermute | solution.py:34
  187.5 22.7 %collective-permute-start.31 = (bf16[80,1536]{1,0:T(8,128)(2,1)S(1)}, bf16[80,1536]{1,0:T(8,128)(2,1)S(1)}, u32[]{:S(2)}, u32[]{:S(2)}) collective-permute-start(bf16[80,1536]{1,0:T(8,128)(2,1)S(1)} %collective-permute-done.22.refs_1_), channel_id=1, source_target_pairs={{0,64},{1,65},{2,66},{3,67},{4,68},{5,69},{6,70},{7,71},{8,24},{9,... | collective-permute-start | bytes 737288 | tf_op jit(solution)/shard_map/ppermute | solution.py:34
  193.2 24.9 %collective-permute-start.24 = (bf16[80,1536]{1,0:T(8,128)(2,1)S(1)}, bf16[80,1536]{1,0:T(8,128)(2,1)S(1)}, u32[]{:S(2)}, u32[]{:S(2)}) collective-permute-start(bf16[80,1536]{1,0:T(8,128)(2,1)S(1)} %collective-permute-done.22.refs_1_), channel_id=1, source_target_pairs={{0,8},{1,9},{2,10},{3,11},{4,12},{5,13},{6,14},{7,15},{8,0},{9,1},... | collective-permute-start | bytes 737288 | tf_op jit(solution)/shard_map/ppermute | solution.py:34
  196.8 21.3 %collective-permute-start.26 = (bf16[80,1536]{1,0:T(8,128)(2,1)S(1)}, bf16[80,1536]{1,0:T(8,128)(2,1)S(1)}, u32[]{:S(2)}, u32[]{:S(2)}) collective-permute-start(bf16[80,1536]{1,0:T(8,128)(2,1)S(1)} %collective-permute-done.25.refs_2_), channel_id=1, source_target_pairs={{0,8},{1,9},{2,10},{3,11},{4,12},{5,13},{6,14},{7,15},{8,0},{9,1},... | collective-permute-start | bytes 737288 | tf_op jit(solution)/shard_map/ppermute | solution.py:34
  197.2 27.9 %collective-permute-start.28 = (bf16[80,1536]{1,0:T(8,128)(2,1)S(1)}, bf16[80,1536]{1,0:T(8,128)(2,1)S(1)}, u32[]{:S(2)}, u32[]{:S(2)}) collective-permute-start(bf16[80,1536]{1,0:T(8,128)(2,1)S(1)} %collective-permute-done.27.refs_3_), channel_id=1, source_target_pairs={{0,8},{1,9},{2,10},{3,11},{4,12},{5,13},{6,14},{7,15},{8,0},{9,1},... | collective-permute-start | bytes 737288 | tf_op jit(solution)/shard_map/ppermute | solution.py:34
  202.3 22.9 %collective-permute-start.30 = (bf16[80,1536]{1,0:T(8,128)(2,1)S(1)}, bf16[80,1536]{1,0:T(8,128)(2,1)S(1)}, u32[]{:S(2)}, u32[]{:S(2)}) collective-permute-start(bf16[80,1536]{1,0:T(8,128)(2,1)S(1)} %collective-permute-done.29.refs_4_), channel_id=1, source_target_pairs={{0,8},{1,9},{2,10},{3,11},{4,12},{5,13},{6,14},{7,15},{8,0},{9,1},... | collective-permute-start | bytes 737288 | tf_op jit(solution)/shard_map/ppermute | solution.py:34
  210.2 15.0 %collective-permute-start.34 = (bf16[80,1536]{1,0:T(8,128)(2,1)S(1)}, bf16[80,1536]{1,0:T(8,128)(2,1)S(1)}, u32[]{:S(2)}, u32[]{:S(2)}) collective-permute-start(bf16[80,1536]{1,0:T(8,128)(2,1)S(1)} %collective-permute-done.33.refs_6_), channel_id=1, source_target_pairs={{0,8},{1,9},{2,10},{3,11},{4,12},{5,13},{6,14},{7,15},{8,0},{9,1},... | collective-permute-start | bytes 737288 | tf_op jit(solution)/shard_map/ppermute | solution.py:34
  (25 other events, 261.8 us)
Sparse Core Ops, SparseCore 0:
  99.0 39.3 reduce-scatter.1
  173.5 49.4 all-gather.1

commit v10 on v9

--- a/solution.py
+++ b/solution.py
@@ -10,7 +10,7 @@
 
 AXES = ("inter", "intra")
 WIDTHS = (1024, 768)
-SPLIT = 2048
+SPLIT = 2560
 
 
 def device(x, y, z, c):

time: 239 us -> 234 us (0.979)
  starting transfers between devices: 70.2 us -> 60.6 us
  waiting for transfers between devices: 102 us -> 106 us
    all_gather x1, waiting for transfers between devices: 0.02 us -> 11.3 us  [body(): gathered = lax.all_gather(fresh[:, :SPLIT], 'inter', axis=0, tiled=True)]
    ppermute x37, starting transfers between devices: 70.1 us -> 60.5 us  [send(): return lax.ppermute(value, AXES, permutation(move))]
    ppermute x37, waiting for transfers between devices: 101 us -> 95 us  [send(): return lax.ppermute(value, AXES, permutation(move))]
    unnamed x36 -> x34, local copies, waits for them, and re-layouts: 7.09 us -> 7.45 us
  transfers between devices with their start and end apart: 39 -> 39, of which waited for: 21 -> 20; matrix products, arithmetic and copies ran while one was open for 3% -> 2% of each run, Pallas kernels for 13% -> 13%
where the time goes in v10:
time: 234 us
  waiting for transfers between devices  106 us (45%)
  starting transfers between devices  60.6 us (26%)
  Pallas kernels  33 us (14%)
  between operations  14.4 us (6%)
  other arithmetic  9.81 us (4%)
  local copies, waits for them, and re-layouts  9.53 us (4%)
    ppermute x37, waiting for transfers between devices, send(): return lax.ppermute(value, AXES, permutation(move))  95 us
    ppermute x37, starting transfers between devices, send(): return lax.ppermute(value, AXES, permutation(move))  60.5 us
    pallas_call x2, Pallas kernels, partial_sums(): pl.pallas_call(kernel, in_specs=[SMEM] + [pl.BlockSpec(memory_space=pltpu...  21.2 us
    all_gather x1, waiting for transfers between devices, body(): gathered = lax.all_gather(fresh[:, :SPLIT], 'inter', axis=0, tiled=True)  11.3 us
    unnamed x34, local copies, waits for them, and re-layouts  7.45 us
    pallas_call x1, Pallas kernels, pack(): pl.pallas_call(kernel, in_specs=[SMEM, VMEM, VMEM], out_specs=[VMEM] * 4,...  5.66 us
  transfers between devices with their start and end apart: 39, of which 20 were waited for; matrix products, arithmetic and copies ran while one was open for 2% of the time, Pallas kernels for 13%

profile of v10, /device:TPU:1, one launch (start us, length us, event | category | flops | bytes accessed | tf_op | source)
XLA Modules:
  0.0 233.6 jit_solution(17160914874862237972)
XLA Ops:
  10.1 1.8 collective-permute-done
  17.0 2.2 collective-permute-done.1.other_ref
  19.2 5.7 %pack_cotangent.1 = (bf16[2560,384]{1,0:T(8,128)(2,1)S(1)}, bf16[2560,384]{1,0:T(8,128)(2,1)S(1)}, bf16[2560,384]{1,0:T(8,128)(2,1)S(1)}, bf16[2560,384]{1,0:T(8,128)(2,1)S(1)}) custom-call(s32[4]{0:T(128)S(1)} %pad_add_fusion.where_ref, bf16[192,10240]{1,0:T(8,128)(2,1)} %mine_ref.1, bf16[192,10240]{1,0:T(8,128)(2,1)} %collective-permute-done.1.other_ref), custom_call_target="tpu_custom_call" | custom-call | bytes 15728640 | tf_op jit(solution)/shard_map/pack_cotangent/pallas_call | solution.py:86
  26.2 6.8 %collective-permute-done.3.refs_6_ = bf16[384,1024]{1,0:T(8,128)(2,1)S(1)} collective-permute-done((bf16[384,1024]{1,0:T(8,128)(2,1)S(1)}, bf16[384,1024]{1,0:T(8,128)(2,1)S(1)}, u32[]{:S(2)}, u32[]{:S(2)}) %collective-permute-start.3) | collective-permute-done | bytes 786464 | tf_op jit(solution)/shard_map/ppermute | solution.py:34
  36.2 1.8 collective-permute-start.6
  39.6 20.7 %collective-permute-done.5.refs_1_ = bf16[2560,384]{1,0:T(8,128)(2,1)S(1)} collective-permute-done((bf16[2560,384]{1,0:T(8,128)(2,1)S(1)}, bf16[2560,384]{1,0:T(8,128)(2,1)S(1)}, u32[]{:S(2)}, u32[]{:S(2)}) %collective-permute-start.5) | collective-permute-done | bytes 1966112 | tf_op jit(solution)/shard_map/ppermute | solution.py:34
  60.3 20.3 %collective-permute-done.6.refs_2_ = bf16[2560,384]{1,0:T(8,128)(2,1)S(1)} collective-permute-done((bf16[2560,384]{1,0:T(8,128)(2,1)S(1)}, bf16[2560,384]{1,0:T(8,128)(2,1)S(1)}, u32[]{:S(2)}, u32[]{:S(2)}) %collective-permute-start.6) | collective-permute-done | bytes 1966112 | tf_op jit(solution)/shard_map/ppermute | solution.py:34
  82.6 2.2 collective-permute-start.8
  85.3 10.9 %partial_sums.2 = bf16[4,4,160,1024]{3,2,1,0:T(8,128)(2,1)S(1)} custom-call(s32[4]{0:T(128)S(1)} %pad_add_fusion.where_ref, bf16[2560,384]{1,0:T(8,128)(2,1)} %copy-done.2, bf16[2560,384]{1,0:T(8,128)(2,1)} %copy-done.14, bf16[2560,384]{1,0:T(8,128)(2,1)} %copy-done.15, bf16[2560,384]{1,0:T(8,128)(2,1)} %copy-done.16, bf16[384,1024]{1,0:T(8,128)(2,1)S(1)} %slice.116.refs_4_, ...), custom_call_target="tpu_custom_call" | custom-call | flops 8053063680 | bytes 16252928 | tf_op jit(solution)/shard_map/partial_sums/pallas_call | solution.py:161
  96.2 2.3 %copy-done.1 = bf16[4,4,160,1024]{3,2,1,0:T(8,128)(2,1)} copy-done((bf16[4,4,160,1024]{3,2,1,0:T(8,128)(2,1)}, bf16[4,4,160,1024]{3,2,1,0:T(8,128)(2,1)S(1)}, u32[]{:S(2)}) %copy-start.1) | copy-done | bytes 5242904
  98.9 10.3 %partial_sums.3 = (bf16[2,4,80,768]{3,2,1,0:T(8,128)(2,1)S(1)}, bf16[2,4,80,768]{3,2,1,0:T(8,128)(2,1)S(1)}, bf16[4,80,768]{2,1,0:T(8,128)(2,1)S(1)}, bf16[4,80,...) custom-call(s32[4]{0:T(128)S(1)} %pad_add_fusion.where_ref, bf16[2560,384]{1,0:T(8,128)(2,1)} %copy-done.2, ...), custom_call_target="tpu_custom_call" | custom-call | flops 6039797760 | bytes 14155776 | tf_op jit(solution)/shard_map/partial_sums/pallas_call | solution.py:161
  109.2 2.9 %collective-permute-start.13 = (bf16[2,4,80,768]{3,2,1,0:T(8,128)(2,1)S(1)}, bf16[2,4,80,768]{3,2,1,0:T(8,128)(2,1)S(1)}, u32[]{:S(2)}, u32[]{:S(2)}) collective-permute-start(bf16[2,4,80,768]{3,2,1,0:T(8,128)(2,1)S(1)} %get-tuple-element.69), channel_id=1, source_target_pairs={{0,48},{1,49},{2,50},{3,51},{4,52},{5,53},{6,54},{7,55},{8,56},{9,... | collective-permute-start | bytes 2949128 | tf_op jit(solution)/shard_map/ppermute | solution.py:34
  112.1 16.8 %collective-permute-done.13 = bf16[2,4,80,768]{3,2,1,0:T(8,128)(2,1)S(1)} collective-permute-done((bf16[2,4,80,768]{3,2,1,0:T(8,128)(2,1)S(1)}, bf16[2,4,80,768]{3,2,1,0:T(8,128)(2,1)S(1)}, u32[]{:S(2)}, u32[]{:S(2)}) %collective-permute-start.13) | collective-permute-done | bytes 983072 | tf_op jit(solution)/shard_map/ppermute | solution.py:34
  129.1 3.6 %collective-permute-start.14 = (bf16[4,80,768]{2,1,0:T(8,128)(2,1)S(1)}, bf16[4,80,768]{2,1,0:T(8,128)(2,1)S(1)}, u32[]{:S(2)}, u32[]{:S(2)}) collective-permute-start(bf16[4,80,768]{2,1,0:T(8,128)(2,1)S(1)} %fusion.7), channel_id=1, source_target_pairs={{0,48},{1,49},{2,50},{3,51},{4,52},{5,53},{6,54},{7,55},{8,56},{9,... | collective-permute-start | bytes 1474568 | tf_op jit(solution)/shard_map/ppermute | solution.py:34
  132.9 6.1 %collective-permute-done.14 = bf16[4,80,768]{2,1,0:T(8,128)(2,1)S(1)} collective-permute-done((bf16[4,80,768]{2,1,0:T(8,128)(2,1)S(1)}, bf16[4,80,768]{2,1,0:T(8,128)(2,1)S(1)}, u32[]{:S(2)}, u32[]{:S(2)}) %collective-permute-start.14) | collective-permute-done | bytes 491552 | tf_op jit(solution)/shard_map/ppermute | solution.py:34
  139.0 3.2 %collective-permute-done.12 = bf16[4,80,768]{2,1,0:T(8,128)(2,1)} collective-permute-done((bf16[4,80,768]{2,1,0:T(8,128)(2,1)S(1)}, bf16[4,80,768]{2,1,0:T(8,128)(2,1)}, u32[]{:S(2)}, u32[]{:S(2)}) %collective-permute-start.12) | collective-permute-done | bytes 491552 | tf_op jit(solution)/shard_map/ppermute | solution.py:34
  143.7 5.2 %collective-permute-start.20 = (bf16[160,768]{1,0:T(8,128)(2,1)S(1)}, bf16[160,768]{1,0:T(8,128)(2,1)S(1)}, u32[]{:S(2)}, u32[]{:S(2)}) collective-permute-start(bf16[160,768]{1,0:T(8,128)(2,1)S(1)} %pad_maximum_fusion.6), channel_id=1, source_target_pairs={{0,4},{1,5},{2,6},{3,7},{4,0},{5,1},{6,2},{7,3},{8,9},{9,8},{10,11... | collective-permute-start | bytes 737288 | tf_op jit(solution)/shard_map/ppermute | solution.py:34
  150.0 2.7 %collective-permute-start.16 = (bf16[160,1024]{1,0:T(8,128)(2,1)S(1)}, bf16[160,1024]{1,0:T(8,128)(2,1)S(1)}, u32[]{:S(2)}, u32[]{:S(2)}) collective-permute-start(bf16[160,1024]{1,0:T(8,128)(2,1)S(1)} %get-tuple-element.100), channel_id=1, source_target_pairs={{0,48},{1,49},{2,50},{3,51},{4,52},{5,53},{6,54},{7,55},{8,56},{9,... | collective-permute-start | bytes 983048 | tf_op jit(solution)/shard_map/ppermute | solution.py:34
  154.0 2.8 %collective-permute-done.19 = bf16[160,768]{1,0:T(8,128)(2,1)S(1)} collective-permute-done((bf16[160,768]{1,0:T(8,128)(2,1)S(1)}, bf16[160,768]{1,0:T(8,128)(2,1)S(1)}, u32[]{:S(2)}, u32[]{:S(2)}) %collective-permute-start.19) | collective-permute-done | bytes 245792 | tf_op jit(solution)/shard_map/ppermute | solution.py:34
  156.8 3.4 %collective-permute-done.18 = bf16[160,768]{1,0:T(8,128)(2,1)S(1)} collective-permute-done((bf16[160,768]{1,0:T(8,128)(2,1)S(1)}, bf16[160,768]{1,0:T(8,128)(2,1)S(1)}, u32[]{:S(2)}, u32[]{:S(2)}) %collective-permute-start.18) | collective-permute-done | bytes 245792 | tf_op jit(solution)/shard_map/ppermute | solution.py:34
  160.4 3.0 %collective-permute-done.17 = bf16[160,1024]{1,0:T(8,128)(2,1)S(1)} collective-permute-done((bf16[160,1024]{1,0:T(8,128)(2,1)S(1)}, bf16[160,1024]{1,0:T(8,128)(2,1)S(1)}, u32[]{:S(2)}, u32[]{:S(2)}) %collective-permute-start.17) | collective-permute-done | bytes 327712 | tf_op jit(solution)/shard_map/ppermute | solution.py:34
  163.8 5.6 %collective-permute-start.21 = (bf16[80,1792]{1,0:T(8,128)(2,1)S(1)}, bf16[80,1792]{1,0:T(8,128)(2,1)S(1)}, u32[]{:S(2)}, u32[]{:S(2)}) collective-permute-start(bf16[80,1792]{1,0:T(8,128)(2,1)S(1)} %broadcast_select_fusion.4), channel_id=1, source_target_pairs={{0,8},{1,9},{2,10},{3,11},{4,12},{5,13},{6,14},{7,15},{8,0},{9,1},... | collective-permute-start | bytes 860168 | tf_op jit(solution)/shard_map/ppermute | solution.py:34
  170.8 1.9 convert_multiply_fusion
  174.3 2.6 %collective-permute-start.27 = (bf16[80,1024]{1,0:T(8,128)(2,1)S(1)}, bf16[80,1024]{1,0:T(8,128)(2,1)S(1)}, u32[]{:S(2)}, u32[]{:S(2)}) collective-permute-start(bf16[80,1024]{1,0:T(8,128)(2,1)S(1)} %slice.164.refs_0_), channel_id=1, source_target_pairs={{0,32},{1,33},{2,34},{3,35},{4,36},{5,37},{6,38},{7,39},{8,56},{9,... | collective-permute-start | bytes 491528 | tf_op jit(solution)/shard_map/ppermute | solution.py:34
  181.4 3.4 %collective-permute-start.24 = (bf16[80,1024]{1,0:T(8,128)(2,1)S(1)}, bf16[80,1024]{1,0:T(8,128)(2,1)S(1)}, u32[]{:S(2)}, u32[]{:S(2)}) collective-permute-start(bf16[80,1024]{1,0:T(8,128)(2,1)S(1)} %collective-permute-done.22.refs_1_), channel_id=1, source_target_pairs={{0,8},{1,9},{2,10},{3,11},{4,12},{5,13},{6,14},{7,15},{8,0},{9,1},... | collective-permute-start | bytes 491528 | tf_op jit(solution)/shard_map/ppermute | solution.py:34
  184.9 3.5 %collective-permute-start.33 = (bf16[80,1024]{1,0:T(8,128)(2,1)S(1)}, bf16[80,1024]{1,0:T(8,128)(2,1)S(1)}, u32[]{:S(2)}, u32[]{:S(2)}) collective-permute-start(bf16[80,1024]{1,0:T(8,128)(2,1)S(1)} %get-tuple-element.108), channel_id=1, source_target_pairs={{0,64},{1,65},{2,66},{3,67},{4,68},{5,69},{6,70},{7,71},{8,56},{9,... | collective-permute-start | bytes 491528 | tf_op jit(solution)/shard_map/ppermute | solution.py:34
  191.0 5.6 %collective-permute-start.28 = (bf16[80,1024]{1,0:T(8,128)(2,1)S(1)}, bf16[80,1024]{1,0:T(8,128)(2,1)S(1)}, u32[]{:S(2)}, u32[]{:S(2)}) collective-permute-start(bf16[80,1024]{1,0:T(8,128)(2,1)S(1)} %collective-permute-done.27.refs_3_), channel_id=1, source_target_pairs={{0,8},{1,9},{2,10},{3,11},{4,12},{5,13},{6,14},{7,15},{8,0},{9,1},... | collective-permute-start | bytes 491528 | tf_op jit(solution)/shard_map/ppermute | solution.py:34
  197.5 4.4 %collective-permute-start.30 = (bf16[80,1024]{1,0:T(8,128)(2,1)S(1)}, bf16[80,1024]{1,0:T(8,128)(2,1)S(1)}, u32[]{:S(2)}, u32[]{:S(2)}) collective-permute-start(bf16[80,1024]{1,0:T(8,128)(2,1)S(1)} %collective-permute-done.29.refs_4_), channel_id=1, source_target_pairs={{0,8},{1,9},{2,10},{3,11},{4,12},{5,13},{6,14},{7,15},{8,0},{9,1},... | collective-permute-start | bytes 491528 | tf_op jit(solution)/shard_map/ppermute | solution.py:34
  202.5 4.0 %multiply_subtract_fusion = (f32[80,3584]{1,0:T(8,128)}, f32[80,3584]{1,0:T(8,128)}, f32[80,3584]{1,0:T(8,128)}) fusion(f32[80,3584]{1,0:T(8,128)S(1)} %copy-done.6, f32[80,3584]{1,0:T(8,128)} %get-tuple-element.82, f32[80,3584]{1,0:T(8,128)} %param.16, f32[80,3584]{1,0:T(8,128)S(1)} %copy-done.7), kind=kLoop, calls=%fused_computation.9 | loop fusion | flops 4300800 | bytes 8028160 | tf_op jit(solution)/shard_map/sub | solution.py:307
  209.9 11.3 %all-gather.2.cloned.1.call-done.gathered_ref = bf16[1280,2560]{1,0:T(8,128)(2,1)} async-done(((bf16[80,2560]{1,0:T(8,128)(2,1)}), bf16[1280,2560]{1,0:T(8,128)(2,1)}) %all-gather.2.cloned.1.call-update) | async-done | bytes 6553616 | tf_op jit(solution)/shard_map/all_gather | solution.py:358
  221.1 2.9 %copy-done = bf16[1280,2560]{1,0:T(8,128)(2,1)S(1)} copy-done((bf16[1280,2560]{1,0:T(8,128)(2,1)S(1)}, bf16[1280,2560]{1,0:T(8,128)(2,1)}, u32[]{:S(2)}) %copy-start) | copy-done | bytes 6553624
  224.0 2.8 %place_columns.1 = bf16[1280,3584]{1,0:T(8,128)(2,1)} custom-call(bf16[1280,3584]{1,0:T(8,128)(2,1)} %place_rows.3.copy_ref, bf16[1280,2560]{1,0:T(8,128)(2,1)S(1)} %copy-done), custom_call_target="tpu_custom_call", output_to_operand_aliasing={{}: (0, {})} | custom-call | tf_op jit(solution)/shard_map/place_columns/pallas_call | solution.py:259
  (112 shorter events, 36.6 us)
Async XLA Ops:
  7.2 135.0 %reduce-scatter.2.cloned.1.call-start = ((), (), s32[]{:S(2)}) async-start(), calls=%async_computation.1 | async-start | bytes 6553600 | tf_op jit(solution)/shard_map/reduce_scatter | solution.py:341
  12.0 7.2 %collective-permute-start.1 = (bf16[192,10240]{1,0:T(8,128)(2,1)}, bf16[192,10240]{1,0:T(8,128)(2,1)}, u32[]{:S(2)}, u32[]{:S(2)}) collective-permute-start(bf16[192,10240]{1,0:T(8,128)(2,1)} %mine_ref.1), channel_id=1, source_target_pairs={{0,8},{1,9},{2,10},{3,11},{4,12},{5,13},{6,14},{7,15},{8,0},{9,1},... | collective-permute-start | bytes 11796488 | tf_op jit(solution)/shard_map/ppermute | solution.py:34
  12.6 13.6 %collective-permute-start.2 = (bf16[384,1024]{1,0:T(8,128)(2,1)S(1)}, bf16[384,1024]{1,0:T(8,128)(2,1)S(1)}, u32[]{:S(2)}, u32[]{:S(2)}) collective-permute-start(bf16[384,1024]{1,0:T(8,128)(2,1)S(1)} %slice.116.refs_4_), channel_id=1, source_target_pairs={{0,64},{1,65},{2,66},{3,67},{4,68},{5,69},{6,70},{7,71},{8,10},{9,... | collective-permute-start | bytes 2359304 | tf_op jit(solution)/shard_map/ppermute | solution.py:34
  13.9 19.1 %collective-permute-start.3 = (bf16[384,1024]{1,0:T(8,128)(2,1)S(1)}, bf16[384,1024]{1,0:T(8,128)(2,1)S(1)}, u32[]{:S(2)}, u32[]{:S(2)}) collective-permute-start(bf16[384,1024]{1,0:T(8,128)(2,1)S(1)} %slice.116.refs_4_), channel_id=1, source_target_pairs={{0,65},{1,64},{2,67},{3,66},{4,69},{5,68},{6,71},{7,70},{8,14},{9,... | collective-permute-start | bytes 2359304 | tf_op jit(solution)/shard_map/ppermute | solution.py:34
  15.6 18.8 %collective-permute-start.4 = (bf16[384,1024]{1,0:T(8,128)(2,1)S(1)}, bf16[384,1024]{1,0:T(8,128)(2,1)S(1)}, u32[]{:S(2)}, u32[]{:S(2)}) collective-permute-start(bf16[384,1024]{1,0:T(8,128)(2,1)S(1)} %slice.116.refs_4_), channel_id=1, source_target_pairs={{0,1},{1,0},{2,3},{3,2},{4,5},{5,4},{6,7},{7,6},{8,12},{9,13},{10,... | collective-permute-start | bytes 2359304 | tf_op jit(solution)/shard_map/ppermute | solution.py:34
  35.3 25.0 %collective-permute-start.5 = (bf16[2560,384]{1,0:T(8,128)(2,1)S(1)}, bf16[2560,384]{1,0:T(8,128)(2,1)S(1)}, u32[]{:S(2)}, u32[]{:S(2)}) collective-permute-start(bf16[2560,384]{1,0:T(8,128)(2,1)S(1)} %get-tuple-element.50), channel_id=1, source_target_pairs={{0,64},{1,65},{2,66},{3,67},{4,68},{5,69},{6,70},{7,71},{8,10},{9,... | collective-permute-start | bytes 5898248 | tf_op jit(solution)/shard_map/ppermute | solution.py:34
  36.2 44.5 %collective-permute-start.6 = (bf16[2560,384]{1,0:T(8,128)(2,1)S(1)}, bf16[2560,384]{1,0:T(8,128)(2,1)S(1)}, u32[]{:S(2)}, u32[]{:S(2)}) collective-permute-start(bf16[2560,384]{1,0:T(8,128)(2,1)S(1)} %get-tuple-element.51), channel_id=1, source_target_pairs={{0,65},{1,64},{2,67},{3,66},{4,69},{5,68},{6,71},{7,70},{8,14},{9,... | collective-permute-start | bytes 5898248 | tf_op jit(solution)/shard_map/ppermute | solution.py:34
  38.0 43.8 %collective-permute-start.7 = (bf16[2560,384]{1,0:T(8,128)(2,1)S(1)}, bf16[2560,384]{1,0:T(8,128)(2,1)S(1)}, u32[]{:S(2)}, u32[]{:S(2)}) collective-permute-start(bf16[2560,384]{1,0:T(8,128)(2,1)S(1)} %get-tuple-element.52), channel_id=1, source_target_pairs={{0,1},{1,0},{2,3},{3,2},{4,5},{5,4},{6,7},{7,6},{8,12},{9,13},{10,... | collective-permute-start | bytes 5898248 | tf_op jit(solution)/shard_map/ppermute | solution.py:34
  81.9 16.7 %collective-permute-start.10 = (bf16[384,768]{1,0:T(8,128)(2,1)S(1)}, bf16[384,768]{1,0:T(8,128)(2,1)}, u32[]{:S(2)}, u32[]{:S(2)}) collective-permute-start(bf16[384,768]{1,0:T(8,128)(2,1)S(1)} %slice.117.refs_4_), channel_id=1, source_target_pairs={{0,1},{1,0},{2,3},{3,2},{4,5},{5,4},{6,7},{7,6},{8,12},{9,13},{10,... | collective-permute-start | bytes 1769480 | tf_op jit(solution)/shard_map/ppermute | solution.py:34
  82.6 16.3 %collective-permute-start.8 = (bf16[384,768]{1,0:T(8,128)(2,1)S(1)}, bf16[384,768]{1,0:T(8,128)(2,1)}, u32[]{:S(2)}, u32[]{:S(2)}) collective-permute-start(bf16[384,768]{1,0:T(8,128)(2,1)S(1)} %slice.117.refs_4_), channel_id=1, source_target_pairs={{0,64},{1,65},{2,66},{3,67},{4,68},{5,69},{6,70},{7,71},{8,10},{9,... | collective-permute-start | bytes 1769480 | tf_op jit(solution)/shard_map/ppermute | solution.py:34
  84.7 14.1 %collective-permute-start.9 = (bf16[384,768]{1,0:T(8,128)(2,1)S(1)}, bf16[384,768]{1,0:T(8,128)(2,1)}, u32[]{:S(2)}, u32[]{:S(2)}) collective-permute-start(bf16[384,768]{1,0:T(8,128)(2,1)S(1)} %slice.117.refs_4_), channel_id=1, source_target_pairs={{0,65},{1,64},{2,67},{3,66},{4,69},{5,68},{6,71},{7,70},{8,14},{9,... | collective-permute-start | bytes 1769480 | tf_op jit(solution)/shard_map/ppermute | solution.py:34
  98.8 122.3 %all-gather.2.cloned.1.call-start = ((), (), s32[]{:S(2)}) async-start(), calls=%async_computation.2 | async-start | bytes 6963200 | tf_op jit(solution)/shard_map/all_gather | solution.py:358
  109.2 19.7 %collective-permute-start.13 = (bf16[2,4,80,768]{3,2,1,0:T(8,128)(2,1)S(1)}, bf16[2,4,80,768]{3,2,1,0:T(8,128)(2,1)S(1)}, u32[]{:S(2)}, u32[]{:S(2)}) collective-permute-start(bf16[2,4,80,768]{3,2,1,0:T(8,128)(2,1)S(1)} %get-tuple-element.69), channel_id=1, source_target_pairs={{0,48},{1,49},{2,50},{3,51},{4,52},{5,53},{6,54},{7,55},{8,56},{9,... | collective-permute-start | bytes 2949128 | tf_op jit(solution)/shard_map/ppermute | solution.py:34
  112.1 20.5 %collective-permute-start.11 = (bf16[2,4,80,768]{3,2,1,0:T(8,128)(2,1)S(1)}, bf16[2,4,80,768]{3,2,1,0:T(8,128)(2,1)S(1)}, u32[]{:S(2)}, u32[]{:S(2)}) collective-permute-start(bf16[2,4,80,768]{3,2,1,0:T(8,128)(2,1)S(1)} %get-tuple-element.67), channel_id=1, source_target_pairs={{0,16},{1,17},{2,18},{3,19},{4,20},{5,21},{6,22},{7,23},{8,24},{9,... | collective-permute-start | bytes 2949128 | tf_op jit(solution)/shard_map/ppermute | solution.py:34
  129.1 9.9 %collective-permute-start.14 = (bf16[4,80,768]{2,1,0:T(8,128)(2,1)S(1)}, bf16[4,80,768]{2,1,0:T(8,128)(2,1)S(1)}, u32[]{:S(2)}, u32[]{:S(2)}) collective-permute-start(bf16[4,80,768]{2,1,0:T(8,128)(2,1)S(1)} %fusion.7), channel_id=1, source_target_pairs={{0,48},{1,49},{2,50},{3,51},{4,52},{5,53},{6,54},{7,55},{8,56},{9,... | collective-permute-start | bytes 1474568 | tf_op jit(solution)/shard_map/ppermute | solution.py:34
  132.8 9.4 %collective-permute-start.12 = (bf16[4,80,768]{2,1,0:T(8,128)(2,1)S(1)}, bf16[4,80,768]{2,1,0:T(8,128)(2,1)}, u32[]{:S(2)}, u32[]{:S(2)}) collective-permute-start(bf16[4,80,768]{2,1,0:T(8,128)(2,1)S(1)} %fusion.8), channel_id=1, source_target_pairs={{0,16},{1,17},{2,18},{3,19},{4,20},{5,21},{6,22},{7,23},{8,24},{9,... | collective-permute-start | bytes 1474568 | tf_op jit(solution)/shard_map/ppermute | solution.py:34
  143.7 9.0 %collective-permute-start.20 = (bf16[160,768]{1,0:T(8,128)(2,1)S(1)}, bf16[160,768]{1,0:T(8,128)(2,1)S(1)}, u32[]{:S(2)}, u32[]{:S(2)}) collective-permute-start(bf16[160,768]{1,0:T(8,128)(2,1)S(1)} %pad_maximum_fusion.6), channel_id=1, source_target_pairs={{0,4},{1,5},{2,6},{3,7},{4,0},{5,1},{6,2},{7,3},{8,9},{9,8},{10,11... | collective-permute-start | bytes 737288 | tf_op jit(solution)/shard_map/ppermute | solution.py:34
  148.9 8.0 %collective-permute-start.19 = (bf16[160,768]{1,0:T(8,128)(2,1)S(1)}, bf16[160,768]{1,0:T(8,128)(2,1)S(1)}, u32[]{:S(2)}, u32[]{:S(2)}) collective-permute-start(bf16[160,768]{1,0:T(8,128)(2,1)S(1)} %pad_maximum_fusion.5), channel_id=1, source_target_pairs={{0,6},{1,7},{2,0},{3,1},{4,2},{5,3},{6,4},{7,5},{8,73},{9,72},{10,... | collective-permute-start | bytes 737288 | tf_op jit(solution)/shard_map/ppermute | solution.py:34
  149.9 10.3 %collective-permute-start.15 = (bf16[160,1024]{1,0:T(8,128)(2,1)S(1)}, bf16[160,1024]{1,0:T(8,128)(2,1)S(1)}, u32[]{:S(2)}, u32[]{:S(2)}) collective-permute-start(bf16[160,1024]{1,0:T(8,128)(2,1)S(1)} %get-tuple-element.101), channel_id=1, source_target_pairs={{0,16},{1,17},{2,18},{3,19},{4,20},{5,21},{6,22},{7,23},{8,24},{9,... | collective-permute-start | bytes 983048 | tf_op jit(solution)/shard_map/ppermute | solution.py:34
  150.0 10.4 %collective-permute-start.16 = (bf16[160,1024]{1,0:T(8,128)(2,1)S(1)}, bf16[160,1024]{1,0:T(8,128)(2,1)S(1)}, u32[]{:S(2)}, u32[]{:S(2)}) collective-permute-start(bf16[160,1024]{1,0:T(8,128)(2,1)S(1)} %get-tuple-element.100), channel_id=1, source_target_pairs={{0,48},{1,49},{2,50},{3,51},{4,52},{5,53},{6,54},{7,55},{8,56},{9,... | collective-permute-start | bytes 983048 | tf_op jit(solution)/shard_map/ppermute | solution.py:34
  152.7 10.7 %collective-permute-start.17 = (bf16[160,1024]{1,0:T(8,128)(2,1)S(1)}, bf16[160,1024]{1,0:T(8,128)(2,1)S(1)}, u32[]{:S(2)}, u32[]{:S(2)}) collective-permute-start(bf16[160,1024]{1,0:T(8,128)(2,1)S(1)} %get-tuple-element.99), channel_id=1, source_target_pairs={{0,32},{1,33},{2,34},{3,35},{4,36},{5,37},{6,38},{7,39},{8,40},{9,... | collective-permute-start | bytes 983048 | tf_op jit(solution)/shard_map/ppermute | solution.py:34
  152.7 7.5 %collective-permute-start.18 = (bf16[160,768]{1,0:T(8,128)(2,1)S(1)}, bf16[160,768]{1,0:T(8,128)(2,1)S(1)}, u32[]{:S(2)}, u32[]{:S(2)}) collective-permute-start(bf16[160,768]{1,0:T(8,128)(2,1)S(1)} %pad_maximum_fusion.4), channel_id=1, source_target_pairs={{0,2},{1,3},{2,4},{3,5},{4,6},{5,7},{6,0},{7,1},{8,72},{9,73},{10,... | collective-permute-start | bytes 737288 | tf_op jit(solution)/shard_map/ppermute | solution.py:34
  174.2 7.2 %collective-permute-start.25 = (bf16[80,1024]{1,0:T(8,128)(2,1)S(1)}, bf16[80,1024]{1,0:T(8,128)(2,1)S(1)}, u32[]{:S(2)}, u32[]{:S(2)}) collective-permute-start(bf16[80,1024]{1,0:T(8,128)(2,1)S(1)} %slice.164.refs_0_), channel_id=1, source_target_pairs={{0,48},{1,49},{2,50},{3,51},{4,52},{5,53},{6,54},{7,55},{8,24},{9,... | collective-permute-start | bytes 491528 | tf_op jit(solution)/shard_map/ppermute | solution.py:34
  174.3 10.5 %collective-permute-start.27 = (bf16[80,1024]{1,0:T(8,128)(2,1)S(1)}, bf16[80,1024]{1,0:T(8,128)(2,1)S(1)}, u32[]{:S(2)}, u32[]{:S(2)}) collective-permute-start(bf16[80,1024]{1,0:T(8,128)(2,1)S(1)} %slice.164.refs_0_), channel_id=1, source_target_pairs={{0,32},{1,33},{2,34},{3,35},{4,36},{5,37},{6,38},{7,39},{8,56},{9,... | collective-permute-start | bytes 491528 | tf_op jit(solution)/shard_map/ppermute | solution.py:34
  176.9 11.4 %collective-permute-start.29 = (bf16[80,1024]{1,0:T(8,128)(2,1)S(1)}, bf16[80,1024]{1,0:T(8,128)(2,1)S(1)}, u32[]{:S(2)}, u32[]{:S(2)}) collective-permute-start(bf16[80,1024]{1,0:T(8,128)(2,1)S(1)} %slice.164.refs_0_), channel_id=1, source_target_pairs={{0,64},{1,65},{2,66},{3,67},{4,68},{5,69},{6,70},{7,71},{8,40},{9,... | collective-permute-start | bytes 491528 | tf_op jit(solution)/shard_map/ppermute | solution.py:34
  177.6 10.8 %collective-permute-start.23 = (bf16[80,1024]{1,0:T(8,128)(2,1)S(1)}, bf16[80,1024]{1,0:T(8,128)(2,1)S(1)}, u32[]{:S(2)}, u32[]{:S(2)}) collective-permute-start(bf16[80,1024]{1,0:T(8,128)(2,1)S(1)} %slice.164.refs_0_), channel_id=1, source_target_pairs={{0,8},{1,9},{2,10},{3,11},{4,12},{5,13},{6,14},{7,15},{8,0},{9,1},... | collective-permute-start | bytes 491528 | tf_op jit(solution)/shard_map/ppermute | solution.py:34
  178.8 23.1 %collective-permute-start.31 = (bf16[80,1024]{1,0:T(8,128)(2,1)S(1)}, bf16[80,1024]{1,0:T(8,128)(2,1)S(1)}, u32[]{:S(2)}, u32[]{:S(2)}) collective-permute-start(bf16[80,1024]{1,0:T(8,128)(2,1)S(1)} %collective-permute-done.22.refs_1_), channel_id=1, source_target_pairs={{0,64},{1,65},{2,66},{3,67},{4,68},{5,69},{6,70},{7,71},{8,24},{9,... | collective-permute-start | bytes 491528 | tf_op jit(solution)/shard_map/ppermute | solution.py:34
  181.4 20.5 %collective-permute-start.24 = (bf16[80,1024]{1,0:T(8,128)(2,1)S(1)}, bf16[80,1024]{1,0:T(8,128)(2,1)S(1)}, u32[]{:S(2)}, u32[]{:S(2)}) collective-permute-start(bf16[80,1024]{1,0:T(8,128)(2,1)S(1)} %collective-permute-done.22.refs_1_), channel_id=1, source_target_pairs={{0,8},{1,9},{2,10},{3,11},{4,12},{5,13},{6,14},{7,15},{8,0},{9,1},... | collective-permute-start | bytes 491528 | tf_op jit(solution)/shard_map/ppermute | solution.py:34
  188.3 9.1 %collective-permute-start.35 = (bf16[80,1024]{1,0:T(8,128)(2,1)S(1)}, bf16[80,1024]{1,0:T(8,128)(2,1)S(1)}, u32[]{:S(2)}, u32[]{:S(2)}) collective-permute-start(bf16[80,1024]{1,0:T(8,128)(2,1)S(1)} %get-tuple-element.107), channel_id=1, source_target_pairs={{0,64},{1,65},{2,66},{3,67},{4,68},{5,69},{6,70},{7,71},{8,40},{9,... | collective-permute-start | bytes 491528 | tf_op jit(solution)/shard_map/ppermute | solution.py:34
  188.3 14.1 %collective-permute-start.26 = (bf16[80,1024]{1,0:T(8,128)(2,1)S(1)}, bf16[80,1024]{1,0:T(8,128)(2,1)S(1)}, u32[]{:S(2)}, u32[]{:S(2)}) collective-permute-start(bf16[80,1024]{1,0:T(8,128)(2,1)S(1)} %collective-permute-done.25.refs_2_), channel_id=1, source_target_pairs={{0,8},{1,9},{2,10},{3,11},{4,12},{5,13},{6,14},{7,15},{8,0},{9,1},... | collective-permute-start | bytes 491528 | tf_op jit(solution)/shard_map/ppermute | solution.py:34
  191.0 17.1 %collective-permute-start.28 = (bf16[80,1024]{1,0:T(8,128)(2,1)S(1)}, bf16[80,1024]{1,0:T(8,128)(2,1)S(1)}, u32[]{:S(2)}, u32[]{:S(2)}) collective-permute-start(bf16[80,1024]{1,0:T(8,128)(2,1)S(1)} %collective-permute-done.27.refs_3_), channel_id=1, source_target_pairs={{0,8},{1,9},{2,10},{3,11},{4,12},{5,13},{6,14},{7,15},{8,0},{9,1},... | collective-permute-start | bytes 491528 | tf_op jit(solution)/shard_map/ppermute | solution.py:34
  197.5 10.7 %collective-permute-start.30 = (bf16[80,1024]{1,0:T(8,128)(2,1)S(1)}, bf16[80,1024]{1,0:T(8,128)(2,1)S(1)}, u32[]{:S(2)}, u32[]{:S(2)}) collective-permute-start(bf16[80,1024]{1,0:T(8,128)(2,1)S(1)} %collective-permute-done.29.refs_4_), channel_id=1, source_target_pairs={{0,8},{1,9},{2,10},{3,11},{4,12},{5,13},{6,14},{7,15},{8,0},{9,1},... | collective-permute-start | bytes 491528 | tf_op jit(solution)/shard_map/ppermute | solution.py:34
  (24 other events, 228.3 us)
Sparse Core Ops, SparseCore 0:
  99.0 39.3 reduce-scatter.1
  173.6 47.4 all-gather.1

commit v11 on v10

--- a/solution.py
+++ b/solution.py
@@ -249,23 +249,39 @@
 def place_columns(copy, gathered):
     rows, columns = copy.shape
     width = gathered.shape[1]
-
-    def kernel(copy_ref, gathered_ref, out_ref, semaphore):
-        copy = pltpu.make_async_copy(gathered_ref, out_ref.at[:, pl.ds(0, width)], semaphore.at[0])
-        copy.start()
-        copy.wait()
+    count = 8
+    chunk = rows // count
+
+    def kernel(copy_ref, gathered_ref, out_ref, held, load_semaphores, store_semaphores):
+        loads, stores = [], []
+        for k in range(count):
+            at = pl.ds(k * chunk, chunk)
+            loads.append(pltpu.make_async_copy(gathered_ref.at[at, :], held.at[at, :], load_semaphores.at[k]))
+            target = out_ref.at[at, pl.ds(0, width)]
+            stores.append(pltpu.make_async_copy(held.at[at, :], target, store_semaphores.at[k]))
+        for load in loads:
+            load.start()
+        for load, store in zip(loads, stores):
+            load.wait()
+            store.start()
+        for store in stores:
+            store.wait()
 
     hbm = pl.BlockSpec(memory_space=pltpu.HBM)
     return pl.pallas_call(
         kernel,
-        in_specs=[hbm, VMEM],
+        in_specs=[hbm, hbm],
         out_specs=hbm,
-        scratch_shapes=[pltpu.SemaphoreType.DMA((1,))],
+        scratch_shapes=[
+            pltpu.VMEM((rows, width), jnp.bfloat16),
+            pltpu.SemaphoreType.DMA((count,)),
+            pltpu.SemaphoreType.DMA((count,)),
+        ],
         out_shape=jax.ShapeDtypeStruct((rows, columns), jnp.bfloat16),
         input_output_aliases={0: 0},
-        compiler_params=pltpu.CompilerParams(vmem_limit_bytes=4 * 1024 * 1024),
+        compiler_params=pltpu.CompilerParams(vmem_limit_bytes=12 * 1024 * 1024),
         name="place_columns",
-    )(copy, gathered)
+    )(copy, pltpu.with_memory_space_constraint(gathered, pltpu.HBM))
 
 
 def place_rows(copy, parts, places, rows, columns):

time: 234 us -> 234 us (level)
  Pallas kernels: 33 us -> 35.9 us
  local copies, waits for them, and re-layouts: 9.53 us -> 6.68 us
    pallas_call x1, Pallas kernels: 2.8 us -> 5.67 us  [place_columns(): pl.pallas_call(kernel, in_specs=[hbm, hbm], out_specs=hbm, scratch_shapes...]
    unnamed x34 -> x32, local copies, waits for them, and re-layouts: 7.45 us -> 4.6 us
where the time goes in v11:
time: 234 us
  waiting for transfers between devices  106 us (45%)
  starting transfers between devices  60.6 us (26%)
  Pallas kernels  35.9 us (15%)
  between operations  14.4 us (6%)
  other arithmetic  9.81 us (4%)
  local copies, waits for them, and re-layouts  6.68 us (3%)
    ppermute x37, waiting for transfers between devices, send(): return lax.ppermute(value, AXES, permutation(move))  95 us
    ppermute x37, starting transfers between devices, send(): return lax.ppermute(value, AXES, permutation(move))  60.5 us
    pallas_call x2, Pallas kernels, partial_sums(): pl.pallas_call(kernel, in_specs=[SMEM] + [pl.BlockSpec(memory_space=pltpu...  21.2 us
    all_gather x1, waiting for transfers between devices, body(): gathered = lax.all_gather(fresh[:, :SPLIT], 'inter', axis=0, tiled=True)  11.3 us
    pallas_call x1, Pallas kernels, place_columns(): pl.pallas_call(kernel, in_specs=[hbm, hbm], out_specs=hbm, scratch_shapes...  5.67 us
    pallas_call x1, Pallas kernels, pack(): pl.pallas_call(kernel, in_specs=[SMEM, VMEM, VMEM], out_specs=[VMEM] * 4,...  5.66 us
  transfers between devices with their start and end apart: 39, of which 20 were waited for; matrix products, arithmetic and copies ran while one was open for 2% of the time, Pallas kernels for 13%

profile of v11, /device:TPU:1, one launch (start us, length us, event | category | flops | bytes accessed | tf_op | source)
XLA Modules:
  0.0 233.6 jit_solution(89950769535709241)
XLA Ops:
  10.1 1.8 collective-permute-done
  13.9 1.7 collective-permute-start.3
  17.0 2.2 collective-permute-done.1.other_ref
  19.2 5.7 %pack_cotangent.1 = (bf16[2560,384]{1,0:T(8,128)(2,1)S(1)}, bf16[2560,384]{1,0:T(8,128)(2,1)S(1)}, bf16[2560,384]{1,0:T(8,128)(2,1)S(1)}, bf16[2560,384]{1,0:T(8,128)(2,1)S(1)}) custom-call(s32[4]{0:T(128)S(1)} %pad_add_fusion.where_ref, bf16[192,10240]{1,0:T(8,128)(2,1)} %mine_ref.1, bf16[192,10240]{1,0:T(8,128)(2,1)} %collective-permute-done.1.other_ref), custom_call_target="tpu_custom_call" | custom-call | bytes 15728640 | tf_op jit(solution)/shard_map/pack_cotangent/pallas_call | solution.py:86
  26.2 6.8 %collective-permute-done.3.refs_6_ = bf16[384,1024]{1,0:T(8,128)(2,1)S(1)} collective-permute-done((bf16[384,1024]{1,0:T(8,128)(2,1)S(1)}, bf16[384,1024]{1,0:T(8,128)(2,1)S(1)}, u32[]{:S(2)}, u32[]{:S(2)}) %collective-permute-start.3) | collective-permute-done | bytes 786464 | tf_op jit(solution)/shard_map/ppermute | solution.py:34
  36.2 1.8 collective-permute-start.6
  39.6 20.7 %collective-permute-done.5.refs_1_ = bf16[2560,384]{1,0:T(8,128)(2,1)S(1)} collective-permute-done((bf16[2560,384]{1,0:T(8,128)(2,1)S(1)}, bf16[2560,384]{1,0:T(8,128)(2,1)S(1)}, u32[]{:S(2)}, u32[]{:S(2)}) %collective-permute-start.5) | collective-permute-done | bytes 1966112 | tf_op jit(solution)/shard_map/ppermute | solution.py:34
  60.3 20.3 %collective-permute-done.6.refs_2_ = bf16[2560,384]{1,0:T(8,128)(2,1)S(1)} collective-permute-done((bf16[2560,384]{1,0:T(8,128)(2,1)S(1)}, bf16[2560,384]{1,0:T(8,128)(2,1)S(1)}, u32[]{:S(2)}, u32[]{:S(2)}) %collective-permute-start.6) | collective-permute-done | bytes 1966112 | tf_op jit(solution)/shard_map/ppermute | solution.py:34
  82.6 2.2 collective-permute-start.8
  85.3 10.9 %partial_sums.2 = bf16[4,4,160,1024]{3,2,1,0:T(8,128)(2,1)S(1)} custom-call(s32[4]{0:T(128)S(1)} %pad_add_fusion.where_ref, bf16[2560,384]{1,0:T(8,128)(2,1)} %copy-done.1, bf16[2560,384]{1,0:T(8,128)(2,1)} %copy-done.13, bf16[2560,384]{1,0:T(8,128)(2,1)} %copy-done.14, bf16[2560,384]{1,0:T(8,128)(2,1)} %copy-done.15, bf16[384,1024]{1,0:T(8,128)(2,1)S(1)} %slice.116.refs_4_, ...), custom_call_target="tpu_custom_call" | custom-call | flops 8053063680 | bytes 16252928 | tf_op jit(solution)/shard_map/partial_sums/pallas_call | solution.py:161
  96.2 2.3 %copy-done = bf16[4,4,160,1024]{3,2,1,0:T(8,128)(2,1)} copy-done((bf16[4,4,160,1024]{3,2,1,0:T(8,128)(2,1)}, bf16[4,4,160,1024]{3,2,1,0:T(8,128)(2,1)S(1)}, u32[]{:S(2)}) %copy-start) | copy-done | bytes 5242904
  98.9 10.3 %partial_sums.3 = (bf16[2,4,80,768]{3,2,1,0:T(8,128)(2,1)S(1)}, bf16[2,4,80,768]{3,2,1,0:T(8,128)(2,1)S(1)}, bf16[4,80,768]{2,1,0:T(8,128)(2,1)S(1)}, bf16[4,80,...) custom-call(s32[4]{0:T(128)S(1)} %pad_add_fusion.where_ref, bf16[2560,384]{1,0:T(8,128)(2,1)} %copy-done.1, ...), custom_call_target="tpu_custom_call" | custom-call | flops 6039797760 | bytes 14155776 | tf_op jit(solution)/shard_map/partial_sums/pallas_call | solution.py:161
  109.2 2.9 %collective-permute-start.13 = (bf16[2,4,80,768]{3,2,1,0:T(8,128)(2,1)S(1)}, bf16[2,4,80,768]{3,2,1,0:T(8,128)(2,1)S(1)}, u32[]{:S(2)}, u32[]{:S(2)}) collective-permute-start(bf16[2,4,80,768]{3,2,1,0:T(8,128)(2,1)S(1)} %get-tuple-element.69), channel_id=1, source_target_pairs={{0,48},{1,49},{2,50},{3,51},{4,52},{5,53},{6,54},{7,55},{8,56},{9,... | collective-permute-start | bytes 2949128 | tf_op jit(solution)/shard_map/ppermute | solution.py:34
  112.1 16.8 %collective-permute-done.13 = bf16[2,4,80,768]{3,2,1,0:T(8,128)(2,1)S(1)} collective-permute-done((bf16[2,4,80,768]{3,2,1,0:T(8,128)(2,1)S(1)}, bf16[2,4,80,768]{3,2,1,0:T(8,128)(2,1)S(1)}, u32[]{:S(2)}, u32[]{:S(2)}) %collective-permute-start.13) | collective-permute-done | bytes 983072 | tf_op jit(solution)/shard_map/ppermute | solution.py:34
  129.1 3.6 %collective-permute-start.14 = (bf16[4,80,768]{2,1,0:T(8,128)(2,1)S(1)}, bf16[4,80,768]{2,1,0:T(8,128)(2,1)S(1)}, u32[]{:S(2)}, u32[]{:S(2)}) collective-permute-start(bf16[4,80,768]{2,1,0:T(8,128)(2,1)S(1)} %fusion.7), channel_id=1, source_target_pairs={{0,48},{1,49},{2,50},{3,51},{4,52},{5,53},{6,54},{7,55},{8,56},{9,... | collective-permute-start | bytes 1474568 | tf_op jit(solution)/shard_map/ppermute | solution.py:34
  132.9 6.1 %collective-permute-done.14 = bf16[4,80,768]{2,1,0:T(8,128)(2,1)S(1)} collective-permute-done((bf16[4,80,768]{2,1,0:T(8,128)(2,1)S(1)}, bf16[4,80,768]{2,1,0:T(8,128)(2,1)S(1)}, u32[]{:S(2)}, u32[]{:S(2)}) %collective-permute-start.14) | collective-permute-done | bytes 491552 | tf_op jit(solution)/shard_map/ppermute | solution.py:34
  139.0 3.2 %collective-permute-done.12 = bf16[4,80,768]{2,1,0:T(8,128)(2,1)} collective-permute-done((bf16[4,80,768]{2,1,0:T(8,128)(2,1)S(1)}, bf16[4,80,768]{2,1,0:T(8,128)(2,1)}, u32[]{:S(2)}, u32[]{:S(2)}) %collective-permute-start.12) | collective-permute-done | bytes 491552 | tf_op jit(solution)/shard_map/ppermute | solution.py:34
  143.7 5.2 %collective-permute-start.20 = (bf16[160,768]{1,0:T(8,128)(2,1)S(1)}, bf16[160,768]{1,0:T(8,128)(2,1)S(1)}, u32[]{:S(2)}, u32[]{:S(2)}) collective-permute-start(bf16[160,768]{1,0:T(8,128)(2,1)S(1)} %pad_maximum_fusion.6), channel_id=1, source_target_pairs={{0,4},{1,5},{2,6},{3,7},{4,0},{5,1},{6,2},{7,3},{8,9},{9,8},{10,11... | collective-permute-start | bytes 737288 | tf_op jit(solution)/shard_map/ppermute | solution.py:34
  150.0 2.7 %collective-permute-start.16 = (bf16[160,1024]{1,0:T(8,128)(2,1)S(1)}, bf16[160,1024]{1,0:T(8,128)(2,1)S(1)}, u32[]{:S(2)}, u32[]{:S(2)}) collective-permute-start(bf16[160,1024]{1,0:T(8,128)(2,1)S(1)} %get-tuple-element.100), channel_id=1, source_target_pairs={{0,48},{1,49},{2,50},{3,51},{4,52},{5,53},{6,54},{7,55},{8,56},{9,... | collective-permute-start | bytes 983048 | tf_op jit(solution)/shard_map/ppermute | solution.py:34
  154.0 2.8 %collective-permute-done.19 = bf16[160,768]{1,0:T(8,128)(2,1)S(1)} collective-permute-done((bf16[160,768]{1,0:T(8,128)(2,1)S(1)}, bf16[160,768]{1,0:T(8,128)(2,1)S(1)}, u32[]{:S(2)}, u32[]{:S(2)}) %collective-permute-start.19) | collective-permute-done | bytes 245792 | tf_op jit(solution)/shard_map/ppermute | solution.py:34
  156.8 3.4 %collective-permute-done.18 = bf16[160,768]{1,0:T(8,128)(2,1)S(1)} collective-permute-done((bf16[160,768]{1,0:T(8,128)(2,1)S(1)}, bf16[160,768]{1,0:T(8,128)(2,1)S(1)}, u32[]{:S(2)}, u32[]{:S(2)}) %collective-permute-start.18) | collective-permute-done | bytes 245792 | tf_op jit(solution)/shard_map/ppermute | solution.py:34
  160.4 3.0 %collective-permute-done.17 = bf16[160,1024]{1,0:T(8,128)(2,1)S(1)} collective-permute-done((bf16[160,1024]{1,0:T(8,128)(2,1)S(1)}, bf16[160,1024]{1,0:T(8,128)(2,1)S(1)}, u32[]{:S(2)}, u32[]{:S(2)}) %collective-permute-start.17) | collective-permute-done | bytes 327712 | tf_op jit(solution)/shard_map/ppermute | solution.py:34
  163.8 5.6 %collective-permute-start.21 = (bf16[80,1792]{1,0:T(8,128)(2,1)S(1)}, bf16[80,1792]{1,0:T(8,128)(2,1)S(1)}, u32[]{:S(2)}, u32[]{:S(2)}) collective-permute-start(bf16[80,1792]{1,0:T(8,128)(2,1)S(1)} %broadcast_select_fusion.4), channel_id=1, source_target_pairs={{0,8},{1,9},{2,10},{3,11},{4,12},{5,13},{6,14},{7,15},{8,0},{9,1},... | collective-permute-start | bytes 860168 | tf_op jit(solution)/shard_map/ppermute | solution.py:34
  170.8 1.9 convert_multiply_fusion
  174.3 2.6 %collective-permute-start.27 = (bf16[80,1024]{1,0:T(8,128)(2,1)S(1)}, bf16[80,1024]{1,0:T(8,128)(2,1)S(1)}, u32[]{:S(2)}, u32[]{:S(2)}) collective-permute-start(bf16[80,1024]{1,0:T(8,128)(2,1)S(1)} %slice.164.refs_0_), channel_id=1, source_target_pairs={{0,32},{1,33},{2,34},{3,35},{4,36},{5,37},{6,38},{7,39},{8,56},{9,... | collective-permute-start | bytes 491528 | tf_op jit(solution)/shard_map/ppermute | solution.py:34
  181.4 3.4 %collective-permute-start.24 = (bf16[80,1024]{1,0:T(8,128)(2,1)S(1)}, bf16[80,1024]{1,0:T(8,128)(2,1)S(1)}, u32[]{:S(2)}, u32[]{:S(2)}) collective-permute-start(bf16[80,1024]{1,0:T(8,128)(2,1)S(1)} %collective-permute-done.22.refs_1_), channel_id=1, source_target_pairs={{0,8},{1,9},{2,10},{3,11},{4,12},{5,13},{6,14},{7,15},{8,0},{9,1},... | collective-permute-start | bytes 491528 | tf_op jit(solution)/shard_map/ppermute | solution.py:34
  184.9 3.5 %collective-permute-start.33 = (bf16[80,1024]{1,0:T(8,128)(2,1)S(1)}, bf16[80,1024]{1,0:T(8,128)(2,1)S(1)}, u32[]{:S(2)}, u32[]{:S(2)}) collective-permute-start(bf16[80,1024]{1,0:T(8,128)(2,1)S(1)} %get-tuple-element.108), channel_id=1, source_target_pairs={{0,64},{1,65},{2,66},{3,67},{4,68},{5,69},{6,70},{7,71},{8,56},{9,... | collective-permute-start | bytes 491528 | tf_op jit(solution)/shard_map/ppermute | solution.py:34
  191.0 5.6 %collective-permute-start.28 = (bf16[80,1024]{1,0:T(8,128)(2,1)S(1)}, bf16[80,1024]{1,0:T(8,128)(2,1)S(1)}, u32[]{:S(2)}, u32[]{:S(2)}) collective-permute-start(bf16[80,1024]{1,0:T(8,128)(2,1)S(1)} %collective-permute-done.27.refs_3_), channel_id=1, source_target_pairs={{0,8},{1,9},{2,10},{3,11},{4,12},{5,13},{6,14},{7,15},{8,0},{9,1},... | collective-permute-start | bytes 491528 | tf_op jit(solution)/shard_map/ppermute | solution.py:34
  197.5 4.4 %collective-permute-start.30 = (bf16[80,1024]{1,0:T(8,128)(2,1)S(1)}, bf16[80,1024]{1,0:T(8,128)(2,1)S(1)}, u32[]{:S(2)}, u32[]{:S(2)}) collective-permute-start(bf16[80,1024]{1,0:T(8,128)(2,1)S(1)} %collective-permute-done.29.refs_4_), channel_id=1, source_target_pairs={{0,8},{1,9},{2,10},{3,11},{4,12},{5,13},{6,14},{7,15},{8,0},{9,1},... | collective-permute-start | bytes 491528 | tf_op jit(solution)/shard_map/ppermute | solution.py:34
  202.5 4.0 %multiply_subtract_fusion = (f32[80,3584]{1,0:T(8,128)}, f32[80,3584]{1,0:T(8,128)}, f32[80,3584]{1,0:T(8,128)}) fusion(f32[80,3584]{1,0:T(8,128)S(1)} %copy-done.5, f32[80,3584]{1,0:T(8,128)} %get-tuple-element.82, f32[80,3584]{1,0:T(8,128)} %param.16, f32[80,3584]{1,0:T(8,128)S(1)} %copy-done.6), kind=kLoop, calls=%fused_computation.9 | loop fusion | flops 4300800 | bytes 8028160 | tf_op jit(solution)/shard_map/sub | solution.py:323
  209.9 11.3 %all-gather.2.cloned.1.call-done.gathered_ref = bf16[1280,2560]{1,0:T(8,128)(2,1)} async-done(((bf16[80,2560]{1,0:T(8,128)(2,1)}), bf16[1280,2560]{1,0:T(8,128)(2,1)}) %all-gather.2.cloned.1.call-update) | async-done | bytes 6553616 | tf_op jit(solution)/shard_map/all_gather | solution.py:374
  221.1 5.7 %place_columns.1 = bf16[1280,3584]{1,0:T(8,128)(2,1)} custom-call(bf16[1280,3584]{1,0:T(8,128)(2,1)} %place_rows.3.copy_ref, bf16[1280,2560]{1,0:T(8,128)(2,1)} %all-gather.2.cloned.1.call-done.gathered_ref), custom_call_target="tpu_custom_call", output_to_operand_aliasing={{}: (0, {})} | custom-call | tf_op jit(solution)/shard_map/place_columns/pallas_call | solution.py:271
  (110 shorter events, 34.9 us)
Async XLA Ops:
  7.2 135.0 %reduce-scatter.2.cloned.1.call-start = ((), (), s32[]{:S(2)}) async-start(), calls=%async_computation.1 | async-start | bytes 6553600 | tf_op jit(solution)/shard_map/reduce_scatter | solution.py:357
  12.0 7.2 %collective-permute-start.1 = (bf16[192,10240]{1,0:T(8,128)(2,1)}, bf16[192,10240]{1,0:T(8,128)(2,1)}, u32[]{:S(2)}, u32[]{:S(2)}) collective-permute-start(bf16[192,10240]{1,0:T(8,128)(2,1)} %mine_ref.1), channel_id=1, source_target_pairs={{0,8},{1,9},{2,10},{3,11},{4,12},{5,13},{6,14},{7,15},{8,0},{9,1},... | collective-permute-start | bytes 11796488 | tf_op jit(solution)/shard_map/ppermute | solution.py:34
  12.6 13.6 %collective-permute-start.2 = (bf16[384,1024]{1,0:T(8,128)(2,1)S(1)}, bf16[384,1024]{1,0:T(8,128)(2,1)S(1)}, u32[]{:S(2)}, u32[]{:S(2)}) collective-permute-start(bf16[384,1024]{1,0:T(8,128)(2,1)S(1)} %slice.116.refs_4_), channel_id=1, source_target_pairs={{0,64},{1,65},{2,66},{3,67},{4,68},{5,69},{6,70},{7,71},{8,10},{9,... | collective-permute-start | bytes 2359304 | tf_op jit(solution)/shard_map/ppermute | solution.py:34
  13.9 19.1 %collective-permute-start.3 = (bf16[384,1024]{1,0:T(8,128)(2,1)S(1)}, bf16[384,1024]{1,0:T(8,128)(2,1)S(1)}, u32[]{:S(2)}, u32[]{:S(2)}) collective-permute-start(bf16[384,1024]{1,0:T(8,128)(2,1)S(1)} %slice.116.refs_4_), channel_id=1, source_target_pairs={{0,65},{1,64},{2,67},{3,66},{4,69},{5,68},{6,71},{7,70},{8,14},{9,... | collective-permute-start | bytes 2359304 | tf_op jit(solution)/shard_map/ppermute | solution.py:34
  15.6 18.8 %collective-permute-start.4 = (bf16[384,1024]{1,0:T(8,128)(2,1)S(1)}, bf16[384,1024]{1,0:T(8,128)(2,1)S(1)}, u32[]{:S(2)}, u32[]{:S(2)}) collective-permute-start(bf16[384,1024]{1,0:T(8,128)(2,1)S(1)} %slice.116.refs_4_), channel_id=1, source_target_pairs={{0,1},{1,0},{2,3},{3,2},{4,5},{5,4},{6,7},{7,6},{8,12},{9,13},{10,... | collective-permute-start | bytes 2359304 | tf_op jit(solution)/shard_map/ppermute | solution.py:34
  35.3 25.0 %collective-permute-start.5 = (bf16[2560,384]{1,0:T(8,128)(2,1)S(1)}, bf16[2560,384]{1,0:T(8,128)(2,1)S(1)}, u32[]{:S(2)}, u32[]{:S(2)}) collective-permute-start(bf16[2560,384]{1,0:T(8,128)(2,1)S(1)} %get-tuple-element.50), channel_id=1, source_target_pairs={{0,64},{1,65},{2,66},{3,67},{4,68},{5,69},{6,70},{7,71},{8,10},{9,... | collective-permute-start | bytes 5898248 | tf_op jit(solution)/shard_map/ppermute | solution.py:34
  36.2 44.5 %collective-permute-start.6 = (bf16[2560,384]{1,0:T(8,128)(2,1)S(1)}, bf16[2560,384]{1,0:T(8,128)(2,1)S(1)}, u32[]{:S(2)}, u32[]{:S(2)}) collective-permute-start(bf16[2560,384]{1,0:T(8,128)(2,1)S(1)} %get-tuple-element.51), channel_id=1, source_target_pairs={{0,65},{1,64},{2,67},{3,66},{4,69},{5,68},{6,71},{7,70},{8,14},{9,... | collective-permute-start | bytes 5898248 | tf_op jit(solution)/shard_map/ppermute | solution.py:34
  38.0 43.8 %collective-permute-start.7 = (bf16[2560,384]{1,0:T(8,128)(2,1)S(1)}, bf16[2560,384]{1,0:T(8,128)(2,1)S(1)}, u32[]{:S(2)}, u32[]{:S(2)}) collective-permute-start(bf16[2560,384]{1,0:T(8,128)(2,1)S(1)} %get-tuple-element.52), channel_id=1, source_target_pairs={{0,1},{1,0},{2,3},{3,2},{4,5},{5,4},{6,7},{7,6},{8,12},{9,13},{10,... | collective-permute-start | bytes 5898248 | tf_op jit(solution)/shard_map/ppermute | solution.py:34
  81.9 16.7 %collective-permute-start.10 = (bf16[384,768]{1,0:T(8,128)(2,1)S(1)}, bf16[384,768]{1,0:T(8,128)(2,1)}, u32[]{:S(2)}, u32[]{:S(2)}) collective-permute-start(bf16[384,768]{1,0:T(8,128)(2,1)S(1)} %slice.117.refs_4_), channel_id=1, source_target_pairs={{0,1},{1,0},{2,3},{3,2},{4,5},{5,4},{6,7},{7,6},{8,12},{9,13},{10,... | collective-permute-start | bytes 1769480 | tf_op jit(solution)/shard_map/ppermute | solution.py:34
  82.6 16.3 %collective-permute-start.8 = (bf16[384,768]{1,0:T(8,128)(2,1)S(1)}, bf16[384,768]{1,0:T(8,128)(2,1)}, u32[]{:S(2)}, u32[]{:S(2)}) collective-permute-start(bf16[384,768]{1,0:T(8,128)(2,1)S(1)} %slice.117.refs_4_), channel_id=1, source_target_pairs={{0,64},{1,65},{2,66},{3,67},{4,68},{5,69},{6,70},{7,71},{8,10},{9,... | collective-permute-start | bytes 1769480 | tf_op jit(solution)/shard_map/ppermute | solution.py:34
  84.7 14.1 %collective-permute-start.9 = (bf16[384,768]{1,0:T(8,128)(2,1)S(1)}, bf16[384,768]{1,0:T(8,128)(2,1)}, u32[]{:S(2)}, u32[]{:S(2)}) collective-permute-start(bf16[384,768]{1,0:T(8,128)(2,1)S(1)} %slice.117.refs_4_), channel_id=1, source_target_pairs={{0,65},{1,64},{2,67},{3,66},{4,69},{5,68},{6,71},{7,70},{8,14},{9,... | collective-permute-start | bytes 1769480 | tf_op jit(solution)/shard_map/ppermute | solution.py:34
  98.8 122.3 %all-gather.2.cloned.1.call-start = ((), (), s32[]{:S(2)}) async-start(), calls=%async_computation.2 | async-start | bytes 6963200 | tf_op jit(solution)/shard_map/all_gather | solution.py:374
  109.2 19.7 %collective-permute-start.13 = (bf16[2,4,80,768]{3,2,1,0:T(8,128)(2,1)S(1)}, bf16[2,4,80,768]{3,2,1,0:T(8,128)(2,1)S(1)}, u32[]{:S(2)}, u32[]{:S(2)}) collective-permute-start(bf16[2,4,80,768]{3,2,1,0:T(8,128)(2,1)S(1)} %get-tuple-element.69), channel_id=1, source_target_pairs={{0,48},{1,49},{2,50},{3,51},{4,52},{5,53},{6,54},{7,55},{8,56},{9,... | collective-permute-start | bytes 2949128 | tf_op jit(solution)/shard_map/ppermute | solution.py:34
  112.1 20.5 %collective-permute-start.11 = (bf16[2,4,80,768]{3,2,1,0:T(8,128)(2,1)S(1)}, bf16[2,4,80,768]{3,2,1,0:T(8,128)(2,1)S(1)}, u32[]{:S(2)}, u32[]{:S(2)}) collective-permute-start(bf16[2,4,80,768]{3,2,1,0:T(8,128)(2,1)S(1)} %get-tuple-element.67), channel_id=1, source_target_pairs={{0,16},{1,17},{2,18},{3,19},{4,20},{5,21},{6,22},{7,23},{8,24},{9,... | collective-permute-start | bytes 2949128 | tf_op jit(solution)/shard_map/ppermute | solution.py:34
  129.1 9.9 %collective-permute-start.14 = (bf16[4,80,768]{2,1,0:T(8,128)(2,1)S(1)}, bf16[4,80,768]{2,1,0:T(8,128)(2,1)S(1)}, u32[]{:S(2)}, u32[]{:S(2)}) collective-permute-start(bf16[4,80,768]{2,1,0:T(8,128)(2,1)S(1)} %fusion.7), channel_id=1, source_target_pairs={{0,48},{1,49},{2,50},{3,51},{4,52},{5,53},{6,54},{7,55},{8,56},{9,... | collective-permute-start | bytes 1474568 | tf_op jit(solution)/shard_map/ppermute | solution.py:34
  132.8 9.4 %collective-permute-start.12 = (bf16[4,80,768]{2,1,0:T(8,128)(2,1)S(1)}, bf16[4,80,768]{2,1,0:T(8,128)(2,1)}, u32[]{:S(2)}, u32[]{:S(2)}) collective-permute-start(bf16[4,80,768]{2,1,0:T(8,128)(2,1)S(1)} %fusion.8), channel_id=1, source_target_pairs={{0,16},{1,17},{2,18},{3,19},{4,20},{5,21},{6,22},{7,23},{8,24},{9,... | collective-permute-start | bytes 1474568 | tf_op jit(solution)/shard_map/ppermute | solution.py:34
  143.7 9.0 %collective-permute-start.20 = (bf16[160,768]{1,0:T(8,128)(2,1)S(1)}, bf16[160,768]{1,0:T(8,128)(2,1)S(1)}, u32[]{:S(2)}, u32[]{:S(2)}) collective-permute-start(bf16[160,768]{1,0:T(8,128)(2,1)S(1)} %pad_maximum_fusion.6), channel_id=1, source_target_pairs={{0,4},{1,5},{2,6},{3,7},{4,0},{5,1},{6,2},{7,3},{8,9},{9,8},{10,11... | collective-permute-start | bytes 737288 | tf_op jit(solution)/shard_map/ppermute | solution.py:34
  148.9 8.0 %collective-permute-start.19 = (bf16[160,768]{1,0:T(8,128)(2,1)S(1)}, bf16[160,768]{1,0:T(8,128)(2,1)S(1)}, u32[]{:S(2)}, u32[]{:S(2)}) collective-permute-start(bf16[160,768]{1,0:T(8,128)(2,1)S(1)} %pad_maximum_fusion.5), channel_id=1, source_target_pairs={{0,6},{1,7},{2,0},{3,1},{4,2},{5,3},{6,4},{7,5},{8,73},{9,72},{10,... | collective-permute-start | bytes 737288 | tf_op jit(solution)/shard_map/ppermute | solution.py:34
  149.9 10.3 %collective-permute-start.15 = (bf16[160,1024]{1,0:T(8,128)(2,1)S(1)}, bf16[160,1024]{1,0:T(8,128)(2,1)S(1)}, u32[]{:S(2)}, u32[]{:S(2)}) collective-permute-start(bf16[160,1024]{1,0:T(8,128)(2,1)S(1)} %get-tuple-element.101), channel_id=1, source_target_pairs={{0,16},{1,17},{2,18},{3,19},{4,20},{5,21},{6,22},{7,23},{8,24},{9,... | collective-permute-start | bytes 983048 | tf_op jit(solution)/shard_map/ppermute | solution.py:34
  150.0 10.4 %collective-permute-start.16 = (bf16[160,1024]{1,0:T(8,128)(2,1)S(1)}, bf16[160,1024]{1,0:T(8,128)(2,1)S(1)}, u32[]{:S(2)}, u32[]{:S(2)}) collective-permute-start(bf16[160,1024]{1,0:T(8,128)(2,1)S(1)} %get-tuple-element.100), channel_id=1, source_target_pairs={{0,48},{1,49},{2,50},{3,51},{4,52},{5,53},{6,54},{7,55},{8,56},{9,... | collective-permute-start | bytes 983048 | tf_op jit(solution)/shard_map/ppermute | solution.py:34
  152.7 10.7 %collective-permute-start.17 = (bf16[160,1024]{1,0:T(8,128)(2,1)S(1)}, bf16[160,1024]{1,0:T(8,128)(2,1)S(1)}, u32[]{:S(2)}, u32[]{:S(2)}) collective-permute-start(bf16[160,1024]{1,0:T(8,128)(2,1)S(1)} %get-tuple-element.99), channel_id=1, source_target_pairs={{0,32},{1,33},{2,34},{3,35},{4,36},{5,37},{6,38},{7,39},{8,40},{9,... | collective-permute-start | bytes 983048 | tf_op jit(solution)/shard_map/ppermute | solution.py:34
  152.7 7.5 %collective-permute-start.18 = (bf16[160,768]{1,0:T(8,128)(2,1)S(1)}, bf16[160,768]{1,0:T(8,128)(2,1)S(1)}, u32[]{:S(2)}, u32[]{:S(2)}) collective-permute-start(bf16[160,768]{1,0:T(8,128)(2,1)S(1)} %pad_maximum_fusion.4), channel_id=1, source_target_pairs={{0,2},{1,3},{2,4},{3,5},{4,6},{5,7},{6,0},{7,1},{8,72},{9,73},{10,... | collective-permute-start | bytes 737288 | tf_op jit(solution)/shard_map/ppermute | solution.py:34
  174.2 7.2 %collective-permute-start.25 = (bf16[80,1024]{1,0:T(8,128)(2,1)S(1)}, bf16[80,1024]{1,0:T(8,128)(2,1)S(1)}, u32[]{:S(2)}, u32[]{:S(2)}) collective-permute-start(bf16[80,1024]{1,0:T(8,128)(2,1)S(1)} %slice.164.refs_0_), channel_id=1, source_target_pairs={{0,48},{1,49},{2,50},{3,51},{4,52},{5,53},{6,54},{7,55},{8,24},{9,... | collective-permute-start | bytes 491528 | tf_op jit(solution)/shard_map/ppermute | solution.py:34
  174.3 10.5 %collective-permute-start.27 = (bf16[80,1024]{1,0:T(8,128)(2,1)S(1)}, bf16[80,1024]{1,0:T(8,128)(2,1)S(1)}, u32[]{:S(2)}, u32[]{:S(2)}) collective-permute-start(bf16[80,1024]{1,0:T(8,128)(2,1)S(1)} %slice.164.refs_0_), channel_id=1, source_target_pairs={{0,32},{1,33},{2,34},{3,35},{4,36},{5,37},{6,38},{7,39},{8,56},{9,... | collective-permute-start | bytes 491528 | tf_op jit(solution)/shard_map/ppermute | solution.py:34
  176.9 11.4 %collective-permute-start.29 = (bf16[80,1024]{1,0:T(8,128)(2,1)S(1)}, bf16[80,1024]{1,0:T(8,128)(2,1)S(1)}, u32[]{:S(2)}, u32[]{:S(2)}) collective-permute-start(bf16[80,1024]{1,0:T(8,128)(2,1)S(1)} %slice.164.refs_0_), channel_id=1, source_target_pairs={{0,64},{1,65},{2,66},{3,67},{4,68},{5,69},{6,70},{7,71},{8,40},{9,... | collective-permute-start | bytes 491528 | tf_op jit(solution)/shard_map/ppermute | solution.py:34
  177.6 10.8 %collective-permute-start.23 = (bf16[80,1024]{1,0:T(8,128)(2,1)S(1)}, bf16[80,1024]{1,0:T(8,128)(2,1)S(1)}, u32[]{:S(2)}, u32[]{:S(2)}) collective-permute-start(bf16[80,1024]{1,0:T(8,128)(2,1)S(1)} %slice.164.refs_0_), channel_id=1, source_target_pairs={{0,8},{1,9},{2,10},{3,11},{4,12},{5,13},{6,14},{7,15},{8,0},{9,1},... | collective-permute-start | bytes 491528 | tf_op jit(solution)/shard_map/ppermute | solution.py:34
  178.8 23.1 %collective-permute-start.31 = (bf16[80,1024]{1,0:T(8,128)(2,1)S(1)}, bf16[80,1024]{1,0:T(8,128)(2,1)S(1)}, u32[]{:S(2)}, u32[]{:S(2)}) collective-permute-start(bf16[80,1024]{1,0:T(8,128)(2,1)S(1)} %collective-permute-done.22.refs_1_), channel_id=1, source_target_pairs={{0,64},{1,65},{2,66},{3,67},{4,68},{5,69},{6,70},{7,71},{8,24},{9,... | collective-permute-start | bytes 491528 | tf_op jit(solution)/shard_map/ppermute | solution.py:34
  181.4 20.5 %collective-permute-start.24 = (bf16[80,1024]{1,0:T(8,128)(2,1)S(1)}, bf16[80,1024]{1,0:T(8,128)(2,1)S(1)}, u32[]{:S(2)}, u32[]{:S(2)}) collective-permute-start(bf16[80,1024]{1,0:T(8,128)(2,1)S(1)} %collective-permute-done.22.refs_1_), channel_id=1, source_target_pairs={{0,8},{1,9},{2,10},{3,11},{4,12},{5,13},{6,14},{7,15},{8,0},{9,1},... | collective-permute-start | bytes 491528 | tf_op jit(solution)/shard_map/ppermute | solution.py:34
  188.3 9.1 %collective-permute-start.35 = (bf16[80,1024]{1,0:T(8,128)(2,1)S(1)}, bf16[80,1024]{1,0:T(8,128)(2,1)S(1)}, u32[]{:S(2)}, u32[]{:S(2)}) collective-permute-start(bf16[80,1024]{1,0:T(8,128)(2,1)S(1)} %get-tuple-element.107), channel_id=1, source_target_pairs={{0,64},{1,65},{2,66},{3,67},{4,68},{5,69},{6,70},{7,71},{8,40},{9,... | collective-permute-start | bytes 491528 | tf_op jit(solution)/shard_map/ppermute | solution.py:34
  188.3 14.1 %collective-permute-start.26 = (bf16[80,1024]{1,0:T(8,128)(2,1)S(1)}, bf16[80,1024]{1,0:T(8,128)(2,1)S(1)}, u32[]{:S(2)}, u32[]{:S(2)}) collective-permute-start(bf16[80,1024]{1,0:T(8,128)(2,1)S(1)} %collective-permute-done.25.refs_2_), channel_id=1, source_target_pairs={{0,8},{1,9},{2,10},{3,11},{4,12},{5,13},{6,14},{7,15},{8,0},{9,1},... | collective-permute-start | bytes 491528 | tf_op jit(solution)/shard_map/ppermute | solution.py:34
  191.0 17.1 %collective-permute-start.28 = (bf16[80,1024]{1,0:T(8,128)(2,1)S(1)}, bf16[80,1024]{1,0:T(8,128)(2,1)S(1)}, u32[]{:S(2)}, u32[]{:S(2)}) collective-permute-start(bf16[80,1024]{1,0:T(8,128)(2,1)S(1)} %collective-permute-done.27.refs_3_), channel_id=1, source_target_pairs={{0,8},{1,9},{2,10},{3,11},{4,12},{5,13},{6,14},{7,15},{8,0},{9,1},... | collective-permute-start | bytes 491528 | tf_op jit(solution)/shard_map/ppermute | solution.py:34
  197.5 10.7 %collective-permute-start.30 = (bf16[80,1024]{1,0:T(8,128)(2,1)S(1)}, bf16[80,1024]{1,0:T(8,128)(2,1)S(1)}, u32[]{:S(2)}, u32[]{:S(2)}) collective-permute-start(bf16[80,1024]{1,0:T(8,128)(2,1)S(1)} %collective-permute-done.29.refs_4_), channel_id=1, source_target_pairs={{0,8},{1,9},{2,10},{3,11},{4,12},{5,13},{6,14},{7,15},{8,0},{9,1},... | collective-permute-start | bytes 491528 | tf_op jit(solution)/shard_map/ppermute | solution.py:34
  (23 other events, 225.4 us)
Sparse Core Ops, SparseCore 0:
  99.0 39.3 reduce-scatter.1
  173.6 47.4 all-gather.1
